TPU v7x, 32 devices: a whole 2x2x4 slice. The times are simulated.
32 devices in a mesh: group: 8 (over z, core), tensor: 4 (over y, x).
Axes of the slice: x: 2, y: 2, z: 4, core: 2. Of those that a mesh axis runs over, the one named last changes fastest.
Arguments:
- hidden_x: bfloat16 [16, 8, 8192], P('group', None, 'tensor'), may hold values from -6 to 6
- base_weight: bfloat16 [2048, 8192], P(None, 'tensor'), may hold values from -0.0625 to 0.0625
- delta_codes: bfloat16 [2048, 8192], P('group', 'tensor'), may hold values from -4 to 4
- delta_scales: bfloat16 [2048, 64], P('group', 'tensor'), may hold values from 0.0019989014 to 0.019897461
- owner_map: int32 [8], replicated, may hold values from 0 to 7, each once
- kv_cache: bfloat16 [16, 1024, 2048], P('group', 'tensor'), may hold values from -6 to 6
- queries: bfloat16 [16, 8, 8192], P('group'), may hold values from -180 to 180
- lengths: int32 [16], P('group'), may hold values from 256 to 1024, as said below
Outputs:
- new_kv: bfloat16 [16, 8, 2048], P('group', None, 'tensor')
- attended: bfloat16 [16, 8, 8192], P('group', None, 'tensor')
Inputs may be any that keep to these rules, and one draw needn't show every extreme that they name: `owner_map`: a permutation of the shard indices. Row r's entries are its first lengths[r] cache positions; some row is full.
All inputs are finite; a program needn't handle non-finite values.
Results may differ from a plain program's by a relative error of at most 0.009.
Values may be sent and summed in bfloat16 or wider, within the bound.
No kernel may reach another device: no remote copies, remote signals or barrier semaphores. Data moves between devices by JAX's collectives and lax.ppermute only.
A program may use at most 64 MiB of HBM per device.

v0:
```python
import jax
import jax.numpy as jnp
from jax import lax
from jax.sharding import PartitionSpec as P

H = 64
KVH = 8
HD = 128


NEGATIVE = -1e30


def joined_2(x, axis, combine):
    everything = jax.tree.map(lambda part: lax.all_gather(part, axis), x)
    initial = jax.tree.map(lambda part: part[0], everything)

    def step(k, so_far):
        return combine(so_far, jax.tree.map(lambda part: part[k], everything))

    return lax.fori_loop(1, lax.axis_size(axis), step, initial)


def dequantize(code_values, block_scales):
    blocks = block_scales.shape[1]
    widened = code_values.astype(jnp.float32).reshape(code_values.shape[0], blocks, -1)
    return (
        (widened * block_scales.astype(jnp.float32)[:, :, None])
        .reshape(code_values.shape[0], -1)
        .astype(jnp.bfloat16)
    )


def combine(left_part, right_part):
    left_peak, left_total, left_sum = left_part
    right_peak, right_total, right_sum = right_part
    joined = jnp.maximum(left_peak, right_peak)
    left_scale = jnp.exp(left_peak - joined)
    right_scale = jnp.exp(right_peak - joined)
    return (
        joined,
        left_total * left_scale + right_total * right_scale,
        left_sum * left_scale[..., None] + right_sum * right_scale[..., None],
    )


def on_device(
    hidden_x, base_weight, delta_codes, delta_scales, owner_map, kv_cache, queries, lengths
):
    score_scale = HD ** (-0.5)
    kv_width = KVH * HD
    per_group = H // KVH
    group_count = lax.axis_size("group")
    tensor_count = lax.axis_size("tensor")
    tensor_place = lax.axis_index("tensor")
    row_count, step_count, local_width = hidden_x.shape
    token_rows = hidden_x.reshape(row_count * step_count, local_width)
    base_part = jnp.einsum("rd,od->ro", token_rows, base_weight, preferred_element_type=jnp.float32)
    codes_all, scales_all = (
        lax.all_gather(delta_codes, "group", axis=0, tiled=True),
        lax.all_gather(delta_scales, "group", axis=0, tiled=True),
    )
    delta_part = jnp.einsum(
        "rd,od->ro",
        token_rows,
        dequantize(codes_all, scales_all),
        preferred_element_type=jnp.float32,
    )
    owner_block = delta_part.shape[1] // group_count
    reorder = (owner_map[:, None] == jnp.arange(group_count, dtype=jnp.int32)[None, :]).astype(
        jnp.float32
    )
    ordered = jnp.einsum(
        "rgo,gb->rbo",
        delta_part.reshape(-1, group_count, owner_block),
        reorder,
        precision=lax.Precision.HIGHEST,
    ).reshape(delta_part.shape)
    summed = lax.psum(base_part + ordered, "tensor")
    new_all = summed.astype(jnp.bfloat16).reshape(row_count, step_count, -1)
    slice_width = new_all.shape[2] // tensor_count
    new_out = lax.dynamic_slice_in_dim(new_all, tensor_place * slice_width, slice_width, 2)
    grouped_query = queries.reshape(row_count, step_count, KVH, per_group, HD)
    cache_keys = kv_cache[:, :, :kv_width].reshape(row_count, -1, KVH, HD)
    cache_values = kv_cache[:, :, kv_width:].reshape(row_count, -1, KVH, HD)
    cache_len = cache_keys.shape[1]
    scores = (
        jnp.einsum(
            "rskgd,rckd->rskgc", grouped_query, cache_keys, preferred_element_type=jnp.float32
        )
        * score_scale
    )
    positions = tensor_place * cache_len + jnp.arange(cache_len, dtype=jnp.int32)
    usable = (positions[None, :] < lengths[:, None])[:, None, None, None, :]
    block_peak = jnp.max(jnp.where(usable, scores, NEGATIVE), axis=-1)
    weights = jnp.where(usable, jnp.exp(scores - block_peak[..., None]), 0.0)
    weight_total = jnp.sum(weights, axis=-1)
    weighted = jnp.einsum(
        "rskgc,rckd->rskgd",
        weights.astype(jnp.bfloat16),
        cache_values,
        preferred_element_type=jnp.float32,
    )
    heads_own = H // tensor_count
    head_start = tensor_place * heads_own
    peak_all, total_all, sum_all = joined_2((block_peak, weight_total, weighted), "tensor", combine)
    peak_own = lax.dynamic_slice_in_dim(
        peak_all.reshape(row_count, step_count, H), head_start, heads_own, 2
    )
    total_own = lax.dynamic_slice_in_dim(
        total_all.reshape(row_count, step_count, H), head_start, heads_own, 2
    )
    sum_own = lax.dynamic_slice_in_dim(
        sum_all.reshape(row_count, step_count, H, HD), head_start, heads_own, 2
    )
    head_ids = head_start + jnp.arange(heads_own, dtype=jnp.int32)
    selector = (head_ids[:, None] // per_group == jnp.arange(KVH, dtype=jnp.int32)[None, :]).astype(
        jnp.bfloat16
    )
    appended = new_all.reshape(row_count, step_count, 2, KVH, HD)
    own_keys = jnp.einsum(
        "rtkd,hk->rthd", appended[:, :, 0], selector, preferred_element_type=jnp.float32
    ).astype(jnp.bfloat16)
    own_values = jnp.einsum(
        "rtkd,hk->rthd", appended[:, :, 1], selector, preferred_element_type=jnp.float32
    ).astype(jnp.bfloat16)
    own_query = lax.dynamic_slice_in_dim(
        queries.reshape(row_count, step_count, H, HD), head_start, heads_own, 2
    )
    near_scores = (
        jnp.einsum("rshd,rthd->rsht", own_query, own_keys, preferred_element_type=jnp.float32)
        * score_scale
    )
    causal = (jnp.arange(step_count)[:, None] >= jnp.arange(step_count)[None, :])[None, :, None, :]
    near_peak = jnp.max(jnp.where(causal, near_scores, NEGATIVE), axis=-1)
    near_weights = jnp.where(causal, jnp.exp(near_scores - near_peak[..., None]), 0.0)
    near_total = jnp.sum(near_weights, axis=-1)
    near_sum = jnp.einsum(
        "rsht,rthd->rshd",
        near_weights.astype(jnp.bfloat16),
        own_values,
        preferred_element_type=jnp.float32,
    )
    joined_peak = jnp.maximum(peak_own, near_peak)
    cache_scale = jnp.exp(peak_own - joined_peak)
    near_scale = jnp.exp(near_peak - joined_peak)
    numerator = sum_own * cache_scale[..., None] + near_sum * near_scale[..., None]
    denominator = total_own * cache_scale + near_total * near_scale
    attended = (
        (numerator / denominator[..., None])
        .astype(jnp.bfloat16)
        .reshape(row_count, step_count, heads_own * HD)
    )
    return (new_out, attended)


def solution(mesh):
    in_specs = (
        P("group", None, "tensor"),
        P(None, "tensor"),
        P("group", "tensor"),
        P("group", "tensor"),
        P(),
        P("group", "tensor", None),
        P("group", None, None),
        P("group"),
    )
    out_specs = (P("group", None, "tensor"), P("group", None, "tensor"))
    return jax.shard_map(
        on_device, mesh=mesh, in_specs=in_specs, out_specs=out_specs, check_vma=False
    )
```

profile of v0, /device:TPU:0, one launch (start us, length us, event | category | flops | bytes accessed | tf_op | source)
XLA Modules:
  0.0 182.9 jit_solution(1539241382402844429)
XLA Ops:
  7.2 0.0 copy-start
  7.2 0.0 copy-start.4
  7.2 0.0 all-gather.8.cloned.1.call-start
  7.3 0.0 copy-start.2
  7.3 1.7 fusion.48
  9.0 0.5 copy.75
  9.5 0.5 copy.76
  10.1 0.0 copy-done.4
  10.1 0.1 broadcast_compare_fusion
  10.1 0.0 copy-done
  10.1 0.4 select_reduce_fusion
  10.5 0.5 convolution_bitcast_fusion
  11.0 0.9 copy.57
  11.9 0.0 all-gather.8.cloned.1.call-update
  11.9 0.0 all-gather.6.cloned.1.call-start
  12.0 0.7 all-gather.6.cloned.1.call-update
  12.7 0.0 copy-done.2
  12.7 15.6 %all_gather.25 = bf16[2048,16]{0,1:T(8,128)(2,1)S(1)} all-gather(bf16[256,16]{0,1:T(8,128)(2,1)S(1)} %copy-done.2), channel_id=1, replica_groups=mesh['group'=8,'tensor'=4] {'group'}, dimensions={0}, use_global_device_ids=true | all-gather | bytes 73728 | tf_op jit(solution)/shard_map/all_gather | solution.py:61
  28.4 0.2 copy.49
  28.6 9.0 %all-gather = f32[8,8,8,8]{3,2,1,0:T(8,128)S(1)} all-gather(f32[2,8,8,8]{3,2,1,0:T(8,128)S(1)} %copy.53), channel_id=2, replica_groups=mesh['group'=8,'tensor'=4] {'tensor'}, dimensions={0}, use_global_device_ids=true | all-gather | bytes 20480 | tf_op jit(solution)/shard_map/all_gather | solution.py:15
  37.6 0.4 fusion.15
  38.0 11.9 %all-gather.1 = f32[8,8,8,8]{3,2,1,0:T(8,128)S(1)} all-gather(f32[2,8,8,8]{3,2,1,0:T(8,128)S(1)} %copy.54), channel_id=3, replica_groups=mesh['group'=8,'tensor'=4] {'tensor'}, dimensions={0}, use_global_device_ids=true | all-gather | bytes 20480 | tf_op jit(solution)/shard_map/all_gather | solution.py:15
  49.9 2.3 %all-gather.8.cloned.1.call-done = f32[8,8,8,8,128]{4,3,2,1,0:T(8,128)} async-done(((f32[2,8,8,8,128]{4,3,2,1,0:T(8,128)}), f32[8,8,8,8,128]{4,3,2,1,0:T(8,128)}) %all-gather.8.cloned.1.call-update) | async-done | bytes 2097168 | tf_op jit(solution)/shard_map/all_gather | solution.py:15
  52.2 1.1 slice.33
  53.3 4.6 %while.19 = (s32[]{:T(128)}, f32[2,8,8,8]{3,2,1,0:T(8,128)S(1)}, f32[2,8,8,8]{3,2,1,0:T(8,128)S(1)}, f32[2,8,8,8,128]{4,3,2,1,0:T(8,128)S(1)}, f32[4,2,8,8,8]{4,...) while((s32[]{:T(128)}, f32[2,8,8,8]{3,2,1,0:T(8,128)S(1)}, ...), condition=%wide.region_4.5_spmd, body=%wide.region_3.4_spmd.sunk | while | flops 399365 | bytes 1613975 | solution.py:21
  53.3 0.1 fusion.57
  53.4 1.4 fusion.58
  54.9 0.1 fusion.57
  54.9 1.4 fusion.58
  56.4 0.1 fusion.57
  56.5 1.4 fusion.58
  57.9 0.3 copy.58
  58.2 0.1 reshape.138
  58.3 0.1 reshape.136
  58.4 0.0 copy-start.1
  58.4 77.5 %all-gather.6.cloned.1.call-done = bf16[2048,2048]{1,0:T(8,128)(2,1)} async-done(((bf16[256,2048]{1,0:T(8,128)(2,1)}), bf16[2048,2048]{1,0:T(8,128)(2,1)}) %all-gather.6.cloned.1.call-update) | async-done | bytes 8388624 | tf_op jit(solution)/shard_map/all_gather | solution.py:60
  135.9 4.6 %mul.132 = f32[2048,16,128]{2,1,0:T(8,128)S(1)} broadcast(f32[2048,16]{1,0:T(8,128)S(1)} %copy.49), dimensions={0,1} | broadcast | bytes 16908288 | tf_op jit(solution)/shard_map/mul | solution.py:28
  140.5 0.0 copy-done.1
  140.5 0.0 copy-start.3
  140.5 8.5 %fusion.4 = f32[2048,16]{0,1:T(8,128)S(1)} fusion(f32[256,8,16,128]{3,2,1,0:T(8,128)S(1)} %bitcast.115, bf16[2048,2048]{1,0:T(8,128)(2,1)} %all-gather.6.cloned.1.call-done, bf16[2,8,2048]{2,1,0:T(8,128)(2,1)S(1)} %copy-done.1), kind=kOutput, calls=%fused_computation.10 | convolution fusion | flops 146800640 | bytes 25362432 | tf_op jit(solution)/shard_map/rd,od->ro/dot_general | solution.py:63
  149.0 0.0 copy-done.3
  149.0 0.2 fusion.35
  149.3 5.6 %convolution_add_fusion = f32[16,2048]{1,0:T(8,128)S(1)} fusion(f32[16,2048]{1,0:T(8,128)S(1)} %bitcast.122, bf16[2048,2048]{1,0:T(8,128)(2,1)} %param.11, bf16[2,8,2048]{2,1,0:T(8,128)(2,1)S(1)} %copy-done.1), kind=kOutput, calls=%fused_computation.11 | convolution fusion | flops 134250496 | bytes 8716288 | tf_op jit(solution)/shard_map/rd,od->ro/dot_general | solution.py:58
  154.9 18.4 %all-reduce.1 = bf16[16,2048]{1,0:T(8,128)(2,1)S(1)} all-reduce(f32[16,2048]{1,0:T(8,128)S(1)} %convolution_add_fusion), channel_id=1, replica_groups=mesh['group'=8,'tensor'=4] {'tensor'}, use_global_device_ids=true, to_apply=%region_0.0 | all-reduce | flops 32768 | bytes 196608 | tf_op jit(solution)/shard_map/psum | solution.py:79
  173.3 0.2 fusion.12
  173.5 0.2 fusion.27
  173.7 0.1 copy.61
  173.8 0.1 fusion.21
  173.9 0.1 fusion.30
  174.0 0.1 copy.65
  174.1 0.2 fusion.13
  174.4 0.1 multiply_add_fusion
  174.4 0.1 copy.67
  174.5 0.1 copy.66
  174.6 0.1 copy.62
  174.7 0.6 constant_dynamic-slice_fusion
  175.3 0.8 fusion.11
  (10 shorter events, 0.2 us)
Async XLA Ops:
  7.2 3.0 %copy-start = (bf16[2,8,8192]{2,1,0:T(8,128)(2,1)S(1)}, bf16[2,8,8192]{2,1,0:T(8,128)(2,1)}, u32[]{:S(2)}) copy-start(bf16[2,8,8192]{2,1,0:T(8,128)(2,1)} %param.16) | copy-start | bytes 786436
  7.2 2.9 %copy-start.4 = (s32[2]{0:T(128)S(1)}, s32[2]{0:T(128)}, u32[]{:S(2)}) copy-start(s32[2]{0:T(128)} %param.17) | copy-start | bytes 28
  7.2 45.0 %all-gather.8.cloned.1.call-start = ((), (), s32[]{:S(2)}) async-start(), calls=%async_computation.1 | async-start | bytes 2621440 | tf_op jit(solution)/shard_map/all_gather | solution.py:15
  7.3 5.5 %copy-start.2 = (bf16[256,16]{0,1:T(8,128)(2,1)S(1)}, bf16[256,16]{0,1:T(8,128)(2,1)}, u32[]{:S(2)}) copy-start(bf16[256,16]{0,1:T(8,128)(2,1)} %param.13) | copy-start | bytes 24580
  11.9 124.0 %all-gather.6.cloned.1.call-start = ((), (), s32[]{:S(2)}) async-start(), calls=%async_computation | async-start | bytes 9437184 | tf_op jit(solution)/shard_map/all_gather | solution.py:60
  58.4 82.1 %copy-start.1 = (bf16[2,8,2048]{2,1,0:T(8,128)(2,1)S(1)}, bf16[2,8,2048]{2,1,0:T(8,128)(2,1)}, u32[]{:S(2)}) copy-start(bf16[2,8,2048]{2,1,0:T(8,128)(2,1)} %param.10) | copy-start | bytes 196612
  140.5 8.5 %copy-start.3 = (s32[8]{0:T(128)S(1)}, s32[8]{0:T(128)}, u32[]{:S(2)}) copy-start(s32[8]{0:T(128)} %param.14) | copy-start | bytes 100
Sparse Core Ops, SparseCore 0:
  12.1 40.1 all-gather.7
  53.8 82.0 all-gather.5
where the time goes:
time: 183 us
  waiting for transfers between devices  80.5 us (44%)
  blocking collectives  54.9 us (30%)
  matrix products  16.6 us (9%)
  between operations  14.3 us (8%)
  local copies, waits for them, and re-layouts  11.2 us (6%)
  other arithmetic  5.3 us (3%)
    all_gather x1, waiting for transfers between devices, on_device(): lax.all_gather(delta_codes, 'group', axis=0, tiled=True)  77.5 us
    all_gather x2, blocking collectives, joined_2(): everything = jax.tree.map(lambda part: lax.all_gather(part, axis), x)  20.9 us
    psum x1, blocking collectives, on_device(): summed = lax.psum(base_part + ordered, 'tensor')  18.4 us
    all_gather x1, blocking collectives, on_device(): lax.all_gather(delta_scales, 'group', axis=0, tiled=True)  15.6 us
    dot_general x1, matrix products, on_device(): jnp.einsum('rd,od->ro', token_rows, dequantize(codes_all, scales_all), pr...  8.46 us
    dot_general x1, matrix products, on_device(): jnp.einsum('rd,od->ro', token_rows, base_weight, preferred_element_type=j...  5.65 us
    mul x1, local copies, waits for them, and re-layouts, dequantize(): widened * block_scales.astype(jnp.float32)[:, :, None]  4.58 us
    add x3, other arithmetic, combine(): left_sum * left_scale[..., None] + right_sum * right_scale[..., None]  4.33 us
  transfers between devices with their start and end apart: 2, of which 2 were waited for; matrix products, arithmetic and copies ran while one was open for 4% of the time, Pallas kernels for 0%

commit v1 on v0

v1 whole, which is shorter than its diff:
```python
import jax
import jax.numpy as jnp
from jax import lax
from jax.sharding import PartitionSpec as P

H = 64
KVH = 8
HD = 128


NEGATIVE = -1e30


def dequantize(code_values, block_scales):
    blocks = block_scales.shape[1]
    widened = code_values.astype(jnp.float32).reshape(code_values.shape[0], blocks, -1)
    return (
        (widened * block_scales.astype(jnp.float32)[:, :, None])
        .reshape(code_values.shape[0], -1)
        .astype(jnp.bfloat16)
    )


def combine(left_part, right_part):
    left_peak, left_total, left_sum = left_part
    right_peak, right_total, right_sum = right_part
    joined = jnp.maximum(left_peak, right_peak)
    left_scale = jnp.exp(left_peak - joined)
    right_scale = jnp.exp(right_peak - joined)
    return (
        joined,
        left_total * left_scale + right_total * right_scale,
        left_sum * left_scale[..., None] + right_sum * right_scale[..., None],
    )


def swap(x, axis, distance):
    if distance == 0:
        return x
    size = lax.axis_size(axis)
    return lax.ppermute(x, axis, [(k, k ^ distance) for k in range(size)])


def on_device(
    hidden_x, base_weight, delta_codes, delta_scales, owner_map, kv_cache, queries, lengths
):
    score_scale = HD ** (-0.5)
    kv_width = KVH * HD
    per_group = H // KVH
    group_count = lax.axis_size("group")
    tensor_count = lax.axis_size("tensor")
    group_place = lax.axis_index("group")
    tensor_place = lax.axis_index("tensor")
    row_count, step_count, local_width = hidden_x.shape
    tokens = row_count * step_count
    owner_block = delta_codes.shape[0]
    out_width = base_weight.shape[0]
    token_rows = hidden_x.reshape(tokens, local_width)

    pairs = group_count // 2
    gathered = jnp.concatenate([swap(token_rows, "group", 2 * d) for d in range(pairs)], axis=0)
    mate_codes = swap(delta_codes, "group", 1)
    mate_scales = swap(delta_scales, "group", 1)

    grouped_query = queries.reshape(row_count, step_count, KVH, per_group, HD)
    cache_keys = kv_cache[:, :, :kv_width].reshape(row_count, -1, KVH, HD)
    cache_values = kv_cache[:, :, kv_width:].reshape(row_count, -1, KVH, HD)
    cache_len = cache_keys.shape[1]
    scores = (
        jnp.einsum(
            "rskgd,rckd->rskgc", grouped_query, cache_keys, preferred_element_type=jnp.float32
        )
        * score_scale
    )
    positions = tensor_place * cache_len + jnp.arange(cache_len, dtype=jnp.int32)
    usable = (positions[None, :] < lengths[:, None])[:, None, None, None, :]
    block_peak = jnp.max(jnp.where(usable, scores, NEGATIVE), axis=-1)
    weights = jnp.where(usable, jnp.exp(scores - block_peak[..., None]), 0.0)
    weight_total = jnp.sum(weights, axis=-1)
    weighted = jnp.einsum(
        "rskgc,rckd->rskgd",
        weights.astype(jnp.bfloat16),
        cache_values,
        preferred_element_type=jnp.float32,
    )
    heads_own = H // tensor_count
    stats = jnp.stack([block_peak, weight_total], axis=0).reshape(2, row_count, step_count, H)
    sums = weighted.reshape(row_count, step_count, H, HD)
    parts = None
    for dt in range(tensor_count):
        head_to = (tensor_place ^ dt) * heads_own
        stats_part = swap(lax.dynamic_slice_in_dim(stats, head_to, heads_own, 3), "tensor", dt)
        sums_part = swap(lax.dynamic_slice_in_dim(sums, head_to, heads_own, 2), "tensor", dt)
        part = (stats_part[0], stats_part[1], sums_part)
        parts = part if parts is None else combine(parts, part)
    peak_own, total_own, sum_own = parts

    own = lax.dot_general(
        gathered,
        dequantize(delta_codes, delta_scales),
        (((1,), (1,)), ((), ())),
        preferred_element_type=jnp.float32,
    )
    mate = lax.dot_general(
        gathered,
        dequantize(mate_codes, mate_scales),
        (((1,), (1,)), ((), ())),
        preferred_element_type=jnp.float32,
    )
    both = []
    for k, part in enumerate((own, mate)):
        block = owner_map[group_place ^ k]
        base_rows = lax.dynamic_slice_in_dim(base_weight, block * owner_block, owner_block, 0)
        both.append(
            part
            + lax.dot_general(
                gathered,
                base_rows,
                (((1,), (1,)), ((), ())),
                preferred_element_type=jnp.float32,
            )
        )
    partial = jnp.stack(both, axis=1).reshape(pairs, tokens, 2, owner_block)
    arrived = jnp.stack([swap(partial[d], "group", 2 * d) for d in range(pairs)], axis=0)
    blocks = arrived.transpose(0, 2, 1, 3).reshape(group_count, tokens, owner_block)
    shard_of = jnp.zeros((group_count,), jnp.int32).at[owner_map].set(
        jnp.arange(group_count, dtype=jnp.int32)
    )
    ordered = (
        jnp.take(blocks, shard_of ^ group_place, axis=0)
        .transpose(1, 0, 2)
        .reshape(tokens, out_width)
    )

    slice_width = out_width // tensor_count
    near_heads = max(1, heads_own // per_group)
    near_width = near_heads * HD
    summed = None
    for dt in range(tensor_count):
        to = tensor_place ^ dt
        near_start = (to * heads_own // per_group) * HD
        piece = jnp.concatenate(
            [
                lax.dynamic_slice_in_dim(ordered, near_start, near_width, 1),
                lax.dynamic_slice_in_dim(ordered, kv_width + near_start, near_width, 1),
                lax.dynamic_slice_in_dim(ordered, to * slice_width, slice_width, 1),
            ],
            axis=1,
        )
        piece = swap(piece, "tensor", dt)
        summed = piece if summed is None else summed + piece
    stored = summed.astype(jnp.bfloat16).reshape(row_count, step_count, -1)
    new_out = stored[:, :, 2 * near_width :]
    new_keys = stored[:, :, :near_width].reshape(row_count, step_count, near_heads, HD)
    new_values = stored[:, :, near_width : 2 * near_width].reshape(
        row_count, step_count, near_heads, HD
    )
    own_query = lax.dynamic_slice_in_dim(
        queries.reshape(row_count, step_count, H, HD), tensor_place * heads_own, heads_own, 2
    ).reshape(row_count, step_count, near_heads, -1, HD)
    near_scores = (
        jnp.einsum("rskgd,rtkd->rskgt", own_query, new_keys, preferred_element_type=jnp.float32)
        * score_scale
    )
    causal = (jnp.arange(step_count)[:, None] >= jnp.arange(step_count)[None, :])[
        None, :, None, None, :
    ]
    near_peak = jnp.max(jnp.where(causal, near_scores, NEGATIVE), axis=-1)
    near_weights = jnp.where(causal, jnp.exp(near_scores - near_peak[..., None]), 0.0)
    near_total = jnp.sum(near_weights, axis=-1)
    near_sum = jnp.einsum(
        "rskgt,rtkd->rskgd",
        near_weights.astype(jnp.bfloat16),
        new_values,
        preferred_element_type=jnp.float32,
    )
    shape = (row_count, step_count, heads_own)
    _, denominator, numerator = combine(
        (peak_own, total_own, sum_own),
        (near_peak.reshape(shape), near_total.reshape(shape), near_sum.reshape(shape + (HD,))),
    )
    attended = (
        (numerator / denominator[..., None])
        .astype(jnp.bfloat16)
        .reshape(row_count, step_count, heads_own * HD)
    )
    return (new_out, attended)


def solution(mesh):
    in_specs = (
        P("group", None, "tensor"),
        P(None, "tensor"),
        P("group", "tensor"),
        P("group", "tensor"),
        P(),
        P("group", "tensor", None),
        P("group", None, None),
        P("group"),
    )
    out_specs = (P("group", None, "tensor"), P("group", None, "tensor"))
    return jax.shard_map(
        on_device, mesh=mesh, in_specs=in_specs, out_specs=out_specs, check_vma=False
    )
```

time: 183 us -> 50.1 us (0.27)
  waiting for transfers between devices: 80.5 us -> 5.55 us
  blocking collectives: 54.9 us -> 0 us
  starting transfers between devices: 0.08 us -> 23.1 us
  between operations: 14.3 us -> 2.43 us
  matrix products: 16.6 us -> 8.86 us
  other arithmetic: 5.3 us -> 1.97 us
  local copies, waits for them, and re-layouts: 11.2 us -> 7.89 us
    all_gather x2 -> x0, waiting for transfers between devices: 79.8 us -> none  [the longest x1 77.5 us: on_device(): lax.all_gather(delta_codes, 'group', axis=0, tiled=True)]
    all_gather x3 -> x0, blocking collectives: 36.5 us -> none  [the longest x2 20.9 us: joined_2(): everything = jax.tree.map(lambda part: lax.all_gather(part, axis), x)]
    ppermute x0 -> x17, starting transfers between devices: none -> 23.1 us  [swap(): return lax.ppermute(x, axis, [(k, k ^ distance) for k in range(size)])]
    psum x1 -> x0, blocking collectives: 18.4 us -> none  [on_device(): summed = lax.psum(base_part + ordered, 'tensor')]
    dot_general x7 -> x6, matrix products: 15.7 us -> 7 us  [the longest x2 3.45 us: on_device(): lax.dot_general(gathered, base_rows, (((1,), (1,)), ((), ())), preferred_...]
    ppermute x0 -> x17, waiting for transfers between devices: none -> 5.55 us  [swap(): return lax.ppermute(x, axis, [(k, k ^ distance) for k in range(size)])]
    add x4 -> x0, other arithmetic: 4.41 us -> none  [the longest x3 4.33 us: combine(): left_sum * left_scale[..., None] + right_sum * right_scale[..., None]]
    mul x1 -> x2, local copies, waits for them, and re-layouts: 4.58 us -> 1.21 us  [dequantize(): widened * block_scales.astype(jnp.float32)[:, :, None]]
  transfers between devices with their start and end apart: 2 -> 17, of which waited for: 2 -> 5; matrix products, arithmetic and copies ran while one was open for 4% -> 35% of each run, Pallas kernels for 0% -> 0%
where the time goes in v1:
time: 50.1 us; the launch traced here: 49.8 us
  starting transfers between devices  23.1 us (46%)
  matrix products  8.86 us (18%)
  local copies, waits for them, and re-layouts  7.89 us (16%)
  waiting for transfers between devices  5.55 us (11%)
  between operations  2.43 us (5%)
  other arithmetic  1.97 us (4%)
    ppermute x17, starting transfers between devices, swap(): return lax.ppermute(x, axis, [(k, k ^ distance) for k in range(size)])  23.1 us
    ppermute x17, waiting for transfers between devices, swap(): return lax.ppermute(x, axis, [(k, k ^ distance) for k in range(size)])  5.55 us
    dot_general x2, matrix products, on_device(): lax.dot_general(gathered, base_rows, (((1,), (1,)), ((), ())), preferred_...  3.45 us
    dot_general x1, matrix products, on_device(): lax.dot_general(gathered, dequantize(mate_codes, mate_scales), (((1,), (1...  2.06 us
    slice x1, local copies, waits for them, and re-layouts, on_device(): cache_keys = kv_cache[:, :, :kv_width].reshape(row_count, -1, KVH, HD)  1.71 us
    dot_general x1, matrix products, on_device(): jnp.einsum('rskgd,rckd->rskgc', grouped_query, cache_keys, preferred_elem...  1.33 us
    mul x2, local copies, waits for them, and re-layouts, dequantize(): widened * block_scales.astype(jnp.float32)[:, :, None]  1.21 us
    unnamed x16, local copies, waits for them, and re-layouts  1.13 us
  transfers between devices with their start and end apart: 17, of which 5 were waited for; matrix products, arithmetic and copies ran while one was open for 35% of the time, Pallas kernels for 0%

profile of v1, /device:TPU:0, one launch (start us, length us, event | category | flops | bytes accessed | tf_op | source)
XLA Modules:
  0.0 49.8 jit_solution(2059629702459816774)
XLA Ops:
  0.6 5.1 %collective-permute-start.2 = (bf16[16,2048]{1,0:T(8,128)(2,1)}, bf16[16,2048]{1,0:T(8,128)(2,1)S(1)}, u32[]{:S(2)}, u32[]{:S(2)}) collective-permute-start(bf16[16,2048]{1,0:T(8,128)(2,1)} %bitcast.183), channel_id=1, source_target_pairs={{0,24},{4,28},{8,16},{12,20},{16,8},{20,12},{24,0},{28,4},{1,25},{... | collective-permute-start | bytes 196616 | tf_op jit(solution)/shard_map/ppermute | solution.py:41
  5.7 0.0 collective-permute-start.1
  5.7 0.6 %collective-permute-start = (bf16[16,2048]{1,0:T(8,128)(2,1)}, bf16[16,2048]{1,0:T(8,128)(2,1)S(1)}, u32[]{:S(2)}, u32[]{:S(2)}) collective-permute-start(bf16[16,2048]{1,0:T(8,128)(2,1)} %bitcast.185), channel_id=1, source_target_pairs={{0,8},{4,12},{8,0},{12,4},{16,24},{20,28},{24,16},{28,20},{1,9},{5... | collective-permute-start | bytes 196616 | tf_op jit(solution)/shard_map/ppermute | solution.py:41
  6.4 0.0 collective-permute-start.4
  6.4 0.5 %collective-permute-start.3 = (bf16[256,2048]{1,0:T(8,128)(2,1)}, bf16[256,2048]{1,0:T(8,128)(2,1)}, u32[]{:S(2)}, u32[]{:S(2)}) collective-permute-start(bf16[256,2048]{1,0:T(8,128)(2,1)} %param.10), channel_id=1, source_target_pairs={{0,4},{4,0},{8,12},{12,8},{16,20},{20,16},{24,28},{28,24},{1,5},{5... | collective-permute-start | bytes 3145736 | tf_op jit(solution)/shard_map/ppermute | solution.py:41
  6.9 0.7 %compare_select_fusion.1 = s32[8]{0:T(128)S(1)} fusion(s32[8]{0:T(128)} %param.12), kind=kLoop, calls=%fused_computation.124 | loop fusion | flops 24 | bytes 64 | tf_op jit(solution)/shard_map/select_n | solution.py:126
  7.6 1.7 %fusion.62 = (bf16[2,256,1024]{2,1,0:T(8,128)(2,1)S(1)}, bf16[2,256,1024]{2,1,0:T(8,128)(2,1)S(1)}) fusion(bf16[2,256,2048]{2,1,0:T(8,128)(2,1)} %param.13), kind=kLoop, calls=%fused_computation.132 | loop fusion | bytes 4194304 | tf_op jit(solution)/shard_map/slice | solution.py:66
  9.3 0.0 copy-start.5
  9.3 0.5 %copy.81 = bf16[2,256,1024]{1,2,0:T(8,128)(2,1)S(1)} copy(bf16[2,256,1024]{2,1,0:T(8,128)(2,1)S(1)} %get-tuple-element.16) | data formatting | bytes 2097152
  9.8 0.5 %copy.80 = bf16[2,256,1024]{1,2,0:T(8,128)(2,1)S(1)} copy(bf16[2,256,1024]{2,1,0:T(8,128)(2,1)S(1)} %get-tuple-element.15) | data formatting | bytes 2097152
  10.4 0.1 broadcast_compare_fusion
  10.4 1.3 %select_reduce_fusion = (f32[2,8,8,8]{3,1,2,0:T(8,128)S(1)}, f32[2,8,8,8,256]{4,3,1,2,0:T(8,128)S(1)}) fusion(pred[2,256]{1,0:T(4,128)(4,1)S(1)} %broadcast_compare_fusion, bf16[2,256,8,128,1]{1,3,4,2,0:T(8,128)(2,1)S(1)} %bitcast.181, bf16[2,8,8,8,128]{4,1,3,2,0:T(8,128)(2,1)} %bitcast.190), kind=kOutput, calls=%fused_computation.17 | convolution fusion | flops 67894272 | bytes 2363904 | tf_op jit(solution)/shard_map/rskgd,rckd->rskgc/dot_general | solution.py:70
  11.8 0.4 fusion.12
  12.2 0.0 copy-start.3
  12.2 0.0 copy-start.4
  12.2 0.0 copy-start.1
  12.3 0.5 %convolution_bitcast_fusion = f32[2,8,8,8,128]{4,3,1,2,0:T(8,128)S(1)} fusion(bf16[2,256,8,128,1]{1,3,4,2,0:T(8,128)(2,1)S(1)} %bitcast.176, f32[2,8,8,8,256]{4,3,1,2,0:T(8,128)S(1)} %get-tuple-element.44, f32[2,8,8,8]{3,1,2,0:T(8,128)S(1)} %get-tuple-element.43, pred[2,256]{1,0:T(4,128)(4,1)S(1)} %broadcast_compare_fusion), kind=kOutput, calls=%fused_computation.8 | convolution fusion | flops 67895296 | bytes 2626048 | tf_op jit(solution)/shard_map/rskgc,rckd->rskgd/dot_general | solution.py:80
  12.8 0.1 copy.101
  12.8 0.1 stack.37
  13.0 0.1 stack.38
  13.0 0.6 %scatter_custom_fusion = s32[8]{0:T(128)S(1)} fusion(s32[8]{0:T(128)S(1)} %compare_select_fusion.1, s32[8]{0:T(128)S(1)} %iota.23, s32[]{:T(128)} %constant.74.clone.1), kind=kCustom, calls=%fused_computation.128 | custom fusion | bytes 36 | tf_op jit(solution)/shard_map/scatter | solution.py:126
  13.7 0.1 constant_dynamic-slice_fusion.5
  13.9 0.1 copy.55
  14.0 0.6 %fusion.63 = (s32[1]{0:T(128)}, s32[1]{0:T(128)}) fusion(s32[8]{0:T(128)S(1)} %copy-done.4, s32[]{:T(128)S(6)} %select_n.111, s32[]{:T(128)S(6)} %select_n.113), kind=kLoop, calls=%fused_computation.133 | loop fusion | bytes 24 | tf_op jit(solution)/shard_map/dynamic_slice | solution.py:112
  15.9 0.0 collective-permute-done.4
  15.9 2.7 %collective-permute-start.16 = (f32[2,8,16,128]{3,2,1,0:T(8,128)S(1)}, f32[2,8,16,128]{3,2,1,0:T(8,128)S(1)}, u32[]{:S(2)}, u32[]{:S(2)}) collective-permute-start(f32[2,8,16,128]{3,2,1,0:T(8,128)S(1)} %get-tuple-element.18), channel_id=1, source_target_pairs={{0,3},{1,2},{2,1},{3,0},{4,7},{5,6},{6,5},{7,4},{8,11},{9,10},{10,... | collective-permute-start | bytes 393224 | tf_op jit(solution)/shard_map/ppermute | solution.py:41
  18.5 0.1 copy.56
  18.6 0.0 collective-permute-done.2
  18.7 0.6 %collective-permute-start.14 = (f32[2,8,16,128]{3,2,1,0:T(8,128)S(1)}, f32[2,8,16,128]{3,2,1,0:T(8,128)S(1)}, u32[]{:S(2)}, u32[]{:S(2)}) collective-permute-start(f32[2,8,16,128]{3,2,1,0:T(8,128)S(1)} %get-tuple-element.19), channel_id=1, source_target_pairs={{0,2},{1,3},{2,0},{3,1},{4,6},{5,7},{6,4},{7,5},{8,10},{9,11},{10,... | collective-permute-start | bytes 393224 | tf_op jit(solution)/shard_map/ppermute | solution.py:41
  19.2 0.0 collective-permute-done
  19.2 1.7 %fusion.10 = f32[64,256]{1,0:T(8,128)S(1)} fusion(bf16[2048,2048]{1,0:T(8,128)(2,1)} %param.9, s32[]{:T(128)S(6)} %select_n.112, bf16[16,2048]{1,0:T(8,128)(2,1)S(1)} %collective-permute-done.2, bf16[16,2048]{1,0:T(8,128)(2,1)S(1)} %collective-permute-done.1, bf16[16,2048]{1,0:T(8,128)(2,1)S(1)} %collective-permute-done, bf16[16,2048]{1,0:T(8,128)(2,1)S(1)} %bitcast.186), kind=kOutput, calls=%fused_computation.20 | convolution fusion | flops 68157440 | bytes 1376260 | tf_op jit(solution)/shard_map/dot_general | solution.py:116
  20.9 0.0 copy-start
  20.9 1.8 %fusion.8 = f32[64,256]{1,0:T(8,128)S(1)} fusion(bf16[2048,2048]{1,0:T(8,128)(2,1)} %param.9, s32[]{:T(128)S(6)} %select_n.114, bf16[16,2048]{1,0:T(8,128)(2,1)S(1)} %collective-permute-done.2, bf16[16,2048]{1,0:T(8,128)(2,1)S(1)} %collective-permute-done.1, bf16[16,2048]{1,0:T(8,128)(2,1)S(1)} %collective-permute-done, bf16[16,2048]{1,0:T(8,128)(2,1)S(1)} %bitcast.187), kind=kOutput, calls=%fused_computation.18 | convolution fusion | flops 68157440 | bytes 1376260 | tf_op jit(solution)/shard_map/dot_general | solution.py:116
  22.7 0.6 %mul.216 = f32[256,16,128]{2,1,0:T(8,128)S(1)} broadcast(f32[256,16]{1,0:T(8,128)S(1)} %copy.55), dimensions={0,1} | broadcast | bytes 2113536 | tf_op jit(solution)/shard_map/mul | solution.py:18
  23.3 0.8 %fusion.5 = f32[64,1,256]{2,0,1:T(8,128)S(1)} fusion(f32[64,256]{1,0:T(8,128)S(1)} %fusion.10, f32[32,8,16,128]{3,2,1,0:T(8,128)S(1)} %bitcast.175, bf16[256,2048]{1,0:T(8,128)(2,1)S(1)} %copy-done, bf16[16,2048]{1,0:T(8,128)(2,1)S(1)} %collective-permute-done.2, bf16[16,2048]{1,0:T(8,128)(2,1)S(1)} %collective-permute-done.1, ...), kind=kOutput, calls=%fused_computation.15 | convolution fusion | flops 69746688 | bytes 3538944 | tf_op jit(solution)/shard_map/dot_general | solution.py:98
  24.1 0.6 %mul.221 = f32[256,16,128]{2,1,0:T(8,128)S(1)} broadcast(f32[256,16]{1,0:T(8,128)S(1)} %copy.56), dimensions={0,1} | broadcast | bytes 2113536 | tf_op jit(solution)/shard_map/mul | solution.py:18
  24.7 0.0 copy-start.2
  24.8 2.1 %fusion.4 = f32[64,1,256]{2,0,1:T(8,128)S(1)} fusion(f32[64,256]{1,0:T(8,128)S(1)} %fusion.8, f32[32,8,16,128]{3,2,1,0:T(8,128)S(1)} %bitcast.174, bf16[256,2048]{1,0:T(8,128)(2,1)} %collective-permute-done.3, bf16[16,2048]{1,0:T(8,128)(2,1)S(1)} %collective-permute-done.2, bf16[16,2048]{1,0:T(8,128)(2,1)S(1)} %collective-permute-done.1, ...), kind=kOutput, calls=%fused_computation.13 | convolution fusion | flops 69746688 | bytes 3538944 | tf_op jit(solution)/shard_map/dot_general | solution.py:104
  26.8 3.7 %collective-permute-start.7 = (f32[16,2,256]{2,0,1:T(8,128)S(1)}, f32[16,2,256]{2,0,1:T(8,128)S(1)}, u32[]{:S(2)}, u32[]{:S(2)}) collective-permute-start(f32[16,2,256]{2,0,1:T(8,128)S(1)} %get-tuple-element.34), channel_id=1, source_target_pairs={{0,24},{4,28},{8,16},{12,20},{16,8},{20,12},{24,0},{28,4},{1,25},{... | collective-permute-start | bytes 98312 | tf_op jit(solution)/shard_map/ppermute | solution.py:41
  30.5 0.8 %collective-permute-start.5 = (f32[16,2,256]{2,0,1:T(8,128)S(1)}, f32[16,2,256]{2,0,1:T(8,128)S(1)}, u32[]{:S(2)}, u32[]{:S(2)}) collective-permute-start(f32[16,2,256]{2,0,1:T(8,128)S(1)} %get-tuple-element.33), channel_id=1, source_target_pairs={{0,8},{4,12},{8,0},{12,4},{16,24},{20,28},{24,16},{28,20},{1,9},{5... | collective-permute-start | bytes 98312 | tf_op jit(solution)/shard_map/ppermute | solution.py:41
  31.4 1.2 %collective-permute-done.7 = f32[16,2,256]{2,0,1:T(8,128)S(1)} collective-permute-done((f32[16,2,256]{2,0,1:T(8,128)S(1)}, f32[16,2,256]{2,0,1:T(8,128)S(1)}, u32[]{:S(2)}, u32[]{:S(2)}) %collective-permute-start.7) | collective-permute-done | bytes 32800 | tf_op jit(solution)/shard_map/ppermute | solution.py:41
  32.6 1.5 %collective-permute-start.13 = (f32[2,2,8,16]{3,2,1,0:T(8,128)S(1)}, f32[2,2,8,16]{3,2,1,0:T(8,128)S(1)}, u32[]{:S(2)}, u32[]{:S(2)}) collective-permute-start(f32[2,2,8,16]{3,2,1,0:T(8,128)S(1)} %get-tuple-element.38), channel_id=1, source_target_pairs={{0,2},{1,3},{2,0},{3,1},{4,6},{5,7},{6,4},{7,5},{8,10},{9,11},{10,... | collective-permute-start | bytes 6152 | tf_op jit(solution)/shard_map/ppermute | solution.py:41
  34.2 1.1 %collective-permute-done.6 = f32[16,2,256]{2,0,1:T(8,128)S(1)} collective-permute-done((f32[16,2,256]{2,0,1:T(8,128)S(1)}, f32[16,2,256]{2,0,1:T(8,128)S(1)}, u32[]{:S(2)}, u32[]{:S(2)}) %collective-permute-start.6) | collective-permute-done | bytes 32800 | tf_op jit(solution)/shard_map/ppermute | solution.py:41
  35.3 0.5 %collective-permute-start.11 = (f32[2,2,8,16]{3,2,1,0:T(8,128)S(1)}, f32[2,2,8,16]{3,2,1,0:T(8,128)S(1)}, u32[]{:S(2)}, u32[]{:S(2)}) collective-permute-start(f32[2,2,8,16]{3,2,1,0:T(8,128)S(1)} %get-tuple-element.36), channel_id=1, source_target_pairs={{0,1},{1,0},{2,3},{3,2},{4,5},{5,4},{6,7},{7,6},{8,9},{9,8},{10,11... | collective-permute-start | bytes 6152 | tf_op jit(solution)/shard_map/ppermute | solution.py:41
  35.9 0.6 %gather_fusion = f32[8,16,256]{2,1,0:T(8,128)S(1)} fusion(f32[8,16,256]{2,1,0:T(8,128)S(1)} %bitcast.182, s32[1024]{0:T(1024)S(1)} %pad_clamp_fusion), kind=kCustom, calls=%fused_computation | custom fusion | bytes 262176 | tf_op jit(solution)/shard_map/jit(_take)/gather | solution.py:130
  36.4 0.1 select_bitcast_fusion
  36.6 2.5 %collective-permute-start.10 = (f32[16,1024]{1,0:T(8,128)S(1)}, f32[16,1024]{1,0:T(8,128)S(1)}, u32[]{:S(2)}, u32[]{:S(2)}) collective-permute-start(f32[16,1024]{1,0:T(8,128)S(1)} %pad_maximum_fusion.4), channel_id=1, source_target_pairs={{0,3},{1,2},{2,1},{3,0},{4,7},{5,6},{6,5},{7,4},{8,11},{9,10},{10,... | collective-permute-start | bytes 196616 | tf_op jit(solution)/shard_map/ppermute | solution.py:41
  39.2 0.6 %collective-permute-start.9 = (f32[16,1024]{1,0:T(8,128)S(1)}, f32[16,1024]{1,0:T(8,128)S(1)}, u32[]{:S(2)}, u32[]{:S(2)}) collective-permute-start(f32[16,1024]{1,0:T(8,128)S(1)} %pad_maximum_fusion.3), channel_id=1, source_target_pairs={{0,2},{1,3},{2,0},{3,1},{4,6},{5,7},{6,4},{7,5},{8,10},{9,11},{10,... | collective-permute-start | bytes 196616 | tf_op jit(solution)/shard_map/ppermute | solution.py:41
  39.7 0.5 %collective-permute-start.8 = (f32[16,1024]{1,0:T(8,128)S(1)}, f32[16,1024]{1,0:T(8,128)S(1)}, u32[]{:S(2)}, u32[]{:S(2)}) collective-permute-start(f32[16,1024]{1,0:T(8,128)S(1)} %pad_maximum_fusion.2), channel_id=1, source_target_pairs={{0,1},{1,0},{2,3},{3,2},{4,5},{5,4},{6,7},{7,6},{8,9},{9,8},{10,11... | collective-permute-start | bytes 196616 | tf_op jit(solution)/shard_map/ppermute | solution.py:41
  40.3 0.1 fusion.51
  40.3 1.5 %collective-permute-done.10 = f32[16,1024]{1,0:T(8,128)S(1)} collective-permute-done((f32[16,1024]{1,0:T(8,128)S(1)}, f32[16,1024]{1,0:T(8,128)S(1)}, u32[]{:S(2)}, u32[]{:S(2)}) %collective-permute-start.10) | collective-permute-done | bytes 65568 | tf_op jit(solution)/shard_map/ppermute | solution.py:41
  41.9 1.5 %collective-permute-start.12 = (f32[2,8,16,128]{3,2,1,0:T(8,128)S(1)}, f32[2,8,16,128]{3,2,1,0:T(8,128)S(1)}, u32[]{:S(2)}, u32[]{:S(2)}) collective-permute-start(f32[2,8,16,128]{3,2,1,0:T(8,128)S(1)} %get-tuple-element.17), channel_id=1, source_target_pairs={{0,1},{1,0},{2,3},{3,2},{4,5},{5,4},{6,7},{7,6},{8,9},{9,8},{10,11... | collective-permute-start | bytes 393224 | tf_op jit(solution)/shard_map/ppermute | solution.py:41
  43.3 0.2 collective-permute-done.9
  43.5 2.0 %collective-permute-start.15 = (f32[2,2,8,16]{3,2,1,0:T(8,128)S(1)}, f32[2,2,8,16]{3,2,1,0:T(8,128)S(1)}, u32[]{:S(2)}, u32[]{:S(2)}) collective-permute-start(f32[2,2,8,16]{3,2,1,0:T(8,128)S(1)} %get-tuple-element.37), channel_id=1, source_target_pairs={{0,3},{1,2},{2,1},{3,0},{4,7},{5,6},{6,5},{7,4},{8,11},{9,10},{10,... | collective-permute-start | bytes 6152 | tf_op jit(solution)/shard_map/ppermute | solution.py:41
  45.6 0.4 select_reduce_fusion.1
  46.0 0.3 convolution_bitcast_fusion.1
  46.3 0.1 fusion.22
  46.4 0.6 %slice.83 = bf16[2,8,512]{2,1,0:T(8,128)(2,1)} slice(bf16[2,8,1024]{2,1,0:T(8,128)(2,1)S(1)} %fusion.32), slice={[0:2], [0:8], [512:1024]} | slice | bytes 32768 | tf_op jit(solution)/shard_map/slice | solution.py:153
  47.0 0.1 reshape.318
  47.1 0.1 reshape.315
  47.2 1.5 %collective-permute-done.15 = f32[2,2,8,16]{3,2,1,0:T(8,128)S(1)} collective-permute-done((f32[2,2,8,16]{3,2,1,0:T(8,128)S(1)}, f32[2,2,8,16]{3,2,1,0:T(8,128)S(1)}, u32[]{:S(2)}, u32[]{:S(2)}) %collective-permute-start.15) | collective-permute-done | bytes 2080 | tf_op jit(solution)/shard_map/ppermute | solution.py:41
  48.7 0.1 fusion.42
  48.8 0.4 fusion.21
  49.2 0.7 %reshape.319 = bf16[2,8,2048]{2,1,0:T(8,128)(2,1)} reshape(bf16[2,8,16,128]{3,2,1,0:T(8,128)(2,1)S(1)} %fusion.21) | data formatting | bytes 131072 | tf_op jit(solution)/shard_map/reshape | solution.py:185
  (38 shorter events, 0.3 us)
Async XLA Ops:
  0.6 18.0 %collective-permute-start.2 = (bf16[16,2048]{1,0:T(8,128)(2,1)}, bf16[16,2048]{1,0:T(8,128)(2,1)S(1)}, u32[]{:S(2)}, u32[]{:S(2)}) collective-permute-start(bf16[16,2048]{1,0:T(8,128)(2,1)} %bitcast.183), channel_id=1, source_target_pairs={{0,24},{4,28},{8,16},{12,20},{16,8},{20,12},{24,0},{28,4},{1,25},{... | collective-permute-start | bytes 196616 | tf_op jit(solution)/shard_map/ppermute | solution.py:41
  5.7 13.5 %collective-permute-start.1 = (bf16[16,2048]{1,0:T(8,128)(2,1)}, bf16[16,2048]{1,0:T(8,128)(2,1)S(1)}, u32[]{:S(2)}, u32[]{:S(2)}) collective-permute-start(bf16[16,2048]{1,0:T(8,128)(2,1)} %bitcast.184), channel_id=1, source_target_pairs={{0,16},{4,20},{8,24},{12,28},{16,0},{20,4},{24,8},{28,12},{1,17},{... | collective-permute-start | bytes 196616 | tf_op jit(solution)/shard_map/ppermute | solution.py:41
  5.7 13.5 %collective-permute-start = (bf16[16,2048]{1,0:T(8,128)(2,1)}, bf16[16,2048]{1,0:T(8,128)(2,1)S(1)}, u32[]{:S(2)}, u32[]{:S(2)}) collective-permute-start(bf16[16,2048]{1,0:T(8,128)(2,1)} %bitcast.185), channel_id=1, source_target_pairs={{0,8},{4,12},{8,0},{12,4},{16,24},{20,28},{24,16},{28,20},{1,9},{5... | collective-permute-start | bytes 196616 | tf_op jit(solution)/shard_map/ppermute | solution.py:41
  6.4 9.5 %collective-permute-start.4 = (bf16[256,16]{0,1:T(8,128)(2,1)}, bf16[256,16]{0,1:T(8,128)(2,1)S(1)}, u32[]{:S(2)}, u32[]{:S(2)}) collective-permute-start(bf16[256,16]{0,1:T(8,128)(2,1)} %param.11), channel_id=1, source_target_pairs={{0,4},{4,0},{8,12},{12,8},{16,20},{20,16},{24,28},{28,24},{1,5},{5... | collective-permute-start | bytes 24584 | tf_op jit(solution)/shard_map/ppermute | solution.py:41
  6.4 17.7 %collective-permute-start.3 = (bf16[256,2048]{1,0:T(8,128)(2,1)}, bf16[256,2048]{1,0:T(8,128)(2,1)}, u32[]{:S(2)}, u32[]{:S(2)}) collective-permute-start(bf16[256,2048]{1,0:T(8,128)(2,1)} %param.10), channel_id=1, source_target_pairs={{0,4},{4,0},{8,12},{12,8},{16,20},{20,16},{24,28},{28,24},{1,5},{5... | collective-permute-start | bytes 3145736 | tf_op jit(solution)/shard_map/ppermute | solution.py:41
  9.3 1.1 %copy-start.5 = (s32[2]{0:T(128)S(1)}, s32[2]{0:T(128)}, u32[]{:S(2)}) copy-start(s32[2]{0:T(128)} %param.15) | copy-start | bytes 28
  12.2 1.6 %copy-start.3 = (bf16[256,16]{0,1:T(8,128)(2,1)S(1)}, bf16[256,16]{0,1:T(8,128)(2,1)}, u32[]{:S(2)}) copy-start(bf16[256,16]{0,1:T(8,128)(2,1)} %param.11) | copy-start | bytes 24580
  12.2 1.7 %copy-start.4 = (s32[8]{0:T(128)S(1)}, s32[8]{0:T(128)}, u32[]{:S(2)}) copy-start(s32[8]{0:T(128)} %param.12) | copy-start | bytes 100
  12.2 7.0 %copy-start.1 = (bf16[2,8,2048]{2,1,0:T(8,128)(2,1)S(1)}, bf16[2,8,2048]{2,1,0:T(8,128)(2,1)}, u32[]{:S(2)}) copy-start(bf16[2,8,2048]{2,1,0:T(8,128)(2,1)} %param.8) | copy-start | bytes 196612
  15.9 32.9 %collective-permute-start.16 = (f32[2,8,16,128]{3,2,1,0:T(8,128)S(1)}, f32[2,8,16,128]{3,2,1,0:T(8,128)S(1)}, u32[]{:S(2)}, u32[]{:S(2)}) collective-permute-start(f32[2,8,16,128]{3,2,1,0:T(8,128)S(1)} %get-tuple-element.18), channel_id=1, source_target_pairs={{0,3},{1,2},{2,1},{3,0},{4,7},{5,6},{6,5},{7,4},{8,11},{9,10},{10,... | collective-permute-start | bytes 393224 | tf_op jit(solution)/shard_map/ppermute | solution.py:41
  18.7 30.1 %collective-permute-start.14 = (f32[2,8,16,128]{3,2,1,0:T(8,128)S(1)}, f32[2,8,16,128]{3,2,1,0:T(8,128)S(1)}, u32[]{:S(2)}, u32[]{:S(2)}) collective-permute-start(f32[2,8,16,128]{3,2,1,0:T(8,128)S(1)} %get-tuple-element.19), channel_id=1, source_target_pairs={{0,2},{1,3},{2,0},{3,1},{4,6},{5,7},{6,4},{7,5},{8,10},{9,11},{10,... | collective-permute-start | bytes 393224 | tf_op jit(solution)/shard_map/ppermute | solution.py:41
  20.9 2.4 %copy-start = (bf16[256,2048]{1,0:T(8,128)(2,1)S(1)}, bf16[256,2048]{1,0:T(8,128)(2,1)}, u32[]{:S(2)}) copy-start(bf16[256,2048]{1,0:T(8,128)(2,1)} %param.10) | copy-start | bytes 3145732
  24.7 6.6 %copy-start.2 = (bf16[2,8,8192]{2,1,0:T(8,128)(2,1)S(1)}, bf16[2,8,8192]{2,1,0:T(8,128)(2,1)}, u32[]{:S(2)}) copy-start(bf16[2,8,8192]{2,1,0:T(8,128)(2,1)} %param.14) | copy-start | bytes 786436
  26.8 5.8 %collective-permute-start.7 = (f32[16,2,256]{2,0,1:T(8,128)S(1)}, f32[16,2,256]{2,0,1:T(8,128)S(1)}, u32[]{:S(2)}, u32[]{:S(2)}) collective-permute-start(f32[16,2,256]{2,0,1:T(8,128)S(1)} %get-tuple-element.34), channel_id=1, source_target_pairs={{0,24},{4,28},{8,16},{12,20},{16,8},{20,12},{24,0},{28,4},{1,25},{... | collective-permute-start | bytes 98312 | tf_op jit(solution)/shard_map/ppermute | solution.py:41
  30.5 4.8 %collective-permute-start.6 = (f32[16,2,256]{2,0,1:T(8,128)S(1)}, f32[16,2,256]{2,0,1:T(8,128)S(1)}, u32[]{:S(2)}, u32[]{:S(2)}) collective-permute-start(f32[16,2,256]{2,0,1:T(8,128)S(1)} %get-tuple-element.35), channel_id=1, source_target_pairs={{0,16},{4,20},{8,24},{12,28},{16,0},{20,4},{24,8},{28,12},{1,17},{... | collective-permute-start | bytes 98312 | tf_op jit(solution)/shard_map/ppermute | solution.py:41
  30.5 5.4 %collective-permute-start.5 = (f32[16,2,256]{2,0,1:T(8,128)S(1)}, f32[16,2,256]{2,0,1:T(8,128)S(1)}, u32[]{:S(2)}, u32[]{:S(2)}) collective-permute-start(f32[16,2,256]{2,0,1:T(8,128)S(1)} %get-tuple-element.33), channel_id=1, source_target_pairs={{0,8},{4,12},{8,0},{12,4},{16,24},{20,28},{24,16},{28,20},{1,9},{5... | collective-permute-start | bytes 98312 | tf_op jit(solution)/shard_map/ppermute | solution.py:41
  32.6 6.5 %collective-permute-start.13 = (f32[2,2,8,16]{3,2,1,0:T(8,128)S(1)}, f32[2,2,8,16]{3,2,1,0:T(8,128)S(1)}, u32[]{:S(2)}, u32[]{:S(2)}) collective-permute-start(f32[2,2,8,16]{3,2,1,0:T(8,128)S(1)} %get-tuple-element.38), channel_id=1, source_target_pairs={{0,2},{1,3},{2,0},{3,1},{4,6},{5,7},{6,4},{7,5},{8,10},{9,11},{10,... | collective-permute-start | bytes 6152 | tf_op jit(solution)/shard_map/ppermute | solution.py:41
  35.3 4.4 %collective-permute-start.11 = (f32[2,2,8,16]{3,2,1,0:T(8,128)S(1)}, f32[2,2,8,16]{3,2,1,0:T(8,128)S(1)}, u32[]{:S(2)}, u32[]{:S(2)}) collective-permute-start(f32[2,2,8,16]{3,2,1,0:T(8,128)S(1)} %get-tuple-element.36), channel_id=1, source_target_pairs={{0,1},{1,0},{2,3},{3,2},{4,5},{5,4},{6,7},{7,6},{8,9},{9,8},{10,11... | collective-permute-start | bytes 6152 | tf_op jit(solution)/shard_map/ppermute | solution.py:41
  36.6 5.3 %collective-permute-start.10 = (f32[16,1024]{1,0:T(8,128)S(1)}, f32[16,1024]{1,0:T(8,128)S(1)}, u32[]{:S(2)}, u32[]{:S(2)}) collective-permute-start(f32[16,1024]{1,0:T(8,128)S(1)} %pad_maximum_fusion.4), channel_id=1, source_target_pairs={{0,3},{1,2},{2,1},{3,0},{4,7},{5,6},{6,5},{7,4},{8,11},{9,10},{10,... | collective-permute-start | bytes 196616 | tf_op jit(solution)/shard_map/ppermute | solution.py:41
  39.2 4.3 %collective-permute-start.9 = (f32[16,1024]{1,0:T(8,128)S(1)}, f32[16,1024]{1,0:T(8,128)S(1)}, u32[]{:S(2)}, u32[]{:S(2)}) collective-permute-start(f32[16,1024]{1,0:T(8,128)S(1)} %pad_maximum_fusion.3), channel_id=1, source_target_pairs={{0,2},{1,3},{2,0},{3,1},{4,6},{5,7},{6,4},{7,5},{8,10},{9,11},{10,... | collective-permute-start | bytes 196616 | tf_op jit(solution)/shard_map/ppermute | solution.py:41
  39.7 5.8 %collective-permute-start.8 = (f32[16,1024]{1,0:T(8,128)S(1)}, f32[16,1024]{1,0:T(8,128)S(1)}, u32[]{:S(2)}, u32[]{:S(2)}) collective-permute-start(f32[16,1024]{1,0:T(8,128)S(1)} %pad_maximum_fusion.2), channel_id=1, source_target_pairs={{0,1},{1,0},{2,3},{3,2},{4,5},{5,4},{6,7},{7,6},{8,9},{9,8},{10,11... | collective-permute-start | bytes 196616 | tf_op jit(solution)/shard_map/ppermute | solution.py:41
  41.9 6.9 %collective-permute-start.12 = (f32[2,8,16,128]{3,2,1,0:T(8,128)S(1)}, f32[2,8,16,128]{3,2,1,0:T(8,128)S(1)}, u32[]{:S(2)}, u32[]{:S(2)}) collective-permute-start(f32[2,8,16,128]{3,2,1,0:T(8,128)S(1)} %get-tuple-element.17), channel_id=1, source_target_pairs={{0,1},{1,0},{2,3},{3,2},{4,5},{5,4},{6,7},{7,6},{8,9},{9,8},{10,11... | collective-permute-start | bytes 393224 | tf_op jit(solution)/shard_map/ppermute | solution.py:41
  43.5 5.2 %collective-permute-start.15 = (f32[2,2,8,16]{3,2,1,0:T(8,128)S(1)}, f32[2,2,8,16]{3,2,1,0:T(8,128)S(1)}, u32[]{:S(2)}, u32[]{:S(2)}) collective-permute-start(f32[2,2,8,16]{3,2,1,0:T(8,128)S(1)} %get-tuple-element.37), channel_id=1, source_target_pairs={{0,3},{1,2},{2,1},{3,0},{4,7},{5,6},{6,5},{7,4},{8,11},{9,10},{10,... | collective-permute-start | bytes 6152 | tf_op jit(solution)/shard_map/ppermute | solution.py:41

commit v2 on v1

--- a/solution.py
+++ b/solution.py
@@ -39,6 +39,14 @@
         return x
     size = lax.axis_size(axis)
     return lax.ppermute(x, axis, [(k, k ^ distance) for k in range(size)])
+
+
+def trade(x, axis, stride):
+    size = lax.axis_size(axis)
+    if stride == 1:
+        return lax.all_to_all(x, axis, 0, 0)
+    groups = [list(range(k, size, stride)) for k in range(stride)]
+    return lax.all_to_all(x, axis, 0, 0, axis_index_groups=groups)
 
 
 def on_device(
@@ -58,7 +66,8 @@
     token_rows = hidden_x.reshape(tokens, local_width)
 
     pairs = group_count // 2
-    gathered = jnp.concatenate([swap(token_rows, "group", 2 * d) for d in range(pairs)], axis=0)
+    copies = jnp.broadcast_to(token_rows[None], (pairs, tokens, local_width))
+    gathered = trade(copies, "group", 2).reshape(pairs * tokens, local_width)
     mate_codes = swap(delta_codes, "group", 1)
     mate_scales = swap(delta_scales, "group", 1)
 
@@ -86,12 +95,16 @@
     heads_own = H // tensor_count
     stats = jnp.stack([block_peak, weight_total], axis=0).reshape(2, row_count, step_count, H)
     sums = weighted.reshape(row_count, step_count, H, HD)
+    stats = trade(stats.reshape(-1, tensor_count, heads_own).transpose(1, 0, 2), "tensor", 1)
+    sums = trade(
+        sums.reshape(row_count, step_count, tensor_count, heads_own, HD).transpose(2, 0, 1, 3, 4),
+        "tensor",
+        1,
+    )
+    stats = stats.reshape(tensor_count, 2, row_count, step_count, heads_own)
     parts = None
-    for dt in range(tensor_count):
-        head_to = (tensor_place ^ dt) * heads_own
-        stats_part = swap(lax.dynamic_slice_in_dim(stats, head_to, heads_own, 3), "tensor", dt)
-        sums_part = swap(lax.dynamic_slice_in_dim(sums, head_to, heads_own, 2), "tensor", dt)
-        part = (stats_part[0], stats_part[1], sums_part)
+    for k in range(tensor_count):
+        part = (stats[k, 0], stats[k, 1], sums[k])
         parts = part if parts is None else combine(parts, part)
     peak_own, total_own, sum_own = parts
 
@@ -121,13 +134,13 @@
             )
         )
     partial = jnp.stack(both, axis=1).reshape(pairs, tokens, 2, owner_block)
-    arrived = jnp.stack([swap(partial[d], "group", 2 * d) for d in range(pairs)], axis=0)
+    arrived = trade(partial, "group", 2)
     blocks = arrived.transpose(0, 2, 1, 3).reshape(group_count, tokens, owner_block)
     shard_of = jnp.zeros((group_count,), jnp.int32).at[owner_map].set(
         jnp.arange(group_count, dtype=jnp.int32)
     )
     ordered = (
-        jnp.take(blocks, shard_of ^ group_place, axis=0)
+        jnp.take(blocks, shard_of ^ (group_place & 1), axis=0)
         .transpose(1, 0, 2)
         .reshape(tokens, out_width)
     )
@@ -135,20 +148,20 @@
     slice_width = out_width // tensor_count
     near_heads = max(1, heads_own // per_group)
     near_width = near_heads * HD
-    summed = None
-    for dt in range(tensor_count):
-        to = tensor_place ^ dt
+    pieces = []
+    for to in range(tensor_count):
         near_start = (to * heads_own // per_group) * HD
-        piece = jnp.concatenate(
-            [
-                lax.dynamic_slice_in_dim(ordered, near_start, near_width, 1),
-                lax.dynamic_slice_in_dim(ordered, kv_width + near_start, near_width, 1),
-                lax.dynamic_slice_in_dim(ordered, to * slice_width, slice_width, 1),
-            ],
-            axis=1,
+        pieces.append(
+            jnp.concatenate(
+                [
+                    ordered[:, near_start : near_start + near_width],
+                    ordered[:, kv_width + near_start : kv_width + near_start + near_width],
+                    ordered[:, to * slice_width : (to + 1) * slice_width],
+                ],
+                axis=1,
+            )
         )
-        piece = swap(piece, "tensor", dt)
-        summed = piece if summed is None else summed + piece
+    summed = jnp.sum(trade(jnp.stack(pieces, axis=0), "tensor", 1), axis=0)
     stored = summed.astype(jnp.bfloat16).reshape(row_count, step_count, -1)
     new_out = stored[:, :, 2 * near_width :]
     new_keys = stored[:, :, :near_width].reshape(row_count, step_count, near_heads, HD)

time: 50.1 us -> 69.5 us (1.39)
  waiting for transfers between devices: 5.55 us -> 21.8 us
  local copies, waits for them, and re-layouts: 7.89 us -> 12 us
  starting transfers between devices: 23.1 us -> 20.8 us
  other arithmetic: 1.97 us -> 3.89 us
  matrix products: 8.86 us -> 7.97 us
    ppermute x17 -> x2, starting transfers between devices: 23.1 us -> 0.6 us  [swap(): return lax.ppermute(x, axis, [(k, k ^ distance) for k in range(size)])]
    all_to_all x0 -> x5, waiting for transfers between devices: none -> 21.8 us  [the longest x3 13.2 us: trade(): return lax.all_to_all(x, axis, 0, 0)]
    all_to_all x0 -> x5, starting transfers between devices: none -> 20.2 us  [the longest x3 12 us: trade(): return lax.all_to_all(x, axis, 0, 0)]
    ppermute x17 -> x2, waiting for transfers between devices: 5.55 us -> 0.01 us  [swap(): return lax.ppermute(x, axis, [(k, k ^ distance) for k in range(size)])]
    another operation x1 -> x5, other arithmetic: 0.01 us -> 1.42 us  [the longest x3 0.76 us: on_device(): summed = jnp.sum(trade(jnp.stack(pieces, axis=0), 'tensor', 1), axis=0)]
    unnamed x16 -> x18, local copies, waits for them, and re-layouts: 1.13 us -> 2.2 us
    dot_general x1, matrix products: 1.33 us -> 0.37 us  [on_device(): jnp.einsum('rskgd,rckd->rskgc', grouped_query, cache_keys, preferred_elem...]
    transpose x0 -> x2, local copies, waits for them, and re-layouts: none -> 0.89 us  [the longest x1 0.88 us: on_device(): sums.reshape(row_count, step_count, tensor_count, heads_own, HD)]
  transfers between devices with their start and end apart: 17 -> 7, of which waited for: 5 -> 5; matrix products, arithmetic and copies ran while one was open for 35% -> 24% of each run, Pallas kernels for 0% -> 0%
where the time goes in v2:
time: 69.5 us; the launch traced here: 68.7 us
  waiting for transfers between devices  21.8 us (31%)
  starting transfers between devices  20.8 us (30%)
  local copies, waits for them, and re-layouts  12 us (17%)
  matrix products  7.97 us (11%)
  other arithmetic  3.89 us (6%)
  between operations  2.33 us (3%)
    all_to_all x3, waiting for transfers between devices, trade(): return lax.all_to_all(x, axis, 0, 0)  13.2 us
    all_to_all x3, starting transfers between devices, trade(): return lax.all_to_all(x, axis, 0, 0)  12 us
    all_to_all x2, waiting for transfers between devices, trade(): return lax.all_to_all(x, axis, 0, 0, axis_index_groups=groups)  8.54 us
    all_to_all x2, starting transfers between devices, trade(): return lax.all_to_all(x, axis, 0, 0, axis_index_groups=groups)  8.19 us
    dot_general x2, matrix products, on_device(): lax.dot_general(gathered, base_rows, (((1,), (1,)), ((), ())), preferred_...  3.34 us
    unnamed x18, local copies, waits for them, and re-layouts  2.2 us
    dot_general x1, matrix products, on_device(): lax.dot_general(gathered, dequantize(mate_codes, mate_scales), (((1,), (1...  2.14 us
    slice x1, local copies, waits for them, and re-layouts, on_device(): cache_keys = kv_cache[:, :, :kv_width].reshape(row_count, -1, KVH, HD)  1.71 us
  transfers between devices with their start and end apart: 7, of which 5 were waited for; matrix products, arithmetic and copies ran while one was open for 24% of the time, Pallas kernels for 0%

profile of v2, /device:TPU:0, one launch (start us, length us, event | category | flops | bytes accessed | tf_op | source)
XLA Modules:
  0.0 68.7 jit_solution(4876849984522400571)
XLA Ops:
  0.6 0.5 collective-permute-start.1
  1.1 0.1 collective-permute-start
  1.2 1.7 %fusion.54 = (bf16[2,256,1024]{2,1,0:T(8,128)(2,1)S(1)}, bf16[2,256,1024]{2,1,0:T(8,128)(2,1)S(1)}) fusion(bf16[2,256,2048]{2,1,0:T(8,128)(2,1)} %param.13), kind=kLoop, calls=%fused_computation.106 | loop fusion | bytes 4194304 | tf_op jit(solution)/shard_map/slice | solution.py:75
  2.9 0.0 copy-start.5
  3.0 0.0 copy-start.1
  3.0 0.5 copy.104
  3.5 0.1 copy-done.5
  3.6 0.1 broadcast_compare_fusion
  3.7 0.2 copy-done.1
  3.9 0.4 select_reduce_fusion
  4.3 0.4 fusion.10
  4.7 0.1 copy.79
  4.9 0.2 reshape_reshape.7
  5.0 0.7 reshape.347
  5.7 5.1 %all-to-all-start.4 = ((f32[4,1,512]{2,1,0:T(1,128)}), f32[4,1,512]{2,1,0:T(1,128)S(1)}, u32[]{:S(2)}, u32[]{:S(2)}) async-start(f32[4,1,512]{2,1,0:T(1,128)} %reshape.347), calls=%async_computation.4 | async-start | bytes 16384 | tf_op jit(solution)/shard_map/all_to_all | solution.py:47
  10.8 0.5 copy.105
  11.4 0.0 copy-start.3
  11.4 0.5 convolution_bitcast_fusion
  11.9 0.6 scatter_custom_fusion
  12.5 3.0 %all-to-all-done.4 = f32[4,1,512]{2,1,0:T(1,128)S(1)} async-done(((f32[4,1,512]{2,1,0:T(1,128)}), f32[4,1,512]{2,1,0:T(1,128)S(1)}, u32[]{:S(2)}, u32[]{:S(2)}) %all-to-all-start.4) | async-done | bytes 8224 | tf_op jit(solution)/shard_map/all_to_all | solution.py:47
  15.5 0.7 %broadcast_in_dim.82 = bf16[4,16,2048]{2,1,0:T(8,128)(2,1)} broadcast(bf16[16,2048]{1,0:T(8,128)(2,1)S(1)} %bitcast.263), dimensions={1,2} | broadcast | bytes 327680 | tf_op jit(solution)/shard_map/broadcast_in_dim | solution.py:69
  16.3 4.9 %all-to-all-start = ((bf16[4,16,2048]{2,1,0:T(8,128)(2,1)}), bf16[4,16,2048]{2,1,0:T(8,128)(2,1)S(1)}, u32[]{:S(2)}, u32[]{:S(2)}) async-start(bf16[4,16,2048]{2,1,0:T(8,128)(2,1)} %broadcast_in_dim.82), calls=%async_computation | async-start | bytes 524288 | tf_op jit(solution)/shard_map/all_to_all | solution.py:49
  21.2 0.1 copy.67
  21.3 0.6 fusion.58
  23.3 0.9 %copy.78 = f32[4,2,8,16,128]{4,3,2,1,0:T(8,128)} copy(f32[4,2,8,16,128]{4,3,0,2,1:T(8,128)S(1)} %bitcast.246) | data formatting | bytes 1048576 | tf_op jit(solution)/shard_map/transpose | solution.py:100
  24.2 0.5 broadcast.80
  24.7 0.7 reduce
  25.4 0.1 reshape.348
  25.5 0.1 copy.80
  25.5 0.8 %copy.68 = f32[256,16]{1,0:T(8,128)S(1)} copy(bf16[256,16]{0,1:T(8,128)(2,1)} %collective-permute-done.1) | data formatting | bytes 24576 | tf_op jit(solution)/shard_map/convert_element_type | solution.py:18
  26.3 2.7 %all-to-all-done = bf16[4,16,2048]{2,1,0:T(8,128)(2,1)S(1)} async-done(((bf16[4,16,2048]{2,1,0:T(8,128)(2,1)}), bf16[4,16,2048]{2,1,0:T(8,128)(2,1)S(1)}, u32[]{:S(2)}, u32[]{:S(2)}) %all-to-all-start) | async-done | bytes 262176 | tf_op jit(solution)/shard_map/all_to_all | solution.py:49
  29.0 1.7 %fusion.7 = f32[256,64]{0,1:T(8,128)S(1)} fusion(bf16[64,2048]{1,0:T(8,128)(2,1)S(1)} %bitcast.241, bf16[2048,2048]{1,0:T(8,128)(2,1)} %param.9, s32[]{:T(128)S(6)} %select_n.50), kind=kOutput, calls=%fused_computation.17 | convolution fusion | flops 67108864 | bytes 1376260 | tf_op jit(solution)/shard_map/dot_general | solution.py:129
  30.7 0.6 mul.202
  31.3 0.9 %fusion.4 = f32[256,64]{0,1:T(8,128)S(1)} fusion(bf16[64,2048]{1,0:T(8,128)(2,1)S(1)} %bitcast.242, f32[32,8,16,128]{3,2,1,0:T(8,128)S(1)} %bitcast.240, bf16[256,2048]{1,0:T(8,128)(2,1)S(1)} %copy-done), kind=kOutput, calls=%fused_computation.14 | convolution fusion | flops 68681728 | bytes 3473408 | tf_op jit(solution)/shard_map/dot_general | solution.py:111
  32.2 1.7 %convolution_add_fusion.1 = f32[256,64]{0,1:T(8,128)S(1)} fusion(f32[256,64]{0,1:T(8,128)S(1)} %fusion.4, bf16[64,2048]{1,0:T(8,128)(2,1)S(1)} %bitcast.243, bf16[2048,2048]{1,0:T(8,128)(2,1)} %param.9, s32[]{:T(128)S(6)} %select_n.48), kind=kOutput, calls=%fused_computation.13 | convolution fusion | flops 67125248 | bytes 1441796 | tf_op jit(solution)/shard_map/dot_general | solution.py:129
  33.9 0.0 collective-permute-done
  33.9 0.6 mul.207
  34.5 2.1 %convolution_add_fusion = f32[256,64]{0,1:T(8,128)S(1)} fusion(f32[256,64]{0,1:T(8,128)S(1)} %fusion.7, bf16[64,2048]{1,0:T(8,128)(2,1)S(1)} %bitcast.244, f32[32,8,16,128]{3,2,1,0:T(8,128)S(1)} %bitcast.239, bf16[256,2048]{1,0:T(8,128)(2,1)} %collective-permute-done), kind=kOutput, calls=%fused_computation.12 | convolution fusion | flops 68698112 | bytes 3538944 | tf_op jit(solution)/shard_map/dot_general | solution.py:117
  36.6 0.7 pad_maximum_fusion.1
  37.3 3.3 %all-to-all-start.1 = ((f32[4,16,2,256]{3,1,2,0:T(8,128)}), f32[4,16,2,256]{3,1,2,0:T(8,128)S(1)}, u32[]{:S(2)}, u32[]{:S(2)}) async-start(f32[4,16,2,256]{3,1,2,0:T(8,128)} %pad_maximum_fusion.1), calls=%async_computation.1 | async-start | bytes 262144 | tf_op jit(solution)/shard_map/all_to_all | solution.py:49
  40.6 5.9 %all-to-all-done.1 = f32[4,16,2,256]{3,1,2,0:T(8,128)S(1)} async-done(((f32[4,16,2,256]{3,1,2,0:T(8,128)}), f32[4,16,2,256]{3,1,2,0:T(8,128)S(1)}, u32[]{:S(2)}, u32[]{:S(2)}) %all-to-all-start.1) | async-done | bytes 131104 | tf_op jit(solution)/shard_map/all_to_all | solution.py:49
  46.5 3.5 %all-to-all-start.3 = ((f32[4,2,8,16,128]{4,3,2,1,0:T(8,128)}), f32[4,2,8,16,128]{4,3,2,1,0:T(8,128)S(1)}, u32[]{:S(2)}, u32[]{:S(2)}) async-start(f32[4,2,8,16,128]{4,3,2,1,0:T(8,128)} %copy.78), calls=%async_computation.3 | async-start | bytes 1048576 | tf_op jit(solution)/shard_map/all_to_all | solution.py:47
  50.0 0.6 gather_fusion
  50.6 0.1 select_bitcast_fusion
  50.7 0.7 %pad_maximum_fusion = f32[4,16,1024]{2,1,0:T(8,128)} fusion(f32[1,16,1024]{2,1,0:T(8,128)S(1)} %get-tuple-element.42, f32[1,16,1024]{2,1,0:T(8,128)S(1)} %get-tuple-element.41, f32[1,16,1024]{2,1,0:T(8,128)S(1)} %get-tuple-element.40, f32[1,16,1024]{2,1,0:T(8,128)S(1)} %get-tuple-element.39), kind=kLoop, calls=%fused_computation.26 | loop fusion | flops 196608 | bytes 524288 | tf_op jit(solution)/shard_map/stack | solution.py:164
  51.5 5.1 %all-to-all-done.3 = f32[4,2,8,16,128]{4,3,2,1,0:T(8,128)S(1)} async-done(((f32[4,2,8,16,128]{4,3,2,1,0:T(8,128)}), f32[4,2,8,16,128]{4,3,2,1,0:T(8,128)S(1)}, u32[]{:S(2)}, u32[]{:S(2)}) %all-to-all-start.3) | async-done | bytes 524320 | tf_op jit(solution)/shard_map/all_to_all | solution.py:47
  56.5 3.4 %all-to-all-start.2 = ((f32[4,16,1024]{2,1,0:T(8,128)}), f32[4,16,1024]{2,1,0:T(8,128)S(1)}, u32[]{:S(2)}, u32[]{:S(2)}) async-start(f32[4,16,1024]{2,1,0:T(8,128)} %pad_maximum_fusion), calls=%async_computation.2 | async-start | bytes 524288 | tf_op jit(solution)/shard_map/all_to_all | solution.py:47
  60.1 5.2 %all-to-all-done.2 = f32[4,16,1024]{2,1,0:T(8,128)S(1)} async-done(((f32[4,16,1024]{2,1,0:T(8,128)}), f32[4,16,1024]{2,1,0:T(8,128)S(1)}, u32[]{:S(2)}, u32[]{:S(2)}) %all-to-all-start.2) | async-done | bytes 262176 | tf_op jit(solution)/shard_map/all_to_all | solution.py:47
  65.3 0.6 slice.130
  65.9 0.4 select_reduce_fusion.1
  66.3 0.3 convolution_bitcast_fusion.1
  66.6 0.1 fusion.22
  66.8 0.1 reshape.322
  66.9 0.1 reshape.319
  67.0 0.1 copy.94
  67.1 0.1 copy.92
  67.2 0.1 copy.89
  67.2 0.1 copy.86
  67.3 0.1 copy.85
  67.4 0.1 copy.84
  67.5 0.1 copy.83
  67.5 0.1 copy.82
  67.6 0.1 copy.81
  67.7 1.0 %fusion.17 = bf16[2,8,2048]{2,1,0:T(8,128)(2,1)} fusion(f32[2,8,2048]{2,1,0:T(8,128)S(1)} %reshape.321, f32[2,8,2048]{2,1,0:T(8,128)S(1)} %squeeze.45, f32[2,8,2048]{2,1,0:T(8,128)S(1)} %squeeze.43, f32[2,8,2048]{2,1,0:T(8,128)S(1)} %squeeze.41, f32[2,8,2048]{2,1,0:T(8,128)S(1)} %squeeze.38, f32[2,8,16]{1,2,0:T(8,128)S(1)} %copy.94, ...), kind=kLoop, calls=%fused_computation.31 | loop fusion | flops 458752 | bytes 730112 | tf_op jit(solution)/shard_map/convert_element_type | solution.py:197
  (35 shorter events, 0.5 us)
Async XLA Ops:
  0.6 24.9 %collective-permute-start.1 = (bf16[256,16]{0,1:T(8,128)(2,1)}, bf16[256,16]{0,1:T(8,128)(2,1)}, u32[]{:S(2)}, u32[]{:S(2)}) collective-permute-start(bf16[256,16]{0,1:T(8,128)(2,1)} %param.11), channel_id=1, source_target_pairs={{0,4},{4,0},{8,12},{12,8},{16,20},{20,16},{24,28},{28,24},{1,5},{5... | collective-permute-start | bytes 24584 | tf_op jit(solution)/shard_map/ppermute | solution.py:41
  1.1 32.7 %collective-permute-start = (bf16[256,2048]{1,0:T(8,128)(2,1)}, bf16[256,2048]{1,0:T(8,128)(2,1)}, u32[]{:S(2)}, u32[]{:S(2)}) collective-permute-start(bf16[256,2048]{1,0:T(8,128)(2,1)} %param.10), channel_id=1, source_target_pairs={{0,4},{4,0},{8,12},{12,8},{16,20},{20,16},{24,28},{28,24},{1,5},{5... | collective-permute-start | bytes 3145736 | tf_op jit(solution)/shard_map/ppermute | solution.py:41
  2.9 0.7 copy-start.5
  3.0 1.0 %copy-start.1 = (bf16[2,8,8192]{2,1,0:T(8,128)(2,1)S(1)}, bf16[2,8,8192]{2,1,0:T(8,128)(2,1)}, u32[]{:S(2)}) copy-start(bf16[2,8,8192]{2,1,0:T(8,128)(2,1)} %param.14) | copy-start | bytes 786436
  5.7 9.8 %all-to-all-start.4 = ((f32[4,1,512]{2,1,0:T(1,128)}), f32[4,1,512]{2,1,0:T(1,128)S(1)}, u32[]{:S(2)}, u32[]{:S(2)}) async-start(f32[4,1,512]{2,1,0:T(1,128)} %reshape.347), calls=%async_computation.4 | async-start | bytes 16384 | tf_op jit(solution)/shard_map/all_to_all | solution.py:47
  10.8 1.1 %copy-start.4 = (s32[8]{0:T(128)S(1)}, s32[8]{0:T(128)}, u32[]{:S(2)}) copy-start(s32[8]{0:T(128)} %param.12) | copy-start | bytes 100
  10.8 4.7 %copy-start.2 = (bf16[2,8,2048]{2,1,0:T(8,128)(2,1)S(1)}, bf16[2,8,2048]{2,1,0:T(8,128)(2,1)}, u32[]{:S(2)}) copy-start(bf16[2,8,2048]{2,1,0:T(8,128)(2,1)} %param.8) | copy-start | bytes 196612
  11.4 9.8 %copy-start.3 = (bf16[256,16]{0,1:T(8,128)(2,1)S(1)}, bf16[256,16]{0,1:T(8,128)(2,1)}, u32[]{:S(2)}) copy-start(bf16[256,16]{0,1:T(8,128)(2,1)} %param.11) | copy-start | bytes 24580
  16.3 12.8 %all-to-all-start = ((bf16[4,16,2048]{2,1,0:T(8,128)(2,1)}), bf16[4,16,2048]{2,1,0:T(8,128)(2,1)S(1)}, u32[]{:S(2)}, u32[]{:S(2)}) async-start(bf16[4,16,2048]{2,1,0:T(8,128)(2,1)} %broadcast_in_dim.82), calls=%async_computation | async-start | bytes 524288 | tf_op jit(solution)/shard_map/all_to_all | solution.py:49
  24.2 7.1 %copy-start = (bf16[256,2048]{1,0:T(8,128)(2,1)S(1)}, bf16[256,2048]{1,0:T(8,128)(2,1)}, u32[]{:S(2)}) copy-start(bf16[256,2048]{1,0:T(8,128)(2,1)} %param.10) | copy-start | bytes 3145732
  37.3 9.2 %all-to-all-start.1 = ((f32[4,16,2,256]{3,1,2,0:T(8,128)}), f32[4,16,2,256]{3,1,2,0:T(8,128)S(1)}, u32[]{:S(2)}, u32[]{:S(2)}) async-start(f32[4,16,2,256]{3,1,2,0:T(8,128)} %pad_maximum_fusion.1), calls=%async_computation.1 | async-start | bytes 262144 | tf_op jit(solution)/shard_map/all_to_all | solution.py:49
  46.5 10.0 %all-to-all-start.3 = ((f32[4,2,8,16,128]{4,3,2,1,0:T(8,128)}), f32[4,2,8,16,128]{4,3,2,1,0:T(8,128)S(1)}, u32[]{:S(2)}, u32[]{:S(2)}) async-start(f32[4,2,8,16,128]{4,3,2,1,0:T(8,128)} %copy.78), calls=%async_computation.3 | async-start | bytes 1048576 | tf_op jit(solution)/shard_map/all_to_all | solution.py:47
  56.5 8.8 %all-to-all-start.2 = ((f32[4,16,1024]{2,1,0:T(8,128)}), f32[4,16,1024]{2,1,0:T(8,128)S(1)}, u32[]{:S(2)}, u32[]{:S(2)}) async-start(f32[4,16,1024]{2,1,0:T(8,128)} %pad_maximum_fusion), calls=%async_computation.2 | async-start | bytes 524288 | tf_op jit(solution)/shard_map/all_to_all | solution.py:47

commit v3 on v0

v3 whole, which is shorter than its diff:
```python
import functools
import jax
import jax.numpy as jnp
from jax import lax
from jax.experimental import pallas as pl
from jax.experimental.pallas import tpu as pltpu
from jax.sharding import PartitionSpec as P

H = 64
KVH = 8
HD = 128
LANES = 128
SUBLANES = 8


NEGATIVE = -1e30
SCORE_SCALE = HD ** (-0.5)
NT = (((1,), (1,)), ((), ()))
TN = (((0,), (0,)), ((), ()))
VMEM = pl.BlockSpec(memory_space=pltpu.VMEM)
SMEM = pl.BlockSpec(memory_space=pltpu.SMEM)
ANY = pl.BlockSpec(memory_space=pl.ANY)


def dot(left, right, dims):
    return lax.dot_general(left, right, dims, preferred_element_type=jnp.float32)


def dequantize(code_values, block_scales):
    blocks = block_scales.shape[1]
    widened = code_values.astype(jnp.float32).reshape(code_values.shape[0], blocks, -1)
    return (
        (widened * block_scales.astype(jnp.float32)[:, :, None])
        .reshape(code_values.shape[0], -1)
        .astype(jnp.bfloat16)
    )


def swap(x, axis, distance):
    size = lax.axis_size(axis)
    return lax.ppermute(x, axis, [(k, k ^ distance) for k in range(size)])


def params(megabytes):
    return pltpu.CompilerParams(vmem_limit_bytes=megabytes << 20)


def head_rows(block, row, steps, heads):
    mine = block[row * steps : (row + 1) * steps]
    return jnp.concatenate([mine[:, h * HD : (h + 1) * HD] for h in range(heads)], axis=0)


def cache_kernel(rows, steps, own, chunk, lengths_ref, query_ref, cache_ref, own_query_ref, *parts):
    place = lax.axis_index("tensor")
    cache_len = cache_ref.shape[0] // rows
    per_group = H // KVH
    chunks = own // chunk
    height = chunk * steps
    position = lax.broadcasted_iota(jnp.int32, (height, cache_len), 1)
    lane = lax.broadcasted_iota(jnp.int32, (chunks * height, LANES), 1)
    for d, part in enumerate(parts):
        totals = [[None] * chunks for _ in range(rows)]
        for j in range(chunks):
            head = (place ^ d) * own + j * chunk
            kv_lane = pl.multiple_of((head // per_group) * HD, HD)
            block = query_ref[:, pl.ds(pl.multiple_of(head * HD, HD), chunk * HD)]
            block = block.astype(jnp.float32)
            for r in range(rows):
                query = head_rows(block, r, steps, chunk).astype(jnp.bfloat16)
                at = (r * chunks + j) * height
                if d == 0:
                    own_query_ref[at : at + height] = query
                here = pl.ds(r * cache_len, cache_len)
                keys = cache_ref[here, pl.ds(kv_lane, HD)]
                values = cache_ref[here, pl.ds(kv_lane + KVH * HD, HD)]
                usable = position < lengths_ref[r] - place * cache_len
                scores = jnp.where(usable, dot(query, keys, NT) * SCORE_SCALE, NEGATIVE)
                peak = jnp.max(scores, axis=1, keepdims=True)
                weights = jnp.where(usable, jnp.exp(scores - peak), 0.0)
                total = jnp.sum(weights, axis=1, keepdims=True)
                part[at : at + height] = jnp.dot(
                    weights.astype(jnp.bfloat16), values, preferred_element_type=jnp.float32
                )
                totals[r][j] = (peak, total)
        stats = []
        for r in range(rows):
            peak = jnp.concatenate([pair[0] for pair in totals[r]], axis=0)
            total = jnp.concatenate([pair[1] for pair in totals[r]], axis=0)
            flat = jnp.where(lane == 0, peak, total)
            if chunks * height < LANES:
                pad = jnp.zeros((LANES - chunks * height, LANES), jnp.float32)
                flat = jnp.concatenate([flat, pad], axis=0)
            stats.append(flat.T[:2])
        stats.append(jnp.zeros((SUBLANES - 2 * rows, LANES), jnp.float32))
        end = rows * chunks * height
        part[end : end + SUBLANES] = jnp.concatenate(stats, axis=0)


def cache_partials(queries, cache, lengths, rows, steps, own, ways):
    chunk = min(own, H // KVH)
    height = rows * own * steps
    part = jax.ShapeDtypeStruct((height + SUBLANES, LANES), jnp.float32)
    out = pl.pallas_call(
        functools.partial(cache_kernel, rows, steps, own, chunk),
        out_shape=[jax.ShapeDtypeStruct((height, HD), jnp.bfloat16)] + [part] * ways,
        in_specs=[SMEM, VMEM, VMEM],
        out_specs=[VMEM] * (1 + ways),
        compiler_params=params(32),
        cost_estimate=pl.CostEstimate(
            flops=4 * height * ways * HD * cache.shape[0] // rows,
            bytes_accessed=2 * cache.size + 2 * queries.size,
            transcendentals=height * ways * cache.shape[0] // rows,
        ),
        name="cache_partials",
    )(lengths, queries, cache)
    return out[0], out[1:]


def project_kernel(pairs, owner_ref, own_ref, mate_ref, base_ref, *refs):
    tokens, outs = refs[:pairs], refs[pairs : 2 * pairs]
    base_blocks, arrived = refs[2 * pairs :]
    place = lax.axis_index("group")
    block = own_ref.shape[0]
    copies = []
    for k in range(2):
        start = pl.multiple_of(owner_ref[place ^ k] * block, block)
        copy = pltpu.make_async_copy(
            base_ref.at[pl.ds(start, block)], base_blocks.at[k], arrived.at[k]
        )
        copy.start()
        copies.append(copy)
    stacked = jnp.concatenate([ref[...] for ref in tokens], axis=0)
    count = tokens[0].shape[0]
    deltas = [dot(ref[...], stacked, NT) for ref in (own_ref, mate_ref)]
    for k in range(2):
        copies[k].wait()
        whole = (dot(base_blocks[k], stacked, NT) + deltas[k]).T
        for d in range(pairs):
            outs[d][:, k * block : (k + 1) * block] = whole[d * count : (d + 1) * count]


def project(owner_map, own, mate, base_weight, tokens):
    pairs = len(tokens)
    block = own.shape[0]
    count, width = tokens[0].shape
    return pl.pallas_call(
        functools.partial(project_kernel, pairs),
        out_shape=[jax.ShapeDtypeStruct((count, 2 * block), jnp.float32)] * pairs,
        in_specs=[SMEM, VMEM, VMEM, ANY] + [VMEM] * pairs,
        out_specs=[VMEM] * pairs,
        scratch_shapes=[
            pltpu.VMEM((2, block, width), jnp.bfloat16),
            pltpu.SemaphoreType.DMA((2,)),
        ],
        compiler_params=params(32),
        cost_estimate=pl.CostEstimate(
            flops=8 * block * width * count * pairs,
            bytes_accessed=8 * block * width,
            transcendentals=0,
        ),
        name="project",
    )(owner_map, own, mate, base_weight, *tokens)


def pack_kernel(pairs, ways, near, wide, owner_ref, *refs):
    arrived, outs, ordered = refs[:pairs], refs[pairs : pairs + ways], refs[-1]
    place = lax.axis_index("group")
    to_place = lax.axis_index("tensor")
    shards, _, block = ordered.shape
    for d in range(pairs):
        for k in range(2):
            ordered[owner_ref[place ^ (2 * d + k)]] = arrived[d][:, k * block : (k + 1) * block]
    for d, out in enumerate(outs):
        to = to_place ^ d
        for n in range(near):
            out[:, n * block : (n + 1) * block] = ordered[to * near + n]
            at = (near + n) * block
            out[:, at : at + block] = ordered[shards // 2 + to * near + n]
        for n in range(wide):
            at = (2 * near + n) * block
            out[:, at : at + block] = ordered[to * wide + n]


def pack_pieces(owner_map, arrived, block, ways, near_width, slice_width):
    pairs = len(arrived)
    count = arrived[0].shape[0]
    shards = 2 * pairs
    kv_width = KVH * HD
    if block % LANES == 0 and near_width % block == 0 and slice_width % block == 0:
        piece = jax.ShapeDtypeStruct((count, 2 * near_width + slice_width), jnp.float32)
        kernel = functools.partial(
            pack_kernel, pairs, ways, near_width // block, slice_width // block
        )
        return pl.pallas_call(
            kernel,
            out_shape=[piece] * ways,
            in_specs=[SMEM] + [VMEM] * pairs,
            out_specs=[VMEM] * ways,
            scratch_shapes=[pltpu.VMEM((shards, count, block), jnp.float32)],
            name="pack_pieces",
        )(owner_map, *arrived)
    blocks = jnp.stack(arrived, axis=0).reshape(pairs, count, 2, block).transpose(0, 2, 1, 3)
    shard_of = jnp.zeros((shards,), jnp.int32).at[owner_map].set(
        jnp.arange(shards, dtype=jnp.int32)
    )
    taken = jnp.take(
        blocks.reshape(shards, count, block), shard_of ^ lax.axis_index("group"), axis=0
    )
    ordered = taken.transpose(1, 0, 2).reshape(count, shards * block)
    per_device = H // ways
    pieces = []
    for d in range(ways):
        to = lax.axis_index("tensor") ^ d
        near = (to * per_device // (H // KVH)) * HD
        parts = [(near, near_width), (kv_width + near, near_width), (to * slice_width, slice_width)]
        cuts = [lax.dynamic_slice_in_dim(ordered, start, width, 1) for start, width in parts]
        pieces.append(jnp.concatenate(cuts, axis=1))
    return pieces


def finish_kernel(rows, steps, own, chunk, near_width, ways, query_ref, *refs):
    pieces, parts = refs[:ways], refs[ways : 2 * ways]
    new_ref, attended_ref = refs[2 * ways :]
    chunks = own // chunk
    height = chunk * steps
    end = rows * chunks * height
    summed = pieces[0][...]
    for piece in pieces[1:]:
        summed = summed + piece[...]
    stored = summed.astype(jnp.bfloat16)
    new_ref[...] = stored[:, 2 * near_width :]
    near = stored[:, : 2 * near_width].astype(jnp.float32)
    key_step = lax.broadcasted_iota(jnp.int32, (steps, height), 0)
    query_step = lax.broadcasted_iota(jnp.int32, (steps, height), 1) % steps
    causal = key_step <= query_step
    stats = [part[end : end + SUBLANES] for part in parts]
    factors, near_sums = [], []
    for r in range(rows):
        peaks, totals = [], []
        for j in range(chunks):
            at = (r * chunks + j) * height
            query = query_ref[at : at + height]
            step_rows = slice(r * steps, (r + 1) * steps)
            keys = near[step_rows, j * HD : (j + 1) * HD].astype(jnp.bfloat16)
            values = near[step_rows, near_width + j * HD : near_width + (j + 1) * HD]
            scores = jnp.where(causal, dot(keys, query, NT) * SCORE_SCALE, NEGATIVE)
            peak = jnp.max(scores, axis=0, keepdims=True)
            weights = jnp.where(causal, jnp.exp(scores - peak), 0.0)
            peaks.append(peak)
            totals.append(jnp.sum(weights, axis=0, keepdims=True))
            near_sums.append(dot(weights.astype(jnp.bfloat16), values.astype(jnp.bfloat16), TN))
        lanes = chunks * height
        pad = [jnp.zeros((1, LANES - lanes), jnp.float32)] if lanes < LANES else []
        peaks = [s[2 * r : 2 * r + 1] for s in stats] + [jnp.concatenate(peaks + pad, axis=1)]
        totals = [s[2 * r + 1 : 2 * r + 2] for s in stats] + [jnp.concatenate(totals + pad, axis=1)]
        top = functools.reduce(jnp.maximum, peaks)
        scales = [jnp.exp(peak - top) for peak in peaks]
        total = sum(scale * one for scale, one in zip(scales, totals))
        if pad:
            total = jnp.where(total == 0.0, 1.0, total)
        factors += [scale / total for scale in scales]
    lines = -(-len(factors) // SUBLANES) * SUBLANES
    if lines > len(factors):
        factors.append(jnp.zeros((lines - len(factors), LANES), jnp.float32))
    columns = jnp.concatenate(factors, axis=0).T
    for j in range(chunks):
        merged = []
        for r in range(rows):
            at = (r * chunks + j) * height
            here = slice(j * height, (j + 1) * height)
            first = r * (ways + 1)
            out = near_sums[r * chunks + j] * columns[here, first + ways : first + ways + 1]
            for d, part in enumerate(parts):
                out = out + part[at : at + height] * columns[here, first + d : first + d + 1]
            merged.append(out)
        for h in range(chunk):
            both = [out[h * steps : (h + 1) * steps] for out in merged]
            lane = (j * chunk + h) * HD
            attended_ref[:, lane : lane + HD] = jnp.concatenate(both, axis=0).astype(jnp.bfloat16)


def finish(own_query, pieces, parts, rows, steps, own, near_width):
    ways = len(pieces)
    count, width = pieces[0].shape
    return pl.pallas_call(
        functools.partial(
            finish_kernel, rows, steps, own, min(own, H // KVH), near_width, ways
        ),
        out_shape=[
            jax.ShapeDtypeStruct((count, width - 2 * near_width), jnp.bfloat16),
            jax.ShapeDtypeStruct((count, own * HD), jnp.bfloat16),
        ],
        in_specs=[VMEM] * (1 + 2 * ways),
        out_specs=[VMEM] * 2,
        name="finish",
    )(own_query, *pieces, *parts)


def on_device(
    hidden_x, base_weight, delta_codes, delta_scales, owner_map, kv_cache, queries, lengths
):
    group_count = lax.axis_size("group")
    tensor_count = lax.axis_size("tensor")
    rows, steps, local_width = hidden_x.shape
    tokens = rows * steps
    owner_block = delta_codes.shape[0]
    heads_own = H // tensor_count
    slice_width = base_weight.shape[0] // tensor_count
    near_width = max(1, heads_own // (H // KVH)) * HD
    pairs = group_count // 2

    mine = hidden_x.reshape(tokens, local_width)
    token_rows = [mine] + [swap(mine, "group", 2 * d) for d in range(1, pairs)]
    own_delta = dequantize(delta_codes, delta_scales)
    mate_delta = swap(own_delta, "group", 1)

    own_query, partials = cache_partials(
        queries.reshape(tokens, H * HD),
        kv_cache.reshape(-1, 2 * KVH * HD),
        lengths,
        rows,
        steps,
        heads_own,
        tensor_count,
    )
    partials = [partials[0]] + [swap(partials[d], "tensor", d) for d in range(1, tensor_count)]

    projected = project(owner_map, own_delta, mate_delta, base_weight, token_rows)
    arrived = [projected[0]] + [swap(projected[d], "group", 2 * d) for d in range(1, pairs)]
    pieces = pack_pieces(owner_map, arrived, owner_block, tensor_count, near_width, slice_width)
    pieces = [pieces[0]] + [swap(pieces[d], "tensor", d) for d in range(1, tensor_count)]
    new_out, attended = finish(own_query, pieces, partials, rows, steps, heads_own, near_width)
    return (new_out.reshape(rows, steps, -1), attended.reshape(rows, steps, -1))


def solution(mesh):
    in_specs = (
        P("group", None, "tensor"),
        P(None, "tensor"),
        P("group", "tensor"),
        P("group", "tensor"),
        P(),
        P("group", "tensor", None),
        P("group", None, None),
        P("group"),
    )
    out_specs = (P("group", None, "tensor"), P("group", None, "tensor"))
    return jax.shard_map(
        on_device, mesh=mesh, in_specs=in_specs, out_specs=out_specs, check_vma=False
    )
```

time: 183 us -> 48.9 us (0.27)
  waiting for transfers between devices: 80.5 us -> 7.25 us
  blocking collectives: 54.9 us -> 0 us
  starting transfers between devices: 0.08 us -> 20.5 us
  matrix products: 16.6 us -> 0 us
  between operations: 14.3 us -> 0.78 us
  Pallas kernels: 0 us -> 11.9 us
  local copies, waits for them, and re-layouts: 11.2 us -> 5.79 us
  other arithmetic: 5.3 us -> 2.32 us
    all_gather x2 -> x0, waiting for transfers between devices: 79.8 us -> none  [the longest x1 77.5 us: on_device(): lax.all_gather(delta_codes, 'group', axis=0, tiled=True)]
    all_gather x3 -> x0, blocking collectives: 36.5 us -> none  [the longest x2 20.9 us: joined_2(): everything = jax.tree.map(lambda part: lax.all_gather(part, axis), x)]
    ppermute x0 -> x13, starting transfers between devices: none -> 20.5 us  [swap(): return lax.ppermute(x, axis, [(k, k ^ distance) for k in range(size)])]
    psum x1 -> x0, blocking collectives: 18.4 us -> none  [on_device(): summed = lax.psum(base_part + ordered, 'tensor')]
    dot_general x9 -> x0, matrix products: 16.6 us -> none  [the longest x1 8.46 us: on_device(): jnp.einsum('rd,od->ro', token_rows, dequantize(codes_all, scales_all), pr...]
    pallas_call x0 -> x4, Pallas kernels: none -> 11.9 us  [the longest x1 4.67 us: cache_partials(): pl.pallas_call(functools.partial(cache_kernel, rows, steps, own, chunk),...]
    ppermute x0 -> x13, waiting for transfers between devices: none -> 7.25 us  [swap(): return lax.ppermute(x, axis, [(k, k ^ distance) for k in range(size)])]
    add x8 -> x0, other arithmetic: 4.61 us -> none  [the longest x3 4.33 us: combine(): left_sum * left_scale[..., None] + right_sum * right_scale[..., None]]
  transfers between devices with their start and end apart: 2 -> 13, of which waited for: 2 -> 4; matrix products, arithmetic and copies ran while one was open for 4% -> 0% of each run, Pallas kernels for 0% -> 18%
where the time goes in v3:
time: 48.9 us; the launch traced here: 48.6 us
  starting transfers between devices  20.5 us (42%)
  Pallas kernels  11.9 us (24%)
  waiting for transfers between devices  7.25 us (15%)
  local copies, waits for them, and re-layouts  5.79 us (12%)
  other arithmetic  2.32 us (5%)
  between operations  0.78 us (2%)
    ppermute x13, starting transfers between devices, swap(): return lax.ppermute(x, axis, [(k, k ^ distance) for k in range(size)])  20.5 us
    ppermute x13, waiting for transfers between devices, swap(): return lax.ppermute(x, axis, [(k, k ^ distance) for k in range(size)])  7.25 us
    pallas_call x1, Pallas kernels, cache_partials(): pl.pallas_call(functools.partial(cache_kernel, rows, steps, own, chunk),...  4.67 us
    unnamed x36, local copies, waits for them, and re-layouts  4.36 us
    pallas_call x1, Pallas kernels, finish(): pl.pallas_call(functools.partial(finish_kernel, rows, steps, own, min(own...  2.93 us
    pallas_call x1, Pallas kernels, project(): pl.pallas_call(functools.partial(project_kernel, pairs), out_shape=[jax.S...  2.73 us
    convert_element_type x1, other arithmetic, dequantize(): return (widened * block_scales.astype(jnp.float32)[:, :, None]).reshape(c...  2.32 us
    pallas_call x1, Pallas kernels, pack_pieces(): pl.pallas_call(kernel, out_shape=[piece] * ways, in_specs=[SMEM] + [VMEM]...  1.52 us
  transfers between devices with their start and end apart: 13, of which 4 were waited for; matrix products, arithmetic and copies ran while one was open for 0% of the time, Pallas kernels for 18%

profile of v3, /device:TPU:0, one launch (start us, length us, event | category | flops | bytes accessed | tf_op | source)
XLA Modules:
  0.0 48.6 jit_solution(10818966540436738547)
XLA Ops:
  0.6 0.0 copy-start.4
  0.6 0.0 copy-start.8
  0.6 0.0 copy-start.7
  0.7 0.8 %copy.10 = f32[256,16]{1,0:T(8,128)S(1)} copy(bf16[256,16]{0,1:T(8,128)(2,1)} %param.11) | data formatting | bytes 24576 | tf_op jit(solution)/shard_map/convert_element_type | solution.py:33
  1.5 0.0 copy-start
  1.5 0.6 %mul.11 = f32[256,16,128]{2,1,0:T(8,128)S(1)} broadcast(f32[256,16]{1,0:T(8,128)S(1)} %copy.10), dimensions={0,1} | broadcast | bytes 2113536 | tf_op jit(solution)/shard_map/mul | solution.py:33
  2.1 2.3 %fusion.own_ref = bf16[256,2048]{1,0:T(8,128)(2,1)S(1)} fusion(f32[32,8,16,128]{3,2,1,0:T(8,128)S(1)} %bitcast.16, bf16[256,2048]{1,0:T(8,128)(2,1)} %param.10), kind=kLoop, calls=%fused_computation.1 | loop fusion | flops 1572864 | bytes 4194304 | tf_op jit(solution)/shard_map/convert_element_type | solution.py:35
  4.4 0.5 %collective-permute-start = (bf16[256,2048]{1,0:T(8,128)(2,1)S(1)}, bf16[256,2048]{1,0:T(8,128)(2,1)S(1)}, u32[]{:S(2)}, u32[]{:S(2)}) collective-permute-start(bf16[256,2048]{1,0:T(8,128)(2,1)S(1)} %fusion.own_ref), channel_id=1, source_target_pairs={{0,4},{4,0},{8,12},{12,8},{16,20},{20,16},{24,28},{28,24},{1,5},{5... | collective-permute-start | bytes 3145736 | tf_op jit(solution)/shard_map/ppermute | solution.py:41
  4.9 0.0 copy-done.4
  5.0 2.7 %collective-permute-start.1 = (bf16[16,2048]{1,0:T(8,128)(2,1)S(1)}, bf16[16,2048]{1,0:T(8,128)(2,1)S(1)}, u32[]{:S(2)}, u32[]{:S(2)}) collective-permute-start(bf16[16,2048]{1,0:T(8,128)(2,1)S(1)} %bitcast.12), channel_id=1, source_target_pairs={{0,8},{4,12},{8,0},{12,4},{16,24},{20,28},{24,16},{28,20},{1,9},{5... | collective-permute-start | bytes 196616 | tf_op jit(solution)/shard_map/ppermute | solution.py:41
  7.6 2.6 %collective-permute-start.2 = (bf16[16,2048]{1,0:T(8,128)(2,1)S(1)}, bf16[16,2048]{1,0:T(8,128)(2,1)S(1)}, u32[]{:S(2)}, u32[]{:S(2)}) collective-permute-start(bf16[16,2048]{1,0:T(8,128)(2,1)S(1)} %bitcast.13), channel_id=1, source_target_pairs={{0,16},{4,20},{8,24},{12,28},{16,0},{20,4},{24,8},{28,12},{1,17},{... | collective-permute-start | bytes 196616 | tf_op jit(solution)/shard_map/ppermute | solution.py:41
  10.2 0.0 collective-permute-start.3
  10.2 0.0 copy-done.8
  10.2 0.0 copy-start.1
  10.2 1.6 %copy-done.1 = bf16[2,256,2048]{2,1,0:T(8,128)(2,1)S(1)} copy-done((bf16[2,256,2048]{2,1,0:T(8,128)(2,1)S(1)}, bf16[2,256,2048]{2,1,0:T(8,128)(2,1)}, u32[]{:S(2)}) %copy-start.1) | copy-done | bytes 2097176
  11.8 0.0 copy-start.2
  11.8 0.9 %copy-done.2 = bf16[2,8,8192]{2,1,0:T(8,128)(2,1)S(1)} copy-done((bf16[2,8,8192]{2,1,0:T(8,128)(2,1)S(1)}, bf16[2,8,8192]{2,1,0:T(8,128)(2,1)}, u32[]{:S(2)}) %copy-start.2) | copy-done | bytes 262168
  12.7 4.7 %cache_partials.1 = (bf16[256,128]{1,0:T(8,128)(2,1)S(1)}, f32[264,128]{1,0:T(8,128)S(1)}, f32[264,128]{1,0:T(8,128)S(1)}, f32[264,128]{1,0:T(8,128)S(1)}, f32[264,128]{1,0:T(8,128)S(1)}) custom-call(s32[2]{0:T(128)S(1)} %copy-done.8, bf16[16,8192]{1,0:T(8,128)(2,1)S(1)} %bitcast.11, bf16[512,2048]{1,0:T(8,128)(2,1)S(1)} %bitcast.10), custom_call_target="tpu_custom_call" | custom-call | flops 134217728 | bytes 2359296 | tf_op jit(solution)/shard_map/cache_partials/pallas_call | solution.py:103
  17.4 0.0 copy-start.3
  17.4 0.0 copy-start.5
  17.4 1.8 %collective-permute-start.10 = (f32[264,128]{1,0:T(8,128)S(1)}, f32[264,128]{1,0:T(8,128)S(1)}, u32[]{:S(2)}, u32[]{:S(2)}) collective-permute-start(f32[264,128]{1,0:T(8,128)S(1)} %get-tuple-element.27), channel_id=1, source_target_pairs={{0,1},{1,0},{2,3},{3,2},{4,5},{5,4},{6,7},{7,6},{8,9},{9,8},{10,11... | collective-permute-start | bytes 405512 | tf_op jit(solution)/shard_map/ppermute | solution.py:41
  19.2 0.0 collective-permute-done.1.refs_1_
  19.2 1.5 %collective-permute-start.11 = (f32[264,128]{1,0:T(8,128)S(1)}, f32[264,128]{1,0:T(8,128)S(1)}, u32[]{:S(2)}, u32[]{:S(2)}) collective-permute-start(f32[264,128]{1,0:T(8,128)S(1)} %get-tuple-element.28), channel_id=1, source_target_pairs={{0,2},{1,3},{2,0},{3,1},{4,6},{5,7},{6,4},{7,5},{8,10},{9,11},{10,... | collective-permute-start | bytes 405512 | tf_op jit(solution)/shard_map/ppermute | solution.py:41
  20.7 0.0 collective-permute-done.2.refs_2_
  20.7 0.3 collective-permute-start.12
  21.0 0.0 collective-permute-done.3.refs_3_
  21.0 0.0 collective-permute-done.mate_ref
  21.0 0.0 copy-done.7
  21.0 0.0 copy-done
  21.0 2.7 %project.1 = (f32[16,512]{1,0:T(8,128)S(1)}, f32[16,512]{1,0:T(8,128)S(1)}, f32[16,512]{1,0:T(8,128)S(1)}, f32[16,512]{1,0:T(8,128)S(1)}) custom-call(s32[8]{0:T(128)S(1)} %copy-done.7, bf16[256,2048]{1,0:T(8,128)(2,1)S(1)} %fusion.own_ref, bf16[256,2048]{1,0:T(8,128)(2,1)S(1)} %collective-permute-done.mate_ref, bf16[2048,2048]{1,0:T(8,128)(2,1)S(1)} %copy-done, ...), custom_call_target="tpu_custom_call" | custom-call | flops 268435456 | bytes 4194304 | tf_op jit(solution)/shard_map/project/pallas_call | solution.py:146
  23.8 0.0 copy-done.3
  23.8 0.0 copy-done.5
  23.8 0.0 copy-start.6
  23.8 0.6 %copy-done.6 = f32[16,512]{1,0:T(8,128)} copy-done((f32[16,512]{1,0:T(8,128)}, f32[16,512]{1,0:T(8,128)S(1)}, u32[]{:S(2)}) %copy-start.6) | copy-done | bytes 32792
  24.4 0.9 %collective-permute-start.4 = (f32[16,512]{1,0:T(8,128)S(1)}, f32[16,512]{1,0:T(8,128)S(1)}, u32[]{:S(2)}, u32[]{:S(2)}) collective-permute-start(f32[16,512]{1,0:T(8,128)S(1)} %get-tuple-element.19), channel_id=1, source_target_pairs={{0,8},{4,12},{8,0},{12,4},{16,24},{20,28},{24,16},{28,20},{1,9},{5... | collective-permute-start | bytes 98312 | tf_op jit(solution)/shard_map/ppermute | solution.py:41
  25.3 3.5 %collective-permute-start.5 = (f32[16,512]{1,0:T(8,128)S(1)}, f32[16,512]{1,0:T(8,128)S(1)}, u32[]{:S(2)}, u32[]{:S(2)}) collective-permute-start(f32[16,512]{1,0:T(8,128)S(1)} %get-tuple-element.20), channel_id=1, source_target_pairs={{0,16},{4,20},{8,24},{12,28},{16,0},{20,4},{24,8},{28,12},{1,17},{... | collective-permute-start | bytes 98312 | tf_op jit(solution)/shard_map/ppermute | solution.py:41
  28.8 0.0 collective-permute-done.4.refs_1_
  28.8 0.0 copy-start.15
  28.8 3.3 %collective-permute-start.6 = (f32[16,512]{1,0:T(8,128)S(1)}, f32[16,512]{1,0:T(8,128)S(1)}, u32[]{:S(2)}, u32[]{:S(2)}) collective-permute-start(f32[16,512]{1,0:T(8,128)S(1)} %get-tuple-element.21), channel_id=1, source_target_pairs={{0,24},{4,28},{8,16},{12,20},{16,8},{20,12},{24,0},{28,4},{1,25},{... | collective-permute-start | bytes 98312 | tf_op jit(solution)/shard_map/ppermute | solution.py:41
  32.1 0.0 collective-permute-done.5.refs_2_
  32.1 0.0 copy-start.16
  32.1 2.4 %collective-permute-done.6.refs_3_ = f32[16,512]{1,0:T(8,128)S(1)} collective-permute-done((f32[16,512]{1,0:T(8,128)S(1)}, f32[16,512]{1,0:T(8,128)S(1)}, u32[]{:S(2)}, u32[]{:S(2)}) %collective-permute-start.6) | collective-permute-done | bytes 32800 | tf_op jit(solution)/shard_map/ppermute | solution.py:41
  34.5 0.0 copy-start.17
  34.5 0.0 copy-done.15
  34.5 0.0 copy-done.16
  34.5 0.6 %copy-done.17 = f32[16,512]{1,0:T(8,128)} copy-done((f32[16,512]{1,0:T(8,128)}, f32[16,512]{1,0:T(8,128)S(1)}, u32[]{:S(2)}) %copy-start.17) | copy-done | bytes 32792
  35.1 1.5 %pack_pieces.1 = (f32[16,1024]{1,0:T(8,128)}, f32[16,1024]{1,0:T(8,128)}, f32[16,1024]{1,0:T(8,128)}, f32[16,1024]{1,0:T(8,128)}) custom-call(s32[8]{0:T(128)} %owner_ref.3, f32[16,512]{1,0:T(8,128)} %copy-done.6, f32[16,512]{1,0:T(8,128)} %copy-done.15, f32[16,512]{1,0:T(8,128)} %copy-done.16, f32[16,512]{1,0:T(8,128)} %copy-done.17), custom_call_target="tpu_custom_call" | custom-call | tf_op jit(solution)/shard_map/pack_pieces/pallas_call | solution.py:194
  36.6 1.5 %collective-permute-start.7 = (f32[16,1024]{1,0:T(8,128)}, f32[16,1024]{1,0:T(8,128)S(1)}, u32[]{:S(2)}, u32[]{:S(2)}) collective-permute-start(f32[16,1024]{1,0:T(8,128)} %get-tuple-element.23), channel_id=1, source_target_pairs={{0,1},{1,0},{2,3},{3,2},{4,5},{5,4},{6,7},{7,6},{8,9},{9,8},{10,11... | collective-permute-start | bytes 196616 | tf_op jit(solution)/shard_map/ppermute | solution.py:41
  38.1 1.5 %collective-permute-start.8 = (f32[16,1024]{1,0:T(8,128)}, f32[16,1024]{1,0:T(8,128)S(1)}, u32[]{:S(2)}, u32[]{:S(2)}) collective-permute-start(f32[16,1024]{1,0:T(8,128)} %get-tuple-element.24), channel_id=1, source_target_pairs={{0,2},{1,3},{2,0},{3,1},{4,6},{5,7},{6,4},{7,5},{8,10},{9,11},{10,... | collective-permute-start | bytes 196616 | tf_op jit(solution)/shard_map/ppermute | solution.py:41
  39.6 0.0 collective-permute-done.10.refs_5_
  39.6 0.5 collective-permute-start.9
  40.1 0.0 collective-permute-done.11.refs_6_
  40.1 0.0 collective-permute-done.12.refs_7_
  40.1 0.0 copy-start.11
  40.1 1.0 %collective-permute-done.7.refs_1_ = f32[16,1024]{1,0:T(8,128)S(1)} collective-permute-done((f32[16,1024]{1,0:T(8,128)}, f32[16,1024]{1,0:T(8,128)S(1)}, u32[]{:S(2)}, u32[]{:S(2)}) %collective-permute-start.7) | collective-permute-done | bytes 65568 | tf_op jit(solution)/shard_map/ppermute | solution.py:41
  41.1 1.5 %collective-permute-done.8.refs_2_ = f32[16,1024]{1,0:T(8,128)S(1)} collective-permute-done((f32[16,1024]{1,0:T(8,128)}, f32[16,1024]{1,0:T(8,128)S(1)}, u32[]{:S(2)}, u32[]{:S(2)}) %collective-permute-start.8) | collective-permute-done | bytes 65568 | tf_op jit(solution)/shard_map/ppermute | solution.py:41
  42.6 2.4 %collective-permute-done.9.refs_3_ = f32[16,1024]{1,0:T(8,128)S(1)} collective-permute-done((f32[16,1024]{1,0:T(8,128)}, f32[16,1024]{1,0:T(8,128)S(1)}, u32[]{:S(2)}, u32[]{:S(2)}) %collective-permute-start.9) | collective-permute-done | bytes 65568 | tf_op jit(solution)/shard_map/ppermute | solution.py:41
  45.0 0.0 copy-done.9
  45.0 0.0 copy-done.10
  45.0 0.0 copy-done.11
  45.0 0.0 copy-done.12
  45.0 0.0 copy-done.13
  45.0 0.6 %copy-done.14 = f32[16,1024]{1,0:T(8,128)} copy-done((f32[16,1024]{1,0:T(8,128)}, f32[16,1024]{1,0:T(8,128)S(1)}, u32[]{:S(2)}) %copy-start.14) | copy-done | bytes 65560
  45.6 2.9 %finish.1 = (bf16[16,512]{1,0:T(8,128)(2,1)}, bf16[16,2048]{1,0:T(8,128)(2,1)}) custom-call(bf16[256,128]{1,0:T(8,128)(2,1)} %copy-done.5, f32[16,1024]{1,0:T(8,128)} %get-tuple-element.22.refs_0_, f32[16,1024]{1,0:T(8,128)} %copy-done.12, f32[16,1024]{1,0:T(8,128)} %copy-done.13, f32[16,1024]{1,0:T(8,128)} %copy-done.14, f32[264,128]{1,0:T(8,128)} %copy-done.3, ...), custom_call_target="tpu_custom_call" | custom-call | tf_op jit(solution)/shard_map/finish/pallas_call | solution.py:285
  (5 shorter events, 0.0 us)
Async XLA Ops:
  0.6 4.3 %copy-start.4 = (bf16[2,8,2048]{2,1,0:T(8,128)(2,1)S(1)}, bf16[2,8,2048]{2,1,0:T(8,128)(2,1)}, u32[]{:S(2)}) copy-start(bf16[2,8,2048]{2,1,0:T(8,128)(2,1)} %param.8) | copy-start | bytes 196612
  0.6 9.6 %copy-start.8 = (s32[2]{0:T(128)S(1)}, s32[2]{0:T(128)}, u32[]{:S(2)}) copy-start(s32[2]{0:T(128)} %lengths_ref.1) | copy-start | bytes 28
  0.6 20.4 %copy-start.7 = (s32[8]{0:T(128)S(1)}, s32[8]{0:T(128)}, u32[]{:S(2)}) copy-start(s32[8]{0:T(128)} %owner_ref.3) | copy-start | bytes 100
  1.5 19.5 %copy-start = (bf16[2048,2048]{1,0:T(8,128)(2,1)S(1)}, bf16[2048,2048]{1,0:T(8,128)(2,1)}, u32[]{:S(2)}) copy-start(bf16[2048,2048]{1,0:T(8,128)(2,1)} %base_ref.1) | copy-start | bytes 25165828
  4.4 16.6 %collective-permute-start = (bf16[256,2048]{1,0:T(8,128)(2,1)S(1)}, bf16[256,2048]{1,0:T(8,128)(2,1)S(1)}, u32[]{:S(2)}, u32[]{:S(2)}) collective-permute-start(bf16[256,2048]{1,0:T(8,128)(2,1)S(1)} %fusion.own_ref), channel_id=1, source_target_pairs={{0,4},{4,0},{8,12},{12,8},{16,20},{20,16},{24,28},{28,24},{1,5},{5... | collective-permute-start | bytes 3145736 | tf_op jit(solution)/shard_map/ppermute | solution.py:41
  5.0 14.3 %collective-permute-start.1 = (bf16[16,2048]{1,0:T(8,128)(2,1)S(1)}, bf16[16,2048]{1,0:T(8,128)(2,1)S(1)}, u32[]{:S(2)}, u32[]{:S(2)}) collective-permute-start(bf16[16,2048]{1,0:T(8,128)(2,1)S(1)} %bitcast.12), channel_id=1, source_target_pairs={{0,8},{4,12},{8,0},{12,4},{16,24},{20,28},{24,16},{28,20},{1,9},{5... | collective-permute-start | bytes 196616 | tf_op jit(solution)/shard_map/ppermute | solution.py:41
  7.6 13.1 %collective-permute-start.2 = (bf16[16,2048]{1,0:T(8,128)(2,1)S(1)}, bf16[16,2048]{1,0:T(8,128)(2,1)S(1)}, u32[]{:S(2)}, u32[]{:S(2)}) collective-permute-start(bf16[16,2048]{1,0:T(8,128)(2,1)S(1)} %bitcast.13), channel_id=1, source_target_pairs={{0,16},{4,20},{8,24},{12,28},{16,0},{20,4},{24,8},{28,12},{1,17},{... | collective-permute-start | bytes 196616 | tf_op jit(solution)/shard_map/ppermute | solution.py:41
  10.2 10.8 %collective-permute-start.3 = (bf16[16,2048]{1,0:T(8,128)(2,1)S(1)}, bf16[16,2048]{1,0:T(8,128)(2,1)S(1)}, u32[]{:S(2)}, u32[]{:S(2)}) collective-permute-start(bf16[16,2048]{1,0:T(8,128)(2,1)S(1)} %bitcast.14), channel_id=1, source_target_pairs={{0,24},{4,28},{8,16},{12,20},{16,8},{20,12},{24,0},{28,4},{1,25},{... | collective-permute-start | bytes 196616 | tf_op jit(solution)/shard_map/ppermute | solution.py:41
  10.2 1.6 %copy-start.1 = (bf16[2,256,2048]{2,1,0:T(8,128)(2,1)S(1)}, bf16[2,256,2048]{2,1,0:T(8,128)(2,1)}, u32[]{:S(2)}) copy-start(bf16[2,256,2048]{2,1,0:T(8,128)(2,1)} %param.13) | copy-start | bytes 6291460
  11.8 0.9 %copy-start.2 = (bf16[2,8,8192]{2,1,0:T(8,128)(2,1)S(1)}, bf16[2,8,8192]{2,1,0:T(8,128)(2,1)}, u32[]{:S(2)}) copy-start(bf16[2,8,8192]{2,1,0:T(8,128)(2,1)} %param.14) | copy-start | bytes 786436
  17.4 6.3 %copy-start.3 = (f32[264,128]{1,0:T(8,128)}, f32[264,128]{1,0:T(8,128)S(1)}, u32[]{:S(2)}) copy-start(f32[264,128]{1,0:T(8,128)S(1)} %get-tuple-element.26.refs_4_) | copy-start | bytes 405508
  17.4 6.3 %copy-start.5 = (bf16[256,128]{1,0:T(8,128)(2,1)}, bf16[256,128]{1,0:T(8,128)(2,1)S(1)}, u32[]{:S(2)}) copy-start(bf16[256,128]{1,0:T(8,128)(2,1)S(1)} %get-tuple-element.17.query_ref) | copy-start | bytes 196612
  17.4 22.2 %collective-permute-start.10 = (f32[264,128]{1,0:T(8,128)S(1)}, f32[264,128]{1,0:T(8,128)S(1)}, u32[]{:S(2)}, u32[]{:S(2)}) collective-permute-start(f32[264,128]{1,0:T(8,128)S(1)} %get-tuple-element.27), channel_id=1, source_target_pairs={{0,1},{1,0},{2,3},{3,2},{4,5},{5,4},{6,7},{7,6},{8,9},{9,8},{10,11... | collective-permute-start | bytes 405512 | tf_op jit(solution)/shard_map/ppermute | solution.py:41
  19.2 20.9 %collective-permute-start.11 = (f32[264,128]{1,0:T(8,128)S(1)}, f32[264,128]{1,0:T(8,128)S(1)}, u32[]{:S(2)}, u32[]{:S(2)}) collective-permute-start(f32[264,128]{1,0:T(8,128)S(1)} %get-tuple-element.28), channel_id=1, source_target_pairs={{0,2},{1,3},{2,0},{3,1},{4,6},{5,7},{6,4},{7,5},{8,10},{9,11},{10,... | collective-permute-start | bytes 405512 | tf_op jit(solution)/shard_map/ppermute | solution.py:41
  20.7 19.4 %collective-permute-start.12 = (f32[264,128]{1,0:T(8,128)S(1)}, f32[264,128]{1,0:T(8,128)S(1)}, u32[]{:S(2)}, u32[]{:S(2)}) collective-permute-start(f32[264,128]{1,0:T(8,128)S(1)} %get-tuple-element.29), channel_id=1, source_target_pairs={{0,3},{1,2},{2,1},{3,0},{4,7},{5,6},{6,5},{7,4},{8,11},{9,10},{10,... | collective-permute-start | bytes 405512 | tf_op jit(solution)/shard_map/ppermute | solution.py:41
  23.8 0.6 %copy-start.6 = (f32[16,512]{1,0:T(8,128)}, f32[16,512]{1,0:T(8,128)S(1)}, u32[]{:S(2)}) copy-start(f32[16,512]{1,0:T(8,128)S(1)} %get-tuple-element.18.refs_0_) | copy-start | bytes 98308
  24.4 4.4 %collective-permute-start.4 = (f32[16,512]{1,0:T(8,128)S(1)}, f32[16,512]{1,0:T(8,128)S(1)}, u32[]{:S(2)}, u32[]{:S(2)}) collective-permute-start(f32[16,512]{1,0:T(8,128)S(1)} %get-tuple-element.19), channel_id=1, source_target_pairs={{0,8},{4,12},{8,0},{12,4},{16,24},{20,28},{24,16},{28,20},{1,9},{5... | collective-permute-start | bytes 98312 | tf_op jit(solution)/shard_map/ppermute | solution.py:41
  25.3 6.8 %collective-permute-start.5 = (f32[16,512]{1,0:T(8,128)S(1)}, f32[16,512]{1,0:T(8,128)S(1)}, u32[]{:S(2)}, u32[]{:S(2)}) collective-permute-start(f32[16,512]{1,0:T(8,128)S(1)} %get-tuple-element.20), channel_id=1, source_target_pairs={{0,16},{4,20},{8,24},{12,28},{16,0},{20,4},{24,8},{28,12},{1,17},{... | collective-permute-start | bytes 98312 | tf_op jit(solution)/shard_map/ppermute | solution.py:41
  28.8 5.7 %copy-start.15 = (f32[16,512]{1,0:T(8,128)}, f32[16,512]{1,0:T(8,128)S(1)}, u32[]{:S(2)}) copy-start(f32[16,512]{1,0:T(8,128)S(1)} %collective-permute-done.4.refs_1_) | copy-start | bytes 98308
  28.8 5.7 %collective-permute-start.6 = (f32[16,512]{1,0:T(8,128)S(1)}, f32[16,512]{1,0:T(8,128)S(1)}, u32[]{:S(2)}, u32[]{:S(2)}) collective-permute-start(f32[16,512]{1,0:T(8,128)S(1)} %get-tuple-element.21), channel_id=1, source_target_pairs={{0,24},{4,28},{8,16},{12,20},{16,8},{20,12},{24,0},{28,4},{1,25},{... | collective-permute-start | bytes 98312 | tf_op jit(solution)/shard_map/ppermute | solution.py:41
  32.1 2.4 %copy-start.16 = (f32[16,512]{1,0:T(8,128)}, f32[16,512]{1,0:T(8,128)S(1)}, u32[]{:S(2)}) copy-start(f32[16,512]{1,0:T(8,128)S(1)} %collective-permute-done.5.refs_2_) | copy-start | bytes 98308
  34.5 0.6 %copy-start.17 = (f32[16,512]{1,0:T(8,128)}, f32[16,512]{1,0:T(8,128)S(1)}, u32[]{:S(2)}) copy-start(f32[16,512]{1,0:T(8,128)S(1)} %collective-permute-done.6.refs_3_) | copy-start | bytes 98308
  36.6 4.5 %collective-permute-start.7 = (f32[16,1024]{1,0:T(8,128)}, f32[16,1024]{1,0:T(8,128)S(1)}, u32[]{:S(2)}, u32[]{:S(2)}) collective-permute-start(f32[16,1024]{1,0:T(8,128)} %get-tuple-element.23), channel_id=1, source_target_pairs={{0,1},{1,0},{2,3},{3,2},{4,5},{5,4},{6,7},{7,6},{8,9},{9,8},{10,11... | collective-permute-start | bytes 196616 | tf_op jit(solution)/shard_map/ppermute | solution.py:41
  38.1 4.5 %collective-permute-start.8 = (f32[16,1024]{1,0:T(8,128)}, f32[16,1024]{1,0:T(8,128)S(1)}, u32[]{:S(2)}, u32[]{:S(2)}) collective-permute-start(f32[16,1024]{1,0:T(8,128)} %get-tuple-element.24), channel_id=1, source_target_pairs={{0,2},{1,3},{2,0},{3,1},{4,6},{5,7},{6,4},{7,5},{8,10},{9,11},{10,... | collective-permute-start | bytes 196616 | tf_op jit(solution)/shard_map/ppermute | solution.py:41
  39.6 5.4 %copy-start.9 = (f32[264,128]{1,0:T(8,128)}, f32[264,128]{1,0:T(8,128)S(1)}, u32[]{:S(2)}) copy-start(f32[264,128]{1,0:T(8,128)S(1)} %collective-permute-done.10.refs_5_) | copy-start | bytes 405508
  39.6 5.4 %collective-permute-start.9 = (f32[16,1024]{1,0:T(8,128)}, f32[16,1024]{1,0:T(8,128)S(1)}, u32[]{:S(2)}, u32[]{:S(2)}) collective-permute-start(f32[16,1024]{1,0:T(8,128)} %get-tuple-element.25), channel_id=1, source_target_pairs={{0,3},{1,2},{2,1},{3,0},{4,7},{5,6},{6,5},{7,4},{8,11},{9,10},{10,... | collective-permute-start | bytes 196616 | tf_op jit(solution)/shard_map/ppermute | solution.py:41
  40.1 4.9 %copy-start.10 = (f32[264,128]{1,0:T(8,128)}, f32[264,128]{1,0:T(8,128)S(1)}, u32[]{:S(2)}) copy-start(f32[264,128]{1,0:T(8,128)S(1)} %collective-permute-done.11.refs_6_) | copy-start | bytes 405508
  40.1 4.9 %copy-start.11 = (f32[264,128]{1,0:T(8,128)}, f32[264,128]{1,0:T(8,128)S(1)}, u32[]{:S(2)}) copy-start(f32[264,128]{1,0:T(8,128)S(1)} %collective-permute-done.12.refs_7_) | copy-start | bytes 405508
  41.1 3.9 %copy-start.12 = (f32[16,1024]{1,0:T(8,128)}, f32[16,1024]{1,0:T(8,128)S(1)}, u32[]{:S(2)}) copy-start(f32[16,1024]{1,0:T(8,128)S(1)} %collective-permute-done.7.refs_1_) | copy-start | bytes 196612
  42.6 2.5 %copy-start.13 = (f32[16,1024]{1,0:T(8,128)}, f32[16,1024]{1,0:T(8,128)S(1)}, u32[]{:S(2)}) copy-start(f32[16,1024]{1,0:T(8,128)S(1)} %collective-permute-done.8.refs_2_) | copy-start | bytes 196612
  45.0 0.6 %copy-start.14 = (f32[16,1024]{1,0:T(8,128)}, f32[16,1024]{1,0:T(8,128)S(1)}, u32[]{:S(2)}) copy-start(f32[16,1024]{1,0:T(8,128)S(1)} %collective-permute-done.9.refs_3_) | copy-start | bytes 196612

commit v4 on v3

--- a/solution.py
+++ b/solution.py
@@ -9,31 +9,25 @@
 H = 64
 KVH = 8
 HD = 128
+BLK = 128
 LANES = 128
 SUBLANES = 8
 
 
 NEGATIVE = -1e30
 SCORE_SCALE = HD ** (-0.5)
+CACHE_KIB = 53 << 10
+WEIGHTS_KIB = 46 << 10
+PROJECT_KIB = 16 << 10
 NT = (((1,), (1,)), ((), ()))
 TN = (((0,), (0,)), ((), ()))
 VMEM = pl.BlockSpec(memory_space=pltpu.VMEM)
 SMEM = pl.BlockSpec(memory_space=pltpu.SMEM)
-ANY = pl.BlockSpec(memory_space=pl.ANY)
+HBM = pl.BlockSpec(memory_space=pltpu.HBM)
 
 
 def dot(left, right, dims):
     return lax.dot_general(left, right, dims, preferred_element_type=jnp.float32)
-
-
-def dequantize(code_values, block_scales):
-    blocks = block_scales.shape[1]
-    widened = code_values.astype(jnp.float32).reshape(code_values.shape[0], blocks, -1)
-    return (
-        (widened * block_scales.astype(jnp.float32)[:, :, None])
-        .reshape(code_values.shape[0], -1)
-        .astype(jnp.bfloat16)
-    )
 
 
 def swap(x, axis, distance):
@@ -41,8 +35,8 @@
     return lax.ppermute(x, axis, [(k, k ^ distance) for k in range(size)])
 
 
-def params(megabytes):
-    return pltpu.CompilerParams(vmem_limit_bytes=megabytes << 20)
+def params(kibibytes):
+    return pltpu.CompilerParams(vmem_limit_bytes=kibibytes << 10)
 
 
 def head_rows(block, row, steps, heads):
@@ -50,116 +44,161 @@
     return jnp.concatenate([mine[:, h * HD : (h + 1) * HD] for h in range(heads)], axis=0)
 
 
-def cache_kernel(rows, steps, own, chunk, lengths_ref, query_ref, cache_ref, own_query_ref, *parts):
+def weights_kernel(owner_ref, own_codes, mate_codes, own_scales, mate_scales, base_hbm, *refs):
+    deltas, base_ref, arrived = refs[:2], refs[2], refs[3]
+    place = lax.axis_index("group")
+    block = own_codes.shape[0]
+    copies = []
+    for k in range(2):
+        start = pl.multiple_of(owner_ref[place ^ k] * block, block)
+        copy = pltpu.make_async_copy(
+            base_hbm.at[pl.ds(start, block)], base_ref.at[k], arrived.at[k]
+        )
+        copy.start()
+        copies.append(copy)
+    for codes_ref, scales_ref, out_ref in zip(
+        (own_codes, mate_codes), (own_scales, mate_scales), deltas
+    ):
+        scales = scales_ref[...].astype(jnp.float32).T
+        for n in range(scales.shape[1]):
+            lanes = slice(n * BLK, (n + 1) * BLK)
+            values = codes_ref[:, lanes].astype(jnp.float32) * scales[:, n : n + 1]
+            out_ref[:, lanes] = values.astype(jnp.bfloat16)
+    for copy in copies:
+        copy.wait()
+
+
+def weights(owner_map, codes, scales, base_weight):
+    delta = jax.ShapeDtypeStruct(codes[0].shape, jnp.bfloat16)
+    return pl.pallas_call(
+        weights_kernel,
+        out_shape=[delta, delta, jax.ShapeDtypeStruct((2,) + delta.shape, jnp.bfloat16)],
+        in_specs=[SMEM] + [VMEM] * 4 + [HBM],
+        out_specs=[VMEM] * 3,
+        scratch_shapes=[pltpu.SemaphoreType.DMA((2,))],
+        compiler_params=params(WEIGHTS_KIB),
+        cost_estimate=pl.CostEstimate(
+            flops=2 * delta.size, bytes_accessed=16 * delta.size, transcendentals=0
+        ),
+        name="weights",
+    )(owner_map, *codes, *[one.T for one in scales], base_weight)
+
+
+def cache_kernel(rows, steps, own, chunk, lengths_ref, tokens_hbm, query_hbm, cache_hbm, *refs):
+    tokens_ref, own_query_ref, parts = refs[0], refs[1], refs[2:-3]
+    query_ref, cache_ref, arrived = refs[-3:]
+    cache_len = cache_ref.shape[0] // rows
+    copies = [pltpu.make_async_copy(query_hbm, query_ref, arrived.at[0])]
+    for r in range(rows):
+        here = pl.ds(r * cache_len, cache_len)
+        copies.append(
+            pltpu.make_async_copy(cache_hbm.at[here], cache_ref.at[here], arrived.at[1 + r])
+        )
+    copies.append(pltpu.make_async_copy(tokens_hbm, tokens_ref, arrived.at[1 + rows]))
+    for copy in copies:
+        copy.start()
+    for copy in copies:
+        copy.wait()
+
     place = lax.axis_index("tensor")
-    cache_len = cache_ref.shape[0] // rows
-    per_group = H // KVH
     chunks = own // chunk
     height = chunk * steps
-    position = lax.broadcasted_iota(jnp.int32, (height, cache_len), 1)
-    lane = lax.broadcasted_iota(jnp.int32, (chunks * height, LANES), 1)
+    width = chunks * HD
+    position = lax.broadcasted_iota(jnp.int32, (cache_len, chunks * height), 0)
+    usable = [position < lengths_ref[r] - place * cache_len for r in range(rows)]
     for d, part in enumerate(parts):
-        totals = [[None] * chunks for _ in range(rows)]
-        for j in range(chunks):
-            head = (place ^ d) * own + j * chunk
-            kv_lane = pl.multiple_of((head // per_group) * HD, HD)
-            block = query_ref[:, pl.ds(pl.multiple_of(head * HD, HD), chunk * HD)]
-            block = block.astype(jnp.float32)
-            for r in range(rows):
-                query = head_rows(block, r, steps, chunk).astype(jnp.bfloat16)
-                at = (r * chunks + j) * height
-                if d == 0:
-                    own_query_ref[at : at + height] = query
-                here = pl.ds(r * cache_len, cache_len)
-                keys = cache_ref[here, pl.ds(kv_lane, HD)]
-                values = cache_ref[here, pl.ds(kv_lane + KVH * HD, HD)]
-                usable = position < lengths_ref[r] - place * cache_len
-                scores = jnp.where(usable, dot(query, keys, NT) * SCORE_SCALE, NEGATIVE)
-                peak = jnp.max(scores, axis=1, keepdims=True)
-                weights = jnp.where(usable, jnp.exp(scores - peak), 0.0)
-                total = jnp.sum(weights, axis=1, keepdims=True)
-                part[at : at + height] = jnp.dot(
-                    weights.astype(jnp.bfloat16), values, preferred_element_type=jnp.float32
-                )
-                totals[r][j] = (peak, total)
+        head = (place ^ d) * own
+        kv_lane = pl.multiple_of((head // (H // KVH)) * HD, HD)
+        block = query_ref[:, pl.ds(pl.multiple_of(head * HD, HD), own * HD)].astype(jnp.float32)
         stats = []
         for r in range(rows):
-            peak = jnp.concatenate([pair[0] for pair in totals[r]], axis=0)
-            total = jnp.concatenate([pair[1] for pair in totals[r]], axis=0)
-            flat = jnp.where(lane == 0, peak, total)
-            if chunks * height < LANES:
-                pad = jnp.zeros((LANES - chunks * height, LANES), jnp.float32)
-                flat = jnp.concatenate([flat, pad], axis=0)
-            stats.append(flat.T[:2])
-        stats.append(jnp.zeros((SUBLANES - 2 * rows, LANES), jnp.float32))
+            at = r * chunks * height
+            query = head_rows(block, r, steps, own)
+            if d == 0:
+                own_query_ref[at : at + chunks * height] = query.astype(jnp.bfloat16)
+            spread = []
+            for j in range(chunks):
+                line = [jnp.zeros((height, HD), jnp.float32)] * chunks
+                line[j] = query[j * height : (j + 1) * height]
+                spread.append(jnp.concatenate(line, axis=1))
+            spread = jnp.concatenate(spread, axis=0).astype(jnp.bfloat16)
+            here = pl.ds(r * cache_len, cache_len)
+            keys = cache_ref[here, pl.ds(kv_lane, width)]
+            values = cache_ref[here, pl.ds(kv_lane + KVH * HD, width)]
+            scores = jnp.where(usable[r], dot(keys, spread, NT) * SCORE_SCALE, 2.0 * NEGATIVE)
+            peak = jnp.maximum(jnp.max(scores, axis=0, keepdims=True), NEGATIVE)
+            weights = jnp.exp(scores - peak)
+            stats += [peak, jnp.sum(weights, axis=0, keepdims=True)]
+            sums = dot(weights.astype(jnp.bfloat16), values, TN)
+            for j in range(chunks):
+                here = slice(j * height, (j + 1) * height)
+                part[at + j * height : at + (j + 1) * height] = sums[here, j * HD : (j + 1) * HD]
+        stats.append(jnp.zeros((SUBLANES - 2 * rows, chunks * height), jnp.float32))
+        stats = jnp.concatenate(stats, axis=0)
+        if chunks * height < LANES:
+            pad = jnp.zeros((SUBLANES, LANES - chunks * height), jnp.float32)
+            stats = jnp.concatenate([stats, pad], axis=1)
         end = rows * chunks * height
-        part[end : end + SUBLANES] = jnp.concatenate(stats, axis=0)
-
-
-def cache_partials(queries, cache, lengths, rows, steps, own, ways):
+        part[end : end + SUBLANES] = stats
+
+
+def cache_partials(tokens, queries, cache, lengths, rows, steps, own, ways):
     chunk = min(own, H // KVH)
     height = rows * own * steps
     part = jax.ShapeDtypeStruct((height + SUBLANES, LANES), jnp.float32)
     out = pl.pallas_call(
         functools.partial(cache_kernel, rows, steps, own, chunk),
-        out_shape=[jax.ShapeDtypeStruct((height, HD), jnp.bfloat16)] + [part] * ways,
-        in_specs=[SMEM, VMEM, VMEM],
-        out_specs=[VMEM] * (1 + ways),
-        compiler_params=params(32),
+        out_shape=[
+            jax.ShapeDtypeStruct(tokens.shape, tokens.dtype),
+            jax.ShapeDtypeStruct((height, HD), jnp.bfloat16),
+        ]
+        + [part] * ways,
+        in_specs=[SMEM, HBM, HBM, HBM],
+        out_specs=[VMEM] * (2 + ways),
+        scratch_shapes=[
+            pltpu.VMEM(queries.shape, queries.dtype),
+            pltpu.VMEM(cache.shape, cache.dtype),
+            pltpu.SemaphoreType.DMA((2 + rows,)),
+        ],
+        compiler_params=params(CACHE_KIB),
         cost_estimate=pl.CostEstimate(
             flops=4 * height * ways * HD * cache.shape[0] // rows,
             bytes_accessed=2 * cache.size + 2 * queries.size,
             transcendentals=height * ways * cache.shape[0] // rows,
         ),
         name="cache_partials",
-    )(lengths, queries, cache)
-    return out[0], out[1:]
-
-
-def project_kernel(pairs, owner_ref, own_ref, mate_ref, base_ref, *refs):
-    tokens, outs = refs[:pairs], refs[pairs : 2 * pairs]
-    base_blocks, arrived = refs[2 * pairs :]
-    place = lax.axis_index("group")
+    )(lengths, tokens, queries, cache)
+    return out[0], out[1], out[2:]
+
+
+def project_kernel(pairs, own_ref, mate_ref, base_ref, *refs):
+    tokens, outs = refs[:pairs], refs[pairs:]
     block = own_ref.shape[0]
-    copies = []
-    for k in range(2):
-        start = pl.multiple_of(owner_ref[place ^ k] * block, block)
-        copy = pltpu.make_async_copy(
-            base_ref.at[pl.ds(start, block)], base_blocks.at[k], arrived.at[k]
-        )
-        copy.start()
-        copies.append(copy)
     stacked = jnp.concatenate([ref[...] for ref in tokens], axis=0)
     count = tokens[0].shape[0]
-    deltas = [dot(ref[...], stacked, NT) for ref in (own_ref, mate_ref)]
-    for k in range(2):
-        copies[k].wait()
-        whole = (dot(base_blocks[k], stacked, NT) + deltas[k]).T
+    for k, delta_ref in enumerate((own_ref, mate_ref)):
+        whole = (dot(base_ref[k], stacked, NT) + dot(delta_ref[...], stacked, NT)).T
         for d in range(pairs):
             outs[d][:, k * block : (k + 1) * block] = whole[d * count : (d + 1) * count]
 
 
-def project(owner_map, own, mate, base_weight, tokens):
+def project(own, mate, base, tokens):
     pairs = len(tokens)
     block = own.shape[0]
     count, width = tokens[0].shape
     return pl.pallas_call(
         functools.partial(project_kernel, pairs),
         out_shape=[jax.ShapeDtypeStruct((count, 2 * block), jnp.float32)] * pairs,
-        in_specs=[SMEM, VMEM, VMEM, ANY] + [VMEM] * pairs,
+        in_specs=[VMEM] * (3 + pairs),
         out_specs=[VMEM] * pairs,
-        scratch_shapes=[
-            pltpu.VMEM((2, block, width), jnp.bfloat16),
-            pltpu.SemaphoreType.DMA((2,)),
-        ],
-        compiler_params=params(32),
+        compiler_params=params(PROJECT_KIB),
         cost_estimate=pl.CostEstimate(
             flops=8 * block * width * count * pairs,
             bytes_accessed=8 * block * width,
             transcendentals=0,
         ),
         name="project",
-    )(owner_map, own, mate, base_weight, *tokens)
+    )(own, mate, base, *tokens)
 
 
 def pack_kernel(pairs, ways, near, wide, owner_ref, *refs):
@@ -197,6 +236,7 @@
             in_specs=[SMEM] + [VMEM] * pairs,
             out_specs=[VMEM] * ways,
             scratch_shapes=[pltpu.VMEM((shards, count, block), jnp.float32)],
+            compiler_params=params(8192),
             name="pack_pieces",
         )(owner_map, *arrived)
     blocks = jnp.stack(arrived, axis=0).reshape(pairs, count, 2, block).transpose(0, 2, 1, 3)
@@ -292,6 +332,7 @@
         ],
         in_specs=[VMEM] * (1 + 2 * ways),
         out_specs=[VMEM] * 2,
+        compiler_params=params(8192),
         name="finish",
     )(own_query, *pieces, *parts)
 
@@ -311,10 +352,11 @@
 
     mine = hidden_x.reshape(tokens, local_width)
     token_rows = [mine] + [swap(mine, "group", 2 * d) for d in range(1, pairs)]
-    own_delta = dequantize(delta_codes, delta_scales)
-    mate_delta = swap(own_delta, "group", 1)
-
-    own_query, partials = cache_partials(
+    codes = [delta_codes, swap(delta_codes, "group", 1)]
+    scales = [delta_scales, swap(delta_scales, "group", 1)]
+
+    own_tokens, own_query, partials = cache_partials(
+        mine,
         queries.reshape(tokens, H * HD),
         kv_cache.reshape(-1, 2 * KVH * HD),
         lengths,
@@ -325,7 +367,8 @@
     )
     partials = [partials[0]] + [swap(partials[d], "tensor", d) for d in range(1, tensor_count)]
 
-    projected = project(owner_map, own_delta, mate_delta, base_weight, token_rows)
+    own_delta, mate_delta, base_blocks = weights(owner_map, codes, scales, base_weight)
+    projected = project(own_delta, mate_delta, base_blocks, [own_tokens] + token_rows[1:])
     arrived = [projected[0]] + [swap(projected[d], "group", 2 * d) for d in range(1, pairs)]
     pieces = pack_pieces(owner_map, arrived, owner_block, tensor_count, near_width, slice_width)
     pieces = [pieces[0]] + [swap(pieces[d], "tensor", d) for d in range(1, tensor_count)]

time: 48.9 us -> 40.7 us (0.83)
  local copies, waits for them, and re-layouts: 5.79 us -> 1.57 us
  other arithmetic: 2.32 us -> 0 us
  Pallas kernels: 11.9 us -> 10.4 us
    unnamed x36 -> x10, local copies, waits for them, and re-layouts: 4.36 us -> 1.57 us
    convert_element_type x1 -> x0, other arithmetic: 2.32 us -> none  [dequantize(): return (widened * block_scales.astype(jnp.float32)[:, :, None]).reshape(c...]
    pallas_call x0 -> x1, Pallas kernels: none -> 2.11 us  [weights(): pl.pallas_call(weights_kernel, out_shape=[delta, delta, jax.ShapeDtypeStr...]
    pallas_call x1, Pallas kernels: 2.73 us -> 1.29 us  [project(): pl.pallas_call(functools.partial(project_kernel, pairs), out_shape=[jax.S...]
    pallas_call x1, Pallas kernels: 2.93 us -> 1.7 us  [finish(): pl.pallas_call(functools.partial(finish_kernel, rows, steps, own, min(own...]
    pallas_call x1, Pallas kernels: 1.52 us -> 0.58 us  [pack_pieces(): pl.pallas_call(kernel, out_shape=[piece] * ways, in_specs=[SMEM] + [VMEM]...]
    convert_element_type x1 -> x0, local copies, waits for them, and re-layouts: 0.83 us -> none  [dequantize(): block_scales.astype(jnp.float32)[:, :, None]]
    mul x1 -> x0, local copies, waits for them, and re-layouts: 0.6 us -> none  [dequantize(): widened * block_scales.astype(jnp.float32)[:, :, None]]
  transfers between devices with their start and end apart: 13 -> 14, of which waited for: 4 -> 4; matrix products, arithmetic and copies ran while one was open for 0% -> 0% of each run, Pallas kernels for 18% -> 22%
where the time goes in v4:
time: 40.7 us; the launch traced here: 40.5 us
  starting transfers between devices  20.7 us (51%)
  Pallas kernels  10.4 us (26%)
  waiting for transfers between devices  7.07 us (17%)
  local copies, waits for them, and re-layouts  1.57 us (4%)
  between operations  0.7 us (2%)
    ppermute x14, starting transfers between devices, swap(): return lax.ppermute(x, axis, [(k, k ^ distance) for k in range(size)])  20.7 us
    ppermute x14, waiting for transfers between devices, swap(): return lax.ppermute(x, axis, [(k, k ^ distance) for k in range(size)])  7.07 us
    pallas_call x1, Pallas kernels, cache_partials(): pl.pallas_call(functools.partial(cache_kernel, rows, steps, own, chunk),...  4.74 us
    pallas_call x1, Pallas kernels, weights(): pl.pallas_call(weights_kernel, out_shape=[delta, delta, jax.ShapeDtypeStr...  2.11 us
    pallas_call x1, Pallas kernels, finish(): pl.pallas_call(functools.partial(finish_kernel, rows, steps, own, min(own...  1.7 us
    unnamed x10, local copies, waits for them, and re-layouts  1.57 us
    pallas_call x1, Pallas kernels, project(): pl.pallas_call(functools.partial(project_kernel, pairs), out_shape=[jax.S...  1.29 us
  transfers between devices with their start and end apart: 14, of which 4 were waited for; matrix products, arithmetic and copies ran while one was open for 0% of the time, Pallas kernels for 22%

profile of v4, /device:TPU:0, one launch (start us, length us, event | category | flops | bytes accessed | tf_op | source)
XLA Modules:
  0.0 40.5 jit_solution(4357995392480976902)
XLA Ops:
  0.6 0.0 copy-start
  0.6 0.5 %collective-permute-start = (bf16[256,2048]{1,0:T(8,128)(2,1)}, bf16[256,2048]{1,0:T(8,128)(2,1)S(1)}, u32[]{:S(2)}, u32[]{:S(2)}) collective-permute-start(bf16[256,2048]{1,0:T(8,128)(2,1)} %own_codes.1), channel_id=1, source_target_pairs={{0,4},{4,0},{8,12},{12,8},{16,20},{20,16},{24,28},{28,24},{1,5},{5... | collective-permute-start | bytes 3145736 | tf_op jit(solution)/shard_map/ppermute | solution.py:35
  1.2 2.6 %collective-permute-start.2 = (bf16[16,2048]{1,0:T(8,128)(2,1)}, bf16[16,2048]{1,0:T(8,128)(2,1)S(1)}, u32[]{:S(2)}, u32[]{:S(2)}) collective-permute-start(bf16[16,2048]{1,0:T(8,128)(2,1)} %bitcast.7), channel_id=1, source_target_pairs={{0,8},{4,12},{8,0},{12,4},{16,24},{20,28},{24,16},{28,20},{1,9},{5... | collective-permute-start | bytes 196616 | tf_op jit(solution)/shard_map/ppermute | solution.py:35
  3.8 2.6 %collective-permute-start.3 = (bf16[16,2048]{1,0:T(8,128)(2,1)}, bf16[16,2048]{1,0:T(8,128)(2,1)S(1)}, u32[]{:S(2)}, u32[]{:S(2)}) collective-permute-start(bf16[16,2048]{1,0:T(8,128)(2,1)} %bitcast.8), channel_id=1, source_target_pairs={{0,16},{4,20},{8,24},{12,28},{16,0},{20,4},{24,8},{28,12},{1,17},{... | collective-permute-start | bytes 196616 | tf_op jit(solution)/shard_map/ppermute | solution.py:35
  6.4 0.0 collective-permute-start.4
  6.4 0.0 collective-permute-start.1
  6.4 0.0 copy-start.1
  6.4 0.9 %copy-done.1 = bf16[2,8,2048]{2,1,0:T(8,128)(2,1)S(1)} copy-done((bf16[2,8,2048]{2,1,0:T(8,128)(2,1)S(1)}, bf16[2,8,2048]{2,1,0:T(8,128)(2,1)}, u32[]{:S(2)}) %copy-start.1) | copy-done | bytes 65560
  7.3 0.0 copy-start.4
  7.3 0.7 %copy-done.4 = s32[2]{0:T(128)S(1)} copy-done((s32[2]{0:T(128)S(1)}, s32[2]{0:T(128)}, u32[]{:S(2)}) %copy-start.4) | copy-done | bytes 32
  8.0 0.0 copy-start.2
  8.0 0.0 copy-start.3
  8.0 4.7 %cache_partials.1 = (bf16[16,2048]{1,0:T(8,128)(2,1)S(1)}, bf16[256,128]{1,0:T(8,128)(2,1)S(1)}, f32[264,128]{1,0:T(8,128)S(1)}, f32[264,128]{1,0:T(8,128)S(1)},...) custom-call(s32[2]{0:T(128)S(1)} %copy-done.4, bf16[16,2048]{1,0:T(8,128)(2,1)S(1)} %bitcast.10, ...), custom_call_target="tpu_custom_call" | custom-call | flops 134217728 | bytes 2359296 | tf_op jit(solution)/shard_map/cache_partials/pallas_call | solution.py:149
  12.7 0.0 collective-permute-done.1
  12.7 1.7 %collective-permute-start.11 = (f32[264,128]{1,0:T(8,128)S(1)}, f32[264,128]{1,0:T(8,128)S(1)}, u32[]{:S(2)}, u32[]{:S(2)}) collective-permute-start(f32[264,128]{1,0:T(8,128)S(1)} %get-tuple-element.35), channel_id=1, source_target_pairs={{0,1},{1,0},{2,3},{3,2},{4,5},{5,4},{6,7},{7,6},{8,9},{9,8},{10,11... | collective-permute-start | bytes 405512 | tf_op jit(solution)/shard_map/ppermute | solution.py:35
  14.5 0.0 collective-permute-done.mate_codes
  14.5 1.5 %collective-permute-start.12 = (f32[264,128]{1,0:T(8,128)S(1)}, f32[264,128]{1,0:T(8,128)S(1)}, u32[]{:S(2)}, u32[]{:S(2)}) collective-permute-start(f32[264,128]{1,0:T(8,128)S(1)} %get-tuple-element.36), channel_id=1, source_target_pairs={{0,2},{1,3},{2,0},{3,1},{4,6},{5,7},{6,4},{7,5},{8,10},{9,11},{10,... | collective-permute-start | bytes 405512 | tf_op jit(solution)/shard_map/ppermute | solution.py:35
  16.0 0.0 copy-done
  16.0 0.0 copy-done.2
  16.0 0.0 copy-done.3
  16.0 2.1 %weights.1 = (bf16[256,2048]{1,0:T(8,128)(2,1)S(1)}, bf16[256,2048]{1,0:T(8,128)(2,1)S(1)}, bf16[2,256,2048]{2,1,0:T(8,128)(2,1)S(1)}) custom-call(s32[8]{0:T(128)S(1)} %copy-done.3, bf16[256,2048]{1,0:T(8,128)(2,1)S(1)} %copy-done, bf16[256,2048]{1,0:T(8,128)(2,1)S(1)} %collective-permute-done.mate_codes, bf16[16,256]{1,0:T(8,128)(2,1)S(1)} %bitcast.11, ...), custom_call_target="tpu_custom_call" | custom-call | flops 1048576 | bytes 8388608 | tf_op jit(solution)/shard_map/weights/pallas_call | solution.py:73
  18.1 0.0 collective-permute-done.2.refs_1_
  18.1 0.4 collective-permute-start.13
  18.5 0.0 collective-permute-done.3.refs_2_
  18.5 0.0 collective-permute-done.4.refs_3_
  18.5 1.3 %project.1 = (f32[16,512]{1,0:T(8,128)S(1)}, f32[16,512]{1,0:T(8,128)S(1)}, f32[16,512]{1,0:T(8,128)S(1)}, f32[16,512]{1,0:T(8,128)S(1)}) custom-call(bf16[256,2048]{1,0:T(8,128)(2,1)S(1)} %get-tuple-element.22.own_ref, bf16[256,2048]{1,0:T(8,128)(2,1)S(1)} %get-tuple-element.23.mate_ref, bf16[2,256,2048]{2,1,0:T(8,128)(2,1)S(1)} %get-tuple-element.24.base_ref, ...), custom_call_target="tpu_custom_call" | custom-call | flops 268435456 | bytes 4194304 | tf_op jit(solution)/shard_map/project/pallas_call | solution.py:189
  19.8 0.9 %collective-permute-start.5 = (f32[16,512]{1,0:T(8,128)S(1)}, f32[16,512]{1,0:T(8,128)S(1)}, u32[]{:S(2)}, u32[]{:S(2)}) collective-permute-start(f32[16,512]{1,0:T(8,128)S(1)} %get-tuple-element.27), channel_id=1, source_target_pairs={{0,8},{4,12},{8,0},{12,4},{16,24},{20,28},{24,16},{28,20},{1,9},{5... | collective-permute-start | bytes 98312 | tf_op jit(solution)/shard_map/ppermute | solution.py:35
  20.7 3.5 %collective-permute-start.6 = (f32[16,512]{1,0:T(8,128)S(1)}, f32[16,512]{1,0:T(8,128)S(1)}, u32[]{:S(2)}, u32[]{:S(2)}) collective-permute-start(f32[16,512]{1,0:T(8,128)S(1)} %get-tuple-element.28), channel_id=1, source_target_pairs={{0,16},{4,20},{8,24},{12,28},{16,0},{20,4},{24,8},{28,12},{1,17},{... | collective-permute-start | bytes 98312 | tf_op jit(solution)/shard_map/ppermute | solution.py:35
  24.2 0.0 collective-permute-done.5.refs_1_
  24.2 3.4 %collective-permute-start.7 = (f32[16,512]{1,0:T(8,128)S(1)}, f32[16,512]{1,0:T(8,128)S(1)}, u32[]{:S(2)}, u32[]{:S(2)}) collective-permute-start(f32[16,512]{1,0:T(8,128)S(1)} %get-tuple-element.29), channel_id=1, source_target_pairs={{0,24},{4,28},{8,16},{12,20},{16,8},{20,12},{24,0},{28,4},{1,25},{... | collective-permute-start | bytes 98312 | tf_op jit(solution)/shard_map/ppermute | solution.py:35
  27.6 0.0 collective-permute-done.6.refs_2_
  27.6 2.4 %collective-permute-done.7.refs_3_ = f32[16,512]{1,0:T(8,128)S(1)} collective-permute-done((f32[16,512]{1,0:T(8,128)S(1)}, f32[16,512]{1,0:T(8,128)S(1)}, u32[]{:S(2)}, u32[]{:S(2)}) %collective-permute-start.7) | collective-permute-done | bytes 32800 | tf_op jit(solution)/shard_map/ppermute | solution.py:35
  29.9 0.6 %pack_pieces.1 = (f32[16,1024]{1,0:T(8,128)S(1)}, f32[16,1024]{1,0:T(8,128)S(1)}, f32[16,1024]{1,0:T(8,128)S(1)}, f32[16,1024]{1,0:T(8,128)S(1)}) custom-call(s32[8]{0:T(128)S(1)} %copy-done.3, f32[16,512]{1,0:T(8,128)S(1)} %get-tuple-element.26.refs_0_, f32[16,512]{1,0:T(8,128)S(1)} %collective-permute-done.5.refs_1_, ...), custom_call_target="tpu_custom_call" | custom-call | tf_op jit(solution)/shard_map/pack_pieces/pallas_call | solution.py:233
  30.5 1.6 %collective-permute-start.8 = (f32[16,1024]{1,0:T(8,128)S(1)}, f32[16,1024]{1,0:T(8,128)S(1)}, u32[]{:S(2)}, u32[]{:S(2)}) collective-permute-start(f32[16,1024]{1,0:T(8,128)S(1)} %get-tuple-element.31), channel_id=1, source_target_pairs={{0,1},{1,0},{2,3},{3,2},{4,5},{5,4},{6,7},{7,6},{8,9},{9,8},{10,11... | collective-permute-start | bytes 196616 | tf_op jit(solution)/shard_map/ppermute | solution.py:35
  32.1 1.5 %collective-permute-start.9 = (f32[16,1024]{1,0:T(8,128)S(1)}, f32[16,1024]{1,0:T(8,128)S(1)}, u32[]{:S(2)}, u32[]{:S(2)}) collective-permute-start(f32[16,1024]{1,0:T(8,128)S(1)} %get-tuple-element.32), channel_id=1, source_target_pairs={{0,2},{1,3},{2,0},{3,1},{4,6},{5,7},{6,4},{7,5},{8,10},{9,11},{10,... | collective-permute-start | bytes 196616 | tf_op jit(solution)/shard_map/ppermute | solution.py:35
  33.6 0.0 collective-permute-done.11.refs_5_
  33.6 0.5 %collective-permute-start.10 = (f32[16,1024]{1,0:T(8,128)S(1)}, f32[16,1024]{1,0:T(8,128)S(1)}, u32[]{:S(2)}, u32[]{:S(2)}) collective-permute-start(f32[16,1024]{1,0:T(8,128)S(1)} %get-tuple-element.33), channel_id=1, source_target_pairs={{0,3},{1,2},{2,1},{3,0},{4,7},{5,6},{6,5},{7,4},{8,11},{9,10},{10,... | collective-permute-start | bytes 196616 | tf_op jit(solution)/shard_map/ppermute | solution.py:35
  34.1 0.0 collective-permute-done.12.refs_6_
  34.1 0.0 collective-permute-done.13.refs_7_
  34.1 0.9 %collective-permute-done.8.refs_1_ = f32[16,1024]{1,0:T(8,128)S(1)} collective-permute-done((f32[16,1024]{1,0:T(8,128)S(1)}, f32[16,1024]{1,0:T(8,128)S(1)}, u32[]{:S(2)}, u32[]{:S(2)}) %collective-permute-start.8) | collective-permute-done | bytes 65568 | tf_op jit(solution)/shard_map/ppermute | solution.py:35
  35.0 1.3 %collective-permute-done.9.refs_2_ = f32[16,1024]{1,0:T(8,128)S(1)} collective-permute-done((f32[16,1024]{1,0:T(8,128)S(1)}, f32[16,1024]{1,0:T(8,128)S(1)}, u32[]{:S(2)}, u32[]{:S(2)}) %collective-permute-start.9) | collective-permute-done | bytes 65568 | tf_op jit(solution)/shard_map/ppermute | solution.py:35
  36.3 2.4 %collective-permute-done.10.refs_3_ = f32[16,1024]{1,0:T(8,128)S(1)} collective-permute-done((f32[16,1024]{1,0:T(8,128)S(1)}, f32[16,1024]{1,0:T(8,128)S(1)}, u32[]{:S(2)}, u32[]{:S(2)}) %collective-permute-start.10) | collective-permute-done | bytes 65568 | tf_op jit(solution)/shard_map/ppermute | solution.py:35
  38.8 1.7 %finish.1 = (bf16[16,512]{1,0:T(8,128)(2,1)}, bf16[16,2048]{1,0:T(8,128)(2,1)}) custom-call(bf16[256,128]{1,0:T(8,128)(2,1)S(1)} %get-tuple-element.21.query_ref, f32[16,1024]{1,0:T(8,128)S(1)} %get-tuple-element.30.refs_0_, f32[16,1024]{1,0:T(8,128)S(1)} %collective-permute-done.8.refs_1_, f32[16,1024]{1,0:T(8,128)S(1)} %collective-permute-done.9.refs_2_, ...), custom_call_target="tpu_custom_call" | custom-call | tf_op jit(solution)/shard_map/finish/pallas_call | solution.py:325
Async XLA Ops:
  0.6 15.4 %copy-start = (bf16[256,2048]{1,0:T(8,128)(2,1)S(1)}, bf16[256,2048]{1,0:T(8,128)(2,1)}, u32[]{:S(2)}) copy-start(bf16[256,2048]{1,0:T(8,128)(2,1)} %own_codes.1) | copy-start | bytes 3145732
  0.6 13.8 %collective-permute-start = (bf16[256,2048]{1,0:T(8,128)(2,1)}, bf16[256,2048]{1,0:T(8,128)(2,1)S(1)}, u32[]{:S(2)}, u32[]{:S(2)}) collective-permute-start(bf16[256,2048]{1,0:T(8,128)(2,1)} %own_codes.1), channel_id=1, source_target_pairs={{0,4},{4,0},{8,12},{12,8},{16,20},{20,16},{24,28},{28,24},{1,5},{5... | collective-permute-start | bytes 3145736 | tf_op jit(solution)/shard_map/ppermute | solution.py:35
  1.2 17.0 %collective-permute-start.2 = (bf16[16,2048]{1,0:T(8,128)(2,1)}, bf16[16,2048]{1,0:T(8,128)(2,1)S(1)}, u32[]{:S(2)}, u32[]{:S(2)}) collective-permute-start(bf16[16,2048]{1,0:T(8,128)(2,1)} %bitcast.7), channel_id=1, source_target_pairs={{0,8},{4,12},{8,0},{12,4},{16,24},{20,28},{24,16},{28,20},{1,9},{5... | collective-permute-start | bytes 196616 | tf_op jit(solution)/shard_map/ppermute | solution.py:35
  3.8 14.7 %collective-permute-start.3 = (bf16[16,2048]{1,0:T(8,128)(2,1)}, bf16[16,2048]{1,0:T(8,128)(2,1)S(1)}, u32[]{:S(2)}, u32[]{:S(2)}) collective-permute-start(bf16[16,2048]{1,0:T(8,128)(2,1)} %bitcast.8), channel_id=1, source_target_pairs={{0,16},{4,20},{8,24},{12,28},{16,0},{20,4},{24,8},{28,12},{1,17},{... | collective-permute-start | bytes 196616 | tf_op jit(solution)/shard_map/ppermute | solution.py:35
  6.4 12.1 %collective-permute-start.4 = (bf16[16,2048]{1,0:T(8,128)(2,1)}, bf16[16,2048]{1,0:T(8,128)(2,1)S(1)}, u32[]{:S(2)}, u32[]{:S(2)}) collective-permute-start(bf16[16,2048]{1,0:T(8,128)(2,1)} %bitcast.9), channel_id=1, source_target_pairs={{0,24},{4,28},{8,16},{12,20},{16,8},{20,12},{24,0},{28,4},{1,25},{... | collective-permute-start | bytes 196616 | tf_op jit(solution)/shard_map/ppermute | solution.py:35
  6.4 6.3 %collective-permute-start.1 = (bf16[256,16]{0,1:T(8,128)(2,1)}, bf16[256,16]{0,1:T(8,128)(2,1)S(1)}, u32[]{:S(2)}, u32[]{:S(2)}) collective-permute-start(bf16[256,16]{0,1:T(8,128)(2,1)} %param.11), channel_id=1, source_target_pairs={{0,4},{4,0},{8,12},{12,8},{16,20},{20,16},{24,28},{28,24},{1,5},{5... | collective-permute-start | bytes 24584 | tf_op jit(solution)/shard_map/ppermute | solution.py:35
  6.4 0.9 %copy-start.1 = (bf16[2,8,2048]{2,1,0:T(8,128)(2,1)S(1)}, bf16[2,8,2048]{2,1,0:T(8,128)(2,1)}, u32[]{:S(2)}) copy-start(bf16[2,8,2048]{2,1,0:T(8,128)(2,1)} %param.8) | copy-start | bytes 196612
  7.3 0.7 %copy-start.4 = (s32[2]{0:T(128)S(1)}, s32[2]{0:T(128)}, u32[]{:S(2)}) copy-start(s32[2]{0:T(128)} %lengths_ref.1) | copy-start | bytes 28
  8.0 8.0 %copy-start.2 = (bf16[256,16]{0,1:T(8,128)(2,1)S(1)}, bf16[256,16]{0,1:T(8,128)(2,1)}, u32[]{:S(2)}) copy-start(bf16[256,16]{0,1:T(8,128)(2,1)} %param.11) | copy-start | bytes 24580
  8.0 8.0 %copy-start.3 = (s32[8]{0:T(128)S(1)}, s32[8]{0:T(128)}, u32[]{:S(2)}) copy-start(s32[8]{0:T(128)} %owner_ref.3) | copy-start | bytes 100
  12.7 20.9 %collective-permute-start.11 = (f32[264,128]{1,0:T(8,128)S(1)}, f32[264,128]{1,0:T(8,128)S(1)}, u32[]{:S(2)}, u32[]{:S(2)}) collective-permute-start(f32[264,128]{1,0:T(8,128)S(1)} %get-tuple-element.35), channel_id=1, source_target_pairs={{0,1},{1,0},{2,3},{3,2},{4,5},{5,4},{6,7},{7,6},{8,9},{9,8},{10,11... | collective-permute-start | bytes 405512 | tf_op jit(solution)/shard_map/ppermute | solution.py:35
  14.5 19.6 %collective-permute-start.12 = (f32[264,128]{1,0:T(8,128)S(1)}, f32[264,128]{1,0:T(8,128)S(1)}, u32[]{:S(2)}, u32[]{:S(2)}) collective-permute-start(f32[264,128]{1,0:T(8,128)S(1)} %get-tuple-element.36), channel_id=1, source_target_pairs={{0,2},{1,3},{2,0},{3,1},{4,6},{5,7},{6,4},{7,5},{8,10},{9,11},{10,... | collective-permute-start | bytes 405512 | tf_op jit(solution)/shard_map/ppermute | solution.py:35
  18.1 15.9 %collective-permute-start.13 = (f32[264,128]{1,0:T(8,128)S(1)}, f32[264,128]{1,0:T(8,128)S(1)}, u32[]{:S(2)}, u32[]{:S(2)}) collective-permute-start(f32[264,128]{1,0:T(8,128)S(1)} %get-tuple-element.37), channel_id=1, source_target_pairs={{0,3},{1,2},{2,1},{3,0},{4,7},{5,6},{6,5},{7,4},{8,11},{9,10},{10,... | collective-permute-start | bytes 405512 | tf_op jit(solution)/shard_map/ppermute | solution.py:35
  19.8 4.4 %collective-permute-start.5 = (f32[16,512]{1,0:T(8,128)S(1)}, f32[16,512]{1,0:T(8,128)S(1)}, u32[]{:S(2)}, u32[]{:S(2)}) collective-permute-start(f32[16,512]{1,0:T(8,128)S(1)} %get-tuple-element.27), channel_id=1, source_target_pairs={{0,8},{4,12},{8,0},{12,4},{16,24},{20,28},{24,16},{28,20},{1,9},{5... | collective-permute-start | bytes 98312 | tf_op jit(solution)/shard_map/ppermute | solution.py:35
  20.7 6.8 %collective-permute-start.6 = (f32[16,512]{1,0:T(8,128)S(1)}, f32[16,512]{1,0:T(8,128)S(1)}, u32[]{:S(2)}, u32[]{:S(2)}) collective-permute-start(f32[16,512]{1,0:T(8,128)S(1)} %get-tuple-element.28), channel_id=1, source_target_pairs={{0,16},{4,20},{8,24},{12,28},{16,0},{20,4},{24,8},{28,12},{1,17},{... | collective-permute-start | bytes 98312 | tf_op jit(solution)/shard_map/ppermute | solution.py:35
  24.2 5.7 %collective-permute-start.7 = (f32[16,512]{1,0:T(8,128)S(1)}, f32[16,512]{1,0:T(8,128)S(1)}, u32[]{:S(2)}, u32[]{:S(2)}) collective-permute-start(f32[16,512]{1,0:T(8,128)S(1)} %get-tuple-element.29), channel_id=1, source_target_pairs={{0,24},{4,28},{8,16},{12,20},{16,8},{20,12},{24,0},{28,4},{1,25},{... | collective-permute-start | bytes 98312 | tf_op jit(solution)/shard_map/ppermute | solution.py:35
  30.5 4.5 %collective-permute-start.8 = (f32[16,1024]{1,0:T(8,128)S(1)}, f32[16,1024]{1,0:T(8,128)S(1)}, u32[]{:S(2)}, u32[]{:S(2)}) collective-permute-start(f32[16,1024]{1,0:T(8,128)S(1)} %get-tuple-element.31), channel_id=1, source_target_pairs={{0,1},{1,0},{2,3},{3,2},{4,5},{5,4},{6,7},{7,6},{8,9},{9,8},{10,11... | collective-permute-start | bytes 196616 | tf_op jit(solution)/shard_map/ppermute | solution.py:35
  32.1 4.3 %collective-permute-start.9 = (f32[16,1024]{1,0:T(8,128)S(1)}, f32[16,1024]{1,0:T(8,128)S(1)}, u32[]{:S(2)}, u32[]{:S(2)}) collective-permute-start(f32[16,1024]{1,0:T(8,128)S(1)} %get-tuple-element.32), channel_id=1, source_target_pairs={{0,2},{1,3},{2,0},{3,1},{4,6},{5,7},{6,4},{7,5},{8,10},{9,11},{10,... | collective-permute-start | bytes 196616 | tf_op jit(solution)/shard_map/ppermute | solution.py:35
  33.6 5.2 %collective-permute-start.10 = (f32[16,1024]{1,0:T(8,128)S(1)}, f32[16,1024]{1,0:T(8,128)S(1)}, u32[]{:S(2)}, u32[]{:S(2)}) collective-permute-start(f32[16,1024]{1,0:T(8,128)S(1)} %get-tuple-element.33), channel_id=1, source_target_pairs={{0,3},{1,2},{2,1},{3,0},{4,7},{5,6},{6,5},{7,4},{8,11},{9,10},{10,... | collective-permute-start | bytes 196616 | tf_op jit(solution)/shard_map/ppermute | solution.py:35

commit v5 on v4

--- a/solution.py
+++ b/solution.py
@@ -16,8 +16,8 @@
 
 NEGATIVE = -1e30
 SCORE_SCALE = HD ** (-0.5)
-CACHE_KIB = 53 << 10
-WEIGHTS_KIB = 46 << 10
+WEIGHTS_KIB = 47 << 10
+CACHE_KIB = 24 << 10
 PROJECT_KIB = 16 << 10
 NT = (((1,), (1,)), ((), ()))
 TN = (((0,), (0,)), ((), ()))
@@ -44,122 +44,101 @@
     return jnp.concatenate([mine[:, h * HD : (h + 1) * HD] for h in range(heads)], axis=0)
 
 
-def weights_kernel(owner_ref, own_codes, mate_codes, own_scales, mate_scales, base_hbm, *refs):
-    deltas, base_ref, arrived = refs[:2], refs[2], refs[3]
-    place = lax.axis_index("group")
-    block = own_codes.shape[0]
-    copies = []
+def weights_kernel(starts_ref, scales_ref, codes_ref, base_hbm, delta_ref, base_ref, arrived):
+    block = codes_ref.shape[0]
+    loads = []
     for k in range(2):
-        start = pl.multiple_of(owner_ref[place ^ k] * block, block)
-        copy = pltpu.make_async_copy(
-            base_hbm.at[pl.ds(start, block)], base_ref.at[k], arrived.at[k]
-        )
-        copy.start()
-        copies.append(copy)
-    for codes_ref, scales_ref, out_ref in zip(
-        (own_codes, mate_codes), (own_scales, mate_scales), deltas
-    ):
-        scales = scales_ref[...].astype(jnp.float32).T
-        for n in range(scales.shape[1]):
-            lanes = slice(n * BLK, (n + 1) * BLK)
-            values = codes_ref[:, lanes].astype(jnp.float32) * scales[:, n : n + 1]
-            out_ref[:, lanes] = values.astype(jnp.bfloat16)
-    for copy in copies:
-        copy.wait()
-
-
-def weights(owner_map, codes, scales, base_weight):
-    delta = jax.ShapeDtypeStruct(codes[0].shape, jnp.bfloat16)
+        start = starts_ref[lax.axis_index("group") ^ k]
+        here = pl.ds(pl.multiple_of(start, block), block)
+        loads.append(pltpu.make_async_copy(base_hbm.at[here], base_ref.at[k], arrived.at[k]))
+        loads[k].start()
+    scales = scales_ref[...].T
+    for n in range(scales.shape[1]):
+        lanes = slice(n * BLK, (n + 1) * BLK)
+        values = codes_ref[:, lanes].astype(jnp.float32) * scales[:, n : n + 1]
+        delta_ref[:, lanes] = values.astype(jnp.bfloat16)
+    for load in loads:
+        load.wait()
+
+
+def weights(starts, scales, codes, base):
     return pl.pallas_call(
         weights_kernel,
-        out_shape=[delta, delta, jax.ShapeDtypeStruct((2,) + delta.shape, jnp.bfloat16)],
-        in_specs=[SMEM] + [VMEM] * 4 + [HBM],
-        out_specs=[VMEM] * 3,
+        out_shape=[
+            jax.ShapeDtypeStruct(codes.shape, jnp.bfloat16),
+            jax.ShapeDtypeStruct((2,) + codes.shape, jnp.bfloat16),
+        ],
+        in_specs=[SMEM, VMEM, VMEM, HBM],
+        out_specs=[VMEM] * 2,
         scratch_shapes=[pltpu.SemaphoreType.DMA((2,))],
         compiler_params=params(WEIGHTS_KIB),
         cost_estimate=pl.CostEstimate(
-            flops=2 * delta.size, bytes_accessed=16 * delta.size, transcendentals=0
+            flops=codes.size, bytes_accessed=12 * codes.size, transcendentals=0
         ),
         name="weights",
-    )(owner_map, *codes, *[one.T for one in scales], base_weight)
-
-
-def cache_kernel(rows, steps, own, chunk, lengths_ref, tokens_hbm, query_hbm, cache_hbm, *refs):
-    tokens_ref, own_query_ref, parts = refs[0], refs[1], refs[2:-3]
-    query_ref, cache_ref, arrived = refs[-3:]
+    )(starts, scales.astype(jnp.float32).T, codes, base)
+
+
+def cache_kernel(rows, steps, own, chunk, limits_ref, query_ref, cache_ref, own_query_ref, *parts):
+    place = lax.axis_index("tensor")
     cache_len = cache_ref.shape[0] // rows
-    copies = [pltpu.make_async_copy(query_hbm, query_ref, arrived.at[0])]
-    for r in range(rows):
-        here = pl.ds(r * cache_len, cache_len)
-        copies.append(
-            pltpu.make_async_copy(cache_hbm.at[here], cache_ref.at[here], arrived.at[1 + r])
-        )
-    copies.append(pltpu.make_async_copy(tokens_hbm, tokens_ref, arrived.at[1 + rows]))
-    for copy in copies:
-        copy.start()
-    for copy in copies:
-        copy.wait()
-
-    place = lax.axis_index("tensor")
     chunks = own // chunk
     height = chunk * steps
     width = chunks * HD
     position = lax.broadcasted_iota(jnp.int32, (cache_len, chunks * height), 0)
-    usable = [position < lengths_ref[r] - place * cache_len for r in range(rows)]
-    for d, part in enumerate(parts):
+
+    def kv_lane(d):
+        return pl.multiple_of(((place ^ d) * own // (H // KVH)) * HD, HD)
+
+    def score(r, d):
         head = (place ^ d) * own
-        kv_lane = pl.multiple_of((head // (H // KVH)) * HD, HD)
-        block = query_ref[:, pl.ds(pl.multiple_of(head * HD, HD), own * HD)].astype(jnp.float32)
-        stats = []
-        for r in range(rows):
+        queries = query_ref[:, pl.ds(pl.multiple_of(head * HD, HD), own * HD)]
+        query = head_rows(queries.astype(jnp.float32), r, steps, own)
+        if d == 0:
             at = r * chunks * height
-            query = head_rows(block, r, steps, own)
-            if d == 0:
-                own_query_ref[at : at + chunks * height] = query.astype(jnp.bfloat16)
-            spread = []
-            for j in range(chunks):
-                line = [jnp.zeros((height, HD), jnp.float32)] * chunks
-                line[j] = query[j * height : (j + 1) * height]
-                spread.append(jnp.concatenate(line, axis=1))
-            spread = jnp.concatenate(spread, axis=0).astype(jnp.bfloat16)
-            here = pl.ds(r * cache_len, cache_len)
-            keys = cache_ref[here, pl.ds(kv_lane, width)]
-            values = cache_ref[here, pl.ds(kv_lane + KVH * HD, width)]
-            scores = jnp.where(usable[r], dot(keys, spread, NT) * SCORE_SCALE, 2.0 * NEGATIVE)
-            peak = jnp.maximum(jnp.max(scores, axis=0, keepdims=True), NEGATIVE)
-            weights = jnp.exp(scores - peak)
-            stats += [peak, jnp.sum(weights, axis=0, keepdims=True)]
-            sums = dot(weights.astype(jnp.bfloat16), values, TN)
-            for j in range(chunks):
-                here = slice(j * height, (j + 1) * height)
-                part[at + j * height : at + (j + 1) * height] = sums[here, j * HD : (j + 1) * HD]
-        stats.append(jnp.zeros((SUBLANES - 2 * rows, chunks * height), jnp.float32))
-        stats = jnp.concatenate(stats, axis=0)
-        if chunks * height < LANES:
-            pad = jnp.zeros((SUBLANES, LANES - chunks * height), jnp.float32)
-            stats = jnp.concatenate([stats, pad], axis=1)
-        end = rows * chunks * height
-        part[end : end + SUBLANES] = stats
-
-
-def cache_partials(tokens, queries, cache, lengths, rows, steps, own, ways):
-    chunk = min(own, H // KVH)
+            own_query_ref[at : at + chunks * height] = query.astype(jnp.bfloat16)
+        spread = []
+        for j in range(chunks):
+            line = [jnp.zeros((height, HD), jnp.float32)] * chunks
+            line[j] = query[j * height : (j + 1) * height]
+            spread.append(jnp.concatenate(line, axis=1))
+        spread = jnp.concatenate(spread, axis=0).astype(jnp.bfloat16)
+        keys = cache_ref[pl.ds(r * cache_len, cache_len), pl.ds(kv_lane(d), width)]
+        return dot(keys, spread, NT)
+
+    units = [(r, d) for r in range(rows) for d in range(len(parts))]
+    ahead = []
+    for n in range(len(units) + 1):
+        if n < len(units):
+            ahead.append(score(*units[n]))
+        if n == 0:
+            continue
+        r, d = units[n - 1]
+        at = r * chunks * height
+        usable = position < limits_ref[r]
+        scores = jnp.where(usable, ahead.pop(0) * SCORE_SCALE, 2.0 * NEGATIVE)
+        peak = jnp.maximum(jnp.max(scores, axis=0, keepdims=True), NEGATIVE)
+        weights = jnp.exp(scores - peak)
+        total = jnp.sum(weights, axis=0, keepdims=True)
+        lane = pl.ds(kv_lane(d) + KVH * HD, width)
+        values = cache_ref[pl.ds(r * cache_len, cache_len), lane]
+        sums = dot(weights.astype(jnp.bfloat16), values, TN)
+        for j in range(chunks):
+            here = slice(j * height, (j + 1) * height)
+            parts[d][at + j * height : at + (j + 1) * height] = sums[here, j * HD : (j + 1) * HD]
+        end = rows * chunks * height + 2 * r
+        parts[d][end : end + 1, : chunks * height] = peak
+        parts[d][end + 1 : end + 2, : chunks * height] = total
+
+
+def cache_partials(limits, queries, cache, rows, steps, own, ways):
     height = rows * own * steps
     part = jax.ShapeDtypeStruct((height + SUBLANES, LANES), jnp.float32)
     out = pl.pallas_call(
-        functools.partial(cache_kernel, rows, steps, own, chunk),
-        out_shape=[
-            jax.ShapeDtypeStruct(tokens.shape, tokens.dtype),
-            jax.ShapeDtypeStruct((height, HD), jnp.bfloat16),
-        ]
-        + [part] * ways,
-        in_specs=[SMEM, HBM, HBM, HBM],
-        out_specs=[VMEM] * (2 + ways),
-        scratch_shapes=[
-            pltpu.VMEM(queries.shape, queries.dtype),
-            pltpu.VMEM(cache.shape, cache.dtype),
-            pltpu.SemaphoreType.DMA((2 + rows,)),
-        ],
+        functools.partial(cache_kernel, rows, steps, own, min(own, H // KVH)),
+        out_shape=[jax.ShapeDtypeStruct((height, HD), jnp.bfloat16)] + [part] * ways,
+        in_specs=[SMEM, VMEM, VMEM],
+        out_specs=[VMEM] * (1 + ways),
         compiler_params=params(CACHE_KIB),
         cost_estimate=pl.CostEstimate(
             flops=4 * height * ways * HD * cache.shape[0] // rows,
@@ -167,8 +146,8 @@
             transcendentals=height * ways * cache.shape[0] // rows,
         ),
         name="cache_partials",
-    )(lengths, tokens, queries, cache)
-    return out[0], out[1], out[2:]
+    )(limits, queries, cache)
+    return out[0], out[1:]
 
 
 def project_kernel(pairs, own_ref, mate_ref, base_ref, *refs):
@@ -352,14 +331,15 @@
 
     mine = hidden_x.reshape(tokens, local_width)
     token_rows = [mine] + [swap(mine, "group", 2 * d) for d in range(1, pairs)]
-    codes = [delta_codes, swap(delta_codes, "group", 1)]
-    scales = [delta_scales, swap(delta_scales, "group", 1)]
-
-    own_tokens, own_query, partials = cache_partials(
-        mine,
+    own_delta, base_blocks = weights(
+        owner_map * owner_block, delta_scales, delta_codes, base_weight
+    )
+    mate_delta = swap(own_delta, "group", 1)
+    cache_len = kv_cache.shape[1]
+    own_query, partials = cache_partials(
+        lengths - lax.axis_index("tensor") * cache_len,
         queries.reshape(tokens, H * HD),
-        kv_cache.reshape(-1, 2 * KVH * HD),
-        lengths,
+        kv_cache.reshape(rows * cache_len, 2 * KVH * HD),
         rows,
         steps,
         heads_own,
@@ -367,8 +347,7 @@
     )
     partials = [partials[0]] + [swap(partials[d], "tensor", d) for d in range(1, tensor_count)]
 
-    own_delta, mate_delta, base_blocks = weights(owner_map, codes, scales, base_weight)
-    projected = project(own_delta, mate_delta, base_blocks, [own_tokens] + token_rows[1:])
+    projected = project(own_delta, mate_delta, base_blocks, token_rows)
     arrived = [projected[0]] + [swap(projected[d], "group", 2 * d) for d in range(1, pairs)]
     pieces = pack_pieces(owner_map, arrived, owner_block, tensor_count, near_width, slice_width)
     pieces = [pieces[0]] + [swap(pieces[d], "tensor", d) for d in range(1, tensor_count)]

time: 40.7 us -> 41.8 us (1.027)
  waiting for transfers between devices: 7.07 us -> 5.56 us
  starting transfers between devices: 20.7 us -> 22.2 us
  other arithmetic: 0 us -> 1.36 us
  Pallas kernels: 10.4 us -> 9.11 us
  local copies, waits for them, and re-layouts: 1.57 us -> 2.58 us
    pallas_call x2, Pallas kernels: 6.85 us -> 4.27 us  [the longest x1 2.3 us: weights(): pl.pallas_call(weights_kernel, out_shape=[jax.ShapeDtypeStruct(codes.shap...]
    ppermute x14 -> x13, waiting for transfers between devices: 7.07 us -> 5.56 us  [swap(): return lax.ppermute(x, axis, [(k, k ^ distance) for k in range(size)])]
    ppermute x14 -> x13, starting transfers between devices: 20.7 us -> 22.2 us  [swap(): return lax.ppermute(x, axis, [(k, k ^ distance) for k in range(size)])]
    pallas_call x1, Pallas kernels: 1.29 us -> 2.56 us  [project(): pl.pallas_call(functools.partial(project_kernel, pairs), out_shape=[jax.S...]
    unnamed x10 -> x16, local copies, waits for them, and re-layouts: 1.57 us -> 2.58 us
    transpose x0 -> x1, other arithmetic: none -> 0.7 us  [weights(): scales.astype(jnp.float32)]
    mul x0 -> x1, other arithmetic: none -> 0.66 us  [on_device(): owner_map * owner_block]
  transfers between devices with their start and end apart: 14 -> 13, of which waited for: 4 -> 4; matrix products, arithmetic and copies ran while one was open for 0% -> 0% of each run, Pallas kernels for 22% -> 12%
where the time goes in v5:
time: 41.8 us; the launch traced here: 41.5 us
  starting transfers between devices  22.2 us (53%)
  Pallas kernels  9.11 us (22%)
  waiting for transfers between devices  5.56 us (13%)
  local copies, waits for them, and re-layouts  2.58 us (6%)
  other arithmetic  1.36 us (3%)
  between operations  0.72 us (2%)
    ppermute x13, starting transfers between devices, swap(): return lax.ppermute(x, axis, [(k, k ^ distance) for k in range(size)])  22.2 us
    ppermute x13, waiting for transfers between devices, swap(): return lax.ppermute(x, axis, [(k, k ^ distance) for k in range(size)])  5.56 us
    unnamed x16, local copies, waits for them, and re-layouts  2.58 us
    pallas_call x1, Pallas kernels, project(): pl.pallas_call(functools.partial(project_kernel, pairs), out_shape=[jax.S...  2.56 us
    pallas_call x1, Pallas kernels, weights(): pl.pallas_call(weights_kernel, out_shape=[jax.ShapeDtypeStruct(codes.shap...  2.3 us
    pallas_call x1, Pallas kernels, cache_partials(): pl.pallas_call(functools.partial(cache_kernel, rows, steps, own, min(own,...  1.96 us
    pallas_call x1, Pallas kernels, finish(): pl.pallas_call(functools.partial(finish_kernel, rows, steps, own, min(own...  1.7 us
  transfers between devices with their start and end apart: 13, of which 4 were waited for; matrix products, arithmetic and copies ran while one was open for 0% of the time, Pallas kernels for 12%

profile of v5, /device:TPU:0, one launch (start us, length us, event | category | flops | bytes accessed | tf_op | source)
XLA Modules:
  0.0 41.5 jit_solution(4180537197662716020)
XLA Ops:
  0.6 0.7 %convert_bitcast_fusion.scales_ref = f32[16,256]{1,0:T(8,128)S(1)} fusion(bf16[256,16]{0,1:T(8,128)(2,1)} %param.11), kind=kLoop, calls=%fused_computation | loop fusion | flops 4096 | bytes 24576 | tf_op jit(solution)/shard_map/transpose | solution.py:79
  1.3 0.7 %broadcast_multiply_fusion.starts_ref = s32[8]{0:T(128)S(1)} fusion(s32[8]{0:T(128)} %owner_ref.1), kind=kLoop, calls=%fused_computation.1 | loop fusion | flops 8 | bytes 64 | tf_op jit(solution)/shard_map/mul | solution.py:335
  2.0 0.0 copy-start.3
  2.0 1.2 %copy-done.3 = bf16[256,2048]{1,0:T(8,128)(2,1)S(1)} copy-done((bf16[256,2048]{1,0:T(8,128)(2,1)S(1)}, bf16[256,2048]{1,0:T(8,128)(2,1)}, u32[]{:S(2)}) %copy-start.3) | copy-done | bytes 1048600
  3.2 0.0 copy-start.5
  3.2 0.0 copy-start.7
  3.2 0.0 copy-start
  3.2 0.0 copy-start.4
  3.2 2.3 %weights.1 = (bf16[256,2048]{1,0:T(8,128)(2,1)S(1)}, bf16[2,256,2048]{2,1,0:T(8,128)(2,1)S(1)}) custom-call(s32[8]{0:T(128)S(1)} %broadcast_multiply_fusion.starts_ref, f32[16,256]{1,0:T(8,128)S(1)} %convert_bitcast_fusion.scales_ref, bf16[256,2048]{1,0:T(8,128)(2,1)S(1)} %copy-done.3, bf16[2048,2048]{1,0:T(8,128)(2,1)} %base_hbm.1), custom_call_target="tpu_custom_call" | custom-call | flops 524288 | bytes 6291456 | tf_op jit(solution)/shard_map/weights/pallas_call | solution.py:65
  5.5 0.0 copy-start.1
  5.5 1.3 %copy-done.1 = bf16[2,256,2048]{2,1,0:T(8,128)(2,1)} copy-done((bf16[2,256,2048]{2,1,0:T(8,128)(2,1)}, bf16[2,256,2048]{2,1,0:T(8,128)(2,1)S(1)}, u32[]{:S(2)}) %copy-start.1) | copy-done | bytes 2097176
  6.9 0.5 %collective-permute-start = (bf16[256,2048]{1,0:T(8,128)(2,1)S(1)}, bf16[256,2048]{1,0:T(8,128)(2,1)}, u32[]{:S(2)}, u32[]{:S(2)}) collective-permute-start(bf16[256,2048]{1,0:T(8,128)(2,1)S(1)} %get-tuple-element.20.own_ref), channel_id=1, source_target_pairs={{0,4},{4,0},{8,12},{12,8},{16,20},{20,16},{24,28},{28,24},{1,5},{5... | collective-permute-start | bytes 3145736 | tf_op jit(solution)/shard_map/ppermute | solution.py:35
  7.3 0.0 copy-done.5
  7.3 2.6 %collective-permute-start.1 = (bf16[16,2048]{1,0:T(8,128)(2,1)S(1)}, bf16[16,2048]{1,0:T(8,128)(2,1)S(1)}, u32[]{:S(2)}, u32[]{:S(2)}) collective-permute-start(bf16[16,2048]{1,0:T(8,128)(2,1)S(1)} %bitcast.9), channel_id=1, source_target_pairs={{0,8},{4,12},{8,0},{12,4},{16,24},{20,28},{24,16},{28,20},{1,9},{5... | collective-permute-start | bytes 196616 | tf_op jit(solution)/shard_map/ppermute | solution.py:35
  9.9 2.6 %collective-permute-start.2 = (bf16[16,2048]{1,0:T(8,128)(2,1)S(1)}, bf16[16,2048]{1,0:T(8,128)(2,1)}, u32[]{:S(2)}, u32[]{:S(2)}) collective-permute-start(bf16[16,2048]{1,0:T(8,128)(2,1)S(1)} %bitcast.10), channel_id=1, source_target_pairs={{0,16},{4,20},{8,24},{12,28},{16,0},{20,4},{24,8},{28,12},{1,17},{... | collective-permute-start | bytes 196616 | tf_op jit(solution)/shard_map/ppermute | solution.py:35
  12.5 0.0 collective-permute-start.3
  12.5 0.0 copy-done.7
  12.5 0.0 copy-start.2
  12.5 0.0 copy-done
  12.5 0.0 copy-done.4
  12.5 2.0 %cache_partials.1 = (bf16[256,128]{1,0:T(8,128)(2,1)S(1)}, f32[264,128]{1,0:T(8,128)S(1)}, f32[264,128]{1,0:T(8,128)S(1)}, f32[264,128]{1,0:T(8,128)S(1)}, f32[264,128]{1,0:T(8,128)S(1)}) custom-call(s32[2]{0:T(128)S(1)} %broadcast_subtract_fusion.limits_ref, bf16[16,8192]{1,0:T(8,128)(2,1)S(1)} %bitcast.8, bf16[512,2048]{1,0:T(8,128)(2,1)S(1)} %bitcast.7), custom_call_target="tpu_custom_call" | custom-call | flops 134217728 | bytes 2359296 | tf_op jit(solution)/shard_map/cache_partials/pallas_call | solution.py:137
  14.5 1.8 %collective-permute-start.10 = (f32[264,128]{1,0:T(8,128)S(1)}, f32[264,128]{1,0:T(8,128)S(1)}, u32[]{:S(2)}, u32[]{:S(2)}) collective-permute-start(f32[264,128]{1,0:T(8,128)S(1)} %get-tuple-element.31), channel_id=1, source_target_pairs={{0,1},{1,0},{2,3},{3,2},{4,5},{5,4},{6,7},{7,6},{8,9},{9,8},{10,11... | collective-permute-start | bytes 405512 | tf_op jit(solution)/shard_map/ppermute | solution.py:35
  16.3 0.0 collective-permute-done.1.refs_1_
  16.3 1.5 %collective-permute-start.11 = (f32[264,128]{1,0:T(8,128)S(1)}, f32[264,128]{1,0:T(8,128)S(1)}, u32[]{:S(2)}, u32[]{:S(2)}) collective-permute-start(f32[264,128]{1,0:T(8,128)S(1)} %get-tuple-element.32), channel_id=1, source_target_pairs={{0,2},{1,3},{2,0},{3,1},{4,6},{5,7},{6,4},{7,5},{8,10},{9,11},{10,... | collective-permute-start | bytes 405512 | tf_op jit(solution)/shard_map/ppermute | solution.py:35
  17.8 0.0 collective-permute-done.2.refs_2_
  17.8 1.6 %collective-permute-start.12 = (f32[264,128]{1,0:T(8,128)S(1)}, f32[264,128]{1,0:T(8,128)S(1)}, u32[]{:S(2)}, u32[]{:S(2)}) collective-permute-start(f32[264,128]{1,0:T(8,128)S(1)} %get-tuple-element.33), channel_id=1, source_target_pairs={{0,3},{1,2},{2,1},{3,0},{4,7},{5,6},{6,5},{7,4},{8,11},{9,10},{10,... | collective-permute-start | bytes 405512 | tf_op jit(solution)/shard_map/ppermute | solution.py:35
  19.4 0.0 collective-permute-done.3.refs_3_
  19.4 0.0 collective-permute-done.mate_ref
  19.4 0.0 copy-done.2
  19.4 0.0 copy-start.6
  19.4 2.6 %project.1 = (f32[16,512]{1,0:T(8,128)S(1)}, f32[16,512]{1,0:T(8,128)S(1)}, f32[16,512]{1,0:T(8,128)S(1)}, f32[16,512]{1,0:T(8,128)S(1)}) custom-call(bf16[256,2048]{1,0:T(8,128)(2,1)S(1)} %get-tuple-element.20.own_ref, bf16[256,2048]{1,0:T(8,128)(2,1)} %collective-permute-done.mate_ref, bf16[2,256,2048]{2,1,0:T(8,128)(2,1)S(1)} %copy-done.2, ...), custom_call_target="tpu_custom_call" | custom-call | flops 268435456 | bytes 4194304 | tf_op jit(solution)/shard_map/project/pallas_call | solution.py:168
  22.0 1.3 %collective-permute-start.4 = (f32[16,512]{1,0:T(8,128)S(1)}, f32[16,512]{1,0:T(8,128)S(1)}, u32[]{:S(2)}, u32[]{:S(2)}) collective-permute-start(f32[16,512]{1,0:T(8,128)S(1)} %get-tuple-element.23), channel_id=1, source_target_pairs={{0,8},{4,12},{8,0},{12,4},{16,24},{20,28},{24,16},{28,20},{1,9},{5... | collective-permute-start | bytes 98312 | tf_op jit(solution)/shard_map/ppermute | solution.py:35
  23.3 3.5 %collective-permute-start.5 = (f32[16,512]{1,0:T(8,128)S(1)}, f32[16,512]{1,0:T(8,128)S(1)}, u32[]{:S(2)}, u32[]{:S(2)}) collective-permute-start(f32[16,512]{1,0:T(8,128)S(1)} %get-tuple-element.24), channel_id=1, source_target_pairs={{0,16},{4,20},{8,24},{12,28},{16,0},{20,4},{24,8},{28,12},{1,17},{... | collective-permute-start | bytes 98312 | tf_op jit(solution)/shard_map/ppermute | solution.py:35
  26.8 0.0 collective-permute-done.4.refs_1_
  26.8 3.3 %collective-permute-start.6 = (f32[16,512]{1,0:T(8,128)S(1)}, f32[16,512]{1,0:T(8,128)S(1)}, u32[]{:S(2)}, u32[]{:S(2)}) collective-permute-start(f32[16,512]{1,0:T(8,128)S(1)} %get-tuple-element.25), channel_id=1, source_target_pairs={{0,24},{4,28},{8,16},{12,20},{16,8},{20,12},{24,0},{28,4},{1,25},{... | collective-permute-start | bytes 98312 | tf_op jit(solution)/shard_map/ppermute | solution.py:35
  30.1 0.0 collective-permute-done.5.refs_2_
  30.1 2.4 %collective-permute-done.6.refs_3_ = f32[16,512]{1,0:T(8,128)S(1)} collective-permute-done((f32[16,512]{1,0:T(8,128)S(1)}, f32[16,512]{1,0:T(8,128)S(1)}, u32[]{:S(2)}, u32[]{:S(2)}) %collective-permute-start.6) | collective-permute-done | bytes 32800 | tf_op jit(solution)/shard_map/ppermute | solution.py:35
  32.5 0.0 copy-done.6
  32.5 0.6 %pack_pieces.1 = (f32[16,1024]{1,0:T(8,128)S(1)}, f32[16,1024]{1,0:T(8,128)S(1)}, f32[16,1024]{1,0:T(8,128)S(1)}, f32[16,1024]{1,0:T(8,128)S(1)}) custom-call(s32[8]{0:T(128)S(1)} %copy-done.6, f32[16,512]{1,0:T(8,128)S(1)} %get-tuple-element.22.refs_0_, f32[16,512]{1,0:T(8,128)S(1)} %collective-permute-done.4.refs_1_, ...), custom_call_target="tpu_custom_call" | custom-call | tf_op jit(solution)/shard_map/pack_pieces/pallas_call | solution.py:212
  33.1 0.6 %collective-permute-start.7 = (f32[16,1024]{1,0:T(8,128)S(1)}, f32[16,1024]{1,0:T(8,128)S(1)}, u32[]{:S(2)}, u32[]{:S(2)}) collective-permute-start(f32[16,1024]{1,0:T(8,128)S(1)} %get-tuple-element.27), channel_id=1, source_target_pairs={{0,1},{1,0},{2,3},{3,2},{4,5},{5,4},{6,7},{7,6},{8,9},{9,8},{10,11... | collective-permute-start | bytes 196616 | tf_op jit(solution)/shard_map/ppermute | solution.py:35
  33.7 1.0 %collective-permute-start.8 = (f32[16,1024]{1,0:T(8,128)S(1)}, f32[16,1024]{1,0:T(8,128)S(1)}, u32[]{:S(2)}, u32[]{:S(2)}) collective-permute-start(f32[16,1024]{1,0:T(8,128)S(1)} %get-tuple-element.28), channel_id=1, source_target_pairs={{0,2},{1,3},{2,0},{3,1},{4,6},{5,7},{6,4},{7,5},{8,10},{9,11},{10,... | collective-permute-start | bytes 196616 | tf_op jit(solution)/shard_map/ppermute | solution.py:35
  34.7 0.0 collective-permute-done.10.refs_5_
  34.7 2.0 %collective-permute-start.9 = (f32[16,1024]{1,0:T(8,128)S(1)}, f32[16,1024]{1,0:T(8,128)S(1)}, u32[]{:S(2)}, u32[]{:S(2)}) collective-permute-start(f32[16,1024]{1,0:T(8,128)S(1)} %get-tuple-element.29), channel_id=1, source_target_pairs={{0,3},{1,2},{2,1},{3,0},{4,7},{5,6},{6,5},{7,4},{8,11},{9,10},{10,... | collective-permute-start | bytes 196616 | tf_op jit(solution)/shard_map/ppermute | solution.py:35
  36.6 0.0 collective-permute-done.11.refs_6_
  36.6 0.0 collective-permute-done.12.refs_7_
  36.7 0.8 %collective-permute-done.7.refs_1_ = f32[16,1024]{1,0:T(8,128)S(1)} collective-permute-done((f32[16,1024]{1,0:T(8,128)S(1)}, f32[16,1024]{1,0:T(8,128)S(1)}, u32[]{:S(2)}, u32[]{:S(2)}) %collective-permute-start.7) | collective-permute-done | bytes 65568 | tf_op jit(solution)/shard_map/ppermute | solution.py:35
  37.4 0.5 %collective-permute-done.8.refs_2_ = f32[16,1024]{1,0:T(8,128)S(1)} collective-permute-done((f32[16,1024]{1,0:T(8,128)S(1)}, f32[16,1024]{1,0:T(8,128)S(1)}, u32[]{:S(2)}, u32[]{:S(2)}) %collective-permute-start.8) | collective-permute-done | bytes 65568 | tf_op jit(solution)/shard_map/ppermute | solution.py:35
  38.0 1.9 %collective-permute-done.9.refs_3_ = f32[16,1024]{1,0:T(8,128)S(1)} collective-permute-done((f32[16,1024]{1,0:T(8,128)S(1)}, f32[16,1024]{1,0:T(8,128)S(1)}, u32[]{:S(2)}, u32[]{:S(2)}) %collective-permute-start.9) | collective-permute-done | bytes 65568 | tf_op jit(solution)/shard_map/ppermute | solution.py:35
  39.8 1.7 %finish.1 = (bf16[16,512]{1,0:T(8,128)(2,1)}, bf16[16,2048]{1,0:T(8,128)(2,1)}) custom-call(bf16[256,128]{1,0:T(8,128)(2,1)S(1)} %get-tuple-element.19.query_ref, f32[16,1024]{1,0:T(8,128)S(1)} %get-tuple-element.26.refs_0_, f32[16,1024]{1,0:T(8,128)S(1)} %collective-permute-done.7.refs_1_, f32[16,1024]{1,0:T(8,128)S(1)} %collective-permute-done.8.refs_2_, ...), custom_call_target="tpu_custom_call" | custom-call | tf_op jit(solution)/shard_map/finish/pallas_call | solution.py:304
  (1 shorter events, 0.0 us)
Async XLA Ops:
  2.0 1.2 %copy-start.3 = (bf16[256,2048]{1,0:T(8,128)(2,1)S(1)}, bf16[256,2048]{1,0:T(8,128)(2,1)}, u32[]{:S(2)}) copy-start(bf16[256,2048]{1,0:T(8,128)(2,1)} %codes_ref.1) | copy-start | bytes 3145732
  3.2 4.1 %copy-start.5 = (bf16[2,8,2048]{2,1,0:T(8,128)(2,1)S(1)}, bf16[2,8,2048]{2,1,0:T(8,128)(2,1)}, u32[]{:S(2)}) copy-start(bf16[2,8,2048]{2,1,0:T(8,128)(2,1)} %param.8) | copy-start | bytes 196612
  3.2 9.3 %copy-start.7 = (s32[2]{0:T(128)S(1)}, s32[2]{0:T(128)}, u32[]{:S(2)}) copy-start(s32[2]{0:T(128)} %param.15) | copy-start | bytes 28
  3.2 9.3 %copy-start = (bf16[2,256,2048]{2,1,0:T(8,128)(2,1)S(1)}, bf16[2,256,2048]{2,1,0:T(8,128)(2,1)}, u32[]{:S(2)}) copy-start(bf16[2,256,2048]{2,1,0:T(8,128)(2,1)} %param.13) | copy-start | bytes 6291460
  3.2 9.3 %copy-start.4 = (bf16[2,8,8192]{2,1,0:T(8,128)(2,1)S(1)}, bf16[2,8,8192]{2,1,0:T(8,128)(2,1)}, u32[]{:S(2)}) copy-start(bf16[2,8,8192]{2,1,0:T(8,128)(2,1)} %param.14) | copy-start | bytes 786436
  5.5 1.3 %copy-start.1 = (bf16[2,256,2048]{2,1,0:T(8,128)(2,1)}, bf16[2,256,2048]{2,1,0:T(8,128)(2,1)S(1)}, u32[]{:S(2)}) copy-start(bf16[2,256,2048]{2,1,0:T(8,128)(2,1)S(1)} %get-tuple-element.21.base_ref) | copy-start | bytes 6291460
  6.9 12.5 %collective-permute-start = (bf16[256,2048]{1,0:T(8,128)(2,1)S(1)}, bf16[256,2048]{1,0:T(8,128)(2,1)}, u32[]{:S(2)}, u32[]{:S(2)}) collective-permute-start(bf16[256,2048]{1,0:T(8,128)(2,1)S(1)} %get-tuple-element.20.own_ref), channel_id=1, source_target_pairs={{0,4},{4,0},{8,12},{12,8},{16,20},{20,16},{24,28},{28,24},{1,5},{5... | collective-permute-start | bytes 3145736 | tf_op jit(solution)/shard_map/ppermute | solution.py:35
  7.3 8.9 %collective-permute-start.1 = (bf16[16,2048]{1,0:T(8,128)(2,1)S(1)}, bf16[16,2048]{1,0:T(8,128)(2,1)S(1)}, u32[]{:S(2)}, u32[]{:S(2)}) collective-permute-start(bf16[16,2048]{1,0:T(8,128)(2,1)S(1)} %bitcast.9), channel_id=1, source_target_pairs={{0,8},{4,12},{8,0},{12,4},{16,24},{20,28},{24,16},{28,20},{1,9},{5... | collective-permute-start | bytes 196616 | tf_op jit(solution)/shard_map/ppermute | solution.py:35
  9.9 7.9 %collective-permute-start.2 = (bf16[16,2048]{1,0:T(8,128)(2,1)S(1)}, bf16[16,2048]{1,0:T(8,128)(2,1)}, u32[]{:S(2)}, u32[]{:S(2)}) collective-permute-start(bf16[16,2048]{1,0:T(8,128)(2,1)S(1)} %bitcast.10), channel_id=1, source_target_pairs={{0,16},{4,20},{8,24},{12,28},{16,0},{20,4},{24,8},{28,12},{1,17},{... | collective-permute-start | bytes 196616 | tf_op jit(solution)/shard_map/ppermute | solution.py:35
  12.5 6.9 %collective-permute-start.3 = (bf16[16,2048]{1,0:T(8,128)(2,1)S(1)}, bf16[16,2048]{1,0:T(8,128)(2,1)}, u32[]{:S(2)}, u32[]{:S(2)}) collective-permute-start(bf16[16,2048]{1,0:T(8,128)(2,1)S(1)} %bitcast.11), channel_id=1, source_target_pairs={{0,24},{4,28},{8,16},{12,20},{16,8},{20,12},{24,0},{28,4},{1,25},{... | collective-permute-start | bytes 196616 | tf_op jit(solution)/shard_map/ppermute | solution.py:35
  12.5 6.9 %copy-start.2 = (bf16[2,256,2048]{2,1,0:T(8,128)(2,1)S(1)}, bf16[2,256,2048]{2,1,0:T(8,128)(2,1)}, u32[]{:S(2)}) copy-start(bf16[2,256,2048]{2,1,0:T(8,128)(2,1)} %copy-done.1) | copy-start | bytes 6291460
  14.5 20.2 %collective-permute-start.10 = (f32[264,128]{1,0:T(8,128)S(1)}, f32[264,128]{1,0:T(8,128)S(1)}, u32[]{:S(2)}, u32[]{:S(2)}) collective-permute-start(f32[264,128]{1,0:T(8,128)S(1)} %get-tuple-element.31), channel_id=1, source_target_pairs={{0,1},{1,0},{2,3},{3,2},{4,5},{5,4},{6,7},{7,6},{8,9},{9,8},{10,11... | collective-permute-start | bytes 405512 | tf_op jit(solution)/shard_map/ppermute | solution.py:35
  16.3 20.4 %collective-permute-start.11 = (f32[264,128]{1,0:T(8,128)S(1)}, f32[264,128]{1,0:T(8,128)S(1)}, u32[]{:S(2)}, u32[]{:S(2)}) collective-permute-start(f32[264,128]{1,0:T(8,128)S(1)} %get-tuple-element.32), channel_id=1, source_target_pairs={{0,2},{1,3},{2,0},{3,1},{4,6},{5,7},{6,4},{7,5},{8,10},{9,11},{10,... | collective-permute-start | bytes 405512 | tf_op jit(solution)/shard_map/ppermute | solution.py:35
  17.8 18.9 %collective-permute-start.12 = (f32[264,128]{1,0:T(8,128)S(1)}, f32[264,128]{1,0:T(8,128)S(1)}, u32[]{:S(2)}, u32[]{:S(2)}) collective-permute-start(f32[264,128]{1,0:T(8,128)S(1)} %get-tuple-element.33), channel_id=1, source_target_pairs={{0,3},{1,2},{2,1},{3,0},{4,7},{5,6},{6,5},{7,4},{8,11},{9,10},{10,... | collective-permute-start | bytes 405512 | tf_op jit(solution)/shard_map/ppermute | solution.py:35
  19.4 13.1 %copy-start.6 = (s32[8]{0:T(128)S(1)}, s32[8]{0:T(128)}, u32[]{:S(2)}) copy-start(s32[8]{0:T(128)} %owner_ref.1) | copy-start | bytes 100
  22.0 4.8 %collective-permute-start.4 = (f32[16,512]{1,0:T(8,128)S(1)}, f32[16,512]{1,0:T(8,128)S(1)}, u32[]{:S(2)}, u32[]{:S(2)}) collective-permute-start(f32[16,512]{1,0:T(8,128)S(1)} %get-tuple-element.23), channel_id=1, source_target_pairs={{0,8},{4,12},{8,0},{12,4},{16,24},{20,28},{24,16},{28,20},{1,9},{5... | collective-permute-start | bytes 98312 | tf_op jit(solution)/shard_map/ppermute | solution.py:35
  23.3 6.8 %collective-permute-start.5 = (f32[16,512]{1,0:T(8,128)S(1)}, f32[16,512]{1,0:T(8,128)S(1)}, u32[]{:S(2)}, u32[]{:S(2)}) collective-permute-start(f32[16,512]{1,0:T(8,128)S(1)} %get-tuple-element.24), channel_id=1, source_target_pairs={{0,16},{4,20},{8,24},{12,28},{16,0},{20,4},{24,8},{28,12},{1,17},{... | collective-permute-start | bytes 98312 | tf_op jit(solution)/shard_map/ppermute | solution.py:35
  26.8 5.7 %collective-permute-start.6 = (f32[16,512]{1,0:T(8,128)S(1)}, f32[16,512]{1,0:T(8,128)S(1)}, u32[]{:S(2)}, u32[]{:S(2)}) collective-permute-start(f32[16,512]{1,0:T(8,128)S(1)} %get-tuple-element.25), channel_id=1, source_target_pairs={{0,24},{4,28},{8,16},{12,20},{16,8},{20,12},{24,0},{28,4},{1,25},{... | collective-permute-start | bytes 98312 | tf_op jit(solution)/shard_map/ppermute | solution.py:35
  33.1 4.3 %collective-permute-start.7 = (f32[16,1024]{1,0:T(8,128)S(1)}, f32[16,1024]{1,0:T(8,128)S(1)}, u32[]{:S(2)}, u32[]{:S(2)}) collective-permute-start(f32[16,1024]{1,0:T(8,128)S(1)} %get-tuple-element.27), channel_id=1, source_target_pairs={{0,1},{1,0},{2,3},{3,2},{4,5},{5,4},{6,7},{7,6},{8,9},{9,8},{10,11... | collective-permute-start | bytes 196616 | tf_op jit(solution)/shard_map/ppermute | solution.py:35
  33.7 4.3 %collective-permute-start.8 = (f32[16,1024]{1,0:T(8,128)S(1)}, f32[16,1024]{1,0:T(8,128)S(1)}, u32[]{:S(2)}, u32[]{:S(2)}) collective-permute-start(f32[16,1024]{1,0:T(8,128)S(1)} %get-tuple-element.28), channel_id=1, source_target_pairs={{0,2},{1,3},{2,0},{3,1},{4,6},{5,7},{6,4},{7,5},{8,10},{9,11},{10,... | collective-permute-start | bytes 196616 | tf_op jit(solution)/shard_map/ppermute | solution.py:35
  34.7 5.2 %collective-permute-start.9 = (f32[16,1024]{1,0:T(8,128)S(1)}, f32[16,1024]{1,0:T(8,128)S(1)}, u32[]{:S(2)}, u32[]{:S(2)}) collective-permute-start(f32[16,1024]{1,0:T(8,128)S(1)} %get-tuple-element.29), channel_id=1, source_target_pairs={{0,3},{1,2},{2,1},{3,0},{4,7},{5,6},{6,5},{7,4},{8,11},{9,10},{10,... | collective-permute-start | bytes 196616 | tf_op jit(solution)/shard_map/ppermute | solution.py:35

commit v6 on v5

--- a/solution.py
+++ b/solution.py
@@ -16,8 +16,8 @@
 
 NEGATIVE = -1e30
 SCORE_SCALE = HD ** (-0.5)
-WEIGHTS_KIB = 47 << 10
-CACHE_KIB = 24 << 10
+CACHE_KIB = 50 << 10
+WEIGHTS_KIB = 16 << 10
 PROJECT_KIB = 16 << 10
 NT = (((1,), (1,)), ((), ()))
 TN = (((0,), (0,)), ((), ()))
@@ -35,6 +35,10 @@
     return lax.ppermute(x, axis, [(k, k ^ distance) for k in range(size)])
 
 
+def distances(size):
+    return [0] + list(range(size - 1, 0, -1))
+
+
 def params(kibibytes):
     return pltpu.CompilerParams(vmem_limit_bytes=kibibytes << 10)
 
@@ -44,54 +48,66 @@
     return jnp.concatenate([mine[:, h * HD : (h + 1) * HD] for h in range(heads)], axis=0)
 
 
-def weights_kernel(starts_ref, scales_ref, codes_ref, base_hbm, delta_ref, base_ref, arrived):
-    block = codes_ref.shape[0]
-    loads = []
-    for k in range(2):
-        start = starts_ref[lax.axis_index("group") ^ k]
-        here = pl.ds(pl.multiple_of(start, block), block)
-        loads.append(pltpu.make_async_copy(base_hbm.at[here], base_ref.at[k], arrived.at[k]))
-        loads[k].start()
-    scales = scales_ref[...].T
-    for n in range(scales.shape[1]):
-        lanes = slice(n * BLK, (n + 1) * BLK)
-        values = codes_ref[:, lanes].astype(jnp.float32) * scales[:, n : n + 1]
-        delta_ref[:, lanes] = values.astype(jnp.bfloat16)
-    for load in loads:
-        load.wait()
-
-
-def weights(starts, scales, codes, base):
+def weights_kernel(own_codes, mate_codes, own_scales, mate_scales, own_ref, mate_ref):
+    for codes_ref, scales_ref, out_ref in (
+        (own_codes, own_scales, own_ref),
+        (mate_codes, mate_scales, mate_ref),
+    ):
+        scales = scales_ref[...].astype(jnp.float32).T
+        for n in range(scales.shape[1]):
+            lanes = slice(n * BLK, (n + 1) * BLK)
+            values = codes_ref[:, lanes].astype(jnp.float32) * scales[:, n : n + 1]
+            out_ref[:, lanes] = values.astype(jnp.bfloat16)
+
+
+def weights(codes, scales):
     return pl.pallas_call(
         weights_kernel,
-        out_shape=[
-            jax.ShapeDtypeStruct(codes.shape, jnp.bfloat16),
-            jax.ShapeDtypeStruct((2,) + codes.shape, jnp.bfloat16),
-        ],
-        in_specs=[SMEM, VMEM, VMEM, HBM],
+        out_shape=[jax.ShapeDtypeStruct(one.shape, jnp.bfloat16) for one in codes],
+        in_specs=[VMEM] * 4,
         out_specs=[VMEM] * 2,
-        scratch_shapes=[pltpu.SemaphoreType.DMA((2,))],
         compiler_params=params(WEIGHTS_KIB),
         cost_estimate=pl.CostEstimate(
-            flops=codes.size, bytes_accessed=12 * codes.size, transcendentals=0
+            flops=2 * codes[0].size, bytes_accessed=8 * codes[0].size, transcendentals=0
         ),
         name="weights",
-    )(starts, scales.astype(jnp.float32).T, codes, base)
-
-
-def cache_kernel(rows, steps, own, chunk, limits_ref, query_ref, cache_ref, own_query_ref, *parts):
+    )(*codes, *[one.T for one in scales])
+
+
+def cache_kernel(rows, steps, own, chunk, scalars_ref, query_hbm, cache_hbm, base_hbm, *refs):
+    base_ref, own_query_ref, parts = refs[0], refs[1], refs[2:-3]
+    query_ref, cache_ref, arrived = refs[-3:]
     place = lax.axis_index("tensor")
     cache_len = cache_ref.shape[0] // rows
+    block = base_ref.shape[1]
+    shards = lax.axis_size("group")
+    query_load = pltpu.make_async_copy(query_hbm, query_ref, arrived.at[0])
+    cache_loads, base_loads = [], []
+    for r in range(rows):
+        here = pl.ds(r * cache_len, cache_len)
+        cache_loads.append(
+            pltpu.make_async_copy(cache_hbm.at[here], cache_ref.at[here], arrived.at[1 + r])
+        )
+    for k in range(2):
+        start = scalars_ref[lax.axis_index("group") ^ k] * block
+        here = pl.ds(pl.multiple_of(start, block), block)
+        base_loads.append(
+            pltpu.make_async_copy(base_hbm.at[here], base_ref.at[k], arrived.at[1 + rows + k])
+        )
+    for load in [query_load] + cache_loads + base_loads:
+        load.start()
+    query_load.wait()
+
     chunks = own // chunk
     height = chunk * steps
     width = chunks * HD
     position = lax.broadcasted_iota(jnp.int32, (cache_len, chunks * height), 0)
 
     def kv_lane(d):
-        return pl.multiple_of(((place ^ d) * own // (H // KVH)) * HD, HD)
+        return pl.multiple_of(((place ^ order[d]) * own // (H // KVH)) * HD, HD)
 
     def score(r, d):
-        head = (place ^ d) * own
+        head = (place ^ order[d]) * own
         queries = query_ref[:, pl.ds(pl.multiple_of(head * HD, HD), own * HD)]
         query = head_rows(queries.astype(jnp.float32), r, steps, own)
         if d == 0:
@@ -106,16 +122,19 @@
         keys = cache_ref[pl.ds(r * cache_len, cache_len), pl.ds(kv_lane(d), width)]
         return dot(keys, spread, NT)
 
+    order = distances(len(parts))
     units = [(r, d) for r in range(rows) for d in range(len(parts))]
     ahead = []
     for n in range(len(units) + 1):
         if n < len(units):
+            if n % len(parts) == 0:
+                cache_loads[n // len(parts)].wait()
             ahead.append(score(*units[n]))
         if n == 0:
             continue
         r, d = units[n - 1]
         at = r * chunks * height
-        usable = position < limits_ref[r]
+        usable = position < scalars_ref[shards + r] - place * cache_len
         scores = jnp.where(usable, ahead.pop(0) * SCORE_SCALE, 2.0 * NEGATIVE)
         peak = jnp.maximum(jnp.max(scores, axis=0, keepdims=True), NEGATIVE)
         weights = jnp.exp(scores - peak)
@@ -129,25 +148,36 @@
         end = rows * chunks * height + 2 * r
         parts[d][end : end + 1, : chunks * height] = peak
         parts[d][end + 1 : end + 2, : chunks * height] = total
-
-
-def cache_partials(limits, queries, cache, rows, steps, own, ways):
+    for load in base_loads:
+        load.wait()
+
+
+def cache_partials(scalars, queries, cache, base, block, rows, steps, own, ways):
     height = rows * own * steps
     part = jax.ShapeDtypeStruct((height + SUBLANES, LANES), jnp.float32)
     out = pl.pallas_call(
         functools.partial(cache_kernel, rows, steps, own, min(own, H // KVH)),
-        out_shape=[jax.ShapeDtypeStruct((height, HD), jnp.bfloat16)] + [part] * ways,
-        in_specs=[SMEM, VMEM, VMEM],
-        out_specs=[VMEM] * (1 + ways),
+        out_shape=[
+            jax.ShapeDtypeStruct((2, block, base.shape[1]), jnp.bfloat16),
+            jax.ShapeDtypeStruct((height, HD), jnp.bfloat16),
+        ]
+        + [part] * ways,
+        in_specs=[SMEM, HBM, HBM, HBM],
+        out_specs=[VMEM] * (2 + ways),
+        scratch_shapes=[
+            pltpu.VMEM(queries.shape, queries.dtype),
+            pltpu.VMEM(cache.shape, cache.dtype),
+            pltpu.SemaphoreType.DMA((3 + rows,)),
+        ],
         compiler_params=params(CACHE_KIB),
         cost_estimate=pl.CostEstimate(
             flops=4 * height * ways * HD * cache.shape[0] // rows,
-            bytes_accessed=2 * cache.size + 2 * queries.size,
+            bytes_accessed=2 * cache.size + 2 * queries.size + 4 * block * base.shape[1],
             transcendentals=height * ways * cache.shape[0] // rows,
         ),
         name="cache_partials",
-    )(limits, queries, cache)
-    return out[0], out[1:]
+    )(scalars, queries, cache, base)
+    return out[0], out[1], out[2:]
 
 
 def project_kernel(pairs, own_ref, mate_ref, base_ref, *refs):
@@ -157,8 +187,8 @@
     count = tokens[0].shape[0]
     for k, delta_ref in enumerate((own_ref, mate_ref)):
         whole = (dot(base_ref[k], stacked, NT) + dot(delta_ref[...], stacked, NT)).T
-        for d in range(pairs):
-            outs[d][:, k * block : (k + 1) * block] = whole[d * count : (d + 1) * count]
+        for n in range(pairs):
+            outs[n][:, k * block : (k + 1) * block] = whole[n * count : (n + 1) * count]
 
 
 def project(own, mate, base, tokens):
@@ -185,10 +215,10 @@
     place = lax.axis_index("group")
     to_place = lax.axis_index("tensor")
     shards, _, block = ordered.shape
-    for d in range(pairs):
+    for piece, d in zip(arrived, distances(pairs)):
         for k in range(2):
-            ordered[owner_ref[place ^ (2 * d + k)]] = arrived[d][:, k * block : (k + 1) * block]
-    for d, out in enumerate(outs):
+            ordered[owner_ref[place ^ (2 * d + k)]] = piece[:, k * block : (k + 1) * block]
+    for out, d in zip(outs, distances(ways)):
         to = to_place ^ d
         for n in range(near):
             out[:, n * block : (n + 1) * block] = ordered[to * near + n]
@@ -218,7 +248,8 @@
             compiler_params=params(8192),
             name="pack_pieces",
         )(owner_map, *arrived)
-    blocks = jnp.stack(arrived, axis=0).reshape(pairs, count, 2, block).transpose(0, 2, 1, 3)
+    nearest = [arrived[distances(pairs).index(d)] for d in range(pairs)]
+    blocks = jnp.stack(nearest, axis=0).reshape(pairs, count, 2, block).transpose(0, 2, 1, 3)
     shard_of = jnp.zeros((shards,), jnp.int32).at[owner_map].set(
         jnp.arange(shards, dtype=jnp.int32)
     )
@@ -228,7 +259,7 @@
     ordered = taken.transpose(1, 0, 2).reshape(count, shards * block)
     per_device = H // ways
     pieces = []
-    for d in range(ways):
+    for d in distances(ways):
         to = lax.axis_index("tensor") ^ d
         near = (to * per_device // (H // KVH)) * HD
         parts = [(near, near_width), (kv_width + near, near_width), (to * slice_width, slice_width)]
@@ -329,28 +360,36 @@
     near_width = max(1, heads_own // (H // KVH)) * HD
     pairs = group_count // 2
 
+    def exchange(arrays, axis, stride):
+        places = distances(len(arrays))[1:]
+        return [arrays[0]] + [swap(x, axis, stride * d) for x, d in zip(arrays[1:], places)]
+
     mine = hidden_x.reshape(tokens, local_width)
-    token_rows = [mine] + [swap(mine, "group", 2 * d) for d in range(1, pairs)]
-    own_delta, base_blocks = weights(
-        owner_map * owner_block, delta_scales, delta_codes, base_weight
-    )
-    mate_delta = swap(own_delta, "group", 1)
+    token_rows = exchange([mine] * pairs, "group", 2)
+    codes = [delta_codes, swap(delta_codes, "group", 1)]
+    scales = [delta_scales, swap(delta_scales, "group", 1)]
+
     cache_len = kv_cache.shape[1]
-    own_query, partials = cache_partials(
-        lengths - lax.axis_index("tensor") * cache_len,
+    base_blocks, own_query, partials = cache_partials(
+        jnp.concatenate([owner_map, lengths]),
         queries.reshape(tokens, H * HD),
         kv_cache.reshape(rows * cache_len, 2 * KVH * HD),
+        base_weight,
+        owner_block,
         rows,
         steps,
         heads_own,
         tensor_count,
     )
-    partials = [partials[0]] + [swap(partials[d], "tensor", d) for d in range(1, tensor_count)]
-
+    own_delta, mate_delta = weights(codes, scales)
     projected = project(own_delta, mate_delta, base_blocks, token_rows)
-    arrived = [projected[0]] + [swap(projected[d], "group", 2 * d) for d in range(1, pairs)]
+
+    arrived = exchange(projected, "group", 2)
+    held = lax.optimization_barrier((arrived[-1], partials[2:]))
+    arrived, partials = arrived[:-1] + [held[0]], partials[:2] + held[1]
+    partials = exchange(partials, "tensor", 1)
     pieces = pack_pieces(owner_map, arrived, owner_block, tensor_count, near_width, slice_width)
-    pieces = [pieces[0]] + [swap(pieces[d], "tensor", d) for d in range(1, tensor_count)]
+    pieces = exchange(pieces, "tensor", 1)
     new_out, attended = finish(own_query, pieces, partials, rows, steps, heads_own, near_width)
     return (new_out.reshape(rows, steps, -1), attended.reshape(rows, steps, -1))
 

time: 41.8 us -> 39.5 us (0.945)
  waiting for transfers between devices: 5.56 us -> 11.8 us
  starting transfers between devices: 22.2 us -> 17.4 us
  local copies, waits for them, and re-layouts: 2.58 us -> 0.97 us
  Pallas kernels: 9.11 us -> 7.7 us
  other arithmetic: 1.36 us -> 0.75 us
    ppermute x13 -> x14, waiting for transfers between devices: 5.56 us -> 11.8 us  [swap(): return lax.ppermute(x, axis, [(k, k ^ distance) for k in range(size)])]
    ppermute x13 -> x14, starting transfers between devices: 22.2 us -> 17.4 us  [swap(): return lax.ppermute(x, axis, [(k, k ^ distance) for k in range(size)])]
    unnamed x16 -> x10, local copies, waits for them, and re-layouts: 2.58 us -> 0.97 us
    pallas_call x1, Pallas kernels: 2.3 us -> 0.83 us  [weights(): pl.pallas_call(weights_kernel, out_shape=[jax.ShapeDtypeStruct(one.shape,...]
    pallas_call x1, Pallas kernels: 1.96 us -> 3.29 us  [cache_partials(): pl.pallas_call(functools.partial(cache_kernel, rows, steps, own, min(own,...]
    pallas_call x1, Pallas kernels: 2.56 us -> 1.3 us  [project(): pl.pallas_call(functools.partial(project_kernel, pairs), out_shape=[jax.S...]
    concatenate x0 -> x1, other arithmetic: none -> 0.75 us  [on_device(): jnp.concatenate([owner_map, lengths])]
    transpose x1 -> x0, other arithmetic: 0.7 us -> none  [weights(): scales.astype(jnp.float32)]
  transfers between devices with their start and end apart: 13 -> 14, of which waited for: 4 -> 6; matrix products, arithmetic and copies ran while one was open for 0% -> 2% of each run, Pallas kernels for 12% -> 15%
where the time goes in v6:
time: 39.5 us; the launch traced here: 39.4 us
  starting transfers between devices  17.4 us (44%)
  waiting for transfers between devices  11.8 us (30%)
  Pallas kernels  7.7 us (19%)
  local copies, waits for them, and re-layouts  0.97 us (2%)
  other arithmetic  0.75 us (2%)
  between operations  0.72 us (2%)
    ppermute x14, starting transfers between devices, swap(): return lax.ppermute(x, axis, [(k, k ^ distance) for k in range(size)])  17.4 us
    ppermute x14, waiting for transfers between devices, swap(): return lax.ppermute(x, axis, [(k, k ^ distance) for k in range(size)])  11.8 us
    pallas_call x1, Pallas kernels, cache_partials(): pl.pallas_call(functools.partial(cache_kernel, rows, steps, own, min(own,...  3.29 us
    pallas_call x1, Pallas kernels, finish(): pl.pallas_call(functools.partial(finish_kernel, rows, steps, own, min(own...  1.7 us
    pallas_call x1, Pallas kernels, project(): pl.pallas_call(functools.partial(project_kernel, pairs), out_shape=[jax.S...  1.3 us
    unnamed x10, local copies, waits for them, and re-layouts  0.97 us
    pallas_call x1, Pallas kernels, weights(): pl.pallas_call(weights_kernel, out_shape=[jax.ShapeDtypeStruct(one.shape,...  0.83 us
  transfers between devices with their start and end apart: 14, of which 6 were waited for; matrix products, arithmetic and copies ran while one was open for 2% of the time, Pallas kernels for 15%

profile of v6, /device:TPU:0, one launch (start us, length us, event | category | flops | bytes accessed | tf_op | source)
XLA Modules:
  0.0 39.4 jit_solution(8592862921832251716)
XLA Ops:
  0.6 0.5 %collective-permute-start = (bf16[256,2048]{1,0:T(8,128)(2,1)}, bf16[256,2048]{1,0:T(8,128)(2,1)S(1)}, u32[]{:S(2)}, u32[]{:S(2)}) collective-permute-start(bf16[256,2048]{1,0:T(8,128)(2,1)} %own_codes.1), channel_id=1, source_target_pairs={{0,4},{4,0},{8,12},{12,8},{16,20},{20,16},{24,28},{28,24},{1,5},{5... | collective-permute-start | bytes 3145736 | tf_op jit(solution)/shard_map/ppermute | solution.py:35
  1.1 2.7 %collective-permute-start.4 = (bf16[16,2048]{1,0:T(8,128)(2,1)}, bf16[16,2048]{1,0:T(8,128)(2,1)S(1)}, u32[]{:S(2)}, u32[]{:S(2)}) collective-permute-start(bf16[16,2048]{1,0:T(8,128)(2,1)} %bitcast.8), channel_id=1, source_target_pairs={{0,8},{4,12},{8,0},{12,4},{16,24},{20,28},{24,16},{28,20},{1,9},{5... | collective-permute-start | bytes 196616 | tf_op jit(solution)/shard_map/ppermute | solution.py:35
  3.8 2.6 %collective-permute-start.3 = (bf16[16,2048]{1,0:T(8,128)(2,1)}, bf16[16,2048]{1,0:T(8,128)(2,1)S(1)}, u32[]{:S(2)}, u32[]{:S(2)}) collective-permute-start(bf16[16,2048]{1,0:T(8,128)(2,1)} %bitcast.9), channel_id=1, source_target_pairs={{0,16},{4,20},{8,24},{12,28},{16,0},{20,4},{24,8},{28,12},{1,17},{... | collective-permute-start | bytes 196616 | tf_op jit(solution)/shard_map/ppermute | solution.py:35
  6.4 0.0 collective-permute-start.2
  6.4 0.0 collective-permute-start.1
  6.4 0.7 %pad_add_fusion.scalars_ref = s32[10]{0:T(128)S(1)} fusion(s32[2]{0:T(128)} %param.15, s32[8]{0:T(128)} %owner_ref.1), kind=kLoop, calls=%fused_computation | loop fusion | flops 10 | bytes 80 | tf_op jit(solution)/shard_map/concatenate | solution.py:374
  7.1 0.0 copy-start.1
  7.1 0.9 %copy-done.1 = bf16[2,8,8192]{2,1,0:T(8,128)(2,1)S(1)} copy-done((bf16[2,8,8192]{2,1,0:T(8,128)(2,1)S(1)}, bf16[2,8,8192]{2,1,0:T(8,128)(2,1)}, u32[]{:S(2)}) %copy-start.1) | copy-done | bytes 262168
  8.1 0.0 copy-start
  8.1 0.0 copy-start.3
  8.1 3.3 %cache_partials.1 = (bf16[2,256,2048]{2,1,0:T(8,128)(2,1)S(1)}, bf16[256,128]{1,0:T(8,128)(2,1)S(1)}, f32[264,128]{1,0:T(8,128)S(1)}, f32[264,128]{1,0:T(8,128)S...) custom-call(s32[10]{0:T(128)S(1)} %pad_add_fusion.scalars_ref, bf16[16,8192]{1,0:T(8,128)(2,1)S(1)} %bitcast.7, ...), custom_call_target="tpu_custom_call" | custom-call | flops 134217728 | bytes 4456448 | tf_op jit(solution)/shard_map/cache_partials/pallas_call | solution.py:158
  11.4 0.0 copy-start.2
  11.4 0.0 collective-permute-done.1
  11.4 2.7 %collective-permute-start.11 = (f32[264,128]{1,0:T(8,128)S(1)}, f32[264,128]{1,0:T(8,128)S(1)}, u32[]{:S(2)}, u32[]{:S(2)}) collective-permute-start(f32[264,128]{1,0:T(8,128)S(1)} %get-tuple-element.39), channel_id=1, source_target_pairs={{0,3},{1,2},{2,1},{3,0},{4,7},{5,6},{6,5},{7,4},{8,11},{9,10},{10,... | collective-permute-start | bytes 405512 | tf_op jit(solution)/shard_map/ppermute | solution.py:35
  14.1 0.0 collective-permute-done.mate_codes
  14.2 0.0 copy-done
  14.2 0.0 copy-done.3
  14.2 0.8 %weights.1 = (bf16[256,2048]{1,0:T(8,128)(2,1)S(1)}, bf16[256,2048]{1,0:T(8,128)(2,1)S(1)}) custom-call(bf16[256,2048]{1,0:T(8,128)(2,1)S(1)} %copy-done, bf16[256,2048]{1,0:T(8,128)(2,1)S(1)} %collective-permute-done.mate_codes, bf16[16,256]{1,0:T(8,128)(2,1)S(1)} %bitcast.12, bf16[16,256]{1,0:T(8,128)(2,1)S(1)} %bitcast.13), custom_call_target="tpu_custom_call" | custom-call | flops 1048576 | bytes 4194304 | tf_op jit(solution)/shard_map/weights/pallas_call | solution.py:64
  15.0 0.0 collective-permute-done.4.refs_3_
  15.0 0.0 collective-permute-done.3.refs_2_
  15.0 0.0 collective-permute-done.2.refs_1_
  15.0 0.0 copy-done.2
  15.0 0.0 copy-start.4
  15.0 1.3 %project.1 = (f32[16,512]{1,0:T(8,128)S(1)}, f32[16,512]{1,0:T(8,128)S(1)}, f32[16,512]{1,0:T(8,128)S(1)}, f32[16,512]{1,0:T(8,128)S(1)}) custom-call(bf16[256,2048]{1,0:T(8,128)(2,1)S(1)} %get-tuple-element.24.own_ref, bf16[256,2048]{1,0:T(8,128)(2,1)S(1)} %get-tuple-element.25.mate_ref, bf16[2,256,2048]{2,1,0:T(8,128)(2,1)S(1)} %get-tuple-element.26.base_ref, ...), custom_call_target="tpu_custom_call" | custom-call | flops 268435456 | bytes 4194304 | tf_op jit(solution)/shard_map/project/pallas_call | solution.py:198
  16.3 0.7 %collective-permute-start.7 = (f32[16,512]{1,0:T(8,128)S(1)}, f32[16,512]{1,0:T(8,128)S(1)}, u32[]{:S(2)}, u32[]{:S(2)}) collective-permute-start(f32[16,512]{1,0:T(8,128)S(1)} %get-tuple-element.30), channel_id=1, source_target_pairs={{0,8},{4,12},{8,0},{12,4},{16,24},{20,28},{24,16},{28,20},{1,9},{5... | collective-permute-start | bytes 98312 | tf_op jit(solution)/shard_map/ppermute | solution.py:35
  17.1 3.2 %collective-permute-done.7.refs_3_ = f32[16,512]{1,0:T(8,128)S(1)} collective-permute-done((f32[16,512]{1,0:T(8,128)S(1)}, f32[16,512]{1,0:T(8,128)S(1)}, u32[]{:S(2)}, u32[]{:S(2)}) %collective-permute-start.7) | collective-permute-done | bytes 32800 | tf_op jit(solution)/shard_map/ppermute | solution.py:35
  20.3 0.5 %collective-permute-start.12 = (f32[264,128]{1,0:T(8,128)S(1)}, f32[264,128]{1,0:T(8,128)S(1)}, u32[]{:S(2)}, u32[]{:S(2)}) collective-permute-start(f32[264,128]{1,0:T(8,128)S(1)} %get-tuple-element.40), channel_id=1, source_target_pairs={{0,2},{1,3},{2,0},{3,1},{4,6},{5,7},{6,4},{7,5},{8,10},{9,11},{10,... | collective-permute-start | bytes 405512 | tf_op jit(solution)/shard_map/ppermute | solution.py:35
  20.8 0.3 collective-permute-start.13
  21.1 3.8 %collective-permute-start.5 = (f32[16,512]{1,0:T(8,128)S(1)}, f32[16,512]{1,0:T(8,128)S(1)}, u32[]{:S(2)}, u32[]{:S(2)}) collective-permute-start(f32[16,512]{1,0:T(8,128)S(1)} %get-tuple-element.28), channel_id=1, source_target_pairs={{0,24},{4,28},{8,16},{12,20},{16,8},{20,12},{24,0},{28,4},{1,25},{... | collective-permute-start | bytes 98312 | tf_op jit(solution)/shard_map/ppermute | solution.py:35
  25.0 0.0 collective-permute-start.6
  25.0 1.9 %collective-permute-done.5.refs_1_ = f32[16,512]{1,0:T(8,128)S(1)} collective-permute-done((f32[16,512]{1,0:T(8,128)S(1)}, f32[16,512]{1,0:T(8,128)S(1)}, u32[]{:S(2)}, u32[]{:S(2)}) %collective-permute-start.5) | collective-permute-done | bytes 32800 | tf_op jit(solution)/shard_map/ppermute | solution.py:35
  26.9 2.9 %collective-permute-done.6.refs_2_ = f32[16,512]{1,0:T(8,128)S(1)} collective-permute-done((f32[16,512]{1,0:T(8,128)S(1)}, f32[16,512]{1,0:T(8,128)S(1)}, u32[]{:S(2)}, u32[]{:S(2)}) %collective-permute-start.6) | collective-permute-done | bytes 32800 | tf_op jit(solution)/shard_map/ppermute | solution.py:35
  29.8 0.0 copy-done.4
  29.8 0.6 %pack_pieces.1 = (f32[16,1024]{1,0:T(8,128)S(1)}, f32[16,1024]{1,0:T(8,128)S(1)}, f32[16,1024]{1,0:T(8,128)S(1)}, f32[16,1024]{1,0:T(8,128)S(1)}) custom-call(s32[8]{0:T(128)S(1)} %copy-done.4, f32[16,512]{1,0:T(8,128)S(1)} %get-tuple-element.27.refs_0_, f32[16,512]{1,0:T(8,128)S(1)} %collective-permute-done.5.refs_1_, ...), custom_call_target="tpu_custom_call" | custom-call | tf_op jit(solution)/shard_map/pack_pieces/pallas_call | solution.py:242
  30.4 2.5 %collective-permute-start.8 = (f32[16,1024]{1,0:T(8,128)S(1)}, f32[16,1024]{1,0:T(8,128)S(1)}, u32[]{:S(2)}, u32[]{:S(2)}) collective-permute-start(f32[16,1024]{1,0:T(8,128)S(1)} %get-tuple-element.35), channel_id=1, source_target_pairs={{0,3},{1,2},{2,1},{3,0},{4,7},{5,6},{6,5},{7,4},{8,11},{9,10},{10,... | collective-permute-start | bytes 196616 | tf_op jit(solution)/shard_map/ppermute | solution.py:35
  32.9 0.5 %collective-permute-start.9 = (f32[16,1024]{1,0:T(8,128)S(1)}, f32[16,1024]{1,0:T(8,128)S(1)}, u32[]{:S(2)}, u32[]{:S(2)}) collective-permute-start(f32[16,1024]{1,0:T(8,128)S(1)} %get-tuple-element.36), channel_id=1, source_target_pairs={{0,2},{1,3},{2,0},{3,1},{4,6},{5,7},{6,4},{7,5},{8,10},{9,11},{10,... | collective-permute-start | bytes 196616 | tf_op jit(solution)/shard_map/ppermute | solution.py:35
  33.4 0.0 collective-permute-done.11.refs_5_
  33.4 0.5 %collective-permute-start.10 = (f32[16,1024]{1,0:T(8,128)S(1)}, f32[16,1024]{1,0:T(8,128)S(1)}, u32[]{:S(2)}, u32[]{:S(2)}) collective-permute-start(f32[16,1024]{1,0:T(8,128)S(1)} %get-tuple-element.37), channel_id=1, source_target_pairs={{0,1},{1,0},{2,3},{3,2},{4,5},{5,4},{6,7},{7,6},{8,9},{9,8},{10,11... | collective-permute-start | bytes 196616 | tf_op jit(solution)/shard_map/ppermute | solution.py:35
  33.9 1.7 %collective-permute-done.8.refs_1_ = f32[16,1024]{1,0:T(8,128)S(1)} collective-permute-done((f32[16,1024]{1,0:T(8,128)S(1)}, f32[16,1024]{1,0:T(8,128)S(1)}, u32[]{:S(2)}, u32[]{:S(2)}) %collective-permute-start.8) | collective-permute-done | bytes 65568 | tf_op jit(solution)/shard_map/ppermute | solution.py:35
  35.6 1.5 %collective-permute-done.9.refs_2_ = f32[16,1024]{1,0:T(8,128)S(1)} collective-permute-done((f32[16,1024]{1,0:T(8,128)S(1)}, f32[16,1024]{1,0:T(8,128)S(1)}, u32[]{:S(2)}, u32[]{:S(2)}) %collective-permute-start.9) | collective-permute-done | bytes 65568 | tf_op jit(solution)/shard_map/ppermute | solution.py:35
  37.1 0.5 %collective-permute-done.10.refs_3_ = f32[16,1024]{1,0:T(8,128)S(1)} collective-permute-done((f32[16,1024]{1,0:T(8,128)S(1)}, f32[16,1024]{1,0:T(8,128)S(1)}, u32[]{:S(2)}, u32[]{:S(2)}) %collective-permute-start.10) | collective-permute-done | bytes 65568 | tf_op jit(solution)/shard_map/ppermute | solution.py:35
  37.7 0.0 collective-permute-done.12.refs_6_
  37.7 0.0 collective-permute-done.13.refs_7_
  37.7 1.7 %finish.1 = (bf16[16,512]{1,0:T(8,128)(2,1)}, bf16[16,2048]{1,0:T(8,128)(2,1)}) custom-call(bf16[256,128]{1,0:T(8,128)(2,1)S(1)} %get-tuple-element.23.query_ref, f32[16,1024]{1,0:T(8,128)S(1)} %get-tuple-element.34.refs_0_, f32[16,1024]{1,0:T(8,128)S(1)} %collective-permute-done.8.refs_1_, f32[16,1024]{1,0:T(8,128)S(1)} %collective-permute-done.9.refs_2_, ...), custom_call_target="tpu_custom_call" | custom-call | tf_op jit(solution)/shard_map/finish/pallas_call | solution.py:335
Async XLA Ops:
  0.6 13.5 %collective-permute-start = (bf16[256,2048]{1,0:T(8,128)(2,1)}, bf16[256,2048]{1,0:T(8,128)(2,1)S(1)}, u32[]{:S(2)}, u32[]{:S(2)}) collective-permute-start(bf16[256,2048]{1,0:T(8,128)(2,1)} %own_codes.1), channel_id=1, source_target_pairs={{0,4},{4,0},{8,12},{12,8},{16,20},{20,16},{24,28},{28,24},{1,5},{5... | collective-permute-start | bytes 3145736 | tf_op jit(solution)/shard_map/ppermute | solution.py:35
  1.1 13.8 %collective-permute-start.4 = (bf16[16,2048]{1,0:T(8,128)(2,1)}, bf16[16,2048]{1,0:T(8,128)(2,1)S(1)}, u32[]{:S(2)}, u32[]{:S(2)}) collective-permute-start(bf16[16,2048]{1,0:T(8,128)(2,1)} %bitcast.8), channel_id=1, source_target_pairs={{0,8},{4,12},{8,0},{12,4},{16,24},{20,28},{24,16},{28,20},{1,9},{5... | collective-permute-start | bytes 196616 | tf_op jit(solution)/shard_map/ppermute | solution.py:35
  3.8 11.2 %collective-permute-start.3 = (bf16[16,2048]{1,0:T(8,128)(2,1)}, bf16[16,2048]{1,0:T(8,128)(2,1)S(1)}, u32[]{:S(2)}, u32[]{:S(2)}) collective-permute-start(bf16[16,2048]{1,0:T(8,128)(2,1)} %bitcast.9), channel_id=1, source_target_pairs={{0,16},{4,20},{8,24},{12,28},{16,0},{20,4},{24,8},{28,12},{1,17},{... | collective-permute-start | bytes 196616 | tf_op jit(solution)/shard_map/ppermute | solution.py:35
  6.4 8.6 %collective-permute-start.2 = (bf16[16,2048]{1,0:T(8,128)(2,1)}, bf16[16,2048]{1,0:T(8,128)(2,1)S(1)}, u32[]{:S(2)}, u32[]{:S(2)}) collective-permute-start(bf16[16,2048]{1,0:T(8,128)(2,1)} %bitcast.10), channel_id=1, source_target_pairs={{0,24},{4,28},{8,16},{12,20},{16,8},{20,12},{24,0},{28,4},{1,25},{... | collective-permute-start | bytes 196616 | tf_op jit(solution)/shard_map/ppermute | solution.py:35
  6.4 5.0 %collective-permute-start.1 = (bf16[256,16]{0,1:T(8,128)(2,1)}, bf16[256,16]{0,1:T(8,128)(2,1)S(1)}, u32[]{:S(2)}, u32[]{:S(2)}) collective-permute-start(bf16[256,16]{0,1:T(8,128)(2,1)} %param.11), channel_id=1, source_target_pairs={{0,4},{4,0},{8,12},{12,8},{16,20},{20,16},{24,28},{28,24},{1,5},{5... | collective-permute-start | bytes 24584 | tf_op jit(solution)/shard_map/ppermute | solution.py:35
  7.1 0.9 %copy-start.1 = (bf16[2,8,8192]{2,1,0:T(8,128)(2,1)S(1)}, bf16[2,8,8192]{2,1,0:T(8,128)(2,1)}, u32[]{:S(2)}) copy-start(bf16[2,8,8192]{2,1,0:T(8,128)(2,1)} %param.14) | copy-start | bytes 786436
  8.1 6.1 %copy-start = (bf16[256,2048]{1,0:T(8,128)(2,1)S(1)}, bf16[256,2048]{1,0:T(8,128)(2,1)}, u32[]{:S(2)}) copy-start(bf16[256,2048]{1,0:T(8,128)(2,1)} %own_codes.1) | copy-start | bytes 3145732
  8.1 6.1 %copy-start.3 = (bf16[256,16]{0,1:T(8,128)(2,1)S(1)}, bf16[256,16]{0,1:T(8,128)(2,1)}, u32[]{:S(2)}) copy-start(bf16[256,16]{0,1:T(8,128)(2,1)} %param.11) | copy-start | bytes 24580
  11.4 3.6 %copy-start.2 = (bf16[2,8,2048]{2,1,0:T(8,128)(2,1)S(1)}, bf16[2,8,2048]{2,1,0:T(8,128)(2,1)}, u32[]{:S(2)}) copy-start(bf16[2,8,2048]{2,1,0:T(8,128)(2,1)} %param.8) | copy-start | bytes 196612
  11.4 22.0 %collective-permute-start.11 = (f32[264,128]{1,0:T(8,128)S(1)}, f32[264,128]{1,0:T(8,128)S(1)}, u32[]{:S(2)}, u32[]{:S(2)}) collective-permute-start(f32[264,128]{1,0:T(8,128)S(1)} %get-tuple-element.39), channel_id=1, source_target_pairs={{0,3},{1,2},{2,1},{3,0},{4,7},{5,6},{6,5},{7,4},{8,11},{9,10},{10,... | collective-permute-start | bytes 405512 | tf_op jit(solution)/shard_map/ppermute | solution.py:35
  15.0 14.8 %copy-start.4 = (s32[8]{0:T(128)S(1)}, s32[8]{0:T(128)}, u32[]{:S(2)}) copy-start(s32[8]{0:T(128)} %owner_ref.1) | copy-start | bytes 100
  16.3 4.0 %collective-permute-start.7 = (f32[16,512]{1,0:T(8,128)S(1)}, f32[16,512]{1,0:T(8,128)S(1)}, u32[]{:S(2)}, u32[]{:S(2)}) collective-permute-start(f32[16,512]{1,0:T(8,128)S(1)} %get-tuple-element.30), channel_id=1, source_target_pairs={{0,8},{4,12},{8,0},{12,4},{16,24},{20,28},{24,16},{28,20},{1,9},{5... | collective-permute-start | bytes 98312 | tf_op jit(solution)/shard_map/ppermute | solution.py:35
  20.3 17.3 %collective-permute-start.12 = (f32[264,128]{1,0:T(8,128)S(1)}, f32[264,128]{1,0:T(8,128)S(1)}, u32[]{:S(2)}, u32[]{:S(2)}) collective-permute-start(f32[264,128]{1,0:T(8,128)S(1)} %get-tuple-element.40), channel_id=1, source_target_pairs={{0,2},{1,3},{2,0},{3,1},{4,6},{5,7},{6,4},{7,5},{8,10},{9,11},{10,... | collective-permute-start | bytes 405512 | tf_op jit(solution)/shard_map/ppermute | solution.py:35
  20.8 16.8 %collective-permute-start.13 = (f32[264,128]{1,0:T(8,128)S(1)}, f32[264,128]{1,0:T(8,128)S(1)}, u32[]{:S(2)}, u32[]{:S(2)}) collective-permute-start(f32[264,128]{1,0:T(8,128)S(1)} %get-tuple-element.41), channel_id=1, source_target_pairs={{0,1},{1,0},{2,3},{3,2},{4,5},{5,4},{6,7},{7,6},{8,9},{9,8},{10,11... | collective-permute-start | bytes 405512 | tf_op jit(solution)/shard_map/ppermute | solution.py:35
  21.1 5.7 %collective-permute-start.5 = (f32[16,512]{1,0:T(8,128)S(1)}, f32[16,512]{1,0:T(8,128)S(1)}, u32[]{:S(2)}, u32[]{:S(2)}) collective-permute-start(f32[16,512]{1,0:T(8,128)S(1)} %get-tuple-element.28), channel_id=1, source_target_pairs={{0,24},{4,28},{8,16},{12,20},{16,8},{20,12},{24,0},{28,4},{1,25},{... | collective-permute-start | bytes 98312 | tf_op jit(solution)/shard_map/ppermute | solution.py:35
  25.0 4.8 %collective-permute-start.6 = (f32[16,512]{1,0:T(8,128)S(1)}, f32[16,512]{1,0:T(8,128)S(1)}, u32[]{:S(2)}, u32[]{:S(2)}) collective-permute-start(f32[16,512]{1,0:T(8,128)S(1)} %get-tuple-element.29), channel_id=1, source_target_pairs={{0,16},{4,20},{8,24},{12,28},{16,0},{20,4},{24,8},{28,12},{1,17},{... | collective-permute-start | bytes 98312 | tf_op jit(solution)/shard_map/ppermute | solution.py:35
  30.4 5.2 %collective-permute-start.8 = (f32[16,1024]{1,0:T(8,128)S(1)}, f32[16,1024]{1,0:T(8,128)S(1)}, u32[]{:S(2)}, u32[]{:S(2)}) collective-permute-start(f32[16,1024]{1,0:T(8,128)S(1)} %get-tuple-element.35), channel_id=1, source_target_pairs={{0,3},{1,2},{2,1},{3,0},{4,7},{5,6},{6,5},{7,4},{8,11},{9,10},{10,... | collective-permute-start | bytes 196616 | tf_op jit(solution)/shard_map/ppermute | solution.py:35
  32.9 4.3 %collective-permute-start.9 = (f32[16,1024]{1,0:T(8,128)S(1)}, f32[16,1024]{1,0:T(8,128)S(1)}, u32[]{:S(2)}, u32[]{:S(2)}) collective-permute-start(f32[16,1024]{1,0:T(8,128)S(1)} %get-tuple-element.36), channel_id=1, source_target_pairs={{0,2},{1,3},{2,0},{3,1},{4,6},{5,7},{6,4},{7,5},{8,10},{9,11},{10,... | collective-permute-start | bytes 196616 | tf_op jit(solution)/shard_map/ppermute | solution.py:35
  33.4 4.3 %collective-permute-start.10 = (f32[16,1024]{1,0:T(8,128)S(1)}, f32[16,1024]{1,0:T(8,128)S(1)}, u32[]{:S(2)}, u32[]{:S(2)}) collective-permute-start(f32[16,1024]{1,0:T(8,128)S(1)} %get-tuple-element.37), channel_id=1, source_target_pairs={{0,1},{1,0},{2,3},{3,2},{4,5},{5,4},{6,7},{7,6},{8,9},{9,8},{10,11... | collective-permute-start | bytes 196616 | tf_op jit(solution)/shard_map/ppermute | solution.py:35

commit v7 on v6

--- a/solution.py
+++ b/solution.py
@@ -16,7 +16,11 @@
 
 NEGATIVE = -1e30
 SCORE_SCALE = HD ** (-0.5)
-CACHE_KIB = 50 << 10
+CACHE_HINT = 120_000_000
+WEIGHTS_HINT = 100_000
+PROJECT_HINT = 60_000_000
+PACK_HINT = 60_000_000
+CACHE_KIB = 24 << 10
 WEIGHTS_KIB = 16 << 10
 PROJECT_KIB = 16 << 10
 NT = (((1,), (1,)), ((), ()))
@@ -26,6 +30,10 @@
 HBM = pl.BlockSpec(memory_space=pltpu.HBM)
 
 
+def hint(size):
+    return pl.CostEstimate(flops=0, bytes_accessed=size, transcendentals=0)
+
+
 def dot(left, right, dims):
     return lax.dot_general(left, right, dims, preferred_element_type=jnp.float32)
 
@@ -48,55 +56,60 @@
     return jnp.concatenate([mine[:, h * HD : (h + 1) * HD] for h in range(heads)], axis=0)
 
 
-def weights_kernel(own_codes, mate_codes, own_scales, mate_scales, own_ref, mate_ref):
-    for codes_ref, scales_ref, out_ref in (
-        (own_codes, own_scales, own_ref),
-        (mate_codes, mate_scales, mate_ref),
-    ):
-        scales = scales_ref[...].astype(jnp.float32).T
-        for n in range(scales.shape[1]):
+def weights_kernel(
+    own_codes_hbm, own_scales_hbm, mate_codes, mate_scales, own_ref, mate_ref, codes, scales, arrived
+):
+    loads = [
+        pltpu.make_async_copy(own_scales_hbm, scales, arrived.at[0]),
+        pltpu.make_async_copy(own_codes_hbm, codes, arrived.at[1]),
+    ]
+    for load in loads:
+        load.start()
+
+    def dequantize(codes_ref, scales_ref, out_ref):
+        columns = scales_ref[...].astype(jnp.float32).T
+        for n in range(columns.shape[1]):
             lanes = slice(n * BLK, (n + 1) * BLK)
-            values = codes_ref[:, lanes].astype(jnp.float32) * scales[:, n : n + 1]
+            values = codes_ref[:, lanes].astype(jnp.float32) * columns[:, n : n + 1]
             out_ref[:, lanes] = values.astype(jnp.bfloat16)
 
+    dequantize(mate_codes, mate_scales, mate_ref)
+    for load in loads:
+        load.wait()
+    dequantize(codes, scales, own_ref)
+
 
 def weights(codes, scales):
+    own = [pltpu.with_memory_space_constraint(x, pltpu.HBM) for x in (codes[0], scales[0].T)]
     return pl.pallas_call(
         weights_kernel,
         out_shape=[jax.ShapeDtypeStruct(one.shape, jnp.bfloat16) for one in codes],
-        in_specs=[VMEM] * 4,
+        in_specs=[HBM, HBM, VMEM, VMEM],
         out_specs=[VMEM] * 2,
+        scratch_shapes=[
+            pltpu.VMEM(codes[0].shape, codes[0].dtype),
+            pltpu.VMEM(scales[0].shape[::-1], scales[0].dtype),
+            pltpu.SemaphoreType.DMA((2,)),
+        ],
         compiler_params=params(WEIGHTS_KIB),
-        cost_estimate=pl.CostEstimate(
-            flops=2 * codes[0].size, bytes_accessed=8 * codes[0].size, transcendentals=0
-        ),
+        cost_estimate=hint(WEIGHTS_HINT),
         name="weights",
-    )(*codes, *[one.T for one in scales])
-
-
-def cache_kernel(rows, steps, own, chunk, scalars_ref, query_hbm, cache_hbm, base_hbm, *refs):
-    base_ref, own_query_ref, parts = refs[0], refs[1], refs[2:-3]
-    query_ref, cache_ref, arrived = refs[-3:]
+    )(*own, codes[1], scales[1].T)
+
+
+def cache_kernel(
+    rows, steps, own, chunk, owner_ref, lengths_ref, query_ref, cache_ref, base_hbm, *refs
+):
+    base_ref, own_query_ref, parts, arrived = refs[0], refs[1], refs[2:-1], refs[-1]
     place = lax.axis_index("tensor")
     cache_len = cache_ref.shape[0] // rows
     block = base_ref.shape[1]
-    shards = lax.axis_size("group")
-    query_load = pltpu.make_async_copy(query_hbm, query_ref, arrived.at[0])
-    cache_loads, base_loads = [], []
-    for r in range(rows):
-        here = pl.ds(r * cache_len, cache_len)
-        cache_loads.append(
-            pltpu.make_async_copy(cache_hbm.at[here], cache_ref.at[here], arrived.at[1 + r])
-        )
+    base_loads = []
     for k in range(2):
-        start = scalars_ref[lax.axis_index("group") ^ k] * block
+        start = owner_ref[lax.axis_index("group") ^ k] * block
         here = pl.ds(pl.multiple_of(start, block), block)
-        base_loads.append(
-            pltpu.make_async_copy(base_hbm.at[here], base_ref.at[k], arrived.at[1 + rows + k])
-        )
-    for load in [query_load] + cache_loads + base_loads:
-        load.start()
-    query_load.wait()
+        base_loads.append(pltpu.make_async_copy(base_hbm.at[here], base_ref.at[k], arrived.at[k]))
+        base_loads[k].start()
 
     chunks = own // chunk
     height = chunk * steps
@@ -127,14 +140,12 @@
     ahead = []
     for n in range(len(units) + 1):
         if n < len(units):
-            if n % len(parts) == 0:
-                cache_loads[n // len(parts)].wait()
             ahead.append(score(*units[n]))
         if n == 0:
             continue
         r, d = units[n - 1]
         at = r * chunks * height
-        usable = position < scalars_ref[shards + r] - place * cache_len
+        usable = position < lengths_ref[r] - place * cache_len
         scores = jnp.where(usable, ahead.pop(0) * SCORE_SCALE, 2.0 * NEGATIVE)
         peak = jnp.maximum(jnp.max(scores, axis=0, keepdims=True), NEGATIVE)
         weights = jnp.exp(scores - peak)
@@ -152,7 +163,7 @@
         load.wait()
 
 
-def cache_partials(scalars, queries, cache, base, block, rows, steps, own, ways):
+def cache_partials(owner_map, lengths, queries, cache, base, block, rows, steps, own, ways):
     height = rows * own * steps
     part = jax.ShapeDtypeStruct((height + SUBLANES, LANES), jnp.float32)
     out = pl.pallas_call(
@@ -162,21 +173,15 @@
             jax.ShapeDtypeStruct((height, HD), jnp.bfloat16),
         ]
         + [part] * ways,
-        in_specs=[SMEM, HBM, HBM, HBM],
+        in_specs=[SMEM, SMEM, VMEM, VMEM, HBM],
         out_specs=[VMEM] * (2 + ways),
         scratch_shapes=[
-            pltpu.VMEM(queries.shape, queries.dtype),
-            pltpu.VMEM(cache.shape, cache.dtype),
-            pltpu.SemaphoreType.DMA((3 + rows,)),
+            pltpu.SemaphoreType.DMA((2,)),
         ],
         compiler_params=params(CACHE_KIB),
-        cost_estimate=pl.CostEstimate(
-            flops=4 * height * ways * HD * cache.shape[0] // rows,
-            bytes_accessed=2 * cache.size + 2 * queries.size + 4 * block * base.shape[1],
-            transcendentals=height * ways * cache.shape[0] // rows,
-        ),
+        cost_estimate=hint(CACHE_HINT),
         name="cache_partials",
-    )(scalars, queries, cache, base)
+    )(owner_map, lengths, queries, cache, pltpu.with_memory_space_constraint(base, pltpu.HBM))
     return out[0], out[1], out[2:]
 
 
@@ -201,11 +206,7 @@
         in_specs=[VMEM] * (3 + pairs),
         out_specs=[VMEM] * pairs,
         compiler_params=params(PROJECT_KIB),
-        cost_estimate=pl.CostEstimate(
-            flops=8 * block * width * count * pairs,
-            bytes_accessed=8 * block * width,
-            transcendentals=0,
-        ),
+        cost_estimate=hint(PROJECT_HINT),
         name="project",
     )(own, mate, base, *tokens)
 
@@ -246,6 +247,7 @@
             out_specs=[VMEM] * ways,
             scratch_shapes=[pltpu.VMEM((shards, count, block), jnp.float32)],
             compiler_params=params(8192),
+            cost_estimate=hint(PACK_HINT),
             name="pack_pieces",
         )(owner_map, *arrived)
     nearest = [arrived[distances(pairs).index(d)] for d in range(pairs)]
@@ -364,16 +366,17 @@
         places = distances(len(arrays))[1:]
         return [arrays[0]] + [swap(x, axis, stride * d) for x, d in zip(arrays[1:], places)]
 
-    mine = hidden_x.reshape(tokens, local_width)
-    token_rows = exchange([mine] * pairs, "group", 2)
+    token_rows = exchange([hidden_x.reshape(tokens, local_width)] * pairs, "group", 2)
     codes = [delta_codes, swap(delta_codes, "group", 1)]
     scales = [delta_scales, swap(delta_scales, "group", 1)]
 
-    cache_len = kv_cache.shape[1]
+    own_delta, mate_delta = weights(codes, scales)
+    behind, own_delta = lax.optimization_barrier((owner_map, own_delta))
     base_blocks, own_query, partials = cache_partials(
-        jnp.concatenate([owner_map, lengths]),
+        behind,
+        lengths,
         queries.reshape(tokens, H * HD),
-        kv_cache.reshape(rows * cache_len, 2 * KVH * HD),
+        kv_cache.reshape(-1, 2 * KVH * HD),
         base_weight,
         owner_block,
         rows,
@@ -381,13 +384,9 @@
         heads_own,
         tensor_count,
     )
-    own_delta, mate_delta = weights(codes, scales)
+    partials = exchange(partials, "tensor", 1)
     projected = project(own_delta, mate_delta, base_blocks, token_rows)
-
     arrived = exchange(projected, "group", 2)
-    held = lax.optimization_barrier((arrived[-1], partials[2:]))
-    arrived, partials = arrived[:-1] + [held[0]], partials[:2] + held[1]
-    partials = exchange(partials, "tensor", 1)
     pieces = pack_pieces(owner_map, arrived, owner_block, tensor_count, near_width, slice_width)
     pieces = exchange(pieces, "tensor", 1)
     new_out, attended = finish(own_query, pieces, partials, rows, steps, heads_own, near_width)

time: 39.5 us -> 36.4 us (0.922)
  waiting for transfers between devices: 11.8 us -> 7.42 us
  Pallas kernels: 7.7 us -> 8.75 us
  starting transfers between devices: 17.4 us -> 18.3 us
  other arithmetic: 0.75 us -> 0 us
    ppermute x14, waiting for transfers between devices: 11.8 us -> 7.42 us  [swap(): return lax.ppermute(x, axis, [(k, k ^ distance) for k in range(size)])]
    pallas_call x1, Pallas kernels: 0.83 us -> 1.73 us  [weights(): pl.pallas_call(weights_kernel, out_shape=[jax.ShapeDtypeStruct(one.shape,...]
    ppermute x14, starting transfers between devices: 17.4 us -> 18.3 us  [swap(): return lax.ppermute(x, axis, [(k, k ^ distance) for k in range(size)])]
    concatenate x1 -> x0, other arithmetic: 0.75 us -> none  [on_device(): jnp.concatenate([owner_map, lengths])]
  transfers between devices with their start and end apart: 14 -> 14, of which waited for: 6 -> 4; matrix products, arithmetic and copies ran while one was open for 2% -> 0% of each run, Pallas kernels for 15% -> 16%
where the time goes in v7:
time: 36.4 us; the launch traced here: 36.2 us
  starting transfers between devices  18.3 us (50%)
  Pallas kernels  8.75 us (24%)
  waiting for transfers between devices  7.42 us (20%)
  local copies, waits for them, and re-layouts  0.96 us (3%)
  between operations  0.76 us (2%)
    ppermute x14, starting transfers between devices, swap(): return lax.ppermute(x, axis, [(k, k ^ distance) for k in range(size)])  18.3 us
    ppermute x14, waiting for transfers between devices, swap(): return lax.ppermute(x, axis, [(k, k ^ distance) for k in range(size)])  7.42 us
    pallas_call x1, Pallas kernels, cache_partials(): pl.pallas_call(functools.partial(cache_kernel, rows, steps, own, min(own,...  3.43 us
    pallas_call x1, Pallas kernels, weights(): pl.pallas_call(weights_kernel, out_shape=[jax.ShapeDtypeStruct(one.shape,...  1.73 us
    pallas_call x1, Pallas kernels, finish(): pl.pallas_call(functools.partial(finish_kernel, rows, steps, own, min(own...  1.71 us
    pallas_call x1, Pallas kernels, project(): pl.pallas_call(functools.partial(project_kernel, pairs), out_shape=[jax.S...  1.3 us
    unnamed x10, local copies, waits for them, and re-layouts  0.96 us
  transfers between devices with their start and end apart: 14, of which 4 were waited for; matrix products, arithmetic and copies ran while one was open for 0% of the time, Pallas kernels for 16%

profile of v7, /device:TPU:0, one launch (start us, length us, event | category | flops | bytes accessed | tf_op | source)
XLA Modules:
  0.0 36.2 jit_solution(18435839954379044950)
XLA Ops:
  0.6 0.0 copy-start.3
  0.6 0.0 copy-start.4
  0.7 0.0 copy-start
  0.7 0.5 %collective-permute-start = (bf16[256,2048]{1,0:T(8,128)(2,1)}, bf16[256,2048]{1,0:T(8,128)(2,1)S(1)}, u32[]{:S(2)}, u32[]{:S(2)}) collective-permute-start(bf16[256,2048]{1,0:T(8,128)(2,1)} %own_codes_hbm.1), channel_id=1, source_target_pairs={{0,4},{4,0},{8,12},{12,8},{16,20},{20,16},{24,28},{28,24},{1,5},{5... | collective-permute-start | bytes 3145736 | tf_op jit(solution)/shard_map/ppermute | solution.py:43
  1.2 2.6 %collective-permute-start.4 = (bf16[16,2048]{1,0:T(8,128)(2,1)}, bf16[16,2048]{1,0:T(8,128)(2,1)S(1)}, u32[]{:S(2)}, u32[]{:S(2)}) collective-permute-start(bf16[16,2048]{1,0:T(8,128)(2,1)} %bitcast.9), channel_id=1, source_target_pairs={{0,8},{4,12},{8,0},{12,4},{16,24},{20,28},{24,16},{28,20},{1,9},{5... | collective-permute-start | bytes 196616 | tf_op jit(solution)/shard_map/ppermute | solution.py:43
  3.8 2.6 %collective-permute-start.3 = (bf16[16,2048]{1,0:T(8,128)(2,1)}, bf16[16,2048]{1,0:T(8,128)(2,1)S(1)}, u32[]{:S(2)}, u32[]{:S(2)}) collective-permute-start(bf16[16,2048]{1,0:T(8,128)(2,1)} %bitcast.10), channel_id=1, source_target_pairs={{0,16},{4,20},{8,24},{12,28},{16,0},{20,4},{24,8},{28,12},{1,17},{... | collective-permute-start | bytes 196616 | tf_op jit(solution)/shard_map/ppermute | solution.py:43
  6.4 0.0 collective-permute-start.2
  6.4 0.0 collective-permute-start.1
  6.4 1.4 %collective-permute-done.1 = bf16[256,16]{0,1:T(8,128)(2,1)S(1)} collective-permute-done((bf16[256,16]{0,1:T(8,128)(2,1)}, bf16[256,16]{0,1:T(8,128)(2,1)S(1)}, u32[]{:S(2)}, u32[]{:S(2)}) %collective-permute-start.1) | collective-permute-done | bytes 8224 | tf_op jit(solution)/shard_map/ppermute | solution.py:43
  7.8 0.0 collective-permute-done.mate_codes
  7.8 1.7 %weights.1 = (bf16[256,2048]{1,0:T(8,128)(2,1)S(1)}, bf16[256,2048]{1,0:T(8,128)(2,1)S(1)}) custom-call(bf16[256,2048]{1,0:T(8,128)(2,1)} %own_codes_hbm.1, bf16[16,256]{1,0:T(8,128)(2,1)} %bitcast.14, bf16[256,2048]{1,0:T(8,128)(2,1)S(1)} %collective-permute-done.mate_codes, bf16[16,256]{1,0:T(8,128)(2,1)S(1)} %bitcast.13), custom_call_target="tpu_custom_call" | custom-call | bytes 100000 | tf_op jit(solution)/shard_map/weights/pallas_call | solution.py:84
  9.5 0.0 copy-done.3
  9.6 0.0 copy-done.4
  9.6 0.0 copy-done
  9.6 0.0 copy-start.1
  9.6 0.9 %copy-done.1 = bf16[2,8,8192]{2,1,0:T(8,128)(2,1)S(1)} copy-done((bf16[2,8,8192]{2,1,0:T(8,128)(2,1)S(1)}, bf16[2,8,8192]{2,1,0:T(8,128)(2,1)}, u32[]{:S(2)}) %copy-start.1) | copy-done | bytes 262168
  10.5 0.0 copy-start.2
  10.5 3.4 %cache_partials.1 = (bf16[2,256,2048]{2,1,0:T(8,128)(2,1)S(1)}, bf16[256,128]{1,0:T(8,128)(2,1)S(1)}, f32[264,128]{1,0:T(8,128)S(1)}, f32[264,128]{1,0:T(8,128)S...) custom-call(s32[8]{0:T(128)S(1)} %copy-done.3, s32[2]{0:T(128)S(1)} %copy-done.4, bf16[16,8192]{1,0:T(8,128)(2,1)S(1)} %bitcast.8, ...), custom_call_target="tpu_custom_call" | custom-call | bytes 120000000 | tf_op jit(solution)/shard_map/cache_partials/pallas_call | solution.py:169
  14.0 0.0 collective-permute-done.4.refs_3_
  14.0 0.0 collective-permute-done.3.refs_2_
  14.0 0.0 collective-permute-done.2.refs_1_
  14.0 0.0 copy-done.2
  14.0 1.3 %project.1 = (f32[16,512]{1,0:T(8,128)S(1)}, f32[16,512]{1,0:T(8,128)S(1)}, f32[16,512]{1,0:T(8,128)S(1)}, f32[16,512]{1,0:T(8,128)S(1)}) custom-call(bf16[256,2048]{1,0:T(8,128)(2,1)S(1)} %get-tuple-element.25.own_ref, bf16[256,2048]{1,0:T(8,128)(2,1)S(1)} %get-tuple-element.26.mate_ref, bf16[2,256,2048]{2,1,0:T(8,128)(2,1)S(1)} %get-tuple-element.27.base_ref, ...), custom_call_target="tpu_custom_call" | custom-call | bytes 60000000 | tf_op jit(solution)/shard_map/project/pallas_call | solution.py:203
  15.3 3.9 %collective-permute-start.5 = (f32[16,512]{1,0:T(8,128)S(1)}, f32[16,512]{1,0:T(8,128)S(1)}, u32[]{:S(2)}, u32[]{:S(2)}) collective-permute-start(f32[16,512]{1,0:T(8,128)S(1)} %get-tuple-element.29), channel_id=1, source_target_pairs={{0,24},{4,28},{8,16},{12,20},{16,8},{20,12},{24,0},{28,4},{1,25},{... | collective-permute-start | bytes 98312 | tf_op jit(solution)/shard_map/ppermute | solution.py:43
  19.2 0.0 collective-permute-start.6
  19.2 0.6 %collective-permute-start.7 = (f32[16,512]{1,0:T(8,128)S(1)}, f32[16,512]{1,0:T(8,128)S(1)}, u32[]{:S(2)}, u32[]{:S(2)}) collective-permute-start(f32[16,512]{1,0:T(8,128)S(1)} %get-tuple-element.31), channel_id=1, source_target_pairs={{0,8},{4,12},{8,0},{12,4},{16,24},{20,28},{24,16},{28,20},{1,9},{5... | collective-permute-start | bytes 98312 | tf_op jit(solution)/shard_map/ppermute | solution.py:43
  19.8 2.6 %collective-permute-start.11 = (f32[264,128]{1,0:T(8,128)S(1)}, f32[264,128]{1,0:T(8,128)S(1)}, u32[]{:S(2)}, u32[]{:S(2)}) collective-permute-start(f32[264,128]{1,0:T(8,128)S(1)} %get-tuple-element.37), channel_id=1, source_target_pairs={{0,3},{1,2},{2,1},{3,0},{4,7},{5,6},{6,5},{7,4},{8,11},{9,10},{10,... | collective-permute-start | bytes 405512 | tf_op jit(solution)/shard_map/ppermute | solution.py:43
  22.4 0.5 %collective-permute-start.12 = (f32[264,128]{1,0:T(8,128)S(1)}, f32[264,128]{1,0:T(8,128)S(1)}, u32[]{:S(2)}, u32[]{:S(2)}) collective-permute-start(f32[264,128]{1,0:T(8,128)S(1)} %get-tuple-element.38), channel_id=1, source_target_pairs={{0,2},{1,3},{2,0},{3,1},{4,6},{5,7},{6,4},{7,5},{8,10},{9,11},{10,... | collective-permute-start | bytes 405512 | tf_op jit(solution)/shard_map/ppermute | solution.py:43
  22.9 0.0 collective-permute-done.5.refs_1_
  22.9 0.4 %collective-permute-start.13 = (f32[264,128]{1,0:T(8,128)S(1)}, f32[264,128]{1,0:T(8,128)S(1)}, u32[]{:S(2)}, u32[]{:S(2)}) collective-permute-start(f32[264,128]{1,0:T(8,128)S(1)} %get-tuple-element.39), channel_id=1, source_target_pairs={{0,1},{1,0},{2,3},{3,2},{4,5},{5,4},{6,7},{7,6},{8,9},{9,8},{10,11... | collective-permute-start | bytes 405512 | tf_op jit(solution)/shard_map/ppermute | solution.py:43
  23.3 0.7 %collective-permute-done.6.refs_2_ = f32[16,512]{1,0:T(8,128)S(1)} collective-permute-done((f32[16,512]{1,0:T(8,128)S(1)}, f32[16,512]{1,0:T(8,128)S(1)}, u32[]{:S(2)}, u32[]{:S(2)}) %collective-permute-start.6) | collective-permute-done | bytes 32800 | tf_op jit(solution)/shard_map/ppermute | solution.py:43
  24.0 0.0 collective-permute-done.7.refs_3_
  24.0 0.6 %pack_pieces.1 = (f32[16,1024]{1,0:T(8,128)S(1)}, f32[16,1024]{1,0:T(8,128)S(1)}, f32[16,1024]{1,0:T(8,128)S(1)}, f32[16,1024]{1,0:T(8,128)S(1)}) custom-call(s32[8]{0:T(128)S(1)} %copy-done.3, f32[16,512]{1,0:T(8,128)S(1)} %get-tuple-element.28.refs_0_, f32[16,512]{1,0:T(8,128)S(1)} %collective-permute-done.5.refs_1_, ...), custom_call_target="tpu_custom_call" | custom-call | bytes 60000000 | tf_op jit(solution)/shard_map/pack_pieces/pallas_call | solution.py:243
  24.6 2.5 %collective-permute-start.8 = (f32[16,1024]{1,0:T(8,128)S(1)}, f32[16,1024]{1,0:T(8,128)S(1)}, u32[]{:S(2)}, u32[]{:S(2)}) collective-permute-start(f32[16,1024]{1,0:T(8,128)S(1)} %get-tuple-element.33), channel_id=1, source_target_pairs={{0,3},{1,2},{2,1},{3,0},{4,7},{5,6},{6,5},{7,4},{8,11},{9,10},{10,... | collective-permute-start | bytes 196616 | tf_op jit(solution)/shard_map/ppermute | solution.py:43
  27.1 0.5 %collective-permute-start.9 = (f32[16,1024]{1,0:T(8,128)S(1)}, f32[16,1024]{1,0:T(8,128)S(1)}, u32[]{:S(2)}, u32[]{:S(2)}) collective-permute-start(f32[16,1024]{1,0:T(8,128)S(1)} %get-tuple-element.34), channel_id=1, source_target_pairs={{0,2},{1,3},{2,0},{3,1},{4,6},{5,7},{6,4},{7,5},{8,10},{9,11},{10,... | collective-permute-start | bytes 196616 | tf_op jit(solution)/shard_map/ppermute | solution.py:43
  27.6 2.6 %collective-permute-done.8.refs_1_ = f32[16,1024]{1,0:T(8,128)S(1)} collective-permute-done((f32[16,1024]{1,0:T(8,128)S(1)}, f32[16,1024]{1,0:T(8,128)S(1)}, u32[]{:S(2)}, u32[]{:S(2)}) %collective-permute-start.8) | collective-permute-done | bytes 65568 | tf_op jit(solution)/shard_map/ppermute | solution.py:43
  30.2 1.5 %collective-permute-start.10 = (f32[16,1024]{1,0:T(8,128)S(1)}, f32[16,1024]{1,0:T(8,128)S(1)}, u32[]{:S(2)}, u32[]{:S(2)}) collective-permute-start(f32[16,1024]{1,0:T(8,128)S(1)} %get-tuple-element.35), channel_id=1, source_target_pairs={{0,1},{1,0},{2,3},{3,2},{4,5},{5,4},{6,7},{7,6},{8,9},{9,8},{10,11... | collective-permute-start | bytes 196616 | tf_op jit(solution)/shard_map/ppermute | solution.py:43
  31.8 0.0 collective-permute-done.9.refs_2_
  31.8 2.7 %collective-permute-done.10.refs_3_ = f32[16,1024]{1,0:T(8,128)S(1)} collective-permute-done((f32[16,1024]{1,0:T(8,128)S(1)}, f32[16,1024]{1,0:T(8,128)S(1)}, u32[]{:S(2)}, u32[]{:S(2)}) %collective-permute-start.10) | collective-permute-done | bytes 65568 | tf_op jit(solution)/shard_map/ppermute | solution.py:43
  34.5 0.0 collective-permute-done.11.refs_5_
  34.5 0.0 collective-permute-done.12.refs_6_
  34.5 0.0 collective-permute-done.13.refs_7_
  34.5 1.7 %finish.1 = (bf16[16,512]{1,0:T(8,128)(2,1)}, bf16[16,2048]{1,0:T(8,128)(2,1)}) custom-call(bf16[256,128]{1,0:T(8,128)(2,1)S(1)} %get-tuple-element.24.query_ref, f32[16,1024]{1,0:T(8,128)S(1)} %get-tuple-element.32.refs_0_, f32[16,1024]{1,0:T(8,128)S(1)} %collective-permute-done.8.refs_1_, f32[16,1024]{1,0:T(8,128)S(1)} %collective-permute-done.9.refs_2_, ...), custom_call_target="tpu_custom_call" | custom-call | tf_op jit(solution)/shard_map/finish/pallas_call | solution.py:337
Async XLA Ops:
  0.6 8.9 %copy-start.3 = (s32[8]{0:T(128)S(1)}, s32[8]{0:T(128)}, u32[]{:S(2)}) copy-start(s32[8]{0:T(128)} %owner_ref.2) | copy-start | bytes 100
  0.6 8.9 %copy-start.4 = (s32[2]{0:T(128)S(1)}, s32[2]{0:T(128)}, u32[]{:S(2)}) copy-start(s32[2]{0:T(128)} %lengths_ref.1) | copy-start | bytes 28
  0.7 8.9 %copy-start = (bf16[2,256,2048]{2,1,0:T(8,128)(2,1)S(1)}, bf16[2,256,2048]{2,1,0:T(8,128)(2,1)}, u32[]{:S(2)}) copy-start(bf16[2,256,2048]{2,1,0:T(8,128)(2,1)} %param.13) | copy-start | bytes 6291460
  0.7 7.1 %collective-permute-start = (bf16[256,2048]{1,0:T(8,128)(2,1)}, bf16[256,2048]{1,0:T(8,128)(2,1)S(1)}, u32[]{:S(2)}, u32[]{:S(2)}) collective-permute-start(bf16[256,2048]{1,0:T(8,128)(2,1)} %own_codes_hbm.1), channel_id=1, source_target_pairs={{0,4},{4,0},{8,12},{12,8},{16,20},{20,16},{24,28},{28,24},{1,5},{5... | collective-permute-start | bytes 3145736 | tf_op jit(solution)/shard_map/ppermute | solution.py:43
  1.2 12.8 %collective-permute-start.4 = (bf16[16,2048]{1,0:T(8,128)(2,1)}, bf16[16,2048]{1,0:T(8,128)(2,1)S(1)}, u32[]{:S(2)}, u32[]{:S(2)}) collective-permute-start(bf16[16,2048]{1,0:T(8,128)(2,1)} %bitcast.9), channel_id=1, source_target_pairs={{0,8},{4,12},{8,0},{12,4},{16,24},{20,28},{24,16},{28,20},{1,9},{5... | collective-permute-start | bytes 196616 | tf_op jit(solution)/shard_map/ppermute | solution.py:43
  3.8 10.2 %collective-permute-start.3 = (bf16[16,2048]{1,0:T(8,128)(2,1)}, bf16[16,2048]{1,0:T(8,128)(2,1)S(1)}, u32[]{:S(2)}, u32[]{:S(2)}) collective-permute-start(bf16[16,2048]{1,0:T(8,128)(2,1)} %bitcast.10), channel_id=1, source_target_pairs={{0,16},{4,20},{8,24},{12,28},{16,0},{20,4},{24,8},{28,12},{1,17},{... | collective-permute-start | bytes 196616 | tf_op jit(solution)/shard_map/ppermute | solution.py:43
  6.4 7.6 %collective-permute-start.2 = (bf16[16,2048]{1,0:T(8,128)(2,1)}, bf16[16,2048]{1,0:T(8,128)(2,1)S(1)}, u32[]{:S(2)}, u32[]{:S(2)}) collective-permute-start(bf16[16,2048]{1,0:T(8,128)(2,1)} %bitcast.11), channel_id=1, source_target_pairs={{0,24},{4,28},{8,16},{12,20},{16,8},{20,12},{24,0},{28,4},{1,25},{... | collective-permute-start | bytes 196616 | tf_op jit(solution)/shard_map/ppermute | solution.py:43
  6.4 1.4 %collective-permute-start.1 = (bf16[256,16]{0,1:T(8,128)(2,1)}, bf16[256,16]{0,1:T(8,128)(2,1)S(1)}, u32[]{:S(2)}, u32[]{:S(2)}) collective-permute-start(bf16[256,16]{0,1:T(8,128)(2,1)} %param.11), channel_id=1, source_target_pairs={{0,4},{4,0},{8,12},{12,8},{16,20},{20,16},{24,28},{28,24},{1,5},{5... | collective-permute-start | bytes 24584 | tf_op jit(solution)/shard_map/ppermute | solution.py:43
  9.6 1.0 %copy-start.1 = (bf16[2,8,8192]{2,1,0:T(8,128)(2,1)S(1)}, bf16[2,8,8192]{2,1,0:T(8,128)(2,1)}, u32[]{:S(2)}) copy-start(bf16[2,8,8192]{2,1,0:T(8,128)(2,1)} %param.14) | copy-start | bytes 786436
  10.5 3.5 %copy-start.2 = (bf16[2,8,2048]{2,1,0:T(8,128)(2,1)S(1)}, bf16[2,8,2048]{2,1,0:T(8,128)(2,1)}, u32[]{:S(2)}) copy-start(bf16[2,8,2048]{2,1,0:T(8,128)(2,1)} %param.8) | copy-start | bytes 196612
  15.3 7.6 %collective-permute-start.5 = (f32[16,512]{1,0:T(8,128)S(1)}, f32[16,512]{1,0:T(8,128)S(1)}, u32[]{:S(2)}, u32[]{:S(2)}) collective-permute-start(f32[16,512]{1,0:T(8,128)S(1)} %get-tuple-element.29), channel_id=1, source_target_pairs={{0,24},{4,28},{8,16},{12,20},{16,8},{20,12},{24,0},{28,4},{1,25},{... | collective-permute-start | bytes 98312 | tf_op jit(solution)/shard_map/ppermute | solution.py:43
  19.2 4.8 %collective-permute-start.6 = (f32[16,512]{1,0:T(8,128)S(1)}, f32[16,512]{1,0:T(8,128)S(1)}, u32[]{:S(2)}, u32[]{:S(2)}) collective-permute-start(f32[16,512]{1,0:T(8,128)S(1)} %get-tuple-element.30), channel_id=1, source_target_pairs={{0,16},{4,20},{8,24},{12,28},{16,0},{20,4},{24,8},{28,12},{1,17},{... | collective-permute-start | bytes 98312 | tf_op jit(solution)/shard_map/ppermute | solution.py:43
  19.2 4.8 %collective-permute-start.7 = (f32[16,512]{1,0:T(8,128)S(1)}, f32[16,512]{1,0:T(8,128)S(1)}, u32[]{:S(2)}, u32[]{:S(2)}) collective-permute-start(f32[16,512]{1,0:T(8,128)S(1)} %get-tuple-element.31), channel_id=1, source_target_pairs={{0,8},{4,12},{8,0},{12,4},{16,24},{20,28},{24,16},{28,20},{1,9},{5... | collective-permute-start | bytes 98312 | tf_op jit(solution)/shard_map/ppermute | solution.py:43
  19.8 14.7 %collective-permute-start.11 = (f32[264,128]{1,0:T(8,128)S(1)}, f32[264,128]{1,0:T(8,128)S(1)}, u32[]{:S(2)}, u32[]{:S(2)}) collective-permute-start(f32[264,128]{1,0:T(8,128)S(1)} %get-tuple-element.37), channel_id=1, source_target_pairs={{0,3},{1,2},{2,1},{3,0},{4,7},{5,6},{6,5},{7,4},{8,11},{9,10},{10,... | collective-permute-start | bytes 405512 | tf_op jit(solution)/shard_map/ppermute | solution.py:43
  22.4 12.1 %collective-permute-start.12 = (f32[264,128]{1,0:T(8,128)S(1)}, f32[264,128]{1,0:T(8,128)S(1)}, u32[]{:S(2)}, u32[]{:S(2)}) collective-permute-start(f32[264,128]{1,0:T(8,128)S(1)} %get-tuple-element.38), channel_id=1, source_target_pairs={{0,2},{1,3},{2,0},{3,1},{4,6},{5,7},{6,4},{7,5},{8,10},{9,11},{10,... | collective-permute-start | bytes 405512 | tf_op jit(solution)/shard_map/ppermute | solution.py:43
  22.9 11.6 %collective-permute-start.13 = (f32[264,128]{1,0:T(8,128)S(1)}, f32[264,128]{1,0:T(8,128)S(1)}, u32[]{:S(2)}, u32[]{:S(2)}) collective-permute-start(f32[264,128]{1,0:T(8,128)S(1)} %get-tuple-element.39), channel_id=1, source_target_pairs={{0,1},{1,0},{2,3},{3,2},{4,5},{5,4},{6,7},{7,6},{8,9},{9,8},{10,11... | collective-permute-start | bytes 405512 | tf_op jit(solution)/shard_map/ppermute | solution.py:43
  24.6 5.6 %collective-permute-start.8 = (f32[16,1024]{1,0:T(8,128)S(1)}, f32[16,1024]{1,0:T(8,128)S(1)}, u32[]{:S(2)}, u32[]{:S(2)}) collective-permute-start(f32[16,1024]{1,0:T(8,128)S(1)} %get-tuple-element.33), channel_id=1, source_target_pairs={{0,3},{1,2},{2,1},{3,0},{4,7},{5,6},{6,5},{7,4},{8,11},{9,10},{10,... | collective-permute-start | bytes 196616 | tf_op jit(solution)/shard_map/ppermute | solution.py:43
  27.1 4.7 %collective-permute-start.9 = (f32[16,1024]{1,0:T(8,128)S(1)}, f32[16,1024]{1,0:T(8,128)S(1)}, u32[]{:S(2)}, u32[]{:S(2)}) collective-permute-start(f32[16,1024]{1,0:T(8,128)S(1)} %get-tuple-element.34), channel_id=1, source_target_pairs={{0,2},{1,3},{2,0},{3,1},{4,6},{5,7},{6,4},{7,5},{8,10},{9,11},{10,... | collective-permute-start | bytes 196616 | tf_op jit(solution)/shard_map/ppermute | solution.py:43
  30.2 4.3 %collective-permute-start.10 = (f32[16,1024]{1,0:T(8,128)S(1)}, f32[16,1024]{1,0:T(8,128)S(1)}, u32[]{:S(2)}, u32[]{:S(2)}) collective-permute-start(f32[16,1024]{1,0:T(8,128)S(1)} %get-tuple-element.35), channel_id=1, source_target_pairs={{0,1},{1,0},{2,3},{3,2},{4,5},{5,4},{6,7},{7,6},{8,9},{9,8},{10,11... | collective-permute-start | bytes 196616 | tf_op jit(solution)/shard_map/ppermute | solution.py:43

commit v8 on v7

--- a/solution.py
+++ b/solution.py
@@ -17,7 +17,7 @@
 NEGATIVE = -1e30
 SCORE_SCALE = HD ** (-0.5)
 CACHE_HINT = 120_000_000
-WEIGHTS_HINT = 100_000
+WEIGHTS_HINT = 6_000_000
 PROJECT_HINT = 60_000_000
 PACK_HINT = 60_000_000
 CACHE_KIB = 24 << 10
@@ -56,61 +56,81 @@
     return jnp.concatenate([mine[:, h * HD : (h + 1) * HD] for h in range(heads)], axis=0)
 
 
-def weights_kernel(
-    own_codes_hbm, own_scales_hbm, mate_codes, mate_scales, own_ref, mate_ref, codes, scales, arrived
+def dequantize(codes_ref, scales_ref, out_ref):
+    columns = scales_ref[...].astype(jnp.float32).T
+    for n in range(columns.shape[1]):
+        lanes = slice(n * BLK, (n + 1) * BLK)
+        values = codes_ref[:, lanes].astype(jnp.float32) * columns[:, n : n + 1]
+        out_ref[:, lanes] = values.astype(jnp.bfloat16)
+
+
+def own_weights_kernel(
+    owner_hbm, scales_hbm, codes_hbm, base_hbm, out_ref, base_ref, owner_ref, scales_ref, codes_ref,
+    arrived,
 ):
+    place = lax.axis_index("group")
+    block = codes_ref.shape[0]
+    owner_load = pltpu.make_async_copy(owner_hbm, owner_ref, arrived.at[0])
     loads = [
-        pltpu.make_async_copy(own_scales_hbm, scales, arrived.at[0]),
-        pltpu.make_async_copy(own_codes_hbm, codes, arrived.at[1]),
+        pltpu.make_async_copy(scales_hbm, scales_ref, arrived.at[1]),
+        pltpu.make_async_copy(codes_hbm, codes_ref, arrived.at[2]),
     ]
-    for load in loads:
+    for load in [owner_load] + loads:
         load.start()
-
-    def dequantize(codes_ref, scales_ref, out_ref):
-        columns = scales_ref[...].astype(jnp.float32).T
-        for n in range(columns.shape[1]):
-            lanes = slice(n * BLK, (n + 1) * BLK)
-            values = codes_ref[:, lanes].astype(jnp.float32) * columns[:, n : n + 1]
-            out_ref[:, lanes] = values.astype(jnp.bfloat16)
-
-    dequantize(mate_codes, mate_scales, mate_ref)
+    owner_load.wait()
+    base_loads = []
+    for k in range(2):
+        here = pl.ds(pl.multiple_of(owner_ref[place ^ k] * block, block), block)
+        base_loads.append(
+            pltpu.make_async_copy(base_hbm.at[here], base_ref.at[k], arrived.at[3 + k])
+        )
+        base_loads[k].start()
     for load in loads:
         load.wait()
-    dequantize(codes, scales, own_ref)
-
-
-def weights(codes, scales):
-    own = [pltpu.with_memory_space_constraint(x, pltpu.HBM) for x in (codes[0], scales[0].T)]
+    dequantize(codes_ref, scales_ref, out_ref)
+    for load in base_loads:
+        load.wait()
+
+
+def own_weights(owner_map, scales, codes, base):
+    operands = [
+        pltpu.with_memory_space_constraint(x, pltpu.HBM) for x in (owner_map, scales.T, codes, base)
+    ]
     return pl.pallas_call(
-        weights_kernel,
-        out_shape=[jax.ShapeDtypeStruct(one.shape, jnp.bfloat16) for one in codes],
-        in_specs=[HBM, HBM, VMEM, VMEM],
+        own_weights_kernel,
+        out_shape=[
+            jax.ShapeDtypeStruct(codes.shape, jnp.bfloat16),
+            jax.ShapeDtypeStruct((2,) + codes.shape, jnp.bfloat16),
+        ],
+        in_specs=[HBM] * 4,
         out_specs=[VMEM] * 2,
         scratch_shapes=[
-            pltpu.VMEM(codes[0].shape, codes[0].dtype),
-            pltpu.VMEM(scales[0].shape[::-1], scales[0].dtype),
-            pltpu.SemaphoreType.DMA((2,)),
+            pltpu.SMEM(owner_map.shape, owner_map.dtype),
+            pltpu.VMEM(scales.shape[::-1], scales.dtype),
+            pltpu.VMEM(codes.shape, codes.dtype),
+            pltpu.SemaphoreType.DMA((5,)),
         ],
         compiler_params=params(WEIGHTS_KIB),
         cost_estimate=hint(WEIGHTS_HINT),
-        name="weights",
-    )(*own, codes[1], scales[1].T)
-
-
-def cache_kernel(
-    rows, steps, own, chunk, owner_ref, lengths_ref, query_ref, cache_ref, base_hbm, *refs
-):
-    base_ref, own_query_ref, parts, arrived = refs[0], refs[1], refs[2:-1], refs[-1]
+        name="own_weights",
+    )(*operands)
+
+
+def mate_weights(codes, scales):
+    return pl.pallas_call(
+        dequantize,
+        out_shape=jax.ShapeDtypeStruct(codes.shape, jnp.bfloat16),
+        in_specs=[VMEM, VMEM],
+        out_specs=VMEM,
+        compiler_params=params(WEIGHTS_KIB),
+        cost_estimate=hint(8 * codes.size),
+        name="mate_weights",
+    )(codes, scales.T)
+
+
+def cache_kernel(rows, steps, own, chunk, lengths_ref, query_ref, cache_ref, own_query_ref, *parts):
     place = lax.axis_index("tensor")
     cache_len = cache_ref.shape[0] // rows
-    block = base_ref.shape[1]
-    base_loads = []
-    for k in range(2):
-        start = owner_ref[lax.axis_index("group") ^ k] * block
-        here = pl.ds(pl.multiple_of(start, block), block)
-        base_loads.append(pltpu.make_async_copy(base_hbm.at[here], base_ref.at[k], arrived.at[k]))
-        base_loads[k].start()
-
     chunks = own // chunk
     height = chunk * steps
     width = chunks * HD
@@ -159,30 +179,21 @@
         end = rows * chunks * height + 2 * r
         parts[d][end : end + 1, : chunks * height] = peak
         parts[d][end + 1 : end + 2, : chunks * height] = total
-    for load in base_loads:
-        load.wait()
-
-
-def cache_partials(owner_map, lengths, queries, cache, base, block, rows, steps, own, ways):
+
+
+def cache_partials(lengths, queries, cache, rows, steps, own, ways):
     height = rows * own * steps
     part = jax.ShapeDtypeStruct((height + SUBLANES, LANES), jnp.float32)
     out = pl.pallas_call(
         functools.partial(cache_kernel, rows, steps, own, min(own, H // KVH)),
-        out_shape=[
-            jax.ShapeDtypeStruct((2, block, base.shape[1]), jnp.bfloat16),
-            jax.ShapeDtypeStruct((height, HD), jnp.bfloat16),
-        ]
-        + [part] * ways,
-        in_specs=[SMEM, SMEM, VMEM, VMEM, HBM],
-        out_specs=[VMEM] * (2 + ways),
-        scratch_shapes=[
-            pltpu.SemaphoreType.DMA((2,)),
-        ],
+        out_shape=[jax.ShapeDtypeStruct((height, HD), jnp.bfloat16)] + [part] * ways,
+        in_specs=[SMEM, VMEM, VMEM],
+        out_specs=[VMEM] * (1 + ways),
         compiler_params=params(CACHE_KIB),
         cost_estimate=hint(CACHE_HINT),
         name="cache_partials",
-    )(owner_map, lengths, queries, cache, pltpu.with_memory_space_constraint(base, pltpu.HBM))
-    return out[0], out[1], out[2:]
+    )(lengths, queries, cache)
+    return out[0], out[1:]
 
 
 def project_kernel(pairs, own_ref, mate_ref, base_ref, *refs):
@@ -367,24 +378,23 @@
         return [arrays[0]] + [swap(x, axis, stride * d) for x, d in zip(arrays[1:], places)]
 
     token_rows = exchange([hidden_x.reshape(tokens, local_width)] * pairs, "group", 2)
-    codes = [delta_codes, swap(delta_codes, "group", 1)]
-    scales = [delta_scales, swap(delta_scales, "group", 1)]
-
-    own_delta, mate_delta = weights(codes, scales)
-    behind, own_delta = lax.optimization_barrier((owner_map, own_delta))
-    base_blocks, own_query, partials = cache_partials(
+    mate_codes = swap(delta_codes, "group", 1)
+    mate_scales = swap(delta_scales, "group", 1)
+
+    own_delta, base_blocks = own_weights(owner_map, delta_scales, delta_codes, base_weight)
+    mate_delta = mate_weights(mate_codes, mate_scales)
+    behind, mate_delta = lax.optimization_barrier((lengths, mate_delta))
+    own_query, partials = cache_partials(
         behind,
-        lengths,
         queries.reshape(tokens, H * HD),
         kv_cache.reshape(-1, 2 * KVH * HD),
-        base_weight,
-        owner_block,
         rows,
         steps,
         heads_own,
         tensor_count,
     )
     partials = exchange(partials, "tensor", 1)
+    own_query, base_blocks = lax.optimization_barrier((own_query, base_blocks))
     projected = project(own_delta, mate_delta, base_blocks, token_rows)
     arrived = exchange(projected, "group", 2)
     pieces = pack_pieces(owner_map, arrived, owner_block, tensor_count, near_width, slice_width)

time: 36.4 us -> 35.2 us (0.967)
  waiting for transfers between devices: 7.42 us -> 6.52 us
    pallas_call x1, Pallas kernels: 3.43 us -> 1.96 us  [cache_partials(): pl.pallas_call(functools.partial(cache_kernel, rows, steps, own, min(own,...]
    pallas_call x1 -> x2, Pallas kernels: 1.73 us -> 2.93 us  [the longest x1 2.46 us: own_weights(): pl.pallas_call(own_weights_kernel, out_shape=[jax.ShapeDtypeStruct(codes....]
    ppermute x14, waiting for transfers between devices: 7.42 us -> 6.52 us  [swap(): return lax.ppermute(x, axis, [(k, k ^ distance) for k in range(size)])]
where the time goes in v8:
time: 35.2 us; the launch traced here: 35 us
  starting transfers between devices  18.2 us (52%)
  Pallas kernels  8.48 us (24%)
  waiting for transfers between devices  6.52 us (19%)
  local copies, waits for them, and re-layouts  1.08 us (3%)
  between operations  0.74 us (2%)
    ppermute x14, starting transfers between devices, swap(): return lax.ppermute(x, axis, [(k, k ^ distance) for k in range(size)])  18.2 us
    ppermute x14, waiting for transfers between devices, swap(): return lax.ppermute(x, axis, [(k, k ^ distance) for k in range(size)])  6.52 us
    pallas_call x1, Pallas kernels, own_weights(): pl.pallas_call(own_weights_kernel, out_shape=[jax.ShapeDtypeStruct(codes....  2.46 us
    pallas_call x1, Pallas kernels, cache_partials(): pl.pallas_call(functools.partial(cache_kernel, rows, steps, own, min(own,...  1.96 us
    pallas_call x1, Pallas kernels, finish(): pl.pallas_call(functools.partial(finish_kernel, rows, steps, own, min(own...  1.7 us
    pallas_call x1, Pallas kernels, project(): pl.pallas_call(functools.partial(project_kernel, pairs), out_shape=[jax.S...  1.3 us
    unnamed x10, local copies, waits for them, and re-layouts  1.08 us
  transfers between devices with their start and end apart: 14, of which 4 were waited for; matrix products, arithmetic and copies ran while one was open for 0% of the time, Pallas kernels for 16%

profile of v8, /device:TPU:0, one launch (start us, length us, event | category | flops | bytes accessed | tf_op | source)
XLA Modules:
  0.0 35.0 jit_solution(6811111316711384376)
XLA Ops:
  0.6 0.5 %collective-permute-start = (bf16[256,2048]{1,0:T(8,128)(2,1)}, bf16[256,2048]{1,0:T(8,128)(2,1)S(1)}, u32[]{:S(2)}, u32[]{:S(2)}) collective-permute-start(bf16[256,2048]{1,0:T(8,128)(2,1)} %codes_hbm.1), channel_id=1, source_target_pairs={{0,4},{4,0},{8,12},{12,8},{16,20},{20,16},{24,28},{28,24},{1,5},{5... | collective-permute-start | bytes 3145736 | tf_op jit(solution)/shard_map/ppermute | solution.py:43
  1.1 2.6 %collective-permute-start.4 = (bf16[16,2048]{1,0:T(8,128)(2,1)}, bf16[16,2048]{1,0:T(8,128)(2,1)S(1)}, u32[]{:S(2)}, u32[]{:S(2)}) collective-permute-start(bf16[16,2048]{1,0:T(8,128)(2,1)} %bitcast.9), channel_id=1, source_target_pairs={{0,8},{4,12},{8,0},{12,4},{16,24},{20,28},{24,16},{28,20},{1,9},{5... | collective-permute-start | bytes 196616 | tf_op jit(solution)/shard_map/ppermute | solution.py:43
  3.8 2.6 %collective-permute-start.3 = (bf16[16,2048]{1,0:T(8,128)(2,1)}, bf16[16,2048]{1,0:T(8,128)(2,1)S(1)}, u32[]{:S(2)}, u32[]{:S(2)}) collective-permute-start(bf16[16,2048]{1,0:T(8,128)(2,1)} %bitcast.10), channel_id=1, source_target_pairs={{0,16},{4,20},{8,24},{12,28},{16,0},{20,4},{24,8},{28,12},{1,17},{... | collective-permute-start | bytes 196616 | tf_op jit(solution)/shard_map/ppermute | solution.py:43
  6.4 0.0 collective-permute-start.2
  6.4 0.0 collective-permute-start.1
  6.4 0.0 copy-start.1
  6.4 2.5 %own_weights.1 = (bf16[256,2048]{1,0:T(8,128)(2,1)S(1)}, bf16[2,256,2048]{2,1,0:T(8,128)(2,1)S(1)}) custom-call(s32[8]{0:T(128)} %owner_ref.1, bf16[16,256]{1,0:T(8,128)(2,1)} %bitcast.14, bf16[256,2048]{1,0:T(8,128)(2,1)} %codes_hbm.1, bf16[2048,2048]{1,0:T(8,128)(2,1)} %base_hbm.1), custom_call_target="tpu_custom_call" | custom-call | bytes 6000000 | tf_op jit(solution)/shard_map/own_weights/pallas_call | solution.py:99
  8.9 0.0 copy-start
  8.9 0.0 copy-start.4
  8.9 0.0 collective-permute-done.1
  8.9 0.0 collective-permute-done.codes_ref
  8.9 0.0 copy-start.2
  8.9 0.5 %mate_weights.1.mate_ref = bf16[256,2048]{1,0:T(8,128)(2,1)S(1)} custom-call(bf16[256,2048]{1,0:T(8,128)(2,1)S(1)} %collective-permute-done.codes_ref, bf16[16,256]{1,0:T(8,128)(2,1)S(1)} %bitcast.13), custom_call_target="tpu_custom_call" | custom-call | bytes 4194304 | tf_op jit(solution)/shard_map/mate_weights/pallas_call | solution.py:120
  9.4 0.0 copy-done.1
  9.4 1.1 %copy-done = bf16[2,256,2048]{2,1,0:T(8,128)(2,1)S(1)} copy-done((bf16[2,256,2048]{2,1,0:T(8,128)(2,1)S(1)}, bf16[2,256,2048]{2,1,0:T(8,128)(2,1)}, u32[]{:S(2)}) %copy-start) | copy-done | bytes 2097176
  10.5 0.0 copy-done.4
  10.5 2.0 %cache_partials.1 = (bf16[256,128]{1,0:T(8,128)(2,1)S(1)}, f32[264,128]{1,0:T(8,128)S(1)}, f32[264,128]{1,0:T(8,128)S(1)}, f32[264,128]{1,0:T(8,128)S(1)}, f32[264,128]{1,0:T(8,128)S(1)}) custom-call(s32[2]{0:T(128)S(1)} %copy-done.4, bf16[16,8192]{1,0:T(8,128)(2,1)S(1)} %bitcast.8, bf16[512,2048]{1,0:T(8,128)(2,1)S(1)} %bitcast.7), custom_call_target="tpu_custom_call" | custom-call | bytes 120000000 | tf_op jit(solution)/shard_map/cache_partials/pallas_call | solution.py:187
  12.4 0.0 collective-permute-done.4.refs_3_
  12.4 0.0 collective-permute-done.3.refs_2_
  12.5 0.3 collective-permute-done.2.refs_1_
  12.7 0.0 copy-done.2
  12.7 0.0 copy-start.3
  12.7 1.3 %project.1 = (f32[16,512]{1,0:T(8,128)S(1)}, f32[16,512]{1,0:T(8,128)S(1)}, f32[16,512]{1,0:T(8,128)S(1)}, f32[16,512]{1,0:T(8,128)S(1)}) custom-call(bf16[256,2048]{1,0:T(8,128)(2,1)S(1)} %get-tuple-element.27.own_ref, bf16[256,2048]{1,0:T(8,128)(2,1)S(1)} %mate_weights.1.mate_ref, bf16[2,256,2048]{2,1,0:T(8,128)(2,1)S(1)} %get-tuple-element.29.base_ref, ...), custom_call_target="tpu_custom_call" | custom-call | bytes 60000000 | tf_op jit(solution)/shard_map/project/pallas_call | solution.py:214
  14.0 3.6 %collective-permute-start.5 = (f32[16,512]{1,0:T(8,128)S(1)}, f32[16,512]{1,0:T(8,128)S(1)}, u32[]{:S(2)}, u32[]{:S(2)}) collective-permute-start(f32[16,512]{1,0:T(8,128)S(1)} %get-tuple-element.31), channel_id=1, source_target_pairs={{0,24},{4,28},{8,16},{12,20},{16,8},{20,12},{24,0},{28,4},{1,25},{... | collective-permute-start | bytes 98312 | tf_op jit(solution)/shard_map/ppermute | solution.py:43
  17.7 0.0 collective-permute-start.6
  17.7 0.8 %collective-permute-start.7 = (f32[16,512]{1,0:T(8,128)S(1)}, f32[16,512]{1,0:T(8,128)S(1)}, u32[]{:S(2)}, u32[]{:S(2)}) collective-permute-start(f32[16,512]{1,0:T(8,128)S(1)} %get-tuple-element.33), channel_id=1, source_target_pairs={{0,8},{4,12},{8,0},{12,4},{16,24},{20,28},{24,16},{28,20},{1,9},{5... | collective-permute-start | bytes 98312 | tf_op jit(solution)/shard_map/ppermute | solution.py:43
  18.5 2.4 %collective-permute-start.11 = (f32[264,128]{1,0:T(8,128)S(1)}, f32[264,128]{1,0:T(8,128)S(1)}, u32[]{:S(2)}, u32[]{:S(2)}) collective-permute-start(f32[264,128]{1,0:T(8,128)S(1)} %get-tuple-element.39), channel_id=1, source_target_pairs={{0,3},{1,2},{2,1},{3,0},{4,7},{5,6},{6,5},{7,4},{8,11},{9,10},{10,... | collective-permute-start | bytes 405512 | tf_op jit(solution)/shard_map/ppermute | solution.py:43
  20.9 0.5 %collective-permute-start.12 = (f32[264,128]{1,0:T(8,128)S(1)}, f32[264,128]{1,0:T(8,128)S(1)}, u32[]{:S(2)}, u32[]{:S(2)}) collective-permute-start(f32[264,128]{1,0:T(8,128)S(1)} %get-tuple-element.40), channel_id=1, source_target_pairs={{0,2},{1,3},{2,0},{3,1},{4,6},{5,7},{6,4},{7,5},{8,10},{9,11},{10,... | collective-permute-start | bytes 405512 | tf_op jit(solution)/shard_map/ppermute | solution.py:43
  21.4 0.0 collective-permute-done.5.refs_1_
  21.4 0.5 %collective-permute-start.13 = (f32[264,128]{1,0:T(8,128)S(1)}, f32[264,128]{1,0:T(8,128)S(1)}, u32[]{:S(2)}, u32[]{:S(2)}) collective-permute-start(f32[264,128]{1,0:T(8,128)S(1)} %get-tuple-element.41), channel_id=1, source_target_pairs={{0,1},{1,0},{2,3},{3,2},{4,5},{5,4},{6,7},{7,6},{8,9},{9,8},{10,11... | collective-permute-start | bytes 405512 | tf_op jit(solution)/shard_map/ppermute | solution.py:43
  22.0 0.5 %collective-permute-done.6.refs_2_ = f32[16,512]{1,0:T(8,128)S(1)} collective-permute-done((f32[16,512]{1,0:T(8,128)S(1)}, f32[16,512]{1,0:T(8,128)S(1)}, u32[]{:S(2)}, u32[]{:S(2)}) %collective-permute-start.6) | collective-permute-done | bytes 32800 | tf_op jit(solution)/shard_map/ppermute | solution.py:43
  22.5 0.0 collective-permute-done.7.refs_3_
  22.5 0.0 copy-done.3
  22.5 0.6 %pack_pieces.1 = (f32[16,1024]{1,0:T(8,128)S(1)}, f32[16,1024]{1,0:T(8,128)S(1)}, f32[16,1024]{1,0:T(8,128)S(1)}, f32[16,1024]{1,0:T(8,128)S(1)}) custom-call(s32[8]{0:T(128)S(1)} %copy-done.3, f32[16,512]{1,0:T(8,128)S(1)} %get-tuple-element.30.refs_0_, f32[16,512]{1,0:T(8,128)S(1)} %collective-permute-done.5.refs_1_, ...), custom_call_target="tpu_custom_call" | custom-call | bytes 60000000 | tf_op jit(solution)/shard_map/pack_pieces/pallas_call | solution.py:254
  23.1 2.5 %collective-permute-start.8 = (f32[16,1024]{1,0:T(8,128)S(1)}, f32[16,1024]{1,0:T(8,128)S(1)}, u32[]{:S(2)}, u32[]{:S(2)}) collective-permute-start(f32[16,1024]{1,0:T(8,128)S(1)} %get-tuple-element.35), channel_id=1, source_target_pairs={{0,3},{1,2},{2,1},{3,0},{4,7},{5,6},{6,5},{7,4},{8,11},{9,10},{10,... | collective-permute-start | bytes 196616 | tf_op jit(solution)/shard_map/ppermute | solution.py:43
  25.6 0.5 %collective-permute-start.9 = (f32[16,1024]{1,0:T(8,128)S(1)}, f32[16,1024]{1,0:T(8,128)S(1)}, u32[]{:S(2)}, u32[]{:S(2)}) collective-permute-start(f32[16,1024]{1,0:T(8,128)S(1)} %get-tuple-element.36), channel_id=1, source_target_pairs={{0,2},{1,3},{2,0},{3,1},{4,6},{5,7},{6,4},{7,5},{8,10},{9,11},{10,... | collective-permute-start | bytes 196616 | tf_op jit(solution)/shard_map/ppermute | solution.py:43
  26.1 3.0 %collective-permute-done.8.refs_1_ = f32[16,1024]{1,0:T(8,128)S(1)} collective-permute-done((f32[16,1024]{1,0:T(8,128)S(1)}, f32[16,1024]{1,0:T(8,128)S(1)}, u32[]{:S(2)}, u32[]{:S(2)}) %collective-permute-start.8) | collective-permute-done | bytes 65568 | tf_op jit(solution)/shard_map/ppermute | solution.py:43
  29.0 1.5 %collective-permute-start.10 = (f32[16,1024]{1,0:T(8,128)S(1)}, f32[16,1024]{1,0:T(8,128)S(1)}, u32[]{:S(2)}, u32[]{:S(2)}) collective-permute-start(f32[16,1024]{1,0:T(8,128)S(1)} %get-tuple-element.37), channel_id=1, source_target_pairs={{0,1},{1,0},{2,3},{3,2},{4,5},{5,4},{6,7},{7,6},{8,9},{9,8},{10,11... | collective-permute-start | bytes 196616 | tf_op jit(solution)/shard_map/ppermute | solution.py:43
  30.5 0.0 collective-permute-done.9.refs_2_
  30.6 2.8 %collective-permute-done.10.refs_3_ = f32[16,1024]{1,0:T(8,128)S(1)} collective-permute-done((f32[16,1024]{1,0:T(8,128)S(1)}, f32[16,1024]{1,0:T(8,128)S(1)}, u32[]{:S(2)}, u32[]{:S(2)}) %collective-permute-start.10) | collective-permute-done | bytes 65568 | tf_op jit(solution)/shard_map/ppermute | solution.py:43
  33.3 0.0 collective-permute-done.11.refs_5_
  33.3 0.0 collective-permute-done.12.refs_6_
  33.3 0.0 collective-permute-done.13.refs_7_
  33.3 1.7 %finish.1 = (bf16[16,512]{1,0:T(8,128)(2,1)}, bf16[16,2048]{1,0:T(8,128)(2,1)}) custom-call(bf16[256,128]{1,0:T(8,128)(2,1)S(1)} %get-tuple-element.26.query_ref, f32[16,1024]{1,0:T(8,128)S(1)} %get-tuple-element.34.refs_0_, f32[16,1024]{1,0:T(8,128)S(1)} %collective-permute-done.8.refs_1_, f32[16,1024]{1,0:T(8,128)S(1)} %collective-permute-done.9.refs_2_, ...), custom_call_target="tpu_custom_call" | custom-call | tf_op jit(solution)/shard_map/finish/pallas_call | solution.py:348
Async XLA Ops:
  0.6 8.3 %collective-permute-start = (bf16[256,2048]{1,0:T(8,128)(2,1)}, bf16[256,2048]{1,0:T(8,128)(2,1)S(1)}, u32[]{:S(2)}, u32[]{:S(2)}) collective-permute-start(bf16[256,2048]{1,0:T(8,128)(2,1)} %codes_hbm.1), channel_id=1, source_target_pairs={{0,4},{4,0},{8,12},{12,8},{16,20},{20,16},{24,28},{28,24},{1,5},{5... | collective-permute-start | bytes 3145736 | tf_op jit(solution)/shard_map/ppermute | solution.py:43
  1.1 11.3 %collective-permute-start.4 = (bf16[16,2048]{1,0:T(8,128)(2,1)}, bf16[16,2048]{1,0:T(8,128)(2,1)S(1)}, u32[]{:S(2)}, u32[]{:S(2)}) collective-permute-start(bf16[16,2048]{1,0:T(8,128)(2,1)} %bitcast.9), channel_id=1, source_target_pairs={{0,8},{4,12},{8,0},{12,4},{16,24},{20,28},{24,16},{28,20},{1,9},{5... | collective-permute-start | bytes 196616 | tf_op jit(solution)/shard_map/ppermute | solution.py:43
  3.8 8.7 %collective-permute-start.3 = (bf16[16,2048]{1,0:T(8,128)(2,1)}, bf16[16,2048]{1,0:T(8,128)(2,1)S(1)}, u32[]{:S(2)}, u32[]{:S(2)}) collective-permute-start(bf16[16,2048]{1,0:T(8,128)(2,1)} %bitcast.10), channel_id=1, source_target_pairs={{0,16},{4,20},{8,24},{12,28},{16,0},{20,4},{24,8},{28,12},{1,17},{... | collective-permute-start | bytes 196616 | tf_op jit(solution)/shard_map/ppermute | solution.py:43
  6.4 6.3 %collective-permute-start.2 = (bf16[16,2048]{1,0:T(8,128)(2,1)}, bf16[16,2048]{1,0:T(8,128)(2,1)S(1)}, u32[]{:S(2)}, u32[]{:S(2)}) collective-permute-start(bf16[16,2048]{1,0:T(8,128)(2,1)} %bitcast.11), channel_id=1, source_target_pairs={{0,24},{4,28},{8,16},{12,20},{16,8},{20,12},{24,0},{28,4},{1,25},{... | collective-permute-start | bytes 196616 | tf_op jit(solution)/shard_map/ppermute | solution.py:43
  6.4 2.5 %collective-permute-start.1 = (bf16[256,16]{0,1:T(8,128)(2,1)}, bf16[256,16]{0,1:T(8,128)(2,1)S(1)}, u32[]{:S(2)}, u32[]{:S(2)}) collective-permute-start(bf16[256,16]{0,1:T(8,128)(2,1)} %param.11), channel_id=1, source_target_pairs={{0,4},{4,0},{8,12},{12,8},{16,20},{20,16},{24,28},{28,24},{1,5},{5... | collective-permute-start | bytes 24584 | tf_op jit(solution)/shard_map/ppermute | solution.py:43
  6.4 3.0 %copy-start.1 = (bf16[2,8,8192]{2,1,0:T(8,128)(2,1)S(1)}, bf16[2,8,8192]{2,1,0:T(8,128)(2,1)}, u32[]{:S(2)}) copy-start(bf16[2,8,8192]{2,1,0:T(8,128)(2,1)} %param.14) | copy-start | bytes 786436
  8.9 1.6 %copy-start = (bf16[2,256,2048]{2,1,0:T(8,128)(2,1)S(1)}, bf16[2,256,2048]{2,1,0:T(8,128)(2,1)}, u32[]{:S(2)}) copy-start(bf16[2,256,2048]{2,1,0:T(8,128)(2,1)} %param.13) | copy-start | bytes 6291460
  8.9 1.6 %copy-start.4 = (s32[2]{0:T(128)S(1)}, s32[2]{0:T(128)}, u32[]{:S(2)}) copy-start(s32[2]{0:T(128)} %lengths_ref) | copy-start | bytes 28
  8.9 3.8 %copy-start.2 = (bf16[2,8,2048]{2,1,0:T(8,128)(2,1)S(1)}, bf16[2,8,2048]{2,1,0:T(8,128)(2,1)}, u32[]{:S(2)}) copy-start(bf16[2,8,2048]{2,1,0:T(8,128)(2,1)} %param.8) | copy-start | bytes 196612
  12.7 9.8 %copy-start.3 = (s32[8]{0:T(128)S(1)}, s32[8]{0:T(128)}, u32[]{:S(2)}) copy-start(s32[8]{0:T(128)} %owner_ref.1) | copy-start | bytes 100
  14.0 7.4 %collective-permute-start.5 = (f32[16,512]{1,0:T(8,128)S(1)}, f32[16,512]{1,0:T(8,128)S(1)}, u32[]{:S(2)}, u32[]{:S(2)}) collective-permute-start(f32[16,512]{1,0:T(8,128)S(1)} %get-tuple-element.31), channel_id=1, source_target_pairs={{0,24},{4,28},{8,16},{12,20},{16,8},{20,12},{24,0},{28,4},{1,25},{... | collective-permute-start | bytes 98312 | tf_op jit(solution)/shard_map/ppermute | solution.py:43
  17.7 4.8 %collective-permute-start.6 = (f32[16,512]{1,0:T(8,128)S(1)}, f32[16,512]{1,0:T(8,128)S(1)}, u32[]{:S(2)}, u32[]{:S(2)}) collective-permute-start(f32[16,512]{1,0:T(8,128)S(1)} %get-tuple-element.32), channel_id=1, source_target_pairs={{0,16},{4,20},{8,24},{12,28},{16,0},{20,4},{24,8},{28,12},{1,17},{... | collective-permute-start | bytes 98312 | tf_op jit(solution)/shard_map/ppermute | solution.py:43
  17.7 4.8 %collective-permute-start.7 = (f32[16,512]{1,0:T(8,128)S(1)}, f32[16,512]{1,0:T(8,128)S(1)}, u32[]{:S(2)}, u32[]{:S(2)}) collective-permute-start(f32[16,512]{1,0:T(8,128)S(1)} %get-tuple-element.33), channel_id=1, source_target_pairs={{0,8},{4,12},{8,0},{12,4},{16,24},{20,28},{24,16},{28,20},{1,9},{5... | collective-permute-start | bytes 98312 | tf_op jit(solution)/shard_map/ppermute | solution.py:43
  18.5 14.8 %collective-permute-start.11 = (f32[264,128]{1,0:T(8,128)S(1)}, f32[264,128]{1,0:T(8,128)S(1)}, u32[]{:S(2)}, u32[]{:S(2)}) collective-permute-start(f32[264,128]{1,0:T(8,128)S(1)} %get-tuple-element.39), channel_id=1, source_target_pairs={{0,3},{1,2},{2,1},{3,0},{4,7},{5,6},{6,5},{7,4},{8,11},{9,10},{10,... | collective-permute-start | bytes 405512 | tf_op jit(solution)/shard_map/ppermute | solution.py:43
  20.9 12.4 %collective-permute-start.12 = (f32[264,128]{1,0:T(8,128)S(1)}, f32[264,128]{1,0:T(8,128)S(1)}, u32[]{:S(2)}, u32[]{:S(2)}) collective-permute-start(f32[264,128]{1,0:T(8,128)S(1)} %get-tuple-element.40), channel_id=1, source_target_pairs={{0,2},{1,3},{2,0},{3,1},{4,6},{5,7},{6,4},{7,5},{8,10},{9,11},{10,... | collective-permute-start | bytes 405512 | tf_op jit(solution)/shard_map/ppermute | solution.py:43
  21.4 11.9 %collective-permute-start.13 = (f32[264,128]{1,0:T(8,128)S(1)}, f32[264,128]{1,0:T(8,128)S(1)}, u32[]{:S(2)}, u32[]{:S(2)}) collective-permute-start(f32[264,128]{1,0:T(8,128)S(1)} %get-tuple-element.41), channel_id=1, source_target_pairs={{0,1},{1,0},{2,3},{3,2},{4,5},{5,4},{6,7},{7,6},{8,9},{9,8},{10,11... | collective-permute-start | bytes 405512 | tf_op jit(solution)/shard_map/ppermute | solution.py:43
  23.1 6.0 %collective-permute-start.8 = (f32[16,1024]{1,0:T(8,128)S(1)}, f32[16,1024]{1,0:T(8,128)S(1)}, u32[]{:S(2)}, u32[]{:S(2)}) collective-permute-start(f32[16,1024]{1,0:T(8,128)S(1)} %get-tuple-element.35), channel_id=1, source_target_pairs={{0,3},{1,2},{2,1},{3,0},{4,7},{5,6},{6,5},{7,4},{8,11},{9,10},{10,... | collective-permute-start | bytes 196616 | tf_op jit(solution)/shard_map/ppermute | solution.py:43
  25.6 5.0 %collective-permute-start.9 = (f32[16,1024]{1,0:T(8,128)S(1)}, f32[16,1024]{1,0:T(8,128)S(1)}, u32[]{:S(2)}, u32[]{:S(2)}) collective-permute-start(f32[16,1024]{1,0:T(8,128)S(1)} %get-tuple-element.36), channel_id=1, source_target_pairs={{0,2},{1,3},{2,0},{3,1},{4,6},{5,7},{6,4},{7,5},{8,10},{9,11},{10,... | collective-permute-start | bytes 196616 | tf_op jit(solution)/shard_map/ppermute | solution.py:43
  29.0 4.3 %collective-permute-start.10 = (f32[16,1024]{1,0:T(8,128)S(1)}, f32[16,1024]{1,0:T(8,128)S(1)}, u32[]{:S(2)}, u32[]{:S(2)}) collective-permute-start(f32[16,1024]{1,0:T(8,128)S(1)} %get-tuple-element.37), channel_id=1, source_target_pairs={{0,1},{1,0},{2,3},{3,2},{4,5},{5,4},{6,7},{7,6},{8,9},{9,8},{10,11... | collective-permute-start | bytes 196616 | tf_op jit(solution)/shard_map/ppermute | solution.py:43

commit v9 on v8

--- a/solution.py
+++ b/solution.py
@@ -28,6 +28,37 @@
 VMEM = pl.BlockSpec(memory_space=pltpu.VMEM)
 SMEM = pl.BlockSpec(memory_space=pltpu.SMEM)
 HBM = pl.BlockSpec(memory_space=pltpu.HBM)
+
+
+def split(x):
+    high = x.astype(jnp.bfloat16).astype(jnp.float32)
+    middle = (x - high).astype(jnp.bfloat16).astype(jnp.float32)
+    return [high, middle, x - high - middle]
+
+
+def stats_rows(dtype):
+    return SUBLANES if dtype == jnp.float32 else 2 * SUBLANES
+
+
+def put_stats(ref, index, stats):
+    dtype = ref.dtype
+    lines = [x for one in stats for x in ([one] if dtype == jnp.float32 else split(one))]
+    lanes = lines[0].shape[1]
+    count = stats_rows(dtype)
+    lines.append(jnp.zeros((count - len(lines), lanes), jnp.float32))
+    tile = jnp.concatenate(lines, axis=0)
+    if lanes < LANES:
+        tile = jnp.concatenate([tile, jnp.zeros((count, LANES - lanes), jnp.float32)], axis=1)
+    ref[index, ref.shape[1] - count :] = tile.astype(dtype)
+
+
+def get_stats(ref, index, rows):
+    dtype = ref.dtype
+    tile = ref[index, ref.shape[1] - stats_rows(dtype) :].astype(jnp.float32)
+    lines = [tile[n : n + 1] for n in range(2 * rows * (1 if dtype == jnp.float32 else 3))]
+    if dtype != jnp.float32:
+        lines = [a + b + c for a, b, c in zip(lines[::3], lines[1::3], lines[2::3])]
+    return [(lines[2 * r], lines[2 * r + 1]) for r in range(rows)]
 
 
 def hint(size):
@@ -123,12 +154,14 @@
         in_specs=[VMEM, VMEM],
         out_specs=VMEM,
         compiler_params=params(WEIGHTS_KIB),
-        cost_estimate=hint(8 * codes.size),
+        cost_estimate=hint(1000),
         name="mate_weights",
     )(codes, scales.T)
 
 
-def cache_kernel(rows, steps, own, chunk, lengths_ref, query_ref, cache_ref, own_query_ref, *parts):
+def cache_kernel(
+    rows, steps, own, chunk, lengths_ref, query_ref, cache_ref, own_query_ref, kept_ref, sent_ref
+):
     place = lax.axis_index("tensor")
     cache_len = cache_ref.shape[0] // rows
     chunks = own // chunk
@@ -137,10 +170,10 @@
     position = lax.broadcasted_iota(jnp.int32, (cache_len, chunks * height), 0)
 
     def kv_lane(d):
-        return pl.multiple_of(((place ^ order[d]) * own // (H // KVH)) * HD, HD)
+        return pl.multiple_of(((place ^ d) * own // (H // KVH)) * HD, HD)
 
     def score(r, d):
-        head = (place ^ order[d]) * own
+        head = (place ^ d) * own
         queries = query_ref[:, pl.ds(pl.multiple_of(head * HD, HD), own * HD)]
         query = head_rows(queries.astype(jnp.float32), r, steps, own)
         if d == 0:
@@ -155,8 +188,7 @@
         keys = cache_ref[pl.ds(r * cache_len, cache_len), pl.ds(kv_lane(d), width)]
         return dot(keys, spread, NT)
 
-    order = distances(len(parts))
-    units = [(r, d) for r in range(rows) for d in range(len(parts))]
+    units = [(r, d) for d in range(2 * kept_ref.shape[0]) for r in range(rows)]
     ahead = []
     for n in range(len(units) + 1):
         if n < len(units):
@@ -173,27 +205,71 @@
         lane = pl.ds(kv_lane(d) + KVH * HD, width)
         values = cache_ref[pl.ds(r * cache_len, cache_len), lane]
         sums = dot(weights.astype(jnp.bfloat16), values, TN)
+        ref, index = (sent_ref if d % 2 else kept_ref), d // 2
         for j in range(chunks):
             here = slice(j * height, (j + 1) * height)
-            parts[d][at + j * height : at + (j + 1) * height] = sums[here, j * HD : (j + 1) * HD]
-        end = rows * chunks * height + 2 * r
-        parts[d][end : end + 1, : chunks * height] = peak
-        parts[d][end + 1 : end + 2, : chunks * height] = total
+            mine = sums[here, j * HD : (j + 1) * HD].astype(ref.dtype)
+            ref[index, at + j * height : at + (j + 1) * height] = mine
+        stats = (stats if r > 0 else []) + [peak, total]
+        if r == rows - 1:
+            put_stats(ref, index, stats)
+
+
+def part_shape(count, height, dtype):
+    return jax.ShapeDtypeStruct((count, height + stats_rows(dtype), LANES), dtype)
 
 
 def cache_partials(lengths, queries, cache, rows, steps, own, ways):
     height = rows * own * steps
-    part = jax.ShapeDtypeStruct((height + SUBLANES, LANES), jnp.float32)
-    out = pl.pallas_call(
+    return pl.pallas_call(
         functools.partial(cache_kernel, rows, steps, own, min(own, H // KVH)),
-        out_shape=[jax.ShapeDtypeStruct((height, HD), jnp.bfloat16)] + [part] * ways,
+        out_shape=[
+            jax.ShapeDtypeStruct((height, HD), jnp.bfloat16),
+            part_shape(ways // 2, height, jnp.float32),
+            part_shape(ways // 2, height, jnp.bfloat16),
+        ],
         in_specs=[SMEM, VMEM, VMEM],
-        out_specs=[VMEM] * (1 + ways),
+        out_specs=[VMEM] * 3,
         compiler_params=params(CACHE_KIB),
         cost_estimate=hint(CACHE_HINT),
         name="cache_partials",
     )(lengths, queries, cache)
-    return out[0], out[1:]
+
+
+def merge_kernel(rows, span, kept_ref, came_ref, next_ref, sent_ref):
+    for n in range(kept_ref.shape[0]):
+        ref, index = (sent_ref if n % 2 else next_ref), n // 2
+        stats, factors = [], []
+        for one, two in zip(get_stats(kept_ref, n, rows), get_stats(came_ref, n, rows)):
+            peak = jnp.maximum(one[0], two[0])
+            scales = [jnp.exp(one[0] - peak), jnp.exp(two[0] - peak)]
+            stats += [peak, one[1] * scales[0] + two[1] * scales[1]]
+            factors += scales
+        factors.append(jnp.zeros((SUBLANES - len(factors), LANES), jnp.float32))
+        columns = jnp.concatenate(factors, axis=0).T[:span]
+        for r in range(rows):
+            here = slice(r * span, (r + 1) * span)
+            left = kept_ref[n, here] * columns[:, 2 * r : 2 * r + 1]
+            right = came_ref[n, here].astype(jnp.float32) * columns[:, 2 * r + 1 : 2 * r + 2]
+            ref[index, here] = (left + right).astype(ref.dtype)
+        put_stats(ref, index, stats)
+
+
+def merge(kept, came, rows):
+    count = kept.shape[0]
+    height = kept.shape[1] - stats_rows(kept.dtype)
+    return pl.pallas_call(
+        functools.partial(merge_kernel, rows, height // rows),
+        out_shape=[
+            part_shape(count // 2, height, jnp.float32),
+            part_shape(count // 2, height, jnp.bfloat16),
+        ],
+        in_specs=[VMEM] * 2,
+        out_specs=[VMEM] * 2,
+        compiler_params=params(8192),
+        cost_estimate=hint(4 * kept.size),
+        name="merge_partials",
+    )(kept, came)
 
 
 def project_kernel(pairs, own_ref, mate_ref, base_ref, *refs):
@@ -282,11 +358,10 @@
 
 
 def finish_kernel(rows, steps, own, chunk, near_width, ways, query_ref, *refs):
-    pieces, parts = refs[:ways], refs[ways : 2 * ways]
-    new_ref, attended_ref = refs[2 * ways :]
+    pieces, parts = refs[:ways], refs[ways : ways + 2]
+    new_ref, attended_ref = refs[ways + 2 :]
     chunks = own // chunk
     height = chunk * steps
-    end = rows * chunks * height
     summed = pieces[0][...]
     for piece in pieces[1:]:
         summed = summed + piece[...]
@@ -296,7 +371,7 @@
     key_step = lax.broadcasted_iota(jnp.int32, (steps, height), 0)
     query_step = lax.broadcasted_iota(jnp.int32, (steps, height), 1) % steps
     causal = key_step <= query_step
-    stats = [part[end : end + SUBLANES] for part in parts]
+    stats = [get_stats(part, 0, rows) for part in parts]
     factors, near_sums = [], []
     for r in range(rows):
         peaks, totals = [], []
@@ -314,8 +389,8 @@
             near_sums.append(dot(weights.astype(jnp.bfloat16), values.astype(jnp.bfloat16), TN))
         lanes = chunks * height
         pad = [jnp.zeros((1, LANES - lanes), jnp.float32)] if lanes < LANES else []
-        peaks = [s[2 * r : 2 * r + 1] for s in stats] + [jnp.concatenate(peaks + pad, axis=1)]
-        totals = [s[2 * r + 1 : 2 * r + 2] for s in stats] + [jnp.concatenate(totals + pad, axis=1)]
+        peaks = [one[r][0] for one in stats] + [jnp.concatenate(peaks + pad, axis=1)]
+        totals = [one[r][1] for one in stats] + [jnp.concatenate(totals + pad, axis=1)]
         top = functools.reduce(jnp.maximum, peaks)
         scales = [jnp.exp(peak - top) for peak in peaks]
         total = sum(scale * one for scale, one in zip(scales, totals))
@@ -331,10 +406,12 @@
         for r in range(rows):
             at = (r * chunks + j) * height
             here = slice(j * height, (j + 1) * height)
-            first = r * (ways + 1)
-            out = near_sums[r * chunks + j] * columns[here, first + ways : first + ways + 1]
-            for d, part in enumerate(parts):
-                out = out + part[at : at + height] * columns[here, first + d : first + d + 1]
+            first = r * (len(parts) + 1)
+            last = first + len(parts)
+            out = near_sums[r * chunks + j] * columns[here, last : last + 1]
+            for n, part in enumerate(parts):
+                mine = part[0, at : at + height].astype(jnp.float32)
+                out = out + mine * columns[here, first + n : first + n + 1]
             merged.append(out)
         for h in range(chunk):
             both = [out[h * steps : (h + 1) * steps] for out in merged]
@@ -353,7 +430,7 @@
             jax.ShapeDtypeStruct((count, width - 2 * near_width), jnp.bfloat16),
             jax.ShapeDtypeStruct((count, own * HD), jnp.bfloat16),
         ],
-        in_specs=[VMEM] * (1 + 2 * ways),
+        in_specs=[VMEM] * (3 + ways),
         out_specs=[VMEM] * 2,
         compiler_params=params(8192),
         name="finish",
@@ -377,6 +454,9 @@
         places = distances(len(arrays))[1:]
         return [arrays[0]] + [swap(x, axis, stride * d) for x, d in zip(arrays[1:], places)]
 
+    def near_first(arrays):
+        return arrays[:1] + arrays[:0:-1]
+
     token_rows = exchange([hidden_x.reshape(tokens, local_width)] * pairs, "group", 2)
     mate_codes = swap(delta_codes, "group", 1)
     mate_scales = swap(delta_scales, "group", 1)
@@ -384,7 +464,7 @@
     own_delta, base_blocks = own_weights(owner_map, delta_scales, delta_codes, base_weight)
     mate_delta = mate_weights(mate_codes, mate_scales)
     behind, mate_delta = lax.optimization_barrier((lengths, mate_delta))
-    own_query, partials = cache_partials(
+    own_query, kept, sent = cache_partials(
         behind,
         queries.reshape(tokens, H * HD),
         kv_cache.reshape(-1, 2 * KVH * HD),
@@ -393,13 +473,21 @@
         heads_own,
         tensor_count,
     )
-    partials = exchange(partials, "tensor", 1)
     own_query, base_blocks = lax.optimization_barrier((own_query, base_blocks))
-    projected = project(own_delta, mate_delta, base_blocks, token_rows)
-    arrived = exchange(projected, "group", 2)
+    projected = project(own_delta, mate_delta, base_blocks, near_first(token_rows))
+    projected, sent = lax.optimization_barrier((projected, sent))
+    step = 1
+    while step < tensor_count:
+        came = swap(sent, "tensor", step)
+        step *= 2
+        if step < tensor_count:
+            kept, sent = merge(kept, came, rows)
+    arrived = exchange(near_first(projected), "group", 2)
     pieces = pack_pieces(owner_map, arrived, owner_block, tensor_count, near_width, slice_width)
     pieces = exchange(pieces, "tensor", 1)
-    new_out, attended = finish(own_query, pieces, partials, rows, steps, heads_own, near_width)
+    new_out, attended = finish(
+        own_query, pieces, [kept, came], rows, steps, heads_own, near_width
+    )
     return (new_out.reshape(rows, steps, -1), attended.reshape(rows, steps, -1))
 
 

time: 35.2 us -> 32.7 us (0.929)
  waiting for transfers between devices: 6.52 us -> 4.76 us
  starting transfers between devices: 18.2 us -> 17.2 us
    ppermute x14 -> x13, waiting for transfers between devices: 6.52 us -> 4.76 us  [swap(): return lax.ppermute(x, axis, [(k, k ^ distance) for k in range(size)])]
    ppermute x14 -> x13, starting transfers between devices: 18.2 us -> 17.2 us  [swap(): return lax.ppermute(x, axis, [(k, k ^ distance) for k in range(size)])]
  transfers between devices with their start and end apart: 14 -> 13, of which waited for: 4 -> 5; matrix products, arithmetic and copies ran while one was open for 0% -> 0% of each run, Pallas kernels for 16% -> 18%
where the time goes in v9:
time: 32.7 us; the launch traced here: 32.5 us
  starting transfers between devices  17.2 us (53%)
  Pallas kernels  8.69 us (27%)
  waiting for transfers between devices  4.76 us (15%)
  local copies, waits for them, and re-layouts  1.08 us (3%)
  between operations  0.76 us (2%)
    ppermute x13, starting transfers between devices, swap(): return lax.ppermute(x, axis, [(k, k ^ distance) for k in range(size)])  17.2 us
    ppermute x13, waiting for transfers between devices, swap(): return lax.ppermute(x, axis, [(k, k ^ distance) for k in range(size)])  4.76 us
    pallas_call x1, Pallas kernels, own_weights(): pl.pallas_call(own_weights_kernel, out_shape=[jax.ShapeDtypeStruct(codes....  2.46 us
    pallas_call x1, Pallas kernels, cache_partials(): pl.pallas_call(functools.partial(cache_kernel, rows, steps, own, min(own,...  1.96 us
    pallas_call x1, Pallas kernels, finish(): pl.pallas_call(functools.partial(finish_kernel, rows, steps, own, min(own...  1.61 us
    pallas_call x1, Pallas kernels, project(): pl.pallas_call(functools.partial(project_kernel, pairs), out_shape=[jax.S...  1.3 us
    unnamed x10, local copies, waits for them, and re-layouts  1.08 us
  transfers between devices with their start and end apart: 13, of which 5 were waited for; matrix products, arithmetic and copies ran while one was open for 0% of the time, Pallas kernels for 18%

profile of v9, /device:TPU:0, one launch (start us, length us, event | category | flops | bytes accessed | tf_op | source)
XLA Modules:
  0.0 32.5 jit_solution(7545249270578137765)
XLA Ops:
  0.6 0.5 %collective-permute-start = (bf16[256,2048]{1,0:T(8,128)(2,1)}, bf16[256,2048]{1,0:T(8,128)(2,1)S(1)}, u32[]{:S(2)}, u32[]{:S(2)}) collective-permute-start(bf16[256,2048]{1,0:T(8,128)(2,1)} %codes_hbm.1), channel_id=1, source_target_pairs={{0,4},{4,0},{8,12},{12,8},{16,20},{20,16},{24,28},{28,24},{1,5},{5... | collective-permute-start | bytes 3145736 | tf_op jit(solution)/shard_map/ppermute | solution.py:74
  1.1 4.7 %collective-permute-start.4 = (bf16[16,2048]{1,0:T(8,128)(2,1)}, bf16[16,2048]{1,0:T(8,128)(2,1)S(1)}, u32[]{:S(2)}, u32[]{:S(2)}) collective-permute-start(bf16[16,2048]{1,0:T(8,128)(2,1)} %bitcast.9), channel_id=1, source_target_pairs={{0,24},{4,28},{8,16},{12,20},{16,8},{20,12},{24,0},{28,4},{1,25},{... | collective-permute-start | bytes 196616 | tf_op jit(solution)/shard_map/ppermute | solution.py:74
  5.8 0.0 collective-permute-start.3
  5.8 0.6 %collective-permute-start.2 = (bf16[16,2048]{1,0:T(8,128)(2,1)}, bf16[16,2048]{1,0:T(8,128)(2,1)S(1)}, u32[]{:S(2)}, u32[]{:S(2)}) collective-permute-start(bf16[16,2048]{1,0:T(8,128)(2,1)} %bitcast.11), channel_id=1, source_target_pairs={{0,8},{4,12},{8,0},{12,4},{16,24},{20,28},{24,16},{28,20},{1,9},{5... | collective-permute-start | bytes 196616 | tf_op jit(solution)/shard_map/ppermute | solution.py:74
  6.5 0.0 collective-permute-start.1
  6.5 0.0 copy-start.1
  6.5 2.5 %own_weights.1 = (bf16[256,2048]{1,0:T(8,128)(2,1)S(1)}, bf16[2,256,2048]{2,1,0:T(8,128)(2,1)S(1)}) custom-call(s32[8]{0:T(128)} %owner_ref.1, bf16[16,256]{1,0:T(8,128)(2,1)} %bitcast.14, bf16[256,2048]{1,0:T(8,128)(2,1)} %codes_hbm.1, bf16[2048,2048]{1,0:T(8,128)(2,1)} %base_hbm.1), custom_call_target="tpu_custom_call" | custom-call | bytes 6000000 | tf_op jit(solution)/shard_map/own_weights/pallas_call | solution.py:130
  8.9 0.0 copy-start
  9.0 0.0 copy-start.4
  9.0 0.0 collective-permute-done.1
  9.0 0.0 collective-permute-done.codes_ref
  9.0 0.0 copy-start.2
  9.0 0.5 %mate_weights.1.mate_ref = bf16[256,2048]{1,0:T(8,128)(2,1)S(1)} custom-call(bf16[256,2048]{1,0:T(8,128)(2,1)S(1)} %collective-permute-done.codes_ref, bf16[16,256]{1,0:T(8,128)(2,1)S(1)} %bitcast.13), custom_call_target="tpu_custom_call" | custom-call | bytes 1000 | tf_op jit(solution)/shard_map/mate_weights/pallas_call | solution.py:151
  9.5 0.0 copy-done.1
  9.5 1.1 %copy-done = bf16[2,256,2048]{2,1,0:T(8,128)(2,1)S(1)} copy-done((bf16[2,256,2048]{2,1,0:T(8,128)(2,1)S(1)}, bf16[2,256,2048]{2,1,0:T(8,128)(2,1)}, u32[]{:S(2)}) %copy-start) | copy-done | bytes 2097176
  10.5 0.0 copy-done.4
  10.5 2.0 %cache_partials.1 = (bf16[256,128]{1,0:T(8,128)(2,1)S(1)}, f32[2,264,128]{2,1,0:T(8,128)S(1)}, bf16[2,272,128]{2,1,0:T(8,128)(2,1)S(1)}) custom-call(s32[2]{0:T(128)S(1)} %copy-done.4, bf16[16,8192]{1,0:T(8,128)(2,1)S(1)} %bitcast.8, bf16[512,2048]{1,0:T(8,128)(2,1)S(1)} %bitcast.7), custom_call_target="tpu_custom_call" | custom-call | bytes 120000000 | tf_op jit(solution)/shard_map/cache_partials/pallas_call | solution.py:224
  12.5 0.0 collective-permute-done.4.refs_3_
  12.5 0.0 collective-permute-done.3.refs_2_
  12.5 0.0 collective-permute-done.2.refs_1_
  12.5 0.0 copy-done.2
  12.5 0.0 copy-start.3
  12.6 1.3 %project.1 = (f32[16,512]{1,0:T(8,128)S(1)}, f32[16,512]{1,0:T(8,128)S(1)}, f32[16,512]{1,0:T(8,128)S(1)}, f32[16,512]{1,0:T(8,128)S(1)}) custom-call(bf16[256,2048]{1,0:T(8,128)(2,1)S(1)} %get-tuple-element.32.own_ref, bf16[256,2048]{1,0:T(8,128)(2,1)S(1)} %mate_weights.1.mate_ref, bf16[2,256,2048]{2,1,0:T(8,128)(2,1)S(1)} %get-tuple-element.34.base_ref, ...), custom_call_target="tpu_custom_call" | custom-call | bytes 60000000 | tf_op jit(solution)/shard_map/project/pallas_call | solution.py:290
  13.9 1.7 %collective-permute-start.11 = (bf16[2,272,128]{2,1,0:T(8,128)(2,1)S(1)}, bf16[2,272,128]{2,1,0:T(8,128)(2,1)S(1)}, u32[]{:S(2)}, u32[]{:S(2)}) collective-permute-start(bf16[2,272,128]{2,1,0:T(8,128)(2,1)S(1)} %get-tuple-element.49), channel_id=1, source_target_pairs={{0,1},{1,0},{2,3},{3,2},{4,5},{5,4},{6,7},{7,6},{8,9},{9,8},{10,11... | collective-permute-start | bytes 417800 | tf_op jit(solution)/shard_map/ppermute | solution.py:74
  15.6 3.6 %collective-permute-start.5 = (f32[16,512]{1,0:T(8,128)S(1)}, f32[16,512]{1,0:T(8,128)S(1)}, u32[]{:S(2)}, u32[]{:S(2)}) collective-permute-start(f32[16,512]{1,0:T(8,128)S(1)} %get-tuple-element.41), channel_id=1, source_target_pairs={{0,24},{4,28},{8,16},{12,20},{16,8},{20,12},{24,0},{28,4},{1,25},{... | collective-permute-start | bytes 98312 | tf_op jit(solution)/shard_map/ppermute | solution.py:74
  19.2 0.0 collective-permute-start.6
  19.2 0.8 %collective-permute-start.7 = (f32[16,512]{1,0:T(8,128)S(1)}, f32[16,512]{1,0:T(8,128)S(1)}, u32[]{:S(2)}, u32[]{:S(2)}) collective-permute-start(f32[16,512]{1,0:T(8,128)S(1)} %get-tuple-element.43), channel_id=1, source_target_pairs={{0,8},{4,12},{8,0},{12,4},{16,24},{20,28},{24,16},{28,20},{1,9},{5... | collective-permute-start | bytes 98312 | tf_op jit(solution)/shard_map/ppermute | solution.py:74
  19.9 0.1 collective-permute-done.11.came_ref
  20.0 0.3 merge_partials.1
  20.3 1.7 %collective-permute-start.12 = (bf16[1,272,128]{2,1,0:T(8,128)(2,1)S(1)}, bf16[1,272,128]{2,1,0:T(8,128)(2,1)S(1)}, u32[]{:S(2)}, u32[]{:S(2)}) collective-permute-start(bf16[1,272,128]{2,1,0:T(8,128)(2,1)S(1)} %get-tuple-element.51), channel_id=1, source_target_pairs={{0,2},{1,3},{2,0},{3,1},{4,6},{5,7},{6,4},{7,5},{8,10},{9,11},{10,... | collective-permute-start | bytes 208904 | tf_op jit(solution)/shard_map/ppermute | solution.py:74
  22.1 0.0 collective-permute-done.5.refs_1_
  22.1 1.9 %collective-permute-done.6.refs_2_ = f32[16,512]{1,0:T(8,128)S(1)} collective-permute-done((f32[16,512]{1,0:T(8,128)S(1)}, f32[16,512]{1,0:T(8,128)S(1)}, u32[]{:S(2)}, u32[]{:S(2)}) %collective-permute-start.6) | collective-permute-done | bytes 32800 | tf_op jit(solution)/shard_map/ppermute | solution.py:74
  24.0 0.0 collective-permute-done.7.refs_3_
  24.0 0.0 copy-done.3
  24.0 0.6 %pack_pieces.1 = (f32[16,1024]{1,0:T(8,128)S(1)}, f32[16,1024]{1,0:T(8,128)S(1)}, f32[16,1024]{1,0:T(8,128)S(1)}, f32[16,1024]{1,0:T(8,128)S(1)}) custom-call(s32[8]{0:T(128)S(1)} %copy-done.3, f32[16,512]{1,0:T(8,128)S(1)} %get-tuple-element.40.refs_0_, f32[16,512]{1,0:T(8,128)S(1)} %collective-permute-done.5.refs_1_, ...), custom_call_target="tpu_custom_call" | custom-call | bytes 60000000 | tf_op jit(solution)/shard_map/pack_pieces/pallas_call | solution.py:330
  24.6 1.6 %collective-permute-start.8 = (f32[16,1024]{1,0:T(8,128)S(1)}, f32[16,1024]{1,0:T(8,128)S(1)}, u32[]{:S(2)}, u32[]{:S(2)}) collective-permute-start(f32[16,1024]{1,0:T(8,128)S(1)} %get-tuple-element.45), channel_id=1, source_target_pairs={{0,3},{1,2},{2,1},{3,0},{4,7},{5,6},{6,5},{7,4},{8,11},{9,10},{10,... | collective-permute-start | bytes 196616 | tf_op jit(solution)/shard_map/ppermute | solution.py:74
  26.1 0.5 %collective-permute-start.9 = (f32[16,1024]{1,0:T(8,128)S(1)}, f32[16,1024]{1,0:T(8,128)S(1)}, u32[]{:S(2)}, u32[]{:S(2)}) collective-permute-start(f32[16,1024]{1,0:T(8,128)S(1)} %get-tuple-element.46), channel_id=1, source_target_pairs={{0,2},{1,3},{2,0},{3,1},{4,6},{5,7},{6,4},{7,5},{8,10},{9,11},{10,... | collective-permute-start | bytes 196616 | tf_op jit(solution)/shard_map/ppermute | solution.py:74
  26.6 1.5 %collective-permute-start.10 = (f32[16,1024]{1,0:T(8,128)S(1)}, f32[16,1024]{1,0:T(8,128)S(1)}, u32[]{:S(2)}, u32[]{:S(2)}) collective-permute-start(f32[16,1024]{1,0:T(8,128)S(1)} %get-tuple-element.47), channel_id=1, source_target_pairs={{0,1},{1,0},{2,3},{3,2},{4,5},{5,4},{6,7},{7,6},{8,9},{9,8},{10,11... | collective-permute-start | bytes 196616 | tf_op jit(solution)/shard_map/ppermute | solution.py:74
  28.1 1.7 %collective-permute-done.8.refs_1_ = f32[16,1024]{1,0:T(8,128)S(1)} collective-permute-done((f32[16,1024]{1,0:T(8,128)S(1)}, f32[16,1024]{1,0:T(8,128)S(1)}, u32[]{:S(2)}, u32[]{:S(2)}) %collective-permute-start.8) | collective-permute-done | bytes 65568 | tf_op jit(solution)/shard_map/ppermute | solution.py:74
  29.9 0.7 %collective-permute-done.9.refs_2_ = f32[16,1024]{1,0:T(8,128)S(1)} collective-permute-done((f32[16,1024]{1,0:T(8,128)S(1)}, f32[16,1024]{1,0:T(8,128)S(1)}, u32[]{:S(2)}, u32[]{:S(2)}) %collective-permute-start.9) | collective-permute-done | bytes 65568 | tf_op jit(solution)/shard_map/ppermute | solution.py:74
  30.5 0.3 %collective-permute-done.10.refs_3_ = f32[16,1024]{1,0:T(8,128)S(1)} collective-permute-done((f32[16,1024]{1,0:T(8,128)S(1)}, f32[16,1024]{1,0:T(8,128)S(1)}, u32[]{:S(2)}, u32[]{:S(2)}) %collective-permute-start.10) | collective-permute-done | bytes 65568 | tf_op jit(solution)/shard_map/ppermute | solution.py:74
  30.9 0.0 collective-permute-done.12.refs_5_
  30.9 1.6 %finish.1 = (bf16[16,512]{1,0:T(8,128)(2,1)}, bf16[16,2048]{1,0:T(8,128)(2,1)}) custom-call(bf16[256,128]{1,0:T(8,128)(2,1)S(1)} %get-tuple-element.31.query_ref, f32[16,1024]{1,0:T(8,128)S(1)} %get-tuple-element.44.refs_0_, f32[16,1024]{1,0:T(8,128)S(1)} %collective-permute-done.8.refs_1_, f32[16,1024]{1,0:T(8,128)S(1)} %collective-permute-done.9.refs_2_, ...), custom_call_target="tpu_custom_call" | custom-call | tf_op jit(solution)/shard_map/finish/pallas_call | solution.py:425
Async XLA Ops:
  0.6 8.3 %collective-permute-start = (bf16[256,2048]{1,0:T(8,128)(2,1)}, bf16[256,2048]{1,0:T(8,128)(2,1)S(1)}, u32[]{:S(2)}, u32[]{:S(2)}) collective-permute-start(bf16[256,2048]{1,0:T(8,128)(2,1)} %codes_hbm.1), channel_id=1, source_target_pairs={{0,4},{4,0},{8,12},{12,8},{16,20},{20,16},{24,28},{28,24},{1,5},{5... | collective-permute-start | bytes 3145736 | tf_op jit(solution)/shard_map/ppermute | solution.py:74
  1.1 11.4 %collective-permute-start.4 = (bf16[16,2048]{1,0:T(8,128)(2,1)}, bf16[16,2048]{1,0:T(8,128)(2,1)S(1)}, u32[]{:S(2)}, u32[]{:S(2)}) collective-permute-start(bf16[16,2048]{1,0:T(8,128)(2,1)} %bitcast.9), channel_id=1, source_target_pairs={{0,24},{4,28},{8,16},{12,20},{16,8},{20,12},{24,0},{28,4},{1,25},{... | collective-permute-start | bytes 196616 | tf_op jit(solution)/shard_map/ppermute | solution.py:74
  5.8 6.7 %collective-permute-start.3 = (bf16[16,2048]{1,0:T(8,128)(2,1)}, bf16[16,2048]{1,0:T(8,128)(2,1)S(1)}, u32[]{:S(2)}, u32[]{:S(2)}) collective-permute-start(bf16[16,2048]{1,0:T(8,128)(2,1)} %bitcast.10), channel_id=1, source_target_pairs={{0,16},{4,20},{8,24},{12,28},{16,0},{20,4},{24,8},{28,12},{1,17},{... | collective-permute-start | bytes 196616 | tf_op jit(solution)/shard_map/ppermute | solution.py:74
  5.8 6.7 %collective-permute-start.2 = (bf16[16,2048]{1,0:T(8,128)(2,1)}, bf16[16,2048]{1,0:T(8,128)(2,1)S(1)}, u32[]{:S(2)}, u32[]{:S(2)}) collective-permute-start(bf16[16,2048]{1,0:T(8,128)(2,1)} %bitcast.11), channel_id=1, source_target_pairs={{0,8},{4,12},{8,0},{12,4},{16,24},{20,28},{24,16},{28,20},{1,9},{5... | collective-permute-start | bytes 196616 | tf_op jit(solution)/shard_map/ppermute | solution.py:74
  6.5 2.5 %collective-permute-start.1 = (bf16[256,16]{0,1:T(8,128)(2,1)}, bf16[256,16]{0,1:T(8,128)(2,1)S(1)}, u32[]{:S(2)}, u32[]{:S(2)}) collective-permute-start(bf16[256,16]{0,1:T(8,128)(2,1)} %param.11), channel_id=1, source_target_pairs={{0,4},{4,0},{8,12},{12,8},{16,20},{20,16},{24,28},{28,24},{1,5},{5... | collective-permute-start | bytes 24584 | tf_op jit(solution)/shard_map/ppermute | solution.py:74
  6.5 3.0 %copy-start.1 = (bf16[2,8,8192]{2,1,0:T(8,128)(2,1)S(1)}, bf16[2,8,8192]{2,1,0:T(8,128)(2,1)}, u32[]{:S(2)}) copy-start(bf16[2,8,8192]{2,1,0:T(8,128)(2,1)} %param.14) | copy-start | bytes 786436
  8.9 1.6 %copy-start = (bf16[2,256,2048]{2,1,0:T(8,128)(2,1)S(1)}, bf16[2,256,2048]{2,1,0:T(8,128)(2,1)}, u32[]{:S(2)}) copy-start(bf16[2,256,2048]{2,1,0:T(8,128)(2,1)} %param.13) | copy-start | bytes 6291460
  9.0 1.6 %copy-start.4 = (s32[2]{0:T(128)S(1)}, s32[2]{0:T(128)}, u32[]{:S(2)}) copy-start(s32[2]{0:T(128)} %lengths_ref) | copy-start | bytes 28
  9.0 3.6 %copy-start.2 = (bf16[2,8,2048]{2,1,0:T(8,128)(2,1)S(1)}, bf16[2,8,2048]{2,1,0:T(8,128)(2,1)}, u32[]{:S(2)}) copy-start(bf16[2,8,2048]{2,1,0:T(8,128)(2,1)} %param.8) | copy-start | bytes 196612
  12.5 11.4 %copy-start.3 = (s32[8]{0:T(128)S(1)}, s32[8]{0:T(128)}, u32[]{:S(2)}) copy-start(s32[8]{0:T(128)} %owner_ref.1) | copy-start | bytes 100
  13.9 6.1 %collective-permute-start.11 = (bf16[2,272,128]{2,1,0:T(8,128)(2,1)S(1)}, bf16[2,272,128]{2,1,0:T(8,128)(2,1)S(1)}, u32[]{:S(2)}, u32[]{:S(2)}) collective-permute-start(bf16[2,272,128]{2,1,0:T(8,128)(2,1)S(1)} %get-tuple-element.49), channel_id=1, source_target_pairs={{0,1},{1,0},{2,3},{3,2},{4,5},{5,4},{6,7},{7,6},{8,9},{9,8},{10,11... | collective-permute-start | bytes 417800 | tf_op jit(solution)/shard_map/ppermute | solution.py:74
  15.6 6.5 %collective-permute-start.5 = (f32[16,512]{1,0:T(8,128)S(1)}, f32[16,512]{1,0:T(8,128)S(1)}, u32[]{:S(2)}, u32[]{:S(2)}) collective-permute-start(f32[16,512]{1,0:T(8,128)S(1)} %get-tuple-element.41), channel_id=1, source_target_pairs={{0,24},{4,28},{8,16},{12,20},{16,8},{20,12},{24,0},{28,4},{1,25},{... | collective-permute-start | bytes 98312 | tf_op jit(solution)/shard_map/ppermute | solution.py:74
  19.2 4.8 %collective-permute-start.6 = (f32[16,512]{1,0:T(8,128)S(1)}, f32[16,512]{1,0:T(8,128)S(1)}, u32[]{:S(2)}, u32[]{:S(2)}) collective-permute-start(f32[16,512]{1,0:T(8,128)S(1)} %get-tuple-element.42), channel_id=1, source_target_pairs={{0,16},{4,20},{8,24},{12,28},{16,0},{20,4},{24,8},{28,12},{1,17},{... | collective-permute-start | bytes 98312 | tf_op jit(solution)/shard_map/ppermute | solution.py:74
  19.2 4.8 %collective-permute-start.7 = (f32[16,512]{1,0:T(8,128)S(1)}, f32[16,512]{1,0:T(8,128)S(1)}, u32[]{:S(2)}, u32[]{:S(2)}) collective-permute-start(f32[16,512]{1,0:T(8,128)S(1)} %get-tuple-element.43), channel_id=1, source_target_pairs={{0,8},{4,12},{8,0},{12,4},{16,24},{20,28},{24,16},{28,20},{1,9},{5... | collective-permute-start | bytes 98312 | tf_op jit(solution)/shard_map/ppermute | solution.py:74
  20.3 10.6 %collective-permute-start.12 = (bf16[1,272,128]{2,1,0:T(8,128)(2,1)S(1)}, bf16[1,272,128]{2,1,0:T(8,128)(2,1)S(1)}, u32[]{:S(2)}, u32[]{:S(2)}) collective-permute-start(bf16[1,272,128]{2,1,0:T(8,128)(2,1)S(1)} %get-tuple-element.51), channel_id=1, source_target_pairs={{0,2},{1,3},{2,0},{3,1},{4,6},{5,7},{6,4},{7,5},{8,10},{9,11},{10,... | collective-permute-start | bytes 208904 | tf_op jit(solution)/shard_map/ppermute | solution.py:74
  24.6 5.3 %collective-permute-start.8 = (f32[16,1024]{1,0:T(8,128)S(1)}, f32[16,1024]{1,0:T(8,128)S(1)}, u32[]{:S(2)}, u32[]{:S(2)}) collective-permute-start(f32[16,1024]{1,0:T(8,128)S(1)} %get-tuple-element.45), channel_id=1, source_target_pairs={{0,3},{1,2},{2,1},{3,0},{4,7},{5,6},{6,5},{7,4},{8,11},{9,10},{10,... | collective-permute-start | bytes 196616 | tf_op jit(solution)/shard_map/ppermute | solution.py:74
  26.1 4.4 %collective-permute-start.9 = (f32[16,1024]{1,0:T(8,128)S(1)}, f32[16,1024]{1,0:T(8,128)S(1)}, u32[]{:S(2)}, u32[]{:S(2)}) collective-permute-start(f32[16,1024]{1,0:T(8,128)S(1)} %get-tuple-element.46), channel_id=1, source_target_pairs={{0,2},{1,3},{2,0},{3,1},{4,6},{5,7},{6,4},{7,5},{8,10},{9,11},{10,... | collective-permute-start | bytes 196616 | tf_op jit(solution)/shard_map/ppermute | solution.py:74
  26.6 4.3 %collective-permute-start.10 = (f32[16,1024]{1,0:T(8,128)S(1)}, f32[16,1024]{1,0:T(8,128)S(1)}, u32[]{:S(2)}, u32[]{:S(2)}) collective-permute-start(f32[16,1024]{1,0:T(8,128)S(1)} %get-tuple-element.47), channel_id=1, source_target_pairs={{0,1},{1,0},{2,3},{3,2},{4,5},{5,4},{6,7},{7,6},{8,9},{9,8},{10,11... | collective-permute-start | bytes 196616 | tf_op jit(solution)/shard_map/ppermute | solution.py:74

commit v10 on v9

--- a/solution.py
+++ b/solution.py
@@ -95,9 +95,9 @@
         out_ref[:, lanes] = values.astype(jnp.bfloat16)
 
 
-def own_weights_kernel(
-    owner_hbm, scales_hbm, codes_hbm, base_hbm, out_ref, base_ref, owner_ref, scales_ref, codes_ref,
-    arrived,
+def load_kernel(
+    owner_hbm, scales_hbm, codes_hbm, query_hbm, cache_hbm, base_hbm,
+    out_ref, base_ref, query_ref, cache_ref, owner_ref, scales_ref, codes_ref, arrived,
 ):
     place = lax.axis_index("group")
     block = codes_ref.shape[0]
@@ -106,44 +106,49 @@
         pltpu.make_async_copy(scales_hbm, scales_ref, arrived.at[1]),
         pltpu.make_async_copy(codes_hbm, codes_ref, arrived.at[2]),
     ]
-    for load in [owner_load] + loads:
+    later = [
+        pltpu.make_async_copy(query_hbm, query_ref, arrived.at[3]),
+        pltpu.make_async_copy(cache_hbm, cache_ref, arrived.at[4]),
+    ]
+    for load in [owner_load] + loads + later:
         load.start()
     owner_load.wait()
-    base_loads = []
     for k in range(2):
         here = pl.ds(pl.multiple_of(owner_ref[place ^ k] * block, block), block)
-        base_loads.append(
-            pltpu.make_async_copy(base_hbm.at[here], base_ref.at[k], arrived.at[3 + k])
-        )
-        base_loads[k].start()
+        load = pltpu.make_async_copy(base_hbm.at[here], base_ref.at[k], arrived.at[5 + k])
+        load.start()
+        later.append(load)
     for load in loads:
         load.wait()
     dequantize(codes_ref, scales_ref, out_ref)
-    for load in base_loads:
+    for load in later:
         load.wait()
 
 
-def own_weights(owner_map, scales, codes, base):
+def load_operands(owner_map, scales, codes, queries, cache, base):
     operands = [
-        pltpu.with_memory_space_constraint(x, pltpu.HBM) for x in (owner_map, scales.T, codes, base)
+        pltpu.with_memory_space_constraint(x, pltpu.HBM)
+        for x in (owner_map, scales.T, codes, queries, cache, base)
     ]
     return pl.pallas_call(
-        own_weights_kernel,
+        load_kernel,
         out_shape=[
             jax.ShapeDtypeStruct(codes.shape, jnp.bfloat16),
             jax.ShapeDtypeStruct((2,) + codes.shape, jnp.bfloat16),
+            jax.ShapeDtypeStruct(queries.shape, jnp.bfloat16),
+            jax.ShapeDtypeStruct(cache.shape, jnp.bfloat16),
         ],
-        in_specs=[HBM] * 4,
-        out_specs=[VMEM] * 2,
+        in_specs=[HBM] * 6,
+        out_specs=[VMEM] * 4,
         scratch_shapes=[
             pltpu.SMEM(owner_map.shape, owner_map.dtype),
             pltpu.VMEM(scales.shape[::-1], scales.dtype),
             pltpu.VMEM(codes.shape, codes.dtype),
-            pltpu.SemaphoreType.DMA((5,)),
+            pltpu.SemaphoreType.DMA((7,)),
         ],
         compiler_params=params(WEIGHTS_KIB),
         cost_estimate=hint(WEIGHTS_HINT),
-        name="own_weights",
+        name="load_operands",
     )(*operands)
 
 
@@ -461,21 +466,28 @@
     mate_codes = swap(delta_codes, "group", 1)
     mate_scales = swap(delta_scales, "group", 1)
 
-    own_delta, base_blocks = own_weights(owner_map, delta_scales, delta_codes, base_weight)
+    own_delta, base_blocks, all_queries, cache = load_operands(
+        owner_map,
+        delta_scales,
+        delta_codes,
+        queries.reshape(tokens, H * HD),
+        kv_cache.reshape(-1, 2 * KVH * HD),
+        base_weight,
+    )
     mate_delta = mate_weights(mate_codes, mate_scales)
     behind, mate_delta = lax.optimization_barrier((lengths, mate_delta))
     own_query, kept, sent = cache_partials(
         behind,
-        queries.reshape(tokens, H * HD),
-        kv_cache.reshape(-1, 2 * KVH * HD),
+        all_queries,
+        cache,
         rows,
         steps,
         heads_own,
         tensor_count,
     )
     own_query, base_blocks = lax.optimization_barrier((own_query, base_blocks))
+    token_rows, sent = lax.optimization_barrier((token_rows, sent))
     projected = project(own_delta, mate_delta, base_blocks, near_first(token_rows))
-    projected, sent = lax.optimization_barrier((projected, sent))
     step = 1
     while step < tensor_count:
         came = swap(sent, "tensor", step)

time: 32.7 us -> 32.1 us (0.982)
  local copies, waits for them, and re-layouts: 1.08 us -> 0.15 us
  waiting for transfers between devices: 4.76 us -> 5.11 us
    unnamed x10 -> x6, local copies, waits for them, and re-layouts: 1.08 us -> 0.15 us
    ppermute x13, waiting for transfers between devices: 4.76 us -> 5.11 us  [swap(): return lax.ppermute(x, axis, [(k, k ^ distance) for k in range(size)])]
    pallas_call x1, Pallas kernels: 2.46 us -> 2.79 us  [load_operands(): pl.pallas_call(load_kernel, out_shape=[jax.ShapeDtypeStruct(codes.shape,...]
  transfers between devices with their start and end apart: 13 -> 13, of which waited for: 5 -> 5; matrix products, arithmetic and copies ran while one was open for 0% -> 0% of each run, Pallas kernels for 18% -> 23%
where the time goes in v10:
time: 32.1 us; the launch traced here: 31.9 us
  starting transfers between devices  17 us (53%)
  Pallas kernels  9.01 us (28%)
  waiting for transfers between devices  5.11 us (16%)
  between operations  0.71 us (2%)
    ppermute x13, starting transfers between devices, swap(): return lax.ppermute(x, axis, [(k, k ^ distance) for k in range(size)])  17 us
    ppermute x13, waiting for transfers between devices, swap(): return lax.ppermute(x, axis, [(k, k ^ distance) for k in range(size)])  5.11 us
    pallas_call x1, Pallas kernels, load_operands(): pl.pallas_call(load_kernel, out_shape=[jax.ShapeDtypeStruct(codes.shape,...  2.79 us
    pallas_call x1, Pallas kernels, cache_partials(): pl.pallas_call(functools.partial(cache_kernel, rows, steps, own, min(own,...  1.96 us
    pallas_call x1, Pallas kernels, finish(): pl.pallas_call(functools.partial(finish_kernel, rows, steps, own, min(own...  1.61 us
    pallas_call x1, Pallas kernels, project(): pl.pallas_call(functools.partial(project_kernel, pairs), out_shape=[jax.S...  1.29 us
  transfers between devices with their start and end apart: 13, of which 5 were waited for; matrix products, arithmetic and copies ran while one was open for 0% of the time, Pallas kernels for 23%

profile of v10, /device:TPU:0, one launch (start us, length us, event | category | flops | bytes accessed | tf_op | source)
XLA Modules:
  0.0 31.9 jit_solution(1806886083703245085)
XLA Ops:
  0.6 0.5 %collective-permute-start = (bf16[256,2048]{1,0:T(8,128)(2,1)}, bf16[256,2048]{1,0:T(8,128)(2,1)S(1)}, u32[]{:S(2)}, u32[]{:S(2)}) collective-permute-start(bf16[256,2048]{1,0:T(8,128)(2,1)} %codes_hbm.1), channel_id=1, source_target_pairs={{0,4},{4,0},{8,12},{12,8},{16,20},{20,16},{24,28},{28,24},{1,5},{5... | collective-permute-start | bytes 3145736 | tf_op jit(solution)/shard_map/ppermute | solution.py:74
  1.1 4.7 %collective-permute-start.2 = (bf16[16,2048]{1,0:T(8,128)(2,1)}, bf16[16,2048]{1,0:T(8,128)(2,1)S(1)}, u32[]{:S(2)}, u32[]{:S(2)}) collective-permute-start(bf16[16,2048]{1,0:T(8,128)(2,1)} %bitcast.7), channel_id=1, source_target_pairs={{0,24},{4,28},{8,16},{12,20},{16,8},{20,12},{24,0},{28,4},{1,25},{... | collective-permute-start | bytes 196616 | tf_op jit(solution)/shard_map/ppermute | solution.py:74
  5.8 0.0 collective-permute-start.3
  5.8 0.6 %collective-permute-start.4 = (bf16[16,2048]{1,0:T(8,128)(2,1)}, bf16[16,2048]{1,0:T(8,128)(2,1)S(1)}, u32[]{:S(2)}, u32[]{:S(2)}) collective-permute-start(bf16[16,2048]{1,0:T(8,128)(2,1)} %bitcast.9), channel_id=1, source_target_pairs={{0,8},{4,12},{8,0},{12,4},{16,24},{20,28},{24,16},{28,20},{1,9},{5... | collective-permute-start | bytes 196616 | tf_op jit(solution)/shard_map/ppermute | solution.py:74
  6.5 0.0 collective-permute-start.1
  6.5 2.8 %load_operands.1 = (bf16[256,2048]{1,0:T(8,128)(2,1)S(1)}, bf16[2,256,2048]{2,1,0:T(8,128)(2,1)S(1)}, bf16[16,8192]{1,0:T(8,128)(2,1)S(1)}, bf16[512,2048]{1,0:T(8,128)(2,1)S(1)}) custom-call(s32[8]{0:T(128)} %owner_ref.1, bf16[16,256]{1,0:T(8,128)(2,1)} %bitcast.14, bf16[256,2048]{1,0:T(8,128)(2,1)} %codes_hbm.1, bf16[16,8192]{1,0:T(8,128)(2,1)} %bitcast.13, ...), custom_call_target="tpu_custom_call" | custom-call | bytes 6000000 | tf_op jit(solution)/shard_map/load_operands/pallas_call | solution.py:133
  9.3 0.0 copy-start.2
  9.3 0.0 collective-permute-done.1
  9.3 0.0 collective-permute-done.codes_ref
  9.3 0.0 copy-start
  9.3 0.5 %mate_weights.1.mate_ref = bf16[256,2048]{1,0:T(8,128)(2,1)S(1)} custom-call(bf16[256,2048]{1,0:T(8,128)(2,1)S(1)} %collective-permute-done.codes_ref, bf16[16,256]{1,0:T(8,128)(2,1)S(1)} %bitcast.11), custom_call_target="tpu_custom_call" | custom-call | bytes 1000 | tf_op jit(solution)/shard_map/mate_weights/pallas_call | solution.py:156
  9.8 0.1 copy-done.2
  9.9 2.0 %cache_partials.1 = (bf16[256,128]{1,0:T(8,128)(2,1)S(1)}, f32[2,264,128]{2,1,0:T(8,128)S(1)}, bf16[2,272,128]{2,1,0:T(8,128)(2,1)S(1)}) custom-call(s32[2]{0:T(128)S(1)} %copy-done.2, bf16[16,8192]{1,0:T(8,128)(2,1)S(1)} %get-tuple-element.31.query_ref, bf16[512,2048]{1,0:T(8,128)(2,1)S(1)} %get-tuple-element.32.cache_ref), custom_call_target="tpu_custom_call" | custom-call | bytes 120000000 | tf_op jit(solution)/shard_map/cache_partials/pallas_call | solution.py:229
  11.9 0.0 collective-permute-done.2.refs_3_
  11.9 0.2 collective-permute-done.3.refs_2_
  12.1 0.0 collective-permute-done.4.refs_1_
  12.1 1.5 %collective-permute-start.11 = (bf16[2,272,128]{2,1,0:T(8,128)(2,1)S(1)}, bf16[2,272,128]{2,1,0:T(8,128)(2,1)S(1)}, u32[]{:S(2)}, u32[]{:S(2)}) collective-permute-start(bf16[2,272,128]{2,1,0:T(8,128)(2,1)S(1)} %get-tuple-element.53), channel_id=1, source_target_pairs={{0,1},{1,0},{2,3},{3,2},{4,5},{5,4},{6,7},{7,6},{8,9},{9,8},{10,11... | collective-permute-start | bytes 417800 | tf_op jit(solution)/shard_map/ppermute | solution.py:74
  13.6 0.0 copy-done
  13.6 0.0 copy-start.1
  13.6 1.3 %project.1 = (f32[16,512]{1,0:T(8,128)S(1)}, f32[16,512]{1,0:T(8,128)S(1)}, f32[16,512]{1,0:T(8,128)S(1)}, f32[16,512]{1,0:T(8,128)S(1)}) custom-call(bf16[256,2048]{1,0:T(8,128)(2,1)S(1)} %get-tuple-element.36.own_ref, bf16[256,2048]{1,0:T(8,128)(2,1)S(1)} %mate_weights.1.mate_ref, bf16[2,256,2048]{2,1,0:T(8,128)(2,1)S(1)} %get-tuple-element.38.base_ref, ...), custom_call_target="tpu_custom_call" | custom-call | bytes 60000000 | tf_op jit(solution)/shard_map/project/pallas_call | solution.py:295
  14.9 3.7 %collective-permute-start.5 = (f32[16,512]{1,0:T(8,128)S(1)}, f32[16,512]{1,0:T(8,128)S(1)}, u32[]{:S(2)}, u32[]{:S(2)}) collective-permute-start(f32[16,512]{1,0:T(8,128)S(1)} %get-tuple-element.45), channel_id=1, source_target_pairs={{0,24},{4,28},{8,16},{12,20},{16,8},{20,12},{24,0},{28,4},{1,25},{... | collective-permute-start | bytes 98312 | tf_op jit(solution)/shard_map/ppermute | solution.py:74
  18.6 0.0 collective-permute-start.6
  18.6 0.8 %collective-permute-start.7 = (f32[16,512]{1,0:T(8,128)S(1)}, f32[16,512]{1,0:T(8,128)S(1)}, u32[]{:S(2)}, u32[]{:S(2)}) collective-permute-start(f32[16,512]{1,0:T(8,128)S(1)} %get-tuple-element.47), channel_id=1, source_target_pairs={{0,8},{4,12},{8,0},{12,4},{16,24},{20,28},{24,16},{28,20},{1,9},{5... | collective-permute-start | bytes 98312 | tf_op jit(solution)/shard_map/ppermute | solution.py:74
  19.4 0.0 collective-permute-done.11.came_ref
  19.4 0.3 merge_partials.1
  19.7 1.6 %collective-permute-start.12 = (bf16[1,272,128]{2,1,0:T(8,128)(2,1)S(1)}, bf16[1,272,128]{2,1,0:T(8,128)(2,1)S(1)}, u32[]{:S(2)}, u32[]{:S(2)}) collective-permute-start(bf16[1,272,128]{2,1,0:T(8,128)(2,1)S(1)} %get-tuple-element.55), channel_id=1, source_target_pairs={{0,2},{1,3},{2,0},{3,1},{4,6},{5,7},{6,4},{7,5},{8,10},{9,11},{10,... | collective-permute-start | bytes 208904 | tf_op jit(solution)/shard_map/ppermute | solution.py:74
  21.3 0.0 collective-permute-done.5.refs_1_
  21.3 2.1 %collective-permute-done.6.refs_2_ = f32[16,512]{1,0:T(8,128)S(1)} collective-permute-done((f32[16,512]{1,0:T(8,128)S(1)}, f32[16,512]{1,0:T(8,128)S(1)}, u32[]{:S(2)}, u32[]{:S(2)}) %collective-permute-start.6) | collective-permute-done | bytes 32800 | tf_op jit(solution)/shard_map/ppermute | solution.py:74
  23.4 0.0 collective-permute-done.7.refs_3_
  23.4 0.0 copy-done.1
  23.4 0.6 %pack_pieces.1 = (f32[16,1024]{1,0:T(8,128)S(1)}, f32[16,1024]{1,0:T(8,128)S(1)}, f32[16,1024]{1,0:T(8,128)S(1)}, f32[16,1024]{1,0:T(8,128)S(1)}) custom-call(s32[8]{0:T(128)S(1)} %copy-done.1, f32[16,512]{1,0:T(8,128)S(1)} %get-tuple-element.44.refs_0_, f32[16,512]{1,0:T(8,128)S(1)} %collective-permute-done.5.refs_1_, ...), custom_call_target="tpu_custom_call" | custom-call | bytes 60000000 | tf_op jit(solution)/shard_map/pack_pieces/pallas_call | solution.py:335
  24.0 1.5 %collective-permute-start.8 = (f32[16,1024]{1,0:T(8,128)S(1)}, f32[16,1024]{1,0:T(8,128)S(1)}, u32[]{:S(2)}, u32[]{:S(2)}) collective-permute-start(f32[16,1024]{1,0:T(8,128)S(1)} %get-tuple-element.49), channel_id=1, source_target_pairs={{0,3},{1,2},{2,1},{3,0},{4,7},{5,6},{6,5},{7,4},{8,11},{9,10},{10,... | collective-permute-start | bytes 196616 | tf_op jit(solution)/shard_map/ppermute | solution.py:74
  25.6 0.5 %collective-permute-start.9 = (f32[16,1024]{1,0:T(8,128)S(1)}, f32[16,1024]{1,0:T(8,128)S(1)}, u32[]{:S(2)}, u32[]{:S(2)}) collective-permute-start(f32[16,1024]{1,0:T(8,128)S(1)} %get-tuple-element.50), channel_id=1, source_target_pairs={{0,2},{1,3},{2,0},{3,1},{4,6},{5,7},{6,4},{7,5},{8,10},{9,11},{10,... | collective-permute-start | bytes 196616 | tf_op jit(solution)/shard_map/ppermute | solution.py:74
  26.1 1.5 %collective-permute-start.10 = (f32[16,1024]{1,0:T(8,128)S(1)}, f32[16,1024]{1,0:T(8,128)S(1)}, u32[]{:S(2)}, u32[]{:S(2)}) collective-permute-start(f32[16,1024]{1,0:T(8,128)S(1)} %get-tuple-element.51), channel_id=1, source_target_pairs={{0,1},{1,0},{2,3},{3,2},{4,5},{5,4},{6,7},{7,6},{8,9},{9,8},{10,11... | collective-permute-start | bytes 196616 | tf_op jit(solution)/shard_map/ppermute | solution.py:74
  27.6 1.7 %collective-permute-done.8.refs_1_ = f32[16,1024]{1,0:T(8,128)S(1)} collective-permute-done((f32[16,1024]{1,0:T(8,128)S(1)}, f32[16,1024]{1,0:T(8,128)S(1)}, u32[]{:S(2)}, u32[]{:S(2)}) %collective-permute-start.8) | collective-permute-done | bytes 65568 | tf_op jit(solution)/shard_map/ppermute | solution.py:74
  29.3 0.7 %collective-permute-done.9.refs_2_ = f32[16,1024]{1,0:T(8,128)S(1)} collective-permute-done((f32[16,1024]{1,0:T(8,128)S(1)}, f32[16,1024]{1,0:T(8,128)S(1)}, u32[]{:S(2)}, u32[]{:S(2)}) %collective-permute-start.9) | collective-permute-done | bytes 65568 | tf_op jit(solution)/shard_map/ppermute | solution.py:74
  30.0 0.4 %collective-permute-done.10.refs_3_ = f32[16,1024]{1,0:T(8,128)S(1)} collective-permute-done((f32[16,1024]{1,0:T(8,128)S(1)}, f32[16,1024]{1,0:T(8,128)S(1)}, u32[]{:S(2)}, u32[]{:S(2)}) %collective-permute-start.10) | collective-permute-done | bytes 65568 | tf_op jit(solution)/shard_map/ppermute | solution.py:74
  30.3 0.0 collective-permute-done.12.refs_5_
  30.3 1.6 %finish.1 = (bf16[16,512]{1,0:T(8,128)(2,1)}, bf16[16,2048]{1,0:T(8,128)(2,1)}) custom-call(bf16[256,128]{1,0:T(8,128)(2,1)S(1)} %get-tuple-element.35.query_ref, f32[16,1024]{1,0:T(8,128)S(1)} %get-tuple-element.48.refs_0_, f32[16,1024]{1,0:T(8,128)S(1)} %collective-permute-done.8.refs_1_, f32[16,1024]{1,0:T(8,128)S(1)} %collective-permute-done.9.refs_2_, ...), custom_call_target="tpu_custom_call" | custom-call | tf_op jit(solution)/shard_map/finish/pallas_call | solution.py:430
Async XLA Ops:
  0.6 8.7 %collective-permute-start = (bf16[256,2048]{1,0:T(8,128)(2,1)}, bf16[256,2048]{1,0:T(8,128)(2,1)S(1)}, u32[]{:S(2)}, u32[]{:S(2)}) collective-permute-start(bf16[256,2048]{1,0:T(8,128)(2,1)} %codes_hbm.1), channel_id=1, source_target_pairs={{0,4},{4,0},{8,12},{12,8},{16,20},{20,16},{24,28},{28,24},{1,5},{5... | collective-permute-start | bytes 3145736 | tf_op jit(solution)/shard_map/ppermute | solution.py:74
  1.1 10.8 %collective-permute-start.2 = (bf16[16,2048]{1,0:T(8,128)(2,1)}, bf16[16,2048]{1,0:T(8,128)(2,1)S(1)}, u32[]{:S(2)}, u32[]{:S(2)}) collective-permute-start(bf16[16,2048]{1,0:T(8,128)(2,1)} %bitcast.7), channel_id=1, source_target_pairs={{0,24},{4,28},{8,16},{12,20},{16,8},{20,12},{24,0},{28,4},{1,25},{... | collective-permute-start | bytes 196616 | tf_op jit(solution)/shard_map/ppermute | solution.py:74
  5.8 6.3 %collective-permute-start.3 = (bf16[16,2048]{1,0:T(8,128)(2,1)}, bf16[16,2048]{1,0:T(8,128)(2,1)S(1)}, u32[]{:S(2)}, u32[]{:S(2)}) collective-permute-start(bf16[16,2048]{1,0:T(8,128)(2,1)} %bitcast.8), channel_id=1, source_target_pairs={{0,16},{4,20},{8,24},{12,28},{16,0},{20,4},{24,8},{28,12},{1,17},{... | collective-permute-start | bytes 196616 | tf_op jit(solution)/shard_map/ppermute | solution.py:74
  5.8 6.3 %collective-permute-start.4 = (bf16[16,2048]{1,0:T(8,128)(2,1)}, bf16[16,2048]{1,0:T(8,128)(2,1)S(1)}, u32[]{:S(2)}, u32[]{:S(2)}) collective-permute-start(bf16[16,2048]{1,0:T(8,128)(2,1)} %bitcast.9), channel_id=1, source_target_pairs={{0,8},{4,12},{8,0},{12,4},{16,24},{20,28},{24,16},{28,20},{1,9},{5... | collective-permute-start | bytes 196616 | tf_op jit(solution)/shard_map/ppermute | solution.py:74
  6.5 2.8 %collective-permute-start.1 = (bf16[256,16]{0,1:T(8,128)(2,1)}, bf16[256,16]{0,1:T(8,128)(2,1)S(1)}, u32[]{:S(2)}, u32[]{:S(2)}) collective-permute-start(bf16[256,16]{0,1:T(8,128)(2,1)} %param.11), channel_id=1, source_target_pairs={{0,4},{4,0},{8,12},{12,8},{16,20},{20,16},{24,28},{28,24},{1,5},{5... | collective-permute-start | bytes 24584 | tf_op jit(solution)/shard_map/ppermute | solution.py:74
  9.3 0.7 %copy-start.2 = (s32[2]{0:T(128)S(1)}, s32[2]{0:T(128)}, u32[]{:S(2)}) copy-start(s32[2]{0:T(128)} %lengths_ref) | copy-start | bytes 28
  9.3 4.3 %copy-start = (bf16[2,8,2048]{2,1,0:T(8,128)(2,1)S(1)}, bf16[2,8,2048]{2,1,0:T(8,128)(2,1)}, u32[]{:S(2)}) copy-start(bf16[2,8,2048]{2,1,0:T(8,128)(2,1)} %param.8) | copy-start | bytes 196612
  12.1 7.3 %collective-permute-start.11 = (bf16[2,272,128]{2,1,0:T(8,128)(2,1)S(1)}, bf16[2,272,128]{2,1,0:T(8,128)(2,1)S(1)}, u32[]{:S(2)}, u32[]{:S(2)}) collective-permute-start(bf16[2,272,128]{2,1,0:T(8,128)(2,1)S(1)} %get-tuple-element.53), channel_id=1, source_target_pairs={{0,1},{1,0},{2,3},{3,2},{4,5},{5,4},{6,7},{7,6},{8,9},{9,8},{10,11... | collective-permute-start | bytes 417800 | tf_op jit(solution)/shard_map/ppermute | solution.py:74
  13.6 9.8 %copy-start.1 = (s32[8]{0:T(128)S(1)}, s32[8]{0:T(128)}, u32[]{:S(2)}) copy-start(s32[8]{0:T(128)} %owner_ref.1) | copy-start | bytes 100
  14.9 6.4 %collective-permute-start.5 = (f32[16,512]{1,0:T(8,128)S(1)}, f32[16,512]{1,0:T(8,128)S(1)}, u32[]{:S(2)}, u32[]{:S(2)}) collective-permute-start(f32[16,512]{1,0:T(8,128)S(1)} %get-tuple-element.45), channel_id=1, source_target_pairs={{0,24},{4,28},{8,16},{12,20},{16,8},{20,12},{24,0},{28,4},{1,25},{... | collective-permute-start | bytes 98312 | tf_op jit(solution)/shard_map/ppermute | solution.py:74
  18.6 4.8 %collective-permute-start.6 = (f32[16,512]{1,0:T(8,128)S(1)}, f32[16,512]{1,0:T(8,128)S(1)}, u32[]{:S(2)}, u32[]{:S(2)}) collective-permute-start(f32[16,512]{1,0:T(8,128)S(1)} %get-tuple-element.46), channel_id=1, source_target_pairs={{0,16},{4,20},{8,24},{12,28},{16,0},{20,4},{24,8},{28,12},{1,17},{... | collective-permute-start | bytes 98312 | tf_op jit(solution)/shard_map/ppermute | solution.py:74
  18.6 4.8 %collective-permute-start.7 = (f32[16,512]{1,0:T(8,128)S(1)}, f32[16,512]{1,0:T(8,128)S(1)}, u32[]{:S(2)}, u32[]{:S(2)}) collective-permute-start(f32[16,512]{1,0:T(8,128)S(1)} %get-tuple-element.47), channel_id=1, source_target_pairs={{0,8},{4,12},{8,0},{12,4},{16,24},{20,28},{24,16},{28,20},{1,9},{5... | collective-permute-start | bytes 98312 | tf_op jit(solution)/shard_map/ppermute | solution.py:74
  19.7 10.6 %collective-permute-start.12 = (bf16[1,272,128]{2,1,0:T(8,128)(2,1)S(1)}, bf16[1,272,128]{2,1,0:T(8,128)(2,1)S(1)}, u32[]{:S(2)}, u32[]{:S(2)}) collective-permute-start(bf16[1,272,128]{2,1,0:T(8,128)(2,1)S(1)} %get-tuple-element.55), channel_id=1, source_target_pairs={{0,2},{1,3},{2,0},{3,1},{4,6},{5,7},{6,4},{7,5},{8,10},{9,11},{10,... | collective-permute-start | bytes 208904 | tf_op jit(solution)/shard_map/ppermute | solution.py:74
  24.0 5.3 %collective-permute-start.8 = (f32[16,1024]{1,0:T(8,128)S(1)}, f32[16,1024]{1,0:T(8,128)S(1)}, u32[]{:S(2)}, u32[]{:S(2)}) collective-permute-start(f32[16,1024]{1,0:T(8,128)S(1)} %get-tuple-element.49), channel_id=1, source_target_pairs={{0,3},{1,2},{2,1},{3,0},{4,7},{5,6},{6,5},{7,4},{8,11},{9,10},{10,... | collective-permute-start | bytes 196616 | tf_op jit(solution)/shard_map/ppermute | solution.py:74
  25.6 4.4 %collective-permute-start.9 = (f32[16,1024]{1,0:T(8,128)S(1)}, f32[16,1024]{1,0:T(8,128)S(1)}, u32[]{:S(2)}, u32[]{:S(2)}) collective-permute-start(f32[16,1024]{1,0:T(8,128)S(1)} %get-tuple-element.50), channel_id=1, source_target_pairs={{0,2},{1,3},{2,0},{3,1},{4,6},{5,7},{6,4},{7,5},{8,10},{9,11},{10,... | collective-permute-start | bytes 196616 | tf_op jit(solution)/shard_map/ppermute | solution.py:74
  26.1 4.3 %collective-permute-start.10 = (f32[16,1024]{1,0:T(8,128)S(1)}, f32[16,1024]{1,0:T(8,128)S(1)}, u32[]{:S(2)}, u32[]{:S(2)}) collective-permute-start(f32[16,1024]{1,0:T(8,128)S(1)} %get-tuple-element.51), channel_id=1, source_target_pairs={{0,1},{1,0},{2,3},{3,2},{4,5},{5,4},{6,7},{7,6},{8,9},{9,8},{10,11... | collective-permute-start | bytes 196616 | tf_op jit(solution)/shard_map/ppermute | solution.py:74

commit v11 on v9

--- a/solution.py
+++ b/solution.py
@@ -17,7 +17,6 @@
 NEGATIVE = -1e30
 SCORE_SCALE = HD ** (-0.5)
 CACHE_HINT = 120_000_000
-WEIGHTS_HINT = 6_000_000
 PROJECT_HINT = 60_000_000
 PACK_HINT = 60_000_000
 CACHE_KIB = 24 << 10
@@ -95,58 +94,6 @@
         out_ref[:, lanes] = values.astype(jnp.bfloat16)
 
 
-def own_weights_kernel(
-    owner_hbm, scales_hbm, codes_hbm, base_hbm, out_ref, base_ref, owner_ref, scales_ref, codes_ref,
-    arrived,
-):
-    place = lax.axis_index("group")
-    block = codes_ref.shape[0]
-    owner_load = pltpu.make_async_copy(owner_hbm, owner_ref, arrived.at[0])
-    loads = [
-        pltpu.make_async_copy(scales_hbm, scales_ref, arrived.at[1]),
-        pltpu.make_async_copy(codes_hbm, codes_ref, arrived.at[2]),
-    ]
-    for load in [owner_load] + loads:
-        load.start()
-    owner_load.wait()
-    base_loads = []
-    for k in range(2):
-        here = pl.ds(pl.multiple_of(owner_ref[place ^ k] * block, block), block)
-        base_loads.append(
-            pltpu.make_async_copy(base_hbm.at[here], base_ref.at[k], arrived.at[3 + k])
-        )
-        base_loads[k].start()
-    for load in loads:
-        load.wait()
-    dequantize(codes_ref, scales_ref, out_ref)
-    for load in base_loads:
-        load.wait()
-
-
-def own_weights(owner_map, scales, codes, base):
-    operands = [
-        pltpu.with_memory_space_constraint(x, pltpu.HBM) for x in (owner_map, scales.T, codes, base)
-    ]
-    return pl.pallas_call(
-        own_weights_kernel,
-        out_shape=[
-            jax.ShapeDtypeStruct(codes.shape, jnp.bfloat16),
-            jax.ShapeDtypeStruct((2,) + codes.shape, jnp.bfloat16),
-        ],
-        in_specs=[HBM] * 4,
-        out_specs=[VMEM] * 2,
-        scratch_shapes=[
-            pltpu.SMEM(owner_map.shape, owner_map.dtype),
-            pltpu.VMEM(scales.shape[::-1], scales.dtype),
-            pltpu.VMEM(codes.shape, codes.dtype),
-            pltpu.SemaphoreType.DMA((5,)),
-        ],
-        compiler_params=params(WEIGHTS_KIB),
-        cost_estimate=hint(WEIGHTS_HINT),
-        name="own_weights",
-    )(*operands)
-
-
 def mate_weights(codes, scales):
     return pl.pallas_call(
         dequantize,
@@ -159,11 +106,43 @@
     )(codes, scales.T)
 
 
-def cache_kernel(
-    rows, steps, own, chunk, lengths_ref, query_ref, cache_ref, own_query_ref, kept_ref, sent_ref
+def prepare_kernel(
+    rows, steps, own, chunk,
+    owner_hbm, lengths_hbm, scales_hbm, codes_hbm, query_hbm, cache_hbm, base_hbm,
+    delta_ref, base_ref, own_query_ref, kept_ref, sent_ref,
+    owner_ref, lengths_ref, scales_ref, codes_ref, query_ref, cache_ref, arrived,
 ):
     place = lax.axis_index("tensor")
+    block = codes_ref.shape[0]
     cache_len = cache_ref.shape[0] // rows
+    owner_load = pltpu.make_async_copy(owner_hbm, owner_ref, arrived.at[0])
+    first_loads = [
+        pltpu.make_async_copy(lengths_hbm, lengths_ref, arrived.at[1]),
+        pltpu.make_async_copy(scales_hbm, scales_ref, arrived.at[2]),
+        pltpu.make_async_copy(codes_hbm, codes_ref, arrived.at[3]),
+        pltpu.make_async_copy(query_hbm, query_ref, arrived.at[4]),
+    ]
+    cache_loads = []
+    for r in range(rows):
+        here = pl.ds(r * cache_len, cache_len)
+        cache_loads.append(
+            pltpu.make_async_copy(cache_hbm.at[here], cache_ref.at[here], arrived.at[5 + r])
+        )
+    for load in [owner_load] + first_loads + cache_loads:
+        load.start()
+    owner_load.wait()
+    base_loads = []
+    for k in range(2):
+        start = owner_ref[lax.axis_index("group") ^ k] * block
+        here = pl.ds(pl.multiple_of(start, block), block)
+        base_loads.append(
+            pltpu.make_async_copy(base_hbm.at[here], base_ref.at[k], arrived.at[5 + rows + k])
+        )
+        base_loads[k].start()
+    for load in first_loads:
+        load.wait()
+    dequantize(codes_ref, scales_ref, delta_ref)
+
     chunks = own // chunk
     height = chunk * steps
     width = chunks * HD
@@ -188,10 +167,13 @@
         keys = cache_ref[pl.ds(r * cache_len, cache_len), pl.ds(kv_lane(d), width)]
         return dot(keys, spread, NT)
 
-    units = [(r, d) for d in range(2 * kept_ref.shape[0]) for r in range(rows)]
+    units = [(r, d) for r in range(rows) for d in range(2 * kept_ref.shape[0])]
+    stats = [[] for _ in range(2 * kept_ref.shape[0])]
     ahead = []
     for n in range(len(units) + 1):
         if n < len(units):
+            if units[n][1] == 0:
+                cache_loads[units[n][0]].wait()
             ahead.append(score(*units[n]))
         if n == 0:
             continue
@@ -210,33 +192,50 @@
             here = slice(j * height, (j + 1) * height)
             mine = sums[here, j * HD : (j + 1) * HD].astype(ref.dtype)
             ref[index, at + j * height : at + (j + 1) * height] = mine
-        stats = (stats if r > 0 else []) + [peak, total]
+        stats[d] += [peak, total]
         if r == rows - 1:
-            put_stats(ref, index, stats)
+            put_stats(ref, index, stats[d])
+    for load in base_loads:
+        load.wait()
 
 
 def part_shape(count, height, dtype):
     return jax.ShapeDtypeStruct((count, height + stats_rows(dtype), LANES), dtype)
 
 
-def cache_partials(lengths, queries, cache, rows, steps, own, ways):
+def prepare(owner_map, lengths, scales, codes, queries, cache, base, rows, steps, own, ways):
     height = rows * own * steps
+    operands = [
+        pltpu.with_memory_space_constraint(x, pltpu.HBM)
+        for x in (owner_map, lengths, scales.T, codes, queries, cache, base)
+    ]
     return pl.pallas_call(
-        functools.partial(cache_kernel, rows, steps, own, min(own, H // KVH)),
+        functools.partial(prepare_kernel, rows, steps, own, min(own, H // KVH)),
         out_shape=[
+            jax.ShapeDtypeStruct(codes.shape, jnp.bfloat16),
+            jax.ShapeDtypeStruct((2,) + codes.shape, jnp.bfloat16),
             jax.ShapeDtypeStruct((height, HD), jnp.bfloat16),
             part_shape(ways // 2, height, jnp.float32),
             part_shape(ways // 2, height, jnp.bfloat16),
         ],
-        in_specs=[SMEM, VMEM, VMEM],
-        out_specs=[VMEM] * 3,
+        in_specs=[HBM] * len(operands),
+        out_specs=[VMEM] * 5,
+        scratch_shapes=[
+            pltpu.SMEM(owner_map.shape, owner_map.dtype),
+            pltpu.SMEM(lengths.shape, lengths.dtype),
+            pltpu.VMEM(scales.shape[::-1], scales.dtype),
+            pltpu.VMEM(codes.shape, codes.dtype),
+            pltpu.VMEM(queries.shape, queries.dtype),
+            pltpu.VMEM(cache.shape, cache.dtype),
+            pltpu.SemaphoreType.DMA((7 + rows,)),
+        ],
         compiler_params=params(CACHE_KIB),
         cost_estimate=hint(CACHE_HINT),
-        name="cache_partials",
-    )(lengths, queries, cache)
-
-
-def merge_kernel(rows, span, kept_ref, came_ref, next_ref, sent_ref):
+        name="prepare",
+    )(*operands)
+
+
+def merge_kernel(rows, span, kept_ref, came_ref, next_ref, sent_ref=None):
     for n in range(kept_ref.shape[0]):
         ref, index = (sent_ref if n % 2 else next_ref), n // 2
         stats, factors = [], []
@@ -258,14 +257,14 @@
 def merge(kept, came, rows):
     count = kept.shape[0]
     height = kept.shape[1] - stats_rows(kept.dtype)
+    shapes = [part_shape((count + 1) // 2, height, jnp.float32)]
+    if count > 1:
+        shapes.append(part_shape(count // 2, height, jnp.bfloat16))
     return pl.pallas_call(
         functools.partial(merge_kernel, rows, height // rows),
-        out_shape=[
-            part_shape(count // 2, height, jnp.float32),
-            part_shape(count // 2, height, jnp.bfloat16),
-        ],
+        out_shape=shapes,
         in_specs=[VMEM] * 2,
-        out_specs=[VMEM] * 2,
+        out_specs=[VMEM] * len(shapes),
         compiler_params=params(8192),
         cost_estimate=hint(4 * kept.size),
         name="merge_partials",
@@ -358,68 +357,65 @@
 
 
 def finish_kernel(rows, steps, own, chunk, near_width, ways, query_ref, *refs):
-    pieces, parts = refs[:ways], refs[ways : ways + 2]
-    new_ref, attended_ref = refs[ways + 2 :]
+    pieces, part = refs[:ways], refs[ways]
+    new_ref, attended_ref = refs[ways + 1 :]
     chunks = own // chunk
     height = chunk * steps
+    span = chunks * height
     summed = pieces[0][...]
     for piece in pieces[1:]:
         summed = summed + piece[...]
     stored = summed.astype(jnp.bfloat16)
     new_ref[...] = stored[:, 2 * near_width :]
     near = stored[:, : 2 * near_width].astype(jnp.float32)
-    key_step = lax.broadcasted_iota(jnp.int32, (steps, height), 0)
-    query_step = lax.broadcasted_iota(jnp.int32, (steps, height), 1) % steps
+    key_step = lax.broadcasted_iota(jnp.int32, (steps, span), 0)
+    query_step = lax.broadcasted_iota(jnp.int32, (steps, span), 1) % steps
     causal = key_step <= query_step
-    stats = [get_stats(part, 0, rows) for part in parts]
+    scores = []
+    for r in range(rows):
+        spread = []
+        for j in range(chunks):
+            line = [jnp.zeros((height, HD), jnp.bfloat16)] * chunks
+            line[j] = query_ref[r * span + j * height : r * span + (j + 1) * height]
+            spread.append(jnp.concatenate(line, axis=1))
+        keys = near[r * steps : (r + 1) * steps, :near_width].astype(jnp.bfloat16)
+        scores.append(dot(keys, jnp.concatenate(spread, axis=0), NT) * SCORE_SCALE)
     factors, near_sums = [], []
-    for r in range(rows):
-        peaks, totals = [], []
-        for j in range(chunks):
-            at = (r * chunks + j) * height
-            query = query_ref[at : at + height]
-            step_rows = slice(r * steps, (r + 1) * steps)
-            keys = near[step_rows, j * HD : (j + 1) * HD].astype(jnp.bfloat16)
-            values = near[step_rows, near_width + j * HD : near_width + (j + 1) * HD]
-            scores = jnp.where(causal, dot(keys, query, NT) * SCORE_SCALE, NEGATIVE)
-            peak = jnp.max(scores, axis=0, keepdims=True)
-            weights = jnp.where(causal, jnp.exp(scores - peak), 0.0)
-            peaks.append(peak)
-            totals.append(jnp.sum(weights, axis=0, keepdims=True))
-            near_sums.append(dot(weights.astype(jnp.bfloat16), values.astype(jnp.bfloat16), TN))
-        lanes = chunks * height
-        pad = [jnp.zeros((1, LANES - lanes), jnp.float32)] if lanes < LANES else []
-        peaks = [one[r][0] for one in stats] + [jnp.concatenate(peaks + pad, axis=1)]
-        totals = [one[r][1] for one in stats] + [jnp.concatenate(totals + pad, axis=1)]
-        top = functools.reduce(jnp.maximum, peaks)
-        scales = [jnp.exp(peak - top) for peak in peaks]
-        total = sum(scale * one for scale, one in zip(scales, totals))
-        if pad:
-            total = jnp.where(total == 0.0, 1.0, total)
-        factors += [scale / total for scale in scales]
-    lines = -(-len(factors) // SUBLANES) * SUBLANES
-    if lines > len(factors):
-        factors.append(jnp.zeros((lines - len(factors), LANES), jnp.float32))
-    columns = jnp.concatenate(factors, axis=0).T
+    for r, (cache_peak, cache_total) in enumerate(get_stats(part, 0, rows)):
+        masked = jnp.where(causal, scores[r], NEGATIVE)
+        peak = jnp.max(masked, axis=0, keepdims=True)
+        weights = jnp.where(causal, jnp.exp(masked - peak), 0.0)
+        total = jnp.sum(weights, axis=0, keepdims=True)
+        values = near[r * steps : (r + 1) * steps, near_width:].astype(jnp.bfloat16)
+        near_sums.append(dot(weights.astype(jnp.bfloat16), values, TN))
+        cache_peak, cache_total = cache_peak[:, :span], cache_total[:, :span]
+        top = jnp.maximum(peak, cache_peak)
+        scales = [jnp.exp(cache_peak - top), jnp.exp(peak - top)]
+        whole = cache_total * scales[0] + total * scales[1]
+        factors += [scale / whole for scale in scales]
+    factors.append(jnp.zeros((SUBLANES - len(factors), span), jnp.float32))
+    columns = jnp.concatenate(factors, axis=0)
+    if span < LANES:
+        pad = jnp.zeros((SUBLANES, LANES - span), jnp.float32)
+        columns = jnp.concatenate([columns, pad], axis=1)
+    columns = columns.T
     for j in range(chunks):
+        here = slice(j * height, (j + 1) * height)
         merged = []
         for r in range(rows):
-            at = (r * chunks + j) * height
-            here = slice(j * height, (j + 1) * height)
-            first = r * (len(parts) + 1)
-            last = first + len(parts)
-            out = near_sums[r * chunks + j] * columns[here, last : last + 1]
-            for n, part in enumerate(parts):
-                mine = part[0, at : at + height].astype(jnp.float32)
-                out = out + mine * columns[here, first + n : first + n + 1]
-            merged.append(out)
+            cached = part[0, r * span + j * height : r * span + (j + 1) * height]
+            fresh = near_sums[r][here, j * HD : (j + 1) * HD]
+            merged.append(
+                cached * columns[here, 2 * r : 2 * r + 1]
+                + fresh * columns[here, 2 * r + 1 : 2 * r + 2]
+            )
         for h in range(chunk):
             both = [out[h * steps : (h + 1) * steps] for out in merged]
             lane = (j * chunk + h) * HD
             attended_ref[:, lane : lane + HD] = jnp.concatenate(both, axis=0).astype(jnp.bfloat16)
 
 
-def finish(own_query, pieces, parts, rows, steps, own, near_width):
+def finish(own_query, pieces, part, rows, steps, own, near_width):
     ways = len(pieces)
     count, width = pieces[0].shape
     return pl.pallas_call(
@@ -430,11 +426,11 @@
             jax.ShapeDtypeStruct((count, width - 2 * near_width), jnp.bfloat16),
             jax.ShapeDtypeStruct((count, own * HD), jnp.bfloat16),
         ],
-        in_specs=[VMEM] * (3 + ways),
+        in_specs=[VMEM] * (2 + ways),
         out_specs=[VMEM] * 2,
         compiler_params=params(8192),
         name="finish",
-    )(own_query, *pieces, *parts)
+    )(own_query, *pieces, part)
 
 
 def on_device(
@@ -461,33 +457,33 @@
     mate_codes = swap(delta_codes, "group", 1)
     mate_scales = swap(delta_scales, "group", 1)
 
-    own_delta, base_blocks = own_weights(owner_map, delta_scales, delta_codes, base_weight)
-    mate_delta = mate_weights(mate_codes, mate_scales)
-    behind, mate_delta = lax.optimization_barrier((lengths, mate_delta))
-    own_query, kept, sent = cache_partials(
-        behind,
+    own_delta, base_blocks, own_query, kept, sent = prepare(
+        owner_map,
+        lengths,
+        delta_scales,
+        delta_codes,
         queries.reshape(tokens, H * HD),
         kv_cache.reshape(-1, 2 * KVH * HD),
+        base_weight,
         rows,
         steps,
         heads_own,
         tensor_count,
     )
-    own_query, base_blocks = lax.optimization_barrier((own_query, base_blocks))
+    mate_delta = mate_weights(mate_codes, mate_scales)
+    behind = lax.optimization_barrier((*near_first(token_rows), mate_delta, sent))
+    token_rows, mate_delta, sent = near_first(list(behind[:pairs])), behind[-2], behind[-1]
     projected = project(own_delta, mate_delta, base_blocks, near_first(token_rows))
-    projected, sent = lax.optimization_barrier((projected, sent))
     step = 1
     while step < tensor_count:
         came = swap(sent, "tensor", step)
+        kept, *sent = merge(kept, came, rows)
+        sent = sent[0] if sent else None
         step *= 2
-        if step < tensor_count:
-            kept, sent = merge(kept, came, rows)
     arrived = exchange(near_first(projected), "group", 2)
     pieces = pack_pieces(owner_map, arrived, owner_block, tensor_count, near_width, slice_width)
     pieces = exchange(pieces, "tensor", 1)
-    new_out, attended = finish(
-        own_query, pieces, [kept, came], rows, steps, heads_own, near_width
-    )
+    new_out, attended = finish(own_query, pieces, kept, rows, steps, heads_own, near_width)
     return (new_out.reshape(rows, steps, -1), attended.reshape(rows, steps, -1))
 
 

time: 32.7 us -> 30.4 us (0.930)
  Pallas kernels: 8.69 us -> 7.26 us
  local copies, waits for them, and re-layouts: 1.08 us -> 0.01 us
  waiting for transfers between devices: 4.76 us -> 5.34 us
    pallas_call x2 -> x1, Pallas kernels: 4.42 us -> 3.29 us  [prepare(): pl.pallas_call(functools.partial(prepare_kernel, rows, steps, own, min(ow...]
    unnamed x10 -> x4, local copies, waits for them, and re-layouts: 1.08 us -> 0.01 us
    ppermute x13, waiting for transfers between devices: 4.76 us -> 5.34 us  [swap(): return lax.ppermute(x, axis, [(k, k ^ distance) for k in range(size)])]
    pallas_call x1, Pallas kernels: 1.61 us -> 1.06 us  [finish(): pl.pallas_call(functools.partial(finish_kernel, rows, steps, own, min(own...]
  transfers between devices with their start and end apart: 13 -> 13, of which waited for: 5 -> 5; matrix products, arithmetic and copies ran while one was open for 0% -> 0% of each run, Pallas kernels for 18% -> 21%
where the time goes in v11:
time: 30.4 us; the launch traced here: 30.2 us
  starting transfers between devices  16.9 us (56%)
  Pallas kernels  7.26 us (24%)
  waiting for transfers between devices  5.34 us (18%)
  between operations  0.71 us (2%)
    ppermute x13, starting transfers between devices, swap(): return lax.ppermute(x, axis, [(k, k ^ distance) for k in range(size)])  16.9 us
    ppermute x13, waiting for transfers between devices, swap(): return lax.ppermute(x, axis, [(k, k ^ distance) for k in range(size)])  5.34 us
    pallas_call x1, Pallas kernels, prepare(): pl.pallas_call(functools.partial(prepare_kernel, rows, steps, own, min(ow...  3.29 us
    pallas_call x1, Pallas kernels, project(): pl.pallas_call(functools.partial(project_kernel, pairs), out_shape=[jax.S...  1.29 us
    pallas_call x1, Pallas kernels, finish(): pl.pallas_call(functools.partial(finish_kernel, rows, steps, own, min(own...  1.06 us
  transfers between devices with their start and end apart: 13, of which 5 were waited for; matrix products, arithmetic and copies ran while one was open for 0% of the time, Pallas kernels for 21%

profile of v11, /device:TPU:0, one launch (start us, length us, event | category | flops | bytes accessed | tf_op | source)
XLA Modules:
  0.0 30.2 jit_solution(14366167204555848166)
XLA Ops:
  0.6 0.5 %collective-permute-start.3 = (bf16[256,2048]{1,0:T(8,128)(2,1)}, bf16[256,2048]{1,0:T(8,128)(2,1)S(1)}, u32[]{:S(2)}, u32[]{:S(2)}) collective-permute-start(bf16[256,2048]{1,0:T(8,128)(2,1)} %codes_hbm.1), channel_id=1, source_target_pairs={{0,4},{4,0},{8,12},{12,8},{16,20},{20,16},{24,28},{28,24},{1,5},{5... | collective-permute-start | bytes 3145736 | tf_op jit(solution)/shard_map/ppermute | solution.py:73
  1.1 4.7 %collective-permute-start.2 = (bf16[16,2048]{1,0:T(8,128)(2,1)}, bf16[16,2048]{1,0:T(8,128)(2,1)S(1)}, u32[]{:S(2)}, u32[]{:S(2)}) collective-permute-start(bf16[16,2048]{1,0:T(8,128)(2,1)} %bitcast.7), channel_id=1, source_target_pairs={{0,24},{4,28},{8,16},{12,20},{16,8},{20,12},{24,0},{28,4},{1,25},{... | collective-permute-start | bytes 196616 | tf_op jit(solution)/shard_map/ppermute | solution.py:73
  5.8 0.0 collective-permute-start.1
  5.8 0.6 %collective-permute-start = (bf16[16,2048]{1,0:T(8,128)(2,1)}, bf16[16,2048]{1,0:T(8,128)(2,1)S(1)}, u32[]{:S(2)}, u32[]{:S(2)}) collective-permute-start(bf16[16,2048]{1,0:T(8,128)(2,1)} %bitcast.9), channel_id=1, source_target_pairs={{0,8},{4,12},{8,0},{12,4},{16,24},{20,28},{24,16},{28,20},{1,9},{5... | collective-permute-start | bytes 196616 | tf_op jit(solution)/shard_map/ppermute | solution.py:73
  6.5 0.0 collective-permute-start.4
  6.5 3.3 %prepare.1 = (bf16[256,2048]{1,0:T(8,128)(2,1)S(1)}, bf16[2,256,2048]{2,1,0:T(8,128)(2,1)S(1)}, bf16[256,128]{1,0:T(8,128)(2,1)S(1)}, f32[2,264,128]{2,1,0:T(8,128)S(1)}, bf16[2,272,128]{2,1,0:T(8,128)(2,1)S(1)}) custom-call(s32[8]{0:T(128)} %owner_ref.1, s32[2]{0:T(128)} %lengths_hbm.1, bf16[16,256]{1,0:T(8,128)(2,1)} %bitcast.14, ...), custom_call_target="tpu_custom_call" | custom-call | bytes 120000000 | tf_op jit(solution)/shard_map/prepare/pallas_call | solution.py:212
  9.8 0.0 copy-start
  9.8 0.0 collective-permute-done.4
  9.8 0.0 collective-permute-done.3.codes_ref
  9.8 0.5 %mate_weights.1.mate_ref = bf16[256,2048]{1,0:T(8,128)(2,1)S(1)} custom-call(bf16[256,2048]{1,0:T(8,128)(2,1)S(1)} %collective-permute-done.3.codes_ref, bf16[16,256]{1,0:T(8,128)(2,1)S(1)} %bitcast.11), custom_call_target="tpu_custom_call" | custom-call | bytes 1000 | tf_op jit(solution)/shard_map/mate_weights/pallas_call | solution.py:98
  10.3 0.0 collective-permute-done.2.refs_3_
  10.3 1.8 %collective-permute-done.1.refs_2_ = bf16[16,2048]{1,0:T(8,128)(2,1)S(1)} collective-permute-done((bf16[16,2048]{1,0:T(8,128)(2,1)}, bf16[16,2048]{1,0:T(8,128)(2,1)S(1)}, u32[]{:S(2)}, u32[]{:S(2)}) %collective-permute-start.1) | collective-permute-done | bytes 65568 | tf_op jit(solution)/shard_map/ppermute | solution.py:73
  12.1 0.0 collective-permute-done.refs_1_
  12.1 1.5 %collective-permute-start.11 = (bf16[2,272,128]{2,1,0:T(8,128)(2,1)S(1)}, bf16[2,272,128]{2,1,0:T(8,128)(2,1)S(1)}, u32[]{:S(2)}, u32[]{:S(2)}) collective-permute-start(bf16[2,272,128]{2,1,0:T(8,128)(2,1)S(1)} %get-tuple-element.43), channel_id=1, source_target_pairs={{0,1},{1,0},{2,3},{3,2},{4,5},{5,4},{6,7},{7,6},{8,9},{9,8},{10,11... | collective-permute-start | bytes 417800 | tf_op jit(solution)/shard_map/ppermute | solution.py:73
  13.6 0.0 copy-done
  13.6 0.0 copy-start.1
  13.6 1.3 %project.1 = (f32[16,512]{1,0:T(8,128)S(1)}, f32[16,512]{1,0:T(8,128)S(1)}, f32[16,512]{1,0:T(8,128)S(1)}, f32[16,512]{1,0:T(8,128)S(1)}) custom-call(bf16[256,2048]{1,0:T(8,128)(2,1)S(1)} %get-tuple-element.26.own_ref, bf16[256,2048]{1,0:T(8,128)(2,1)S(1)} %mate_weights.1.mate_ref, bf16[2,256,2048]{2,1,0:T(8,128)(2,1)S(1)} %get-tuple-element.29.base_ref, ...), custom_call_target="tpu_custom_call" | custom-call | bytes 60000000 | tf_op jit(solution)/shard_map/project/pallas_call | solution.py:289
  14.9 2.5 %collective-permute-start.5 = (f32[16,512]{1,0:T(8,128)S(1)}, f32[16,512]{1,0:T(8,128)S(1)}, u32[]{:S(2)}, u32[]{:S(2)}) collective-permute-start(f32[16,512]{1,0:T(8,128)S(1)} %get-tuple-element.35), channel_id=1, source_target_pairs={{0,24},{4,28},{8,16},{12,20},{16,8},{20,12},{24,0},{28,4},{1,25},{... | collective-permute-start | bytes 98312 | tf_op jit(solution)/shard_map/ppermute | solution.py:73
  17.4 0.2 collective-permute-start.6
  17.7 1.7 %collective-permute-start.7 = (f32[16,512]{1,0:T(8,128)S(1)}, f32[16,512]{1,0:T(8,128)S(1)}, u32[]{:S(2)}, u32[]{:S(2)}) collective-permute-start(f32[16,512]{1,0:T(8,128)S(1)} %get-tuple-element.37), channel_id=1, source_target_pairs={{0,8},{4,12},{8,0},{12,4},{16,24},{20,28},{24,16},{28,20},{1,9},{5... | collective-permute-start | bytes 98312 | tf_op jit(solution)/shard_map/ppermute | solution.py:73
  19.3 0.0 collective-permute-done.11.came_ref
  19.3 0.3 %merge_partials.2 = (f32[1,264,128]{2,1,0:T(8,128)S(1)}, bf16[1,272,128]{2,1,0:T(8,128)(2,1)S(1)}) custom-call(f32[2,264,128]{2,1,0:T(8,128)S(1)} %get-tuple-element.42.kept_ref, bf16[2,272,128]{2,1,0:T(8,128)(2,1)S(1)} %collective-permute-done.11.came_ref), custom_call_target="tpu_custom_call" | custom-call | bytes 270336 | tf_op jit(solution)/shard_map/merge_partials/pallas_call | solution.py:263
  19.7 1.6 %collective-permute-start.12 = (bf16[1,272,128]{2,1,0:T(8,128)(2,1)S(1)}, bf16[1,272,128]{2,1,0:T(8,128)(2,1)S(1)}, u32[]{:S(2)}, u32[]{:S(2)}) collective-permute-start(bf16[1,272,128]{2,1,0:T(8,128)(2,1)S(1)} %get-tuple-element.45), channel_id=1, source_target_pairs={{0,2},{1,3},{2,0},{3,1},{4,6},{5,7},{6,4},{7,5},{8,10},{9,11},{10,... | collective-permute-start | bytes 208904 | tf_op jit(solution)/shard_map/ppermute | solution.py:73
  21.2 0.0 collective-permute-done.5.refs_1_
  21.2 1.0 %collective-permute-done.6.refs_2_ = f32[16,512]{1,0:T(8,128)S(1)} collective-permute-done((f32[16,512]{1,0:T(8,128)S(1)}, f32[16,512]{1,0:T(8,128)S(1)}, u32[]{:S(2)}, u32[]{:S(2)}) %collective-permute-start.6) | collective-permute-done | bytes 32800 | tf_op jit(solution)/shard_map/ppermute | solution.py:73
  22.2 0.0 collective-permute-done.7.refs_3_
  22.3 0.0 copy-done.1
  22.3 0.6 %pack_pieces.1 = (f32[16,1024]{1,0:T(8,128)S(1)}, f32[16,1024]{1,0:T(8,128)S(1)}, f32[16,1024]{1,0:T(8,128)S(1)}, f32[16,1024]{1,0:T(8,128)S(1)}) custom-call(s32[8]{0:T(128)S(1)} %copy-done.1, f32[16,512]{1,0:T(8,128)S(1)} %get-tuple-element.34.refs_0_, f32[16,512]{1,0:T(8,128)S(1)} %collective-permute-done.5.refs_1_, ...), custom_call_target="tpu_custom_call" | custom-call | bytes 60000000 | tf_op jit(solution)/shard_map/pack_pieces/pallas_call | solution.py:329
  22.8 1.6 %collective-permute-start.8 = (f32[16,1024]{1,0:T(8,128)S(1)}, f32[16,1024]{1,0:T(8,128)S(1)}, u32[]{:S(2)}, u32[]{:S(2)}) collective-permute-start(f32[16,1024]{1,0:T(8,128)S(1)} %get-tuple-element.39), channel_id=1, source_target_pairs={{0,3},{1,2},{2,1},{3,0},{4,7},{5,6},{6,5},{7,4},{8,11},{9,10},{10,... | collective-permute-start | bytes 196616 | tf_op jit(solution)/shard_map/ppermute | solution.py:73
  24.4 0.5 %collective-permute-start.9 = (f32[16,1024]{1,0:T(8,128)S(1)}, f32[16,1024]{1,0:T(8,128)S(1)}, u32[]{:S(2)}, u32[]{:S(2)}) collective-permute-start(f32[16,1024]{1,0:T(8,128)S(1)} %get-tuple-element.40), channel_id=1, source_target_pairs={{0,2},{1,3},{2,0},{3,1},{4,6},{5,7},{6,4},{7,5},{8,10},{9,11},{10,... | collective-permute-start | bytes 196616 | tf_op jit(solution)/shard_map/ppermute | solution.py:73
  24.9 1.5 %collective-permute-start.10 = (f32[16,1024]{1,0:T(8,128)S(1)}, f32[16,1024]{1,0:T(8,128)S(1)}, u32[]{:S(2)}, u32[]{:S(2)}) collective-permute-start(f32[16,1024]{1,0:T(8,128)S(1)} %get-tuple-element.41), channel_id=1, source_target_pairs={{0,1},{1,0},{2,3},{3,2},{4,5},{5,4},{6,7},{7,6},{8,9},{9,8},{10,11... | collective-permute-start | bytes 196616 | tf_op jit(solution)/shard_map/ppermute | solution.py:73
  26.4 0.0 collective-permute-done.12.came_ref
  26.4 0.3 merge_partials.3.refs_4_
  26.7 1.6 %collective-permute-done.8.refs_1_ = f32[16,1024]{1,0:T(8,128)S(1)} collective-permute-done((f32[16,1024]{1,0:T(8,128)S(1)}, f32[16,1024]{1,0:T(8,128)S(1)}, u32[]{:S(2)}, u32[]{:S(2)}) %collective-permute-start.8) | collective-permute-done | bytes 65568 | tf_op jit(solution)/shard_map/ppermute | solution.py:73
  28.3 0.7 %collective-permute-done.9.refs_2_ = f32[16,1024]{1,0:T(8,128)S(1)} collective-permute-done((f32[16,1024]{1,0:T(8,128)S(1)}, f32[16,1024]{1,0:T(8,128)S(1)}, u32[]{:S(2)}, u32[]{:S(2)}) %collective-permute-start.9) | collective-permute-done | bytes 65568 | tf_op jit(solution)/shard_map/ppermute | solution.py:73
  29.0 0.2 collective-permute-done.10.refs_3_
  29.2 1.1 %finish.1 = (bf16[16,512]{1,0:T(8,128)(2,1)}, bf16[16,2048]{1,0:T(8,128)(2,1)}) custom-call(bf16[256,128]{1,0:T(8,128)(2,1)S(1)} %get-tuple-element.25.query_ref, f32[16,1024]{1,0:T(8,128)S(1)} %get-tuple-element.38.refs_0_, f32[16,1024]{1,0:T(8,128)S(1)} %collective-permute-done.8.refs_1_, f32[16,1024]{1,0:T(8,128)S(1)} %collective-permute-done.9.refs_2_, ...), custom_call_target="tpu_custom_call" | custom-call | tf_op jit(solution)/shard_map/finish/pallas_call | solution.py:421
Async XLA Ops:
  0.6 9.2 %collective-permute-start.3 = (bf16[256,2048]{1,0:T(8,128)(2,1)}, bf16[256,2048]{1,0:T(8,128)(2,1)S(1)}, u32[]{:S(2)}, u32[]{:S(2)}) collective-permute-start(bf16[256,2048]{1,0:T(8,128)(2,1)} %codes_hbm.1), channel_id=1, source_target_pairs={{0,4},{4,0},{8,12},{12,8},{16,20},{20,16},{24,28},{28,24},{1,5},{5... | collective-permute-start | bytes 3145736 | tf_op jit(solution)/shard_map/ppermute | solution.py:73
  1.1 9.1 %collective-permute-start.2 = (bf16[16,2048]{1,0:T(8,128)(2,1)}, bf16[16,2048]{1,0:T(8,128)(2,1)S(1)}, u32[]{:S(2)}, u32[]{:S(2)}) collective-permute-start(bf16[16,2048]{1,0:T(8,128)(2,1)} %bitcast.7), channel_id=1, source_target_pairs={{0,24},{4,28},{8,16},{12,20},{16,8},{20,12},{24,0},{28,4},{1,25},{... | collective-permute-start | bytes 196616 | tf_op jit(solution)/shard_map/ppermute | solution.py:73
  5.8 6.3 %collective-permute-start.1 = (bf16[16,2048]{1,0:T(8,128)(2,1)}, bf16[16,2048]{1,0:T(8,128)(2,1)S(1)}, u32[]{:S(2)}, u32[]{:S(2)}) collective-permute-start(bf16[16,2048]{1,0:T(8,128)(2,1)} %bitcast.8), channel_id=1, source_target_pairs={{0,16},{4,20},{8,24},{12,28},{16,0},{20,4},{24,8},{28,12},{1,17},{... | collective-permute-start | bytes 196616 | tf_op jit(solution)/shard_map/ppermute | solution.py:73
  5.8 6.3 %collective-permute-start = (bf16[16,2048]{1,0:T(8,128)(2,1)}, bf16[16,2048]{1,0:T(8,128)(2,1)S(1)}, u32[]{:S(2)}, u32[]{:S(2)}) collective-permute-start(bf16[16,2048]{1,0:T(8,128)(2,1)} %bitcast.9), channel_id=1, source_target_pairs={{0,8},{4,12},{8,0},{12,4},{16,24},{20,28},{24,16},{28,20},{1,9},{5... | collective-permute-start | bytes 196616 | tf_op jit(solution)/shard_map/ppermute | solution.py:73
  6.5 3.3 %collective-permute-start.4 = (bf16[256,16]{0,1:T(8,128)(2,1)}, bf16[256,16]{0,1:T(8,128)(2,1)S(1)}, u32[]{:S(2)}, u32[]{:S(2)}) collective-permute-start(bf16[256,16]{0,1:T(8,128)(2,1)} %param.11), channel_id=1, source_target_pairs={{0,4},{4,0},{8,12},{12,8},{16,20},{20,16},{24,28},{28,24},{1,5},{5... | collective-permute-start | bytes 24584 | tf_op jit(solution)/shard_map/ppermute | solution.py:73
  9.8 3.8 %copy-start = (bf16[2,8,2048]{2,1,0:T(8,128)(2,1)S(1)}, bf16[2,8,2048]{2,1,0:T(8,128)(2,1)}, u32[]{:S(2)}) copy-start(bf16[2,8,2048]{2,1,0:T(8,128)(2,1)} %param.8) | copy-start | bytes 196612
  12.1 7.2 %collective-permute-start.11 = (bf16[2,272,128]{2,1,0:T(8,128)(2,1)S(1)}, bf16[2,272,128]{2,1,0:T(8,128)(2,1)S(1)}, u32[]{:S(2)}, u32[]{:S(2)}) collective-permute-start(bf16[2,272,128]{2,1,0:T(8,128)(2,1)S(1)} %get-tuple-element.43), channel_id=1, source_target_pairs={{0,1},{1,0},{2,3},{3,2},{4,5},{5,4},{6,7},{7,6},{8,9},{9,8},{10,11... | collective-permute-start | bytes 417800 | tf_op jit(solution)/shard_map/ppermute | solution.py:73
  13.6 8.7 %copy-start.1 = (s32[8]{0:T(128)S(1)}, s32[8]{0:T(128)}, u32[]{:S(2)}) copy-start(s32[8]{0:T(128)} %owner_ref.1) | copy-start | bytes 100
  14.9 6.4 %collective-permute-start.5 = (f32[16,512]{1,0:T(8,128)S(1)}, f32[16,512]{1,0:T(8,128)S(1)}, u32[]{:S(2)}, u32[]{:S(2)}) collective-permute-start(f32[16,512]{1,0:T(8,128)S(1)} %get-tuple-element.35), channel_id=1, source_target_pairs={{0,24},{4,28},{8,16},{12,20},{16,8},{20,12},{24,0},{28,4},{1,25},{... | collective-permute-start | bytes 98312 | tf_op jit(solution)/shard_map/ppermute | solution.py:73
  17.4 4.8 %collective-permute-start.6 = (f32[16,512]{1,0:T(8,128)S(1)}, f32[16,512]{1,0:T(8,128)S(1)}, u32[]{:S(2)}, u32[]{:S(2)}) collective-permute-start(f32[16,512]{1,0:T(8,128)S(1)} %get-tuple-element.36), channel_id=1, source_target_pairs={{0,16},{4,20},{8,24},{12,28},{16,0},{20,4},{24,8},{28,12},{1,17},{... | collective-permute-start | bytes 98312 | tf_op jit(solution)/shard_map/ppermute | solution.py:73
  17.7 4.6 %collective-permute-start.7 = (f32[16,512]{1,0:T(8,128)S(1)}, f32[16,512]{1,0:T(8,128)S(1)}, u32[]{:S(2)}, u32[]{:S(2)}) collective-permute-start(f32[16,512]{1,0:T(8,128)S(1)} %get-tuple-element.37), channel_id=1, source_target_pairs={{0,8},{4,12},{8,0},{12,4},{16,24},{20,28},{24,16},{28,20},{1,9},{5... | collective-permute-start | bytes 98312 | tf_op jit(solution)/shard_map/ppermute | solution.py:73
  19.7 6.7 %collective-permute-start.12 = (bf16[1,272,128]{2,1,0:T(8,128)(2,1)S(1)}, bf16[1,272,128]{2,1,0:T(8,128)(2,1)S(1)}, u32[]{:S(2)}, u32[]{:S(2)}) collective-permute-start(bf16[1,272,128]{2,1,0:T(8,128)(2,1)S(1)} %get-tuple-element.45), channel_id=1, source_target_pairs={{0,2},{1,3},{2,0},{3,1},{4,6},{5,7},{6,4},{7,5},{8,10},{9,11},{10,... | collective-permute-start | bytes 208904 | tf_op jit(solution)/shard_map/ppermute | solution.py:73
  22.8 5.4 %collective-permute-start.8 = (f32[16,1024]{1,0:T(8,128)S(1)}, f32[16,1024]{1,0:T(8,128)S(1)}, u32[]{:S(2)}, u32[]{:S(2)}) collective-permute-start(f32[16,1024]{1,0:T(8,128)S(1)} %get-tuple-element.39), channel_id=1, source_target_pairs={{0,3},{1,2},{2,1},{3,0},{4,7},{5,6},{6,5},{7,4},{8,11},{9,10},{10,... | collective-permute-start | bytes 196616 | tf_op jit(solution)/shard_map/ppermute | solution.py:73
  24.4 4.6 %collective-permute-start.9 = (f32[16,1024]{1,0:T(8,128)S(1)}, f32[16,1024]{1,0:T(8,128)S(1)}, u32[]{:S(2)}, u32[]{:S(2)}) collective-permute-start(f32[16,1024]{1,0:T(8,128)S(1)} %get-tuple-element.40), channel_id=1, source_target_pairs={{0,2},{1,3},{2,0},{3,1},{4,6},{5,7},{6,4},{7,5},{8,10},{9,11},{10,... | collective-permute-start | bytes 196616 | tf_op jit(solution)/shard_map/ppermute | solution.py:73
  24.9 4.3 %collective-permute-start.10 = (f32[16,1024]{1,0:T(8,128)S(1)}, f32[16,1024]{1,0:T(8,128)S(1)}, u32[]{:S(2)}, u32[]{:S(2)}) collective-permute-start(f32[16,1024]{1,0:T(8,128)S(1)} %get-tuple-element.41), channel_id=1, source_target_pairs={{0,1},{1,0},{2,3},{3,2},{4,5},{5,4},{6,7},{7,6},{8,9},{9,8},{10,11... | collective-permute-start | bytes 196616 | tf_op jit(solution)/shard_map/ppermute | solution.py:73

commit v12 on v11

--- a/solution.py
+++ b/solution.py
@@ -39,7 +39,7 @@
     return SUBLANES if dtype == jnp.float32 else 2 * SUBLANES
 
 
-def put_stats(ref, index, stats):
+def put_stats(ref, stats):
     dtype = ref.dtype
     lines = [x for one in stats for x in ([one] if dtype == jnp.float32 else split(one))]
     lanes = lines[0].shape[1]
@@ -48,12 +48,12 @@
     tile = jnp.concatenate(lines, axis=0)
     if lanes < LANES:
         tile = jnp.concatenate([tile, jnp.zeros((count, LANES - lanes), jnp.float32)], axis=1)
-    ref[index, ref.shape[1] - count :] = tile.astype(dtype)
-
-
-def get_stats(ref, index, rows):
+    ref[ref.shape[0] - count :] = tile.astype(dtype)
+
+
+def get_stats(ref, rows):
     dtype = ref.dtype
-    tile = ref[index, ref.shape[1] - stats_rows(dtype) :].astype(jnp.float32)
+    tile = ref[ref.shape[0] - stats_rows(dtype) :].astype(jnp.float32)
     lines = [tile[n : n + 1] for n in range(2 * rows * (1 if dtype == jnp.float32 else 3))]
     if dtype != jnp.float32:
         lines = [a + b + c for a, b, c in zip(lines[::3], lines[1::3], lines[2::3])]
@@ -109,9 +109,11 @@
 def prepare_kernel(
     rows, steps, own, chunk,
     owner_hbm, lengths_hbm, scales_hbm, codes_hbm, query_hbm, cache_hbm, base_hbm,
-    delta_ref, base_ref, own_query_ref, kept_ref, sent_ref,
-    owner_ref, lengths_ref, scales_ref, codes_ref, query_ref, cache_ref, arrived,
+    *refs,
 ):
+    delta_ref, base_ref, own_query_ref, parts = refs[0], refs[1], refs[2], refs[3:-7]
+    owner_ref, lengths_ref, scales_ref, codes_ref, query_ref, cache_ref, arrived = refs[-7:]
+    order = distances(len(parts))
     place = lax.axis_index("tensor")
     block = codes_ref.shape[0]
     cache_len = cache_ref.shape[0] // rows
@@ -167,40 +169,40 @@
         keys = cache_ref[pl.ds(r * cache_len, cache_len), pl.ds(kv_lane(d), width)]
         return dot(keys, spread, NT)
 
-    units = [(r, d) for r in range(rows) for d in range(2 * kept_ref.shape[0])]
-    stats = [[] for _ in range(2 * kept_ref.shape[0])]
+    units = [(r, n) for r in range(rows) for n in range(len(parts))]
+    stats = [[] for _ in parts]
     ahead = []
-    for n in range(len(units) + 1):
-        if n < len(units):
-            if units[n][1] == 0:
-                cache_loads[units[n][0]].wait()
-            ahead.append(score(*units[n]))
-        if n == 0:
+    for at in range(len(units) + 1):
+        if at < len(units):
+            r, n = units[at]
+            if n == 0:
+                cache_loads[r].wait()
+            ahead.append(score(r, order[n]))
+        if at == 0:
             continue
-        r, d = units[n - 1]
-        at = r * chunks * height
+        r, n = units[at - 1]
         usable = position < lengths_ref[r] - place * cache_len
         scores = jnp.where(usable, ahead.pop(0) * SCORE_SCALE, 2.0 * NEGATIVE)
         peak = jnp.maximum(jnp.max(scores, axis=0, keepdims=True), NEGATIVE)
         weights = jnp.exp(scores - peak)
         total = jnp.sum(weights, axis=0, keepdims=True)
-        lane = pl.ds(kv_lane(d) + KVH * HD, width)
+        lane = pl.ds(kv_lane(order[n]) + KVH * HD, width)
         values = cache_ref[pl.ds(r * cache_len, cache_len), lane]
         sums = dot(weights.astype(jnp.bfloat16), values, TN)
-        ref, index = (sent_ref if d % 2 else kept_ref), d // 2
         for j in range(chunks):
             here = slice(j * height, (j + 1) * height)
-            mine = sums[here, j * HD : (j + 1) * HD].astype(ref.dtype)
-            ref[index, at + j * height : at + (j + 1) * height] = mine
-        stats[d] += [peak, total]
+            first = (r * chunks + j) * height
+            mine = sums[here, j * HD : (j + 1) * HD].astype(parts[n].dtype)
+            parts[n][first : first + height] = mine
+        stats[n] += [peak, total]
         if r == rows - 1:
-            put_stats(ref, index, stats[d])
+            put_stats(parts[n], stats[n])
     for load in base_loads:
         load.wait()
 
 
-def part_shape(count, height, dtype):
-    return jax.ShapeDtypeStruct((count, height + stats_rows(dtype), LANES), dtype)
+def part_shape(height, dtype):
+    return jax.ShapeDtypeStruct((height + stats_rows(dtype), LANES), dtype)
 
 
 def prepare(owner_map, lengths, scales, codes, queries, cache, base, rows, steps, own, ways):
@@ -209,17 +211,17 @@
         pltpu.with_memory_space_constraint(x, pltpu.HBM)
         for x in (owner_map, lengths, scales.T, codes, queries, cache, base)
     ]
-    return pl.pallas_call(
+    out = pl.pallas_call(
         functools.partial(prepare_kernel, rows, steps, own, min(own, H // KVH)),
         out_shape=[
             jax.ShapeDtypeStruct(codes.shape, jnp.bfloat16),
             jax.ShapeDtypeStruct((2,) + codes.shape, jnp.bfloat16),
             jax.ShapeDtypeStruct((height, HD), jnp.bfloat16),
-            part_shape(ways // 2, height, jnp.float32),
-            part_shape(ways // 2, height, jnp.bfloat16),
-        ],
+            part_shape(height, jnp.float32),
+        ]
+        + [part_shape(height, jnp.bfloat16)] * (ways - 1),
         in_specs=[HBM] * len(operands),
-        out_specs=[VMEM] * 5,
+        out_specs=[VMEM] * (3 + ways),
         scratch_shapes=[
             pltpu.SMEM(owner_map.shape, owner_map.dtype),
             pltpu.SMEM(lengths.shape, lengths.dtype),
@@ -233,42 +235,43 @@
         cost_estimate=hint(CACHE_HINT),
         name="prepare",
     )(*operands)
-
-
-def merge_kernel(rows, span, kept_ref, came_ref, next_ref, sent_ref=None):
-    for n in range(kept_ref.shape[0]):
-        ref, index = (sent_ref if n % 2 else next_ref), n // 2
-        stats, factors = [], []
-        for one, two in zip(get_stats(kept_ref, n, rows), get_stats(came_ref, n, rows)):
-            peak = jnp.maximum(one[0], two[0])
-            scales = [jnp.exp(one[0] - peak), jnp.exp(two[0] - peak)]
-            stats += [peak, one[1] * scales[0] + two[1] * scales[1]]
-            factors += scales
-        factors.append(jnp.zeros((SUBLANES - len(factors), LANES), jnp.float32))
-        columns = jnp.concatenate(factors, axis=0).T[:span]
-        for r in range(rows):
-            here = slice(r * span, (r + 1) * span)
-            left = kept_ref[n, here] * columns[:, 2 * r : 2 * r + 1]
-            right = came_ref[n, here].astype(jnp.float32) * columns[:, 2 * r + 1 : 2 * r + 2]
-            ref[index, here] = (left + right).astype(ref.dtype)
-        put_stats(ref, index, stats)
-
-
-def merge(kept, came, rows):
-    count = kept.shape[0]
-    height = kept.shape[1] - stats_rows(kept.dtype)
-    shapes = [part_shape((count + 1) // 2, height, jnp.float32)]
-    if count > 1:
-        shapes.append(part_shape(count // 2, height, jnp.bfloat16))
+    return out[0], out[1], out[2], out[3:]
+
+
+def merge_kernel(rows, span, *refs):
+    parts, out_ref = refs[:-1], refs[-1]
+    everything = [get_stats(part, rows) for part in parts]
+    stats, factors = [], []
+    for r in range(rows):
+        peak = functools.reduce(jnp.maximum, [one[r][0] for one in everything])
+        scales = [jnp.exp(one[r][0] - peak) for one in everything]
+        stats += [peak, sum(one[r][1] * scale for one, scale in zip(everything, scales))]
+        factors += scales
+    lines = -(-len(factors) // SUBLANES) * SUBLANES
+    if lines > len(factors):
+        factors.append(jnp.zeros((lines - len(factors), LANES), jnp.float32))
+    columns = jnp.concatenate(factors, axis=0).T[:span]
+    for r in range(rows):
+        here = slice(r * span, (r + 1) * span)
+        terms = []
+        for n, part in enumerate(parts):
+            at = r * len(parts) + n
+            terms.append(part[here].astype(jnp.float32) * columns[:, at : at + 1])
+        out_ref[here] = sum(terms[1:], terms[0])
+    put_stats(out_ref, stats)
+
+
+def merge(parts, rows):
+    height = parts[0].shape[0] - stats_rows(parts[0].dtype)
     return pl.pallas_call(
         functools.partial(merge_kernel, rows, height // rows),
-        out_shape=shapes,
-        in_specs=[VMEM] * 2,
-        out_specs=[VMEM] * len(shapes),
+        out_shape=part_shape(height, jnp.float32),
+        in_specs=[VMEM] * len(parts),
+        out_specs=VMEM,
         compiler_params=params(8192),
-        cost_estimate=hint(4 * kept.size),
+        cost_estimate=hint(1000),
         name="merge_partials",
-    )(kept, came)
+    )(*parts)
 
 
 def project_kernel(pairs, own_ref, mate_ref, base_ref, *refs):
@@ -381,7 +384,7 @@
         keys = near[r * steps : (r + 1) * steps, :near_width].astype(jnp.bfloat16)
         scores.append(dot(keys, jnp.concatenate(spread, axis=0), NT) * SCORE_SCALE)
     factors, near_sums = [], []
-    for r, (cache_peak, cache_total) in enumerate(get_stats(part, 0, rows)):
+    for r, (cache_peak, cache_total) in enumerate(get_stats(part, rows)):
         masked = jnp.where(causal, scores[r], NEGATIVE)
         peak = jnp.max(masked, axis=0, keepdims=True)
         weights = jnp.where(causal, jnp.exp(masked - peak), 0.0)
@@ -403,7 +406,7 @@
         here = slice(j * height, (j + 1) * height)
         merged = []
         for r in range(rows):
-            cached = part[0, r * span + j * height : r * span + (j + 1) * height]
+            cached = part[r * span + j * height : r * span + (j + 1) * height]
             fresh = near_sums[r][here, j * HD : (j + 1) * HD]
             merged.append(
                 cached * columns[here, 2 * r : 2 * r + 1]
@@ -457,7 +460,7 @@
     mate_codes = swap(delta_codes, "group", 1)
     mate_scales = swap(delta_scales, "group", 1)
 
-    own_delta, base_blocks, own_query, kept, sent = prepare(
+    own_delta, base_blocks, own_query, partials = prepare(
         owner_map,
         lengths,
         delta_scales,
@@ -471,19 +474,15 @@
         tensor_count,
     )
     mate_delta = mate_weights(mate_codes, mate_scales)
-    behind = lax.optimization_barrier((*near_first(token_rows), mate_delta, sent))
-    token_rows, mate_delta, sent = near_first(list(behind[:pairs])), behind[-2], behind[-1]
+    behind = lax.optimization_barrier((*near_first(token_rows), mate_delta, own_query))
+    token_rows, mate_delta, own_query = near_first(list(behind[:pairs])), behind[-2], behind[-1]
     projected = project(own_delta, mate_delta, base_blocks, near_first(token_rows))
-    step = 1
-    while step < tensor_count:
-        came = swap(sent, "tensor", step)
-        kept, *sent = merge(kept, came, rows)
-        sent = sent[0] if sent else None
-        step *= 2
     arrived = exchange(near_first(projected), "group", 2)
+    partials = exchange(partials, "tensor", 1)
     pieces = pack_pieces(owner_map, arrived, owner_block, tensor_count, near_width, slice_width)
     pieces = exchange(pieces, "tensor", 1)
-    new_out, attended = finish(own_query, pieces, kept, rows, steps, heads_own, near_width)
+    partial = merge(partials, rows)
+    new_out, attended = finish(own_query, pieces, partial, rows, steps, heads_own, near_width)
     return (new_out.reshape(rows, steps, -1), attended.reshape(rows, steps, -1))
 
 

time: 30.4 us -> 30.9 us (1.016)
  starting transfers between devices: 16.9 us -> 17.9 us
    ppermute x13 -> x14, starting transfers between devices: 16.9 us -> 17.9 us  [swap(): return lax.ppermute(x, axis, [(k, k ^ distance) for k in range(size)])]
    ppermute x13 -> x14, waiting for transfers between devices: 5.34 us -> 5.09 us  [swap(): return lax.ppermute(x, axis, [(k, k ^ distance) for k in range(size)])]
  transfers between devices with their start and end apart: 13 -> 14, of which waited for: 5 -> 5; matrix products, arithmetic and copies ran while one was open for 0% -> 0% of each run, Pallas kernels for 21% -> 19%
where the time goes in v12:
time: 30.9 us; the launch traced here: 30.7 us
  starting transfers between devices  17.9 us (58%)
  Pallas kernels  7.04 us (23%)
  waiting for transfers between devices  5.09 us (16%)
  between operations  0.72 us (2%)
    ppermute x14, starting transfers between devices, swap(): return lax.ppermute(x, axis, [(k, k ^ distance) for k in range(size)])  17.9 us
    ppermute x14, waiting for transfers between devices, swap(): return lax.ppermute(x, axis, [(k, k ^ distance) for k in range(size)])  5.09 us
    pallas_call x1, Pallas kernels, prepare(): pl.pallas_call(functools.partial(prepare_kernel, rows, steps, own, min(ow...  3.29 us
    pallas_call x1, Pallas kernels, project(): pl.pallas_call(functools.partial(project_kernel, pairs), out_shape=[jax.S...  1.3 us
    pallas_call x1, Pallas kernels, finish(): pl.pallas_call(functools.partial(finish_kernel, rows, steps, own, min(own...  1.06 us
  transfers between devices with their start and end apart: 14, of which 5 were waited for; matrix products, arithmetic and copies ran while one was open for 0% of the time, Pallas kernels for 19%

profile of v12, /device:TPU:0, one launch (start us, length us, event | category | flops | bytes accessed | tf_op | source)
XLA Modules:
  0.0 30.7 jit_solution(8231011077667092022)
XLA Ops:
  0.6 0.5 %collective-permute-start.3 = (bf16[256,2048]{1,0:T(8,128)(2,1)}, bf16[256,2048]{1,0:T(8,128)(2,1)S(1)}, u32[]{:S(2)}, u32[]{:S(2)}) collective-permute-start(bf16[256,2048]{1,0:T(8,128)(2,1)} %codes_hbm.1), channel_id=1, source_target_pairs={{0,4},{4,0},{8,12},{12,8},{16,20},{20,16},{24,28},{28,24},{1,5},{5... | collective-permute-start | bytes 3145736 | tf_op jit(solution)/shard_map/ppermute | solution.py:73
  1.1 4.7 %collective-permute-start.2 = (bf16[16,2048]{1,0:T(8,128)(2,1)}, bf16[16,2048]{1,0:T(8,128)(2,1)S(1)}, u32[]{:S(2)}, u32[]{:S(2)}) collective-permute-start(bf16[16,2048]{1,0:T(8,128)(2,1)} %bitcast.7), channel_id=1, source_target_pairs={{0,24},{4,28},{8,16},{12,20},{16,8},{20,12},{24,0},{28,4},{1,25},{... | collective-permute-start | bytes 196616 | tf_op jit(solution)/shard_map/ppermute | solution.py:73
  5.8 0.0 collective-permute-start.1
  5.8 0.6 %collective-permute-start = (bf16[16,2048]{1,0:T(8,128)(2,1)}, bf16[16,2048]{1,0:T(8,128)(2,1)S(1)}, u32[]{:S(2)}, u32[]{:S(2)}) collective-permute-start(bf16[16,2048]{1,0:T(8,128)(2,1)} %bitcast.9), channel_id=1, source_target_pairs={{0,8},{4,12},{8,0},{12,4},{16,24},{20,28},{24,16},{28,20},{1,9},{5... | collective-permute-start | bytes 196616 | tf_op jit(solution)/shard_map/ppermute | solution.py:73
  6.5 0.0 collective-permute-start.4
  6.5 3.3 %prepare.1 = (bf16[256,2048]{1,0:T(8,128)(2,1)S(1)}, bf16[2,256,2048]{2,1,0:T(8,128)(2,1)S(1)}, bf16[256,128]{1,0:T(8,128)(2,1)S(1)}, f32[264,128]{1,0:T(8,128)S...) custom-call(s32[8]{0:T(128)} %owner_ref.1, s32[2]{0:T(128)} %lengths_hbm.1, ...), custom_call_target="tpu_custom_call" | custom-call | bytes 120000000 | tf_op jit(solution)/shard_map/prepare/pallas_call | solution.py:214
  9.8 0.0 copy-start
  9.8 0.0 collective-permute-done.4
  9.8 2.7 %collective-permute-start.11 = (bf16[272,128]{1,0:T(8,128)(2,1)S(1)}, bf16[272,128]{1,0:T(8,128)(2,1)S(1)}, u32[]{:S(2)}, u32[]{:S(2)}) collective-permute-start(bf16[272,128]{1,0:T(8,128)(2,1)S(1)} %get-tuple-element.43), channel_id=1, source_target_pairs={{0,3},{1,2},{2,1},{3,0},{4,7},{5,6},{6,5},{7,4},{8,11},{9,10},{10,... | collective-permute-start | bytes 208904 | tf_op jit(solution)/shard_map/ppermute | solution.py:73
  12.4 0.0 collective-permute-done.3.codes_ref
  12.4 0.5 %mate_weights.1.mate_ref = bf16[256,2048]{1,0:T(8,128)(2,1)S(1)} custom-call(bf16[256,2048]{1,0:T(8,128)(2,1)S(1)} %collective-permute-done.3.codes_ref, bf16[16,256]{1,0:T(8,128)(2,1)S(1)} %bitcast.11), custom_call_target="tpu_custom_call" | custom-call | bytes 1000 | tf_op jit(solution)/shard_map/mate_weights/pallas_call | solution.py:98
  12.9 0.0 collective-permute-done.2.refs_3_
  12.9 0.0 collective-permute-done.1.refs_2_
  12.9 0.0 collective-permute-done.refs_1_
  13.0 0.0 copy-done
  13.0 0.0 copy-start.1
  13.0 1.3 %project.1 = (f32[16,512]{1,0:T(8,128)S(1)}, f32[16,512]{1,0:T(8,128)S(1)}, f32[16,512]{1,0:T(8,128)S(1)}, f32[16,512]{1,0:T(8,128)S(1)}) custom-call(bf16[256,2048]{1,0:T(8,128)(2,1)S(1)} %get-tuple-element.27.own_ref, bf16[256,2048]{1,0:T(8,128)(2,1)S(1)} %mate_weights.1.mate_ref, bf16[2,256,2048]{2,1,0:T(8,128)(2,1)S(1)} %get-tuple-element.29.base_ref, ...), custom_call_target="tpu_custom_call" | custom-call | bytes 60000000 | tf_op jit(solution)/shard_map/project/pallas_call | solution.py:292
  14.3 3.7 %collective-permute-start.5 = (f32[16,512]{1,0:T(8,128)S(1)}, f32[16,512]{1,0:T(8,128)S(1)}, u32[]{:S(2)}, u32[]{:S(2)}) collective-permute-start(f32[16,512]{1,0:T(8,128)S(1)} %get-tuple-element.35), channel_id=1, source_target_pairs={{0,24},{4,28},{8,16},{12,20},{16,8},{20,12},{24,0},{28,4},{1,25},{... | collective-permute-start | bytes 98312 | tf_op jit(solution)/shard_map/ppermute | solution.py:73
  17.9 0.0 collective-permute-start.6
  17.9 0.8 %collective-permute-start.7 = (f32[16,512]{1,0:T(8,128)S(1)}, f32[16,512]{1,0:T(8,128)S(1)}, u32[]{:S(2)}, u32[]{:S(2)}) collective-permute-start(f32[16,512]{1,0:T(8,128)S(1)} %get-tuple-element.37), channel_id=1, source_target_pairs={{0,8},{4,12},{8,0},{12,4},{16,24},{20,28},{24,16},{28,20},{1,9},{5... | collective-permute-start | bytes 98312 | tf_op jit(solution)/shard_map/ppermute | solution.py:73
  18.7 0.7 %collective-permute-start.12 = (bf16[272,128]{1,0:T(8,128)(2,1)S(1)}, bf16[272,128]{1,0:T(8,128)(2,1)S(1)}, u32[]{:S(2)}, u32[]{:S(2)}) collective-permute-start(bf16[272,128]{1,0:T(8,128)(2,1)S(1)} %get-tuple-element.44), channel_id=1, source_target_pairs={{0,2},{1,3},{2,0},{3,1},{4,6},{5,7},{6,4},{7,5},{8,10},{9,11},{10,... | collective-permute-start | bytes 208904 | tf_op jit(solution)/shard_map/ppermute | solution.py:73
  19.4 0.8 %collective-permute-done.5.refs_1_ = f32[16,512]{1,0:T(8,128)S(1)} collective-permute-done((f32[16,512]{1,0:T(8,128)S(1)}, f32[16,512]{1,0:T(8,128)S(1)}, u32[]{:S(2)}, u32[]{:S(2)}) %collective-permute-start.5) | collective-permute-done | bytes 32800 | tf_op jit(solution)/shard_map/ppermute | solution.py:73
  20.2 0.7 %collective-permute-start.13 = (bf16[272,128]{1,0:T(8,128)(2,1)S(1)}, bf16[272,128]{1,0:T(8,128)(2,1)S(1)}, u32[]{:S(2)}, u32[]{:S(2)}) collective-permute-start(bf16[272,128]{1,0:T(8,128)(2,1)S(1)} %get-tuple-element.45), channel_id=1, source_target_pairs={{0,1},{1,0},{2,3},{3,2},{4,5},{5,4},{6,7},{7,6},{8,9},{9,8},{10,11... | collective-permute-start | bytes 208904 | tf_op jit(solution)/shard_map/ppermute | solution.py:73
  20.9 1.9 %collective-permute-done.6.refs_2_ = f32[16,512]{1,0:T(8,128)S(1)} collective-permute-done((f32[16,512]{1,0:T(8,128)S(1)}, f32[16,512]{1,0:T(8,128)S(1)}, u32[]{:S(2)}, u32[]{:S(2)}) %collective-permute-start.6) | collective-permute-done | bytes 32800 | tf_op jit(solution)/shard_map/ppermute | solution.py:73
  22.8 0.0 collective-permute-done.7.refs_3_
  22.8 0.0 copy-done.1
  22.8 0.6 %pack_pieces.1 = (f32[16,1024]{1,0:T(8,128)S(1)}, f32[16,1024]{1,0:T(8,128)S(1)}, f32[16,1024]{1,0:T(8,128)S(1)}, f32[16,1024]{1,0:T(8,128)S(1)}) custom-call(s32[8]{0:T(128)S(1)} %copy-done.1, f32[16,512]{1,0:T(8,128)S(1)} %get-tuple-element.34.refs_0_, f32[16,512]{1,0:T(8,128)S(1)} %collective-permute-done.5.refs_1_, ...), custom_call_target="tpu_custom_call" | custom-call | bytes 60000000 | tf_op jit(solution)/shard_map/pack_pieces/pallas_call | solution.py:332
  23.4 0.5 %collective-permute-start.8 = (f32[16,1024]{1,0:T(8,128)S(1)}, f32[16,1024]{1,0:T(8,128)S(1)}, u32[]{:S(2)}, u32[]{:S(2)}) collective-permute-start(f32[16,1024]{1,0:T(8,128)S(1)} %get-tuple-element.39), channel_id=1, source_target_pairs={{0,3},{1,2},{2,1},{3,0},{4,7},{5,6},{6,5},{7,4},{8,11},{9,10},{10,... | collective-permute-start | bytes 196616 | tf_op jit(solution)/shard_map/ppermute | solution.py:73
  23.9 1.5 %collective-permute-start.9 = (f32[16,1024]{1,0:T(8,128)S(1)}, f32[16,1024]{1,0:T(8,128)S(1)}, u32[]{:S(2)}, u32[]{:S(2)}) collective-permute-start(f32[16,1024]{1,0:T(8,128)S(1)} %get-tuple-element.40), channel_id=1, source_target_pairs={{0,2},{1,3},{2,0},{3,1},{4,6},{5,7},{6,4},{7,5},{8,10},{9,11},{10,... | collective-permute-start | bytes 196616 | tf_op jit(solution)/shard_map/ppermute | solution.py:73
  25.4 0.0 collective-permute-done.11.refs_1_
  25.4 1.5 %collective-permute-start.10 = (f32[16,1024]{1,0:T(8,128)S(1)}, f32[16,1024]{1,0:T(8,128)S(1)}, u32[]{:S(2)}, u32[]{:S(2)}) collective-permute-start(f32[16,1024]{1,0:T(8,128)S(1)} %get-tuple-element.41), channel_id=1, source_target_pairs={{0,1},{1,0},{2,3},{3,2},{4,5},{5,4},{6,7},{7,6},{8,9},{9,8},{10,11... | collective-permute-start | bytes 196616 | tf_op jit(solution)/shard_map/ppermute | solution.py:73
  26.9 0.0 collective-permute-done.12.refs_2_
  26.9 0.0 collective-permute-done.13.refs_3_
  26.9 0.3 %merge_partials.1.refs_4_ = f32[264,128]{1,0:T(8,128)S(1)} custom-call(f32[264,128]{1,0:T(8,128)S(1)} %get-tuple-element.42.refs_0_, bf16[272,128]{1,0:T(8,128)(2,1)S(1)} %collective-permute-done.11.refs_1_, bf16[272,128]{1,0:T(8,128)(2,1)S(1)} %collective-permute-done.12.refs_2_, bf16[272,128]{1,0:T(8,128)(2,1)S(1)} %collective-permute-done.13.refs_3_), custom_call_target="tpu_custom_call" | custom-call | bytes 1000 | tf_op jit(solution)/shard_map/merge_partials/pallas_call | solution.py:266
  27.3 1.4 %collective-permute-done.8.refs_1_ = f32[16,1024]{1,0:T(8,128)S(1)} collective-permute-done((f32[16,1024]{1,0:T(8,128)S(1)}, f32[16,1024]{1,0:T(8,128)S(1)}, u32[]{:S(2)}, u32[]{:S(2)}) %collective-permute-start.8) | collective-permute-done | bytes 65568 | tf_op jit(solution)/shard_map/ppermute | solution.py:73
  28.7 0.2 collective-permute-done.9.refs_2_
  28.9 0.8 %collective-permute-done.10.refs_3_ = f32[16,1024]{1,0:T(8,128)S(1)} collective-permute-done((f32[16,1024]{1,0:T(8,128)S(1)}, f32[16,1024]{1,0:T(8,128)S(1)}, u32[]{:S(2)}, u32[]{:S(2)}) %collective-permute-start.10) | collective-permute-done | bytes 65568 | tf_op jit(solution)/shard_map/ppermute | solution.py:73
  29.7 1.1 %finish.1 = (bf16[16,512]{1,0:T(8,128)(2,1)}, bf16[16,2048]{1,0:T(8,128)(2,1)}) custom-call(bf16[256,128]{1,0:T(8,128)(2,1)S(1)} %get-tuple-element.26.query_ref, f32[16,1024]{1,0:T(8,128)S(1)} %get-tuple-element.38.refs_0_, f32[16,1024]{1,0:T(8,128)S(1)} %collective-permute-done.8.refs_1_, f32[16,1024]{1,0:T(8,128)S(1)} %collective-permute-done.9.refs_2_, ...), custom_call_target="tpu_custom_call" | custom-call | tf_op jit(solution)/shard_map/finish/pallas_call | solution.py:424
Async XLA Ops:
  0.6 11.8 %collective-permute-start.3 = (bf16[256,2048]{1,0:T(8,128)(2,1)}, bf16[256,2048]{1,0:T(8,128)(2,1)S(1)}, u32[]{:S(2)}, u32[]{:S(2)}) collective-permute-start(bf16[256,2048]{1,0:T(8,128)(2,1)} %codes_hbm.1), channel_id=1, source_target_pairs={{0,4},{4,0},{8,12},{12,8},{16,20},{20,16},{24,28},{28,24},{1,5},{5... | collective-permute-start | bytes 3145736 | tf_op jit(solution)/shard_map/ppermute | solution.py:73
  1.1 11.8 %collective-permute-start.2 = (bf16[16,2048]{1,0:T(8,128)(2,1)}, bf16[16,2048]{1,0:T(8,128)(2,1)S(1)}, u32[]{:S(2)}, u32[]{:S(2)}) collective-permute-start(bf16[16,2048]{1,0:T(8,128)(2,1)} %bitcast.7), channel_id=1, source_target_pairs={{0,24},{4,28},{8,16},{12,20},{16,8},{20,12},{24,0},{28,4},{1,25},{... | collective-permute-start | bytes 196616 | tf_op jit(solution)/shard_map/ppermute | solution.py:73
  5.8 7.1 %collective-permute-start.1 = (bf16[16,2048]{1,0:T(8,128)(2,1)}, bf16[16,2048]{1,0:T(8,128)(2,1)S(1)}, u32[]{:S(2)}, u32[]{:S(2)}) collective-permute-start(bf16[16,2048]{1,0:T(8,128)(2,1)} %bitcast.8), channel_id=1, source_target_pairs={{0,16},{4,20},{8,24},{12,28},{16,0},{20,4},{24,8},{28,12},{1,17},{... | collective-permute-start | bytes 196616 | tf_op jit(solution)/shard_map/ppermute | solution.py:73
  5.8 7.1 %collective-permute-start = (bf16[16,2048]{1,0:T(8,128)(2,1)}, bf16[16,2048]{1,0:T(8,128)(2,1)S(1)}, u32[]{:S(2)}, u32[]{:S(2)}) collective-permute-start(bf16[16,2048]{1,0:T(8,128)(2,1)} %bitcast.9), channel_id=1, source_target_pairs={{0,8},{4,12},{8,0},{12,4},{16,24},{20,28},{24,16},{28,20},{1,9},{5... | collective-permute-start | bytes 196616 | tf_op jit(solution)/shard_map/ppermute | solution.py:73
  6.5 3.3 %collective-permute-start.4 = (bf16[256,16]{0,1:T(8,128)(2,1)}, bf16[256,16]{0,1:T(8,128)(2,1)S(1)}, u32[]{:S(2)}, u32[]{:S(2)}) collective-permute-start(bf16[256,16]{0,1:T(8,128)(2,1)} %param.11), channel_id=1, source_target_pairs={{0,4},{4,0},{8,12},{12,8},{16,20},{20,16},{24,28},{28,24},{1,5},{5... | collective-permute-start | bytes 24584 | tf_op jit(solution)/shard_map/ppermute | solution.py:73
  9.8 3.2 %copy-start = (bf16[2,8,2048]{2,1,0:T(8,128)(2,1)S(1)}, bf16[2,8,2048]{2,1,0:T(8,128)(2,1)}, u32[]{:S(2)}) copy-start(bf16[2,8,2048]{2,1,0:T(8,128)(2,1)} %param.8) | copy-start | bytes 196612
  9.8 15.6 %collective-permute-start.11 = (bf16[272,128]{1,0:T(8,128)(2,1)S(1)}, bf16[272,128]{1,0:T(8,128)(2,1)S(1)}, u32[]{:S(2)}, u32[]{:S(2)}) collective-permute-start(bf16[272,128]{1,0:T(8,128)(2,1)S(1)} %get-tuple-element.43), channel_id=1, source_target_pairs={{0,3},{1,2},{2,1},{3,0},{4,7},{5,6},{6,5},{7,4},{8,11},{9,10},{10,... | collective-permute-start | bytes 208904 | tf_op jit(solution)/shard_map/ppermute | solution.py:73
  13.0 9.8 %copy-start.1 = (s32[8]{0:T(128)S(1)}, s32[8]{0:T(128)}, u32[]{:S(2)}) copy-start(s32[8]{0:T(128)} %owner_ref.1) | copy-start | bytes 100
  14.3 5.9 %collective-permute-start.5 = (f32[16,512]{1,0:T(8,128)S(1)}, f32[16,512]{1,0:T(8,128)S(1)}, u32[]{:S(2)}, u32[]{:S(2)}) collective-permute-start(f32[16,512]{1,0:T(8,128)S(1)} %get-tuple-element.35), channel_id=1, source_target_pairs={{0,24},{4,28},{8,16},{12,20},{16,8},{20,12},{24,0},{28,4},{1,25},{... | collective-permute-start | bytes 98312 | tf_op jit(solution)/shard_map/ppermute | solution.py:73
  17.9 4.8 %collective-permute-start.6 = (f32[16,512]{1,0:T(8,128)S(1)}, f32[16,512]{1,0:T(8,128)S(1)}, u32[]{:S(2)}, u32[]{:S(2)}) collective-permute-start(f32[16,512]{1,0:T(8,128)S(1)} %get-tuple-element.36), channel_id=1, source_target_pairs={{0,16},{4,20},{8,24},{12,28},{16,0},{20,4},{24,8},{28,12},{1,17},{... | collective-permute-start | bytes 98312 | tf_op jit(solution)/shard_map/ppermute | solution.py:73
  17.9 4.8 %collective-permute-start.7 = (f32[16,512]{1,0:T(8,128)S(1)}, f32[16,512]{1,0:T(8,128)S(1)}, u32[]{:S(2)}, u32[]{:S(2)}) collective-permute-start(f32[16,512]{1,0:T(8,128)S(1)} %get-tuple-element.37), channel_id=1, source_target_pairs={{0,8},{4,12},{8,0},{12,4},{16,24},{20,28},{24,16},{28,20},{1,9},{5... | collective-permute-start | bytes 98312 | tf_op jit(solution)/shard_map/ppermute | solution.py:73
  18.7 8.2 %collective-permute-start.12 = (bf16[272,128]{1,0:T(8,128)(2,1)S(1)}, bf16[272,128]{1,0:T(8,128)(2,1)S(1)}, u32[]{:S(2)}, u32[]{:S(2)}) collective-permute-start(bf16[272,128]{1,0:T(8,128)(2,1)S(1)} %get-tuple-element.44), channel_id=1, source_target_pairs={{0,2},{1,3},{2,0},{3,1},{4,6},{5,7},{6,4},{7,5},{8,10},{9,11},{10,... | collective-permute-start | bytes 208904 | tf_op jit(solution)/shard_map/ppermute | solution.py:73
  20.2 6.7 %collective-permute-start.13 = (bf16[272,128]{1,0:T(8,128)(2,1)S(1)}, bf16[272,128]{1,0:T(8,128)(2,1)S(1)}, u32[]{:S(2)}, u32[]{:S(2)}) collective-permute-start(bf16[272,128]{1,0:T(8,128)(2,1)S(1)} %get-tuple-element.45), channel_id=1, source_target_pairs={{0,1},{1,0},{2,3},{3,2},{4,5},{5,4},{6,7},{7,6},{8,9},{9,8},{10,11... | collective-permute-start | bytes 208904 | tf_op jit(solution)/shard_map/ppermute | solution.py:73
  23.4 5.3 %collective-permute-start.8 = (f32[16,1024]{1,0:T(8,128)S(1)}, f32[16,1024]{1,0:T(8,128)S(1)}, u32[]{:S(2)}, u32[]{:S(2)}) collective-permute-start(f32[16,1024]{1,0:T(8,128)S(1)} %get-tuple-element.39), channel_id=1, source_target_pairs={{0,3},{1,2},{2,1},{3,0},{4,7},{5,6},{6,5},{7,4},{8,11},{9,10},{10,... | collective-permute-start | bytes 196616 | tf_op jit(solution)/shard_map/ppermute | solution.py:73
  23.9 5.0 %collective-permute-start.9 = (f32[16,1024]{1,0:T(8,128)S(1)}, f32[16,1024]{1,0:T(8,128)S(1)}, u32[]{:S(2)}, u32[]{:S(2)}) collective-permute-start(f32[16,1024]{1,0:T(8,128)S(1)} %get-tuple-element.40), channel_id=1, source_target_pairs={{0,2},{1,3},{2,0},{3,1},{4,6},{5,7},{6,4},{7,5},{8,10},{9,11},{10,... | collective-permute-start | bytes 196616 | tf_op jit(solution)/shard_map/ppermute | solution.py:73
  25.4 4.3 %collective-permute-start.10 = (f32[16,1024]{1,0:T(8,128)S(1)}, f32[16,1024]{1,0:T(8,128)S(1)}, u32[]{:S(2)}, u32[]{:S(2)}) collective-permute-start(f32[16,1024]{1,0:T(8,128)S(1)} %get-tuple-element.41), channel_id=1, source_target_pairs={{0,1},{1,0},{2,3},{3,2},{4,5},{5,4},{6,7},{7,6},{8,9},{9,8},{10,11... | collective-permute-start | bytes 196616 | tf_op jit(solution)/shard_map/ppermute | solution.py:73

commit v13 on v11

--- a/solution.py
+++ b/solution.py
@@ -277,7 +277,7 @@
     stacked = jnp.concatenate([ref[...] for ref in tokens], axis=0)
     count = tokens[0].shape[0]
     for k, delta_ref in enumerate((own_ref, mate_ref)):
-        whole = (dot(base_ref[k], stacked, NT) + dot(delta_ref[...], stacked, NT)).T
+        whole = dot(stacked, base_ref[k], NT) + dot(stacked, delta_ref[...], NT)
         for n in range(pairs):
             outs[n][:, k * block : (k + 1) * block] = whole[n * count : (n + 1) * count]
 

time: 30.4 us -> 30.5 us (level)
  no operation moved by 1% of the time
where the time goes in v13:
time: 30.5 us; the launch traced here: 30.3 us
  starting transfers between devices  16.9 us (55%)
  Pallas kernels  7.36 us (24%)
  waiting for transfers between devices  5.33 us (17%)
  between operations  0.7 us (2%)
    ppermute x13, starting transfers between devices, swap(): return lax.ppermute(x, axis, [(k, k ^ distance) for k in range(size)])  16.9 us
    ppermute x13, waiting for transfers between devices, swap(): return lax.ppermute(x, axis, [(k, k ^ distance) for k in range(size)])  5.33 us
    pallas_call x1, Pallas kernels, prepare(): pl.pallas_call(functools.partial(prepare_kernel, rows, steps, own, min(ow...  3.29 us
    pallas_call x1, Pallas kernels, project(): pl.pallas_call(functools.partial(project_kernel, pairs), out_shape=[jax.S...  1.39 us
    pallas_call x1, Pallas kernels, finish(): pl.pallas_call(functools.partial(finish_kernel, rows, steps, own, min(own...  1.06 us
  transfers between devices with their start and end apart: 13, of which 5 were waited for; matrix products, arithmetic and copies ran while one was open for 0% of the time, Pallas kernels for 21%

profile of v13, /device:TPU:0, one launch (start us, length us, event | category | flops | bytes accessed | tf_op | source)
XLA Modules:
  0.0 30.3 jit_solution(1472378421812119783)
XLA Ops:
  0.6 0.5 %collective-permute-start.3 = (bf16[256,2048]{1,0:T(8,128)(2,1)}, bf16[256,2048]{1,0:T(8,128)(2,1)S(1)}, u32[]{:S(2)}, u32[]{:S(2)}) collective-permute-start(bf16[256,2048]{1,0:T(8,128)(2,1)} %codes_hbm.1), channel_id=1, source_target_pairs={{0,4},{4,0},{8,12},{12,8},{16,20},{20,16},{24,28},{28,24},{1,5},{5... | collective-permute-start | bytes 3145736 | tf_op jit(solution)/shard_map/ppermute | solution.py:73
  1.1 4.7 %collective-permute-start.2 = (bf16[16,2048]{1,0:T(8,128)(2,1)}, bf16[16,2048]{1,0:T(8,128)(2,1)S(1)}, u32[]{:S(2)}, u32[]{:S(2)}) collective-permute-start(bf16[16,2048]{1,0:T(8,128)(2,1)} %bitcast.7), channel_id=1, source_target_pairs={{0,24},{4,28},{8,16},{12,20},{16,8},{20,12},{24,0},{28,4},{1,25},{... | collective-permute-start | bytes 196616 | tf_op jit(solution)/shard_map/ppermute | solution.py:73
  5.8 0.0 collective-permute-start.1
  5.8 0.6 %collective-permute-start = (bf16[16,2048]{1,0:T(8,128)(2,1)}, bf16[16,2048]{1,0:T(8,128)(2,1)S(1)}, u32[]{:S(2)}, u32[]{:S(2)}) collective-permute-start(bf16[16,2048]{1,0:T(8,128)(2,1)} %bitcast.9), channel_id=1, source_target_pairs={{0,8},{4,12},{8,0},{12,4},{16,24},{20,28},{24,16},{28,20},{1,9},{5... | collective-permute-start | bytes 196616 | tf_op jit(solution)/shard_map/ppermute | solution.py:73
  6.5 0.0 collective-permute-start.4
  6.5 3.3 %prepare.1 = (bf16[256,2048]{1,0:T(8,128)(2,1)S(1)}, bf16[2,256,2048]{2,1,0:T(8,128)(2,1)S(1)}, bf16[256,128]{1,0:T(8,128)(2,1)S(1)}, f32[2,264,128]{2,1,0:T(8,128)S(1)}, bf16[2,272,128]{2,1,0:T(8,128)(2,1)S(1)}) custom-call(s32[8]{0:T(128)} %owner_ref.1, s32[2]{0:T(128)} %lengths_hbm.1, bf16[16,256]{1,0:T(8,128)(2,1)} %bitcast.14, ...), custom_call_target="tpu_custom_call" | custom-call | bytes 120000000 | tf_op jit(solution)/shard_map/prepare/pallas_call | solution.py:212
  9.8 0.0 copy-start
  9.8 0.0 collective-permute-done.4
  9.8 0.0 collective-permute-done.3.codes_ref
  9.8 0.5 %mate_weights.1.mate_ref = bf16[256,2048]{1,0:T(8,128)(2,1)S(1)} custom-call(bf16[256,2048]{1,0:T(8,128)(2,1)S(1)} %collective-permute-done.3.codes_ref, bf16[16,256]{1,0:T(8,128)(2,1)S(1)} %bitcast.11), custom_call_target="tpu_custom_call" | custom-call | bytes 1000 | tf_op jit(solution)/shard_map/mate_weights/pallas_call | solution.py:98
  10.3 0.0 collective-permute-done.2.refs_3_
  10.3 1.8 %collective-permute-done.1.refs_2_ = bf16[16,2048]{1,0:T(8,128)(2,1)S(1)} collective-permute-done((bf16[16,2048]{1,0:T(8,128)(2,1)}, bf16[16,2048]{1,0:T(8,128)(2,1)S(1)}, u32[]{:S(2)}, u32[]{:S(2)}) %collective-permute-start.1) | collective-permute-done | bytes 65568 | tf_op jit(solution)/shard_map/ppermute | solution.py:73
  12.1 0.0 collective-permute-done.refs_1_
  12.1 1.5 %collective-permute-start.11 = (bf16[2,272,128]{2,1,0:T(8,128)(2,1)S(1)}, bf16[2,272,128]{2,1,0:T(8,128)(2,1)S(1)}, u32[]{:S(2)}, u32[]{:S(2)}) collective-permute-start(bf16[2,272,128]{2,1,0:T(8,128)(2,1)S(1)} %get-tuple-element.43), channel_id=1, source_target_pairs={{0,1},{1,0},{2,3},{3,2},{4,5},{5,4},{6,7},{7,6},{8,9},{9,8},{10,11... | collective-permute-start | bytes 417800 | tf_op jit(solution)/shard_map/ppermute | solution.py:73
  13.6 0.0 copy-done
  13.6 0.0 copy-start.1
  13.6 1.4 %project.1 = (f32[16,512]{1,0:T(8,128)S(1)}, f32[16,512]{1,0:T(8,128)S(1)}, f32[16,512]{1,0:T(8,128)S(1)}, f32[16,512]{1,0:T(8,128)S(1)}) custom-call(bf16[256,2048]{1,0:T(8,128)(2,1)S(1)} %get-tuple-element.26.own_ref, bf16[256,2048]{1,0:T(8,128)(2,1)S(1)} %mate_weights.1.mate_ref, bf16[2,256,2048]{2,1,0:T(8,128)(2,1)S(1)} %get-tuple-element.29.base_ref, ...), custom_call_target="tpu_custom_call" | custom-call | bytes 60000000 | tf_op jit(solution)/shard_map/project/pallas_call | solution.py:289
  15.0 2.5 %collective-permute-start.5 = (f32[16,512]{1,0:T(8,128)S(1)}, f32[16,512]{1,0:T(8,128)S(1)}, u32[]{:S(2)}, u32[]{:S(2)}) collective-permute-start(f32[16,512]{1,0:T(8,128)S(1)} %get-tuple-element.35), channel_id=1, source_target_pairs={{0,24},{4,28},{8,16},{12,20},{16,8},{20,12},{24,0},{28,4},{1,25},{... | collective-permute-start | bytes 98312 | tf_op jit(solution)/shard_map/ppermute | solution.py:73
  17.5 0.2 collective-permute-start.6
  17.7 1.7 %collective-permute-start.7 = (f32[16,512]{1,0:T(8,128)S(1)}, f32[16,512]{1,0:T(8,128)S(1)}, u32[]{:S(2)}, u32[]{:S(2)}) collective-permute-start(f32[16,512]{1,0:T(8,128)S(1)} %get-tuple-element.37), channel_id=1, source_target_pairs={{0,8},{4,12},{8,0},{12,4},{16,24},{20,28},{24,16},{28,20},{1,9},{5... | collective-permute-start | bytes 98312 | tf_op jit(solution)/shard_map/ppermute | solution.py:73
  19.4 0.0 collective-permute-done.11.came_ref
  19.4 0.3 %merge_partials.2 = (f32[1,264,128]{2,1,0:T(8,128)S(1)}, bf16[1,272,128]{2,1,0:T(8,128)(2,1)S(1)}) custom-call(f32[2,264,128]{2,1,0:T(8,128)S(1)} %get-tuple-element.42.kept_ref, bf16[2,272,128]{2,1,0:T(8,128)(2,1)S(1)} %collective-permute-done.11.came_ref), custom_call_target="tpu_custom_call" | custom-call | bytes 270336 | tf_op jit(solution)/shard_map/merge_partials/pallas_call | solution.py:263
  19.8 1.6 %collective-permute-start.12 = (bf16[1,272,128]{2,1,0:T(8,128)(2,1)S(1)}, bf16[1,272,128]{2,1,0:T(8,128)(2,1)S(1)}, u32[]{:S(2)}, u32[]{:S(2)}) collective-permute-start(bf16[1,272,128]{2,1,0:T(8,128)(2,1)S(1)} %get-tuple-element.45), channel_id=1, source_target_pairs={{0,2},{1,3},{2,0},{3,1},{4,6},{5,7},{6,4},{7,5},{8,10},{9,11},{10,... | collective-permute-start | bytes 208904 | tf_op jit(solution)/shard_map/ppermute | solution.py:73
  21.3 0.0 collective-permute-done.5.refs_1_
  21.3 1.0 %collective-permute-done.6.refs_2_ = f32[16,512]{1,0:T(8,128)S(1)} collective-permute-done((f32[16,512]{1,0:T(8,128)S(1)}, f32[16,512]{1,0:T(8,128)S(1)}, u32[]{:S(2)}, u32[]{:S(2)}) %collective-permute-start.6) | collective-permute-done | bytes 32800 | tf_op jit(solution)/shard_map/ppermute | solution.py:73
  22.3 0.0 collective-permute-done.7.refs_3_
  22.3 0.0 copy-done.1
  22.3 0.6 %pack_pieces.1 = (f32[16,1024]{1,0:T(8,128)S(1)}, f32[16,1024]{1,0:T(8,128)S(1)}, f32[16,1024]{1,0:T(8,128)S(1)}, f32[16,1024]{1,0:T(8,128)S(1)}) custom-call(s32[8]{0:T(128)S(1)} %copy-done.1, f32[16,512]{1,0:T(8,128)S(1)} %get-tuple-element.34.refs_0_, f32[16,512]{1,0:T(8,128)S(1)} %collective-permute-done.5.refs_1_, ...), custom_call_target="tpu_custom_call" | custom-call | bytes 60000000 | tf_op jit(solution)/shard_map/pack_pieces/pallas_call | solution.py:329
  22.9 1.6 %collective-permute-start.8 = (f32[16,1024]{1,0:T(8,128)S(1)}, f32[16,1024]{1,0:T(8,128)S(1)}, u32[]{:S(2)}, u32[]{:S(2)}) collective-permute-start(f32[16,1024]{1,0:T(8,128)S(1)} %get-tuple-element.39), channel_id=1, source_target_pairs={{0,3},{1,2},{2,1},{3,0},{4,7},{5,6},{6,5},{7,4},{8,11},{9,10},{10,... | collective-permute-start | bytes 196616 | tf_op jit(solution)/shard_map/ppermute | solution.py:73
  24.5 0.5 %collective-permute-start.9 = (f32[16,1024]{1,0:T(8,128)S(1)}, f32[16,1024]{1,0:T(8,128)S(1)}, u32[]{:S(2)}, u32[]{:S(2)}) collective-permute-start(f32[16,1024]{1,0:T(8,128)S(1)} %get-tuple-element.40), channel_id=1, source_target_pairs={{0,2},{1,3},{2,0},{3,1},{4,6},{5,7},{6,4},{7,5},{8,10},{9,11},{10,... | collective-permute-start | bytes 196616 | tf_op jit(solution)/shard_map/ppermute | solution.py:73
  25.0 1.5 %collective-permute-start.10 = (f32[16,1024]{1,0:T(8,128)S(1)}, f32[16,1024]{1,0:T(8,128)S(1)}, u32[]{:S(2)}, u32[]{:S(2)}) collective-permute-start(f32[16,1024]{1,0:T(8,128)S(1)} %get-tuple-element.41), channel_id=1, source_target_pairs={{0,1},{1,0},{2,3},{3,2},{4,5},{5,4},{6,7},{7,6},{8,9},{9,8},{10,11... | collective-permute-start | bytes 196616 | tf_op jit(solution)/shard_map/ppermute | solution.py:73
  26.5 0.0 collective-permute-done.12.came_ref
  26.5 0.3 merge_partials.3.refs_4_
  26.8 1.6 %collective-permute-done.8.refs_1_ = f32[16,1024]{1,0:T(8,128)S(1)} collective-permute-done((f32[16,1024]{1,0:T(8,128)S(1)}, f32[16,1024]{1,0:T(8,128)S(1)}, u32[]{:S(2)}, u32[]{:S(2)}) %collective-permute-start.8) | collective-permute-done | bytes 65568 | tf_op jit(solution)/shard_map/ppermute | solution.py:73
  28.4 0.7 %collective-permute-done.9.refs_2_ = f32[16,1024]{1,0:T(8,128)S(1)} collective-permute-done((f32[16,1024]{1,0:T(8,128)S(1)}, f32[16,1024]{1,0:T(8,128)S(1)}, u32[]{:S(2)}, u32[]{:S(2)}) %collective-permute-start.9) | collective-permute-done | bytes 65568 | tf_op jit(solution)/shard_map/ppermute | solution.py:73
  29.1 0.2 collective-permute-done.10.refs_3_
  29.3 1.1 %finish.1 = (bf16[16,512]{1,0:T(8,128)(2,1)}, bf16[16,2048]{1,0:T(8,128)(2,1)}) custom-call(bf16[256,128]{1,0:T(8,128)(2,1)S(1)} %get-tuple-element.25.query_ref, f32[16,1024]{1,0:T(8,128)S(1)} %get-tuple-element.38.refs_0_, f32[16,1024]{1,0:T(8,128)S(1)} %collective-permute-done.8.refs_1_, f32[16,1024]{1,0:T(8,128)S(1)} %collective-permute-done.9.refs_2_, ...), custom_call_target="tpu_custom_call" | custom-call | tf_op jit(solution)/shard_map/finish/pallas_call | solution.py:421
Async XLA Ops:
  0.6 9.2 %collective-permute-start.3 = (bf16[256,2048]{1,0:T(8,128)(2,1)}, bf16[256,2048]{1,0:T(8,128)(2,1)S(1)}, u32[]{:S(2)}, u32[]{:S(2)}) collective-permute-start(bf16[256,2048]{1,0:T(8,128)(2,1)} %codes_hbm.1), channel_id=1, source_target_pairs={{0,4},{4,0},{8,12},{12,8},{16,20},{20,16},{24,28},{28,24},{1,5},{5... | collective-permute-start | bytes 3145736 | tf_op jit(solution)/shard_map/ppermute | solution.py:73
  1.1 9.1 %collective-permute-start.2 = (bf16[16,2048]{1,0:T(8,128)(2,1)}, bf16[16,2048]{1,0:T(8,128)(2,1)S(1)}, u32[]{:S(2)}, u32[]{:S(2)}) collective-permute-start(bf16[16,2048]{1,0:T(8,128)(2,1)} %bitcast.7), channel_id=1, source_target_pairs={{0,24},{4,28},{8,16},{12,20},{16,8},{20,12},{24,0},{28,4},{1,25},{... | collective-permute-start | bytes 196616 | tf_op jit(solution)/shard_map/ppermute | solution.py:73
  5.8 6.3 %collective-permute-start.1 = (bf16[16,2048]{1,0:T(8,128)(2,1)}, bf16[16,2048]{1,0:T(8,128)(2,1)S(1)}, u32[]{:S(2)}, u32[]{:S(2)}) collective-permute-start(bf16[16,2048]{1,0:T(8,128)(2,1)} %bitcast.8), channel_id=1, source_target_pairs={{0,16},{4,20},{8,24},{12,28},{16,0},{20,4},{24,8},{28,12},{1,17},{... | collective-permute-start | bytes 196616 | tf_op jit(solution)/shard_map/ppermute | solution.py:73
  5.8 6.3 %collective-permute-start = (bf16[16,2048]{1,0:T(8,128)(2,1)}, bf16[16,2048]{1,0:T(8,128)(2,1)S(1)}, u32[]{:S(2)}, u32[]{:S(2)}) collective-permute-start(bf16[16,2048]{1,0:T(8,128)(2,1)} %bitcast.9), channel_id=1, source_target_pairs={{0,8},{4,12},{8,0},{12,4},{16,24},{20,28},{24,16},{28,20},{1,9},{5... | collective-permute-start | bytes 196616 | tf_op jit(solution)/shard_map/ppermute | solution.py:73
  6.5 3.3 %collective-permute-start.4 = (bf16[256,16]{0,1:T(8,128)(2,1)}, bf16[256,16]{0,1:T(8,128)(2,1)S(1)}, u32[]{:S(2)}, u32[]{:S(2)}) collective-permute-start(bf16[256,16]{0,1:T(8,128)(2,1)} %param.11), channel_id=1, source_target_pairs={{0,4},{4,0},{8,12},{12,8},{16,20},{20,16},{24,28},{28,24},{1,5},{5... | collective-permute-start | bytes 24584 | tf_op jit(solution)/shard_map/ppermute | solution.py:73
  9.8 3.8 %copy-start = (bf16[2,8,2048]{2,1,0:T(8,128)(2,1)S(1)}, bf16[2,8,2048]{2,1,0:T(8,128)(2,1)}, u32[]{:S(2)}) copy-start(bf16[2,8,2048]{2,1,0:T(8,128)(2,1)} %param.8) | copy-start | bytes 196612
  12.1 7.3 %collective-permute-start.11 = (bf16[2,272,128]{2,1,0:T(8,128)(2,1)S(1)}, bf16[2,272,128]{2,1,0:T(8,128)(2,1)S(1)}, u32[]{:S(2)}, u32[]{:S(2)}) collective-permute-start(bf16[2,272,128]{2,1,0:T(8,128)(2,1)S(1)} %get-tuple-element.43), channel_id=1, source_target_pairs={{0,1},{1,0},{2,3},{3,2},{4,5},{5,4},{6,7},{7,6},{8,9},{9,8},{10,11... | collective-permute-start | bytes 417800 | tf_op jit(solution)/shard_map/ppermute | solution.py:73
  13.6 8.7 %copy-start.1 = (s32[8]{0:T(128)S(1)}, s32[8]{0:T(128)}, u32[]{:S(2)}) copy-start(s32[8]{0:T(128)} %owner_ref.1) | copy-start | bytes 100
  15.0 6.4 %collective-permute-start.5 = (f32[16,512]{1,0:T(8,128)S(1)}, f32[16,512]{1,0:T(8,128)S(1)}, u32[]{:S(2)}, u32[]{:S(2)}) collective-permute-start(f32[16,512]{1,0:T(8,128)S(1)} %get-tuple-element.35), channel_id=1, source_target_pairs={{0,24},{4,28},{8,16},{12,20},{16,8},{20,12},{24,0},{28,4},{1,25},{... | collective-permute-start | bytes 98312 | tf_op jit(solution)/shard_map/ppermute | solution.py:73
  17.5 4.8 %collective-permute-start.6 = (f32[16,512]{1,0:T(8,128)S(1)}, f32[16,512]{1,0:T(8,128)S(1)}, u32[]{:S(2)}, u32[]{:S(2)}) collective-permute-start(f32[16,512]{1,0:T(8,128)S(1)} %get-tuple-element.36), channel_id=1, source_target_pairs={{0,16},{4,20},{8,24},{12,28},{16,0},{20,4},{24,8},{28,12},{1,17},{... | collective-permute-start | bytes 98312 | tf_op jit(solution)/shard_map/ppermute | solution.py:73
  17.7 4.6 %collective-permute-start.7 = (f32[16,512]{1,0:T(8,128)S(1)}, f32[16,512]{1,0:T(8,128)S(1)}, u32[]{:S(2)}, u32[]{:S(2)}) collective-permute-start(f32[16,512]{1,0:T(8,128)S(1)} %get-tuple-element.37), channel_id=1, source_target_pairs={{0,8},{4,12},{8,0},{12,4},{16,24},{20,28},{24,16},{28,20},{1,9},{5... | collective-permute-start | bytes 98312 | tf_op jit(solution)/shard_map/ppermute | solution.py:73
  19.8 6.7 %collective-permute-start.12 = (bf16[1,272,128]{2,1,0:T(8,128)(2,1)S(1)}, bf16[1,272,128]{2,1,0:T(8,128)(2,1)S(1)}, u32[]{:S(2)}, u32[]{:S(2)}) collective-permute-start(bf16[1,272,128]{2,1,0:T(8,128)(2,1)S(1)} %get-tuple-element.45), channel_id=1, source_target_pairs={{0,2},{1,3},{2,0},{3,1},{4,6},{5,7},{6,4},{7,5},{8,10},{9,11},{10,... | collective-permute-start | bytes 208904 | tf_op jit(solution)/shard_map/ppermute | solution.py:73
  22.9 5.4 %collective-permute-start.8 = (f32[16,1024]{1,0:T(8,128)S(1)}, f32[16,1024]{1,0:T(8,128)S(1)}, u32[]{:S(2)}, u32[]{:S(2)}) collective-permute-start(f32[16,1024]{1,0:T(8,128)S(1)} %get-tuple-element.39), channel_id=1, source_target_pairs={{0,3},{1,2},{2,1},{3,0},{4,7},{5,6},{6,5},{7,4},{8,11},{9,10},{10,... | collective-permute-start | bytes 196616 | tf_op jit(solution)/shard_map/ppermute | solution.py:73
  24.5 4.6 %collective-permute-start.9 = (f32[16,1024]{1,0:T(8,128)S(1)}, f32[16,1024]{1,0:T(8,128)S(1)}, u32[]{:S(2)}, u32[]{:S(2)}) collective-permute-start(f32[16,1024]{1,0:T(8,128)S(1)} %get-tuple-element.40), channel_id=1, source_target_pairs={{0,2},{1,3},{2,0},{3,1},{4,6},{5,7},{6,4},{7,5},{8,10},{9,11},{10,... | collective-permute-start | bytes 196616 | tf_op jit(solution)/shard_map/ppermute | solution.py:73
  25.0 4.3 %collective-permute-start.10 = (f32[16,1024]{1,0:T(8,128)S(1)}, f32[16,1024]{1,0:T(8,128)S(1)}, u32[]{:S(2)}, u32[]{:S(2)}) collective-permute-start(f32[16,1024]{1,0:T(8,128)S(1)} %get-tuple-element.41), channel_id=1, source_target_pairs={{0,1},{1,0},{2,3},{3,2},{4,5},{5,4},{6,7},{7,6},{8,9},{9,8},{10,11... | collective-permute-start | bytes 196616 | tf_op jit(solution)/shard_map/ppermute | solution.py:73

commit v14 on v11

--- a/solution.py
+++ b/solution.py
@@ -305,15 +305,21 @@
     for piece, d in zip(arrived, distances(pairs)):
         for k in range(2):
             ordered[owner_ref[place ^ (2 * d + k)]] = piece[:, k * block : (k + 1) * block]
+    def put(out, at, values):
+        out[:, at : at + block] = values.astype(out.dtype)
+
     for out, d in zip(outs, distances(ways)):
         to = to_place ^ d
         for n in range(near):
-            out[:, n * block : (n + 1) * block] = ordered[to * near + n]
-            at = (near + n) * block
-            out[:, at : at + block] = ordered[shards // 2 + to * near + n]
+            key = ordered[to * near + n]
+            put(out, n * block, key)
+            if d != 0:
+                put(out, (near + n) * block, key - key.astype(out.dtype).astype(jnp.float32))
+        start = out.shape[1] - (near + wide) * block
+        for n in range(near):
+            put(out, start + n * block, ordered[shards // 2 + to * near + n])
         for n in range(wide):
-            at = (2 * near + n) * block
-            out[:, at : at + block] = ordered[to * wide + n]
+            put(out, start + (near + n) * block, ordered[to * wide + n])
 
 
 def pack_pieces(owner_map, arrived, block, ways, near_width, slice_width):
@@ -323,12 +329,13 @@
     kv_width = KVH * HD
     if block % LANES == 0 and near_width % block == 0 and slice_width % block == 0:
         piece = jax.ShapeDtypeStruct((count, 2 * near_width + slice_width), jnp.float32)
+        sent = jax.ShapeDtypeStruct((count, 3 * near_width + slice_width), jnp.bfloat16)
         kernel = functools.partial(
             pack_kernel, pairs, ways, near_width // block, slice_width // block
         )
         return pl.pallas_call(
             kernel,
-            out_shape=[piece] * ways,
+            out_shape=[piece] + [sent] * (ways - 1),
             in_specs=[SMEM] + [VMEM] * pairs,
             out_specs=[VMEM] * ways,
             scratch_shapes=[pltpu.VMEM((shards, count, block), jnp.float32)],
@@ -352,6 +359,10 @@
         near = (to * per_device // (H // KVH)) * HD
         parts = [(near, near_width), (kv_width + near, near_width), (to * slice_width, slice_width)]
         cuts = [lax.dynamic_slice_in_dim(ordered, start, width, 1) for start, width in parts]
+        if d != 0:
+            rounded = [cut.astype(jnp.bfloat16) for cut in cuts]
+            rest = (cuts[0] - rounded[0].astype(jnp.float32)).astype(jnp.bfloat16)
+            cuts = [rounded[0], rest] + rounded[1:]
         pieces.append(jnp.concatenate(cuts, axis=1))
     return pieces
 
@@ -364,7 +375,9 @@
     span = chunks * height
     summed = pieces[0][...]
     for piece in pieces[1:]:
-        summed = summed + piece[...]
+        came = piece[...].astype(jnp.float32)
+        keys = came[:, :near_width] + came[:, near_width : 2 * near_width]
+        summed = summed + jnp.concatenate([keys, came[:, 2 * near_width :]], axis=1)
     stored = summed.astype(jnp.bfloat16)
     new_ref[...] = stored[:, 2 * near_width :]
     near = stored[:, : 2 * near_width].astype(jnp.float32)

time: 30.4 us -> 30.1 us (level)
  no operation moved by 1% of the time
where the time goes in v14:
time: 30.1 us; the launch traced here: 30 us
  starting transfers between devices  16.9 us (56%)
  Pallas kernels  7.26 us (24%)
  waiting for transfers between devices  5.07 us (17%)
  between operations  0.71 us (2%)
    ppermute x13, starting transfers between devices, swap(): return lax.ppermute(x, axis, [(k, k ^ distance) for k in range(size)])  16.9 us
    ppermute x13, waiting for transfers between devices, swap(): return lax.ppermute(x, axis, [(k, k ^ distance) for k in range(size)])  5.07 us
    pallas_call x1, Pallas kernels, prepare(): pl.pallas_call(functools.partial(prepare_kernel, rows, steps, own, min(ow...  3.29 us
    pallas_call x1, Pallas kernels, project(): pl.pallas_call(functools.partial(project_kernel, pairs), out_shape=[jax.S...  1.29 us
    pallas_call x1, Pallas kernels, finish(): pl.pallas_call(functools.partial(finish_kernel, rows, steps, own, min(own...  1.06 us
  transfers between devices with their start and end apart: 13, of which 5 were waited for; matrix products, arithmetic and copies ran while one was open for 0% of the time, Pallas kernels for 21%

profile of v14, /device:TPU:0, one launch (start us, length us, event | category | flops | bytes accessed | tf_op | source)
XLA Modules:
  0.0 30.0 jit_solution(1285068897811206368)
XLA Ops:
  0.6 0.5 %collective-permute-start.3 = (bf16[256,2048]{1,0:T(8,128)(2,1)}, bf16[256,2048]{1,0:T(8,128)(2,1)S(1)}, u32[]{:S(2)}, u32[]{:S(2)}) collective-permute-start(bf16[256,2048]{1,0:T(8,128)(2,1)} %codes_hbm.1), channel_id=1, source_target_pairs={{0,4},{4,0},{8,12},{12,8},{16,20},{20,16},{24,28},{28,24},{1,5},{5... | collective-permute-start | bytes 3145736 | tf_op jit(solution)/shard_map/ppermute | solution.py:73
  1.1 4.7 %collective-permute-start.2 = (bf16[16,2048]{1,0:T(8,128)(2,1)}, bf16[16,2048]{1,0:T(8,128)(2,1)S(1)}, u32[]{:S(2)}, u32[]{:S(2)}) collective-permute-start(bf16[16,2048]{1,0:T(8,128)(2,1)} %bitcast.7), channel_id=1, source_target_pairs={{0,24},{4,28},{8,16},{12,20},{16,8},{20,12},{24,0},{28,4},{1,25},{... | collective-permute-start | bytes 196616 | tf_op jit(solution)/shard_map/ppermute | solution.py:73
  5.8 0.0 collective-permute-start.1
  5.8 0.6 %collective-permute-start = (bf16[16,2048]{1,0:T(8,128)(2,1)}, bf16[16,2048]{1,0:T(8,128)(2,1)S(1)}, u32[]{:S(2)}, u32[]{:S(2)}) collective-permute-start(bf16[16,2048]{1,0:T(8,128)(2,1)} %bitcast.9), channel_id=1, source_target_pairs={{0,8},{4,12},{8,0},{12,4},{16,24},{20,28},{24,16},{28,20},{1,9},{5... | collective-permute-start | bytes 196616 | tf_op jit(solution)/shard_map/ppermute | solution.py:73
  6.5 0.0 collective-permute-start.4
  6.5 3.3 %prepare.1 = (bf16[256,2048]{1,0:T(8,128)(2,1)S(1)}, bf16[2,256,2048]{2,1,0:T(8,128)(2,1)S(1)}, bf16[256,128]{1,0:T(8,128)(2,1)S(1)}, f32[2,264,128]{2,1,0:T(8,128)S(1)}, bf16[2,272,128]{2,1,0:T(8,128)(2,1)S(1)}) custom-call(s32[8]{0:T(128)} %owner_ref.1, s32[2]{0:T(128)} %lengths_hbm.1, bf16[16,256]{1,0:T(8,128)(2,1)} %bitcast.14, ...), custom_call_target="tpu_custom_call" | custom-call | bytes 120000000 | tf_op jit(solution)/shard_map/prepare/pallas_call | solution.py:212
  9.8 0.0 copy-start
  9.8 0.0 collective-permute-done.4
  9.8 0.0 collective-permute-done.3.codes_ref
  9.8 0.5 %mate_weights.1.mate_ref = bf16[256,2048]{1,0:T(8,128)(2,1)S(1)} custom-call(bf16[256,2048]{1,0:T(8,128)(2,1)S(1)} %collective-permute-done.3.codes_ref, bf16[16,256]{1,0:T(8,128)(2,1)S(1)} %bitcast.11), custom_call_target="tpu_custom_call" | custom-call | bytes 1000 | tf_op jit(solution)/shard_map/mate_weights/pallas_call | solution.py:98
  10.3 0.0 collective-permute-done.2.refs_3_
  10.3 1.8 %collective-permute-done.1.refs_2_ = bf16[16,2048]{1,0:T(8,128)(2,1)S(1)} collective-permute-done((bf16[16,2048]{1,0:T(8,128)(2,1)}, bf16[16,2048]{1,0:T(8,128)(2,1)S(1)}, u32[]{:S(2)}, u32[]{:S(2)}) %collective-permute-start.1) | collective-permute-done | bytes 65568 | tf_op jit(solution)/shard_map/ppermute | solution.py:73
  12.1 0.0 collective-permute-done.refs_1_
  12.1 1.5 %collective-permute-start.11 = (bf16[2,272,128]{2,1,0:T(8,128)(2,1)S(1)}, bf16[2,272,128]{2,1,0:T(8,128)(2,1)S(1)}, u32[]{:S(2)}, u32[]{:S(2)}) collective-permute-start(bf16[2,272,128]{2,1,0:T(8,128)(2,1)S(1)} %get-tuple-element.43), channel_id=1, source_target_pairs={{0,1},{1,0},{2,3},{3,2},{4,5},{5,4},{6,7},{7,6},{8,9},{9,8},{10,11... | collective-permute-start | bytes 417800 | tf_op jit(solution)/shard_map/ppermute | solution.py:73
  13.6 0.0 copy-done
  13.6 0.0 copy-start.1
  13.6 1.3 %project.1 = (f32[16,512]{1,0:T(8,128)S(1)}, f32[16,512]{1,0:T(8,128)S(1)}, f32[16,512]{1,0:T(8,128)S(1)}, f32[16,512]{1,0:T(8,128)S(1)}) custom-call(bf16[256,2048]{1,0:T(8,128)(2,1)S(1)} %get-tuple-element.26.own_ref, bf16[256,2048]{1,0:T(8,128)(2,1)S(1)} %mate_weights.1.mate_ref, bf16[2,256,2048]{2,1,0:T(8,128)(2,1)S(1)} %get-tuple-element.29.base_ref, ...), custom_call_target="tpu_custom_call" | custom-call | bytes 60000000 | tf_op jit(solution)/shard_map/project/pallas_call | solution.py:289
  14.9 2.5 %collective-permute-start.5 = (f32[16,512]{1,0:T(8,128)S(1)}, f32[16,512]{1,0:T(8,128)S(1)}, u32[]{:S(2)}, u32[]{:S(2)}) collective-permute-start(f32[16,512]{1,0:T(8,128)S(1)} %get-tuple-element.35), channel_id=1, source_target_pairs={{0,24},{4,28},{8,16},{12,20},{16,8},{20,12},{24,0},{28,4},{1,25},{... | collective-permute-start | bytes 98312 | tf_op jit(solution)/shard_map/ppermute | solution.py:73
  17.4 0.2 collective-permute-start.6
  17.7 1.7 %collective-permute-start.7 = (f32[16,512]{1,0:T(8,128)S(1)}, f32[16,512]{1,0:T(8,128)S(1)}, u32[]{:S(2)}, u32[]{:S(2)}) collective-permute-start(f32[16,512]{1,0:T(8,128)S(1)} %get-tuple-element.37), channel_id=1, source_target_pairs={{0,8},{4,12},{8,0},{12,4},{16,24},{20,28},{24,16},{28,20},{1,9},{5... | collective-permute-start | bytes 98312 | tf_op jit(solution)/shard_map/ppermute | solution.py:73
  19.3 0.0 collective-permute-done.11.came_ref
  19.3 0.3 %merge_partials.2 = (f32[1,264,128]{2,1,0:T(8,128)S(1)}, bf16[1,272,128]{2,1,0:T(8,128)(2,1)S(1)}) custom-call(f32[2,264,128]{2,1,0:T(8,128)S(1)} %get-tuple-element.42.kept_ref, bf16[2,272,128]{2,1,0:T(8,128)(2,1)S(1)} %collective-permute-done.11.came_ref), custom_call_target="tpu_custom_call" | custom-call | bytes 270336 | tf_op jit(solution)/shard_map/merge_partials/pallas_call | solution.py:263
  19.7 1.6 %collective-permute-start.12 = (bf16[1,272,128]{2,1,0:T(8,128)(2,1)S(1)}, bf16[1,272,128]{2,1,0:T(8,128)(2,1)S(1)}, u32[]{:S(2)}, u32[]{:S(2)}) collective-permute-start(bf16[1,272,128]{2,1,0:T(8,128)(2,1)S(1)} %get-tuple-element.45), channel_id=1, source_target_pairs={{0,2},{1,3},{2,0},{3,1},{4,6},{5,7},{6,4},{7,5},{8,10},{9,11},{10,... | collective-permute-start | bytes 208904 | tf_op jit(solution)/shard_map/ppermute | solution.py:73
  21.2 0.0 collective-permute-done.5.refs_1_
  21.2 1.0 %collective-permute-done.6.refs_2_ = f32[16,512]{1,0:T(8,128)S(1)} collective-permute-done((f32[16,512]{1,0:T(8,128)S(1)}, f32[16,512]{1,0:T(8,128)S(1)}, u32[]{:S(2)}, u32[]{:S(2)}) %collective-permute-start.6) | collective-permute-done | bytes 32800 | tf_op jit(solution)/shard_map/ppermute | solution.py:73
  22.2 0.0 collective-permute-done.7.refs_3_
  22.3 0.0 copy-done.1
  22.3 0.6 %pack_pieces.1 = (f32[16,1024]{1,0:T(8,128)S(1)}, bf16[16,1280]{1,0:T(8,128)(2,1)S(1)}, bf16[16,1280]{1,0:T(8,128)(2,1)S(1)}, bf16[16,1280]{1,0:T(8,128)(2,1)S(1)}) custom-call(s32[8]{0:T(128)S(1)} %copy-done.1, f32[16,512]{1,0:T(8,128)S(1)} %get-tuple-element.34.refs_0_, f32[16,512]{1,0:T(8,128)S(1)} %collective-permute-done.5.refs_1_, ...), custom_call_target="tpu_custom_call" | custom-call | bytes 60000000 | tf_op jit(solution)/shard_map/pack_pieces/pallas_call | solution.py:336
  22.8 1.6 %collective-permute-start.8 = (bf16[16,1280]{1,0:T(8,128)(2,1)S(1)}, bf16[16,1280]{1,0:T(8,128)(2,1)S(1)}, u32[]{:S(2)}, u32[]{:S(2)}) collective-permute-start(bf16[16,1280]{1,0:T(8,128)(2,1)S(1)} %get-tuple-element.39), channel_id=1, source_target_pairs={{0,3},{1,2},{2,1},{3,0},{4,7},{5,6},{6,5},{7,4},{8,11},{9,10},{10,... | collective-permute-start | bytes 122888 | tf_op jit(solution)/shard_map/ppermute | solution.py:73
  24.4 0.5 %collective-permute-start.9 = (bf16[16,1280]{1,0:T(8,128)(2,1)S(1)}, bf16[16,1280]{1,0:T(8,128)(2,1)S(1)}, u32[]{:S(2)}, u32[]{:S(2)}) collective-permute-start(bf16[16,1280]{1,0:T(8,128)(2,1)S(1)} %get-tuple-element.40), channel_id=1, source_target_pairs={{0,2},{1,3},{2,0},{3,1},{4,6},{5,7},{6,4},{7,5},{8,10},{9,11},{10,... | collective-permute-start | bytes 122888 | tf_op jit(solution)/shard_map/ppermute | solution.py:73
  24.9 1.5 %collective-permute-start.10 = (bf16[16,1280]{1,0:T(8,128)(2,1)S(1)}, bf16[16,1280]{1,0:T(8,128)(2,1)S(1)}, u32[]{:S(2)}, u32[]{:S(2)}) collective-permute-start(bf16[16,1280]{1,0:T(8,128)(2,1)S(1)} %get-tuple-element.41), channel_id=1, source_target_pairs={{0,1},{1,0},{2,3},{3,2},{4,5},{5,4},{6,7},{7,6},{8,9},{9,8},{10,11... | collective-permute-start | bytes 122888 | tf_op jit(solution)/shard_map/ppermute | solution.py:73
  26.4 0.0 collective-permute-done.12.came_ref
  26.4 0.3 merge_partials.3.refs_4_
  26.7 1.1 %collective-permute-done.8.refs_1_ = bf16[16,1280]{1,0:T(8,128)(2,1)S(1)} collective-permute-done((bf16[16,1280]{1,0:T(8,128)(2,1)S(1)}, bf16[16,1280]{1,0:T(8,128)(2,1)S(1)}, u32[]{:S(2)}, u32[]{:S(2)}) %collective-permute-start.8) | collective-permute-done | bytes 40992 | tf_op jit(solution)/shard_map/ppermute | solution.py:73
  27.8 0.6 %collective-permute-done.9.refs_2_ = bf16[16,1280]{1,0:T(8,128)(2,1)S(1)} collective-permute-done((bf16[16,1280]{1,0:T(8,128)(2,1)S(1)}, bf16[16,1280]{1,0:T(8,128)(2,1)S(1)}, u32[]{:S(2)}, u32[]{:S(2)}) %collective-permute-start.9) | collective-permute-done | bytes 40992 | tf_op jit(solution)/shard_map/ppermute | solution.py:73
  28.4 0.5 %collective-permute-done.10.refs_3_ = bf16[16,1280]{1,0:T(8,128)(2,1)S(1)} collective-permute-done((bf16[16,1280]{1,0:T(8,128)(2,1)S(1)}, bf16[16,1280]{1,0:T(8,128)(2,1)S(1)}, u32[]{:S(2)}, u32[]{:S(2)}) %collective-permute-start.10) | collective-permute-done | bytes 40992 | tf_op jit(solution)/shard_map/ppermute | solution.py:73
  28.9 1.1 %finish.1 = (bf16[16,512]{1,0:T(8,128)(2,1)}, bf16[16,2048]{1,0:T(8,128)(2,1)}) custom-call(bf16[256,128]{1,0:T(8,128)(2,1)S(1)} %get-tuple-element.25.query_ref, f32[16,1024]{1,0:T(8,128)S(1)} %get-tuple-element.38.refs_0_, bf16[16,1280]{1,0:T(8,128)(2,1)S(1)} %collective-permute-done.8.refs_1_, bf16[16,1280]{1,0:T(8,128)(2,1)S(1)} %collective-permute-done.9.refs_2_, ...), custom_call_target="tpu_custom_call" | custom-call | tf_op jit(solution)/shard_map/finish/pallas_call | solution.py:434
Async XLA Ops:
  0.6 9.2 %collective-permute-start.3 = (bf16[256,2048]{1,0:T(8,128)(2,1)}, bf16[256,2048]{1,0:T(8,128)(2,1)S(1)}, u32[]{:S(2)}, u32[]{:S(2)}) collective-permute-start(bf16[256,2048]{1,0:T(8,128)(2,1)} %codes_hbm.1), channel_id=1, source_target_pairs={{0,4},{4,0},{8,12},{12,8},{16,20},{20,16},{24,28},{28,24},{1,5},{5... | collective-permute-start | bytes 3145736 | tf_op jit(solution)/shard_map/ppermute | solution.py:73
  1.1 9.1 %collective-permute-start.2 = (bf16[16,2048]{1,0:T(8,128)(2,1)}, bf16[16,2048]{1,0:T(8,128)(2,1)S(1)}, u32[]{:S(2)}, u32[]{:S(2)}) collective-permute-start(bf16[16,2048]{1,0:T(8,128)(2,1)} %bitcast.7), channel_id=1, source_target_pairs={{0,24},{4,28},{8,16},{12,20},{16,8},{20,12},{24,0},{28,4},{1,25},{... | collective-permute-start | bytes 196616 | tf_op jit(solution)/shard_map/ppermute | solution.py:73
  5.8 6.3 %collective-permute-start.1 = (bf16[16,2048]{1,0:T(8,128)(2,1)}, bf16[16,2048]{1,0:T(8,128)(2,1)S(1)}, u32[]{:S(2)}, u32[]{:S(2)}) collective-permute-start(bf16[16,2048]{1,0:T(8,128)(2,1)} %bitcast.8), channel_id=1, source_target_pairs={{0,16},{4,20},{8,24},{12,28},{16,0},{20,4},{24,8},{28,12},{1,17},{... | collective-permute-start | bytes 196616 | tf_op jit(solution)/shard_map/ppermute | solution.py:73
  5.8 6.3 %collective-permute-start = (bf16[16,2048]{1,0:T(8,128)(2,1)}, bf16[16,2048]{1,0:T(8,128)(2,1)S(1)}, u32[]{:S(2)}, u32[]{:S(2)}) collective-permute-start(bf16[16,2048]{1,0:T(8,128)(2,1)} %bitcast.9), channel_id=1, source_target_pairs={{0,8},{4,12},{8,0},{12,4},{16,24},{20,28},{24,16},{28,20},{1,9},{5... | collective-permute-start | bytes 196616 | tf_op jit(solution)/shard_map/ppermute | solution.py:73
  6.5 3.3 %collective-permute-start.4 = (bf16[256,16]{0,1:T(8,128)(2,1)}, bf16[256,16]{0,1:T(8,128)(2,1)S(1)}, u32[]{:S(2)}, u32[]{:S(2)}) collective-permute-start(bf16[256,16]{0,1:T(8,128)(2,1)} %param.11), channel_id=1, source_target_pairs={{0,4},{4,0},{8,12},{12,8},{16,20},{20,16},{24,28},{28,24},{1,5},{5... | collective-permute-start | bytes 24584 | tf_op jit(solution)/shard_map/ppermute | solution.py:73
  9.8 3.8 %copy-start = (bf16[2,8,2048]{2,1,0:T(8,128)(2,1)S(1)}, bf16[2,8,2048]{2,1,0:T(8,128)(2,1)}, u32[]{:S(2)}) copy-start(bf16[2,8,2048]{2,1,0:T(8,128)(2,1)} %param.8) | copy-start | bytes 196612
  12.1 7.2 %collective-permute-start.11 = (bf16[2,272,128]{2,1,0:T(8,128)(2,1)S(1)}, bf16[2,272,128]{2,1,0:T(8,128)(2,1)S(1)}, u32[]{:S(2)}, u32[]{:S(2)}) collective-permute-start(bf16[2,272,128]{2,1,0:T(8,128)(2,1)S(1)} %get-tuple-element.43), channel_id=1, source_target_pairs={{0,1},{1,0},{2,3},{3,2},{4,5},{5,4},{6,7},{7,6},{8,9},{9,8},{10,11... | collective-permute-start | bytes 417800 | tf_op jit(solution)/shard_map/ppermute | solution.py:73
  13.6 8.7 %copy-start.1 = (s32[8]{0:T(128)S(1)}, s32[8]{0:T(128)}, u32[]{:S(2)}) copy-start(s32[8]{0:T(128)} %owner_ref.1) | copy-start | bytes 100
  14.9 6.4 %collective-permute-start.5 = (f32[16,512]{1,0:T(8,128)S(1)}, f32[16,512]{1,0:T(8,128)S(1)}, u32[]{:S(2)}, u32[]{:S(2)}) collective-permute-start(f32[16,512]{1,0:T(8,128)S(1)} %get-tuple-element.35), channel_id=1, source_target_pairs={{0,24},{4,28},{8,16},{12,20},{16,8},{20,12},{24,0},{28,4},{1,25},{... | collective-permute-start | bytes 98312 | tf_op jit(solution)/shard_map/ppermute | solution.py:73
  17.4 4.8 %collective-permute-start.6 = (f32[16,512]{1,0:T(8,128)S(1)}, f32[16,512]{1,0:T(8,128)S(1)}, u32[]{:S(2)}, u32[]{:S(2)}) collective-permute-start(f32[16,512]{1,0:T(8,128)S(1)} %get-tuple-element.36), channel_id=1, source_target_pairs={{0,16},{4,20},{8,24},{12,28},{16,0},{20,4},{24,8},{28,12},{1,17},{... | collective-permute-start | bytes 98312 | tf_op jit(solution)/shard_map/ppermute | solution.py:73
  17.7 4.6 %collective-permute-start.7 = (f32[16,512]{1,0:T(8,128)S(1)}, f32[16,512]{1,0:T(8,128)S(1)}, u32[]{:S(2)}, u32[]{:S(2)}) collective-permute-start(f32[16,512]{1,0:T(8,128)S(1)} %get-tuple-element.37), channel_id=1, source_target_pairs={{0,8},{4,12},{8,0},{12,4},{16,24},{20,28},{24,16},{28,20},{1,9},{5... | collective-permute-start | bytes 98312 | tf_op jit(solution)/shard_map/ppermute | solution.py:73
  19.7 6.7 %collective-permute-start.12 = (bf16[1,272,128]{2,1,0:T(8,128)(2,1)S(1)}, bf16[1,272,128]{2,1,0:T(8,128)(2,1)S(1)}, u32[]{:S(2)}, u32[]{:S(2)}) collective-permute-start(bf16[1,272,128]{2,1,0:T(8,128)(2,1)S(1)} %get-tuple-element.45), channel_id=1, source_target_pairs={{0,2},{1,3},{2,0},{3,1},{4,6},{5,7},{6,4},{7,5},{8,10},{9,11},{10,... | collective-permute-start | bytes 208904 | tf_op jit(solution)/shard_map/ppermute | solution.py:73
  22.8 5.0 %collective-permute-start.8 = (bf16[16,1280]{1,0:T(8,128)(2,1)S(1)}, bf16[16,1280]{1,0:T(8,128)(2,1)S(1)}, u32[]{:S(2)}, u32[]{:S(2)}) collective-permute-start(bf16[16,1280]{1,0:T(8,128)(2,1)S(1)} %get-tuple-element.39), channel_id=1, source_target_pairs={{0,3},{1,2},{2,1},{3,0},{4,7},{5,6},{6,5},{7,4},{8,11},{9,10},{10,... | collective-permute-start | bytes 122888 | tf_op jit(solution)/shard_map/ppermute | solution.py:73
  24.4 4.0 %collective-permute-start.9 = (bf16[16,1280]{1,0:T(8,128)(2,1)S(1)}, bf16[16,1280]{1,0:T(8,128)(2,1)S(1)}, u32[]{:S(2)}, u32[]{:S(2)}) collective-permute-start(bf16[16,1280]{1,0:T(8,128)(2,1)S(1)} %get-tuple-element.40), channel_id=1, source_target_pairs={{0,2},{1,3},{2,0},{3,1},{4,6},{5,7},{6,4},{7,5},{8,10},{9,11},{10,... | collective-permute-start | bytes 122888 | tf_op jit(solution)/shard_map/ppermute | solution.py:73
  24.9 4.0 %collective-permute-start.10 = (bf16[16,1280]{1,0:T(8,128)(2,1)S(1)}, bf16[16,1280]{1,0:T(8,128)(2,1)S(1)}, u32[]{:S(2)}, u32[]{:S(2)}) collective-permute-start(bf16[16,1280]{1,0:T(8,128)(2,1)S(1)} %get-tuple-element.41), channel_id=1, source_target_pairs={{0,1},{1,0},{2,3},{3,2},{4,5},{5,4},{6,7},{7,6},{8,9},{9,8},{10,11... | collective-permute-start | bytes 122888 | tf_op jit(solution)/shard_map/ppermute | solution.py:73

commit v15 on v12

--- a/solution.py
+++ b/solution.py
@@ -308,15 +308,21 @@
     for piece, d in zip(arrived, distances(pairs)):
         for k in range(2):
             ordered[owner_ref[place ^ (2 * d + k)]] = piece[:, k * block : (k + 1) * block]
+    def put(out, at, values):
+        out[:, at : at + block] = values.astype(out.dtype)
+
     for out, d in zip(outs, distances(ways)):
         to = to_place ^ d
         for n in range(near):
-            out[:, n * block : (n + 1) * block] = ordered[to * near + n]
-            at = (near + n) * block
-            out[:, at : at + block] = ordered[shards // 2 + to * near + n]
+            key = ordered[to * near + n]
+            put(out, n * block, key)
+            if d != 0:
+                put(out, (near + n) * block, key - key.astype(out.dtype).astype(jnp.float32))
+        start = out.shape[1] - (near + wide) * block
+        for n in range(near):
+            put(out, start + n * block, ordered[shards // 2 + to * near + n])
         for n in range(wide):
-            at = (2 * near + n) * block
-            out[:, at : at + block] = ordered[to * wide + n]
+            put(out, start + (near + n) * block, ordered[to * wide + n])
 
 
 def pack_pieces(owner_map, arrived, block, ways, near_width, slice_width):
@@ -326,12 +332,13 @@
     kv_width = KVH * HD
     if block % LANES == 0 and near_width % block == 0 and slice_width % block == 0:
         piece = jax.ShapeDtypeStruct((count, 2 * near_width + slice_width), jnp.float32)
+        sent = jax.ShapeDtypeStruct((count, 3 * near_width + slice_width), jnp.bfloat16)
         kernel = functools.partial(
             pack_kernel, pairs, ways, near_width // block, slice_width // block
         )
         return pl.pallas_call(
             kernel,
-            out_shape=[piece] * ways,
+            out_shape=[piece] + [sent] * (ways - 1),
             in_specs=[SMEM] + [VMEM] * pairs,
             out_specs=[VMEM] * ways,
             scratch_shapes=[pltpu.VMEM((shards, count, block), jnp.float32)],
@@ -355,6 +362,10 @@
         near = (to * per_device // (H // KVH)) * HD
         parts = [(near, near_width), (kv_width + near, near_width), (to * slice_width, slice_width)]
         cuts = [lax.dynamic_slice_in_dim(ordered, start, width, 1) for start, width in parts]
+        if d != 0:
+            rounded = [cut.astype(jnp.bfloat16) for cut in cuts]
+            rest = (cuts[0] - rounded[0].astype(jnp.float32)).astype(jnp.bfloat16)
+            cuts = [rounded[0], rest] + rounded[1:]
         pieces.append(jnp.concatenate(cuts, axis=1))
     return pieces
 
@@ -367,7 +378,9 @@
     span = chunks * height
     summed = pieces[0][...]
     for piece in pieces[1:]:
-        summed = summed + piece[...]
+        came = piece[...].astype(jnp.float32)
+        keys = came[:, :near_width] + came[:, near_width : 2 * near_width]
+        summed = summed + jnp.concatenate([keys, came[:, 2 * near_width :]], axis=1)
     stored = summed.astype(jnp.bfloat16)
     new_ref[...] = stored[:, 2 * near_width :]
     near = stored[:, : 2 * near_width].astype(jnp.float32)
@@ -481,7 +494,7 @@
     partials = exchange(partials, "tensor", 1)
     pieces = pack_pieces(owner_map, arrived, owner_block, tensor_count, near_width, slice_width)
     pieces = exchange(pieces, "tensor", 1)
-    partial = merge(partials, rows)
+    partial = merge(near_first(partials), rows)
     new_out, attended = finish(own_query, pieces, partial, rows, steps, heads_own, near_width)
     return (new_out.reshape(rows, steps, -1), attended.reshape(rows, steps, -1))
 

time: 30.9 us -> 29.7 us (0.961)
  waiting for transfers between devices: 5.09 us -> 2.48 us
  starting transfers between devices: 17.9 us -> 19.4 us
    ppermute x14, waiting for transfers between devices: 5.09 us -> 2.48 us  [swap(): return lax.ppermute(x, axis, [(k, k ^ distance) for k in range(size)])]
    ppermute x14, starting transfers between devices: 17.9 us -> 19.4 us  [swap(): return lax.ppermute(x, axis, [(k, k ^ distance) for k in range(size)])]
  transfers between devices with their start and end apart: 14 -> 14, of which waited for: 5 -> 5; matrix products, arithmetic and copies ran while one was open for 0% -> 0% of each run, Pallas kernels for 19% -> 20%
where the time goes in v15:
time: 29.7 us; the launch traced here: 29.6 us
  starting transfers between devices  19.4 us (65%)
  Pallas kernels  7.05 us (24%)
  waiting for transfers between devices  2.48 us (8%)
  between operations  0.69 us (2%)
    ppermute x14, starting transfers between devices, swap(): return lax.ppermute(x, axis, [(k, k ^ distance) for k in range(size)])  19.4 us
    pallas_call x1, Pallas kernels, prepare(): pl.pallas_call(functools.partial(prepare_kernel, rows, steps, own, min(ow...  3.29 us
    ppermute x14, waiting for transfers between devices, swap(): return lax.ppermute(x, axis, [(k, k ^ distance) for k in range(size)])  2.48 us
    pallas_call x1, Pallas kernels, project(): pl.pallas_call(functools.partial(project_kernel, pairs), out_shape=[jax.S...  1.3 us
    pallas_call x1, Pallas kernels, finish(): pl.pallas_call(functools.partial(finish_kernel, rows, steps, own, min(own...  1.06 us
  transfers between devices with their start and end apart: 14, of which 5 were waited for; matrix products, arithmetic and copies ran while one was open for 0% of the time, Pallas kernels for 20%

profile of v15, /device:TPU:0, one launch (start us, length us, event | category | flops | bytes accessed | tf_op | source)
XLA Modules:
  0.0 29.6 jit_solution(10775133120969480756)
XLA Ops:
  0.6 0.5 %collective-permute-start.3 = (bf16[256,2048]{1,0:T(8,128)(2,1)}, bf16[256,2048]{1,0:T(8,128)(2,1)S(1)}, u32[]{:S(2)}, u32[]{:S(2)}) collective-permute-start(bf16[256,2048]{1,0:T(8,128)(2,1)} %codes_hbm.1), channel_id=1, source_target_pairs={{0,4},{4,0},{8,12},{12,8},{16,20},{20,16},{24,28},{28,24},{1,5},{5... | collective-permute-start | bytes 3145736 | tf_op jit(solution)/shard_map/ppermute | solution.py:73
  1.1 4.7 %collective-permute-start.2 = (bf16[16,2048]{1,0:T(8,128)(2,1)}, bf16[16,2048]{1,0:T(8,128)(2,1)S(1)}, u32[]{:S(2)}, u32[]{:S(2)}) collective-permute-start(bf16[16,2048]{1,0:T(8,128)(2,1)} %bitcast.7), channel_id=1, source_target_pairs={{0,24},{4,28},{8,16},{12,20},{16,8},{20,12},{24,0},{28,4},{1,25},{... | collective-permute-start | bytes 196616 | tf_op jit(solution)/shard_map/ppermute | solution.py:73
  5.8 0.0 collective-permute-start.1
  5.8 0.6 %collective-permute-start = (bf16[16,2048]{1,0:T(8,128)(2,1)}, bf16[16,2048]{1,0:T(8,128)(2,1)S(1)}, u32[]{:S(2)}, u32[]{:S(2)}) collective-permute-start(bf16[16,2048]{1,0:T(8,128)(2,1)} %bitcast.9), channel_id=1, source_target_pairs={{0,8},{4,12},{8,0},{12,4},{16,24},{20,28},{24,16},{28,20},{1,9},{5... | collective-permute-start | bytes 196616 | tf_op jit(solution)/shard_map/ppermute | solution.py:73
  6.5 0.0 collective-permute-start.4
  6.5 3.3 %prepare.1 = (bf16[256,2048]{1,0:T(8,128)(2,1)S(1)}, bf16[2,256,2048]{2,1,0:T(8,128)(2,1)S(1)}, bf16[256,128]{1,0:T(8,128)(2,1)S(1)}, f32[264,128]{1,0:T(8,128)S...) custom-call(s32[8]{0:T(128)} %owner_ref.1, s32[2]{0:T(128)} %lengths_hbm.1, ...), custom_call_target="tpu_custom_call" | custom-call | bytes 120000000 | tf_op jit(solution)/shard_map/prepare/pallas_call | solution.py:214
  9.8 0.0 copy-start
  9.8 0.0 collective-permute-done.4
  9.8 1.7 %collective-permute-start.11 = (bf16[272,128]{1,0:T(8,128)(2,1)S(1)}, bf16[272,128]{1,0:T(8,128)(2,1)S(1)}, u32[]{:S(2)}, u32[]{:S(2)}) collective-permute-start(bf16[272,128]{1,0:T(8,128)(2,1)S(1)} %get-tuple-element.43), channel_id=1, source_target_pairs={{0,1},{1,0},{2,3},{3,2},{4,5},{5,4},{6,7},{7,6},{8,9},{9,8},{10,11... | collective-permute-start | bytes 208904 | tf_op jit(solution)/shard_map/ppermute | solution.py:73
  11.5 0.0 collective-permute-done.3.codes_ref
  11.5 0.5 %mate_weights.1.mate_ref = bf16[256,2048]{1,0:T(8,128)(2,1)S(1)} custom-call(bf16[256,2048]{1,0:T(8,128)(2,1)S(1)} %collective-permute-done.3.codes_ref, bf16[16,256]{1,0:T(8,128)(2,1)S(1)} %bitcast.11), custom_call_target="tpu_custom_call" | custom-call | bytes 1000 | tf_op jit(solution)/shard_map/mate_weights/pallas_call | solution.py:98
  12.0 0.0 collective-permute-done.2.refs_3_
  12.0 0.1 collective-permute-done.1.refs_2_
  12.1 0.0 collective-permute-done.refs_1_
  12.1 0.0 copy-done
  12.1 0.0 copy-start.1
  12.1 1.3 %project.1 = (f32[16,512]{1,0:T(8,128)S(1)}, f32[16,512]{1,0:T(8,128)S(1)}, f32[16,512]{1,0:T(8,128)S(1)}, f32[16,512]{1,0:T(8,128)S(1)}) custom-call(bf16[256,2048]{1,0:T(8,128)(2,1)S(1)} %get-tuple-element.27.own_ref, bf16[256,2048]{1,0:T(8,128)(2,1)S(1)} %mate_weights.1.mate_ref, bf16[2,256,2048]{2,1,0:T(8,128)(2,1)S(1)} %get-tuple-element.29.base_ref, ...), custom_call_target="tpu_custom_call" | custom-call | bytes 60000000 | tf_op jit(solution)/shard_map/project/pallas_call | solution.py:292
  13.4 3.6 %collective-permute-start.5 = (f32[16,512]{1,0:T(8,128)S(1)}, f32[16,512]{1,0:T(8,128)S(1)}, u32[]{:S(2)}, u32[]{:S(2)}) collective-permute-start(f32[16,512]{1,0:T(8,128)S(1)} %get-tuple-element.35), channel_id=1, source_target_pairs={{0,24},{4,28},{8,16},{12,20},{16,8},{20,12},{24,0},{28,4},{1,25},{... | collective-permute-start | bytes 98312 | tf_op jit(solution)/shard_map/ppermute | solution.py:73
  17.0 0.0 collective-permute-start.6
  17.0 0.9 %collective-permute-start.7 = (f32[16,512]{1,0:T(8,128)S(1)}, f32[16,512]{1,0:T(8,128)S(1)}, u32[]{:S(2)}, u32[]{:S(2)}) collective-permute-start(f32[16,512]{1,0:T(8,128)S(1)} %get-tuple-element.37), channel_id=1, source_target_pairs={{0,8},{4,12},{8,0},{12,4},{16,24},{20,28},{24,16},{28,20},{1,9},{5... | collective-permute-start | bytes 98312 | tf_op jit(solution)/shard_map/ppermute | solution.py:73
  17.9 1.5 %collective-permute-start.12 = (bf16[272,128]{1,0:T(8,128)(2,1)S(1)}, bf16[272,128]{1,0:T(8,128)(2,1)S(1)}, u32[]{:S(2)}, u32[]{:S(2)}) collective-permute-start(bf16[272,128]{1,0:T(8,128)(2,1)S(1)} %get-tuple-element.44), channel_id=1, source_target_pairs={{0,2},{1,3},{2,0},{3,1},{4,6},{5,7},{6,4},{7,5},{8,10},{9,11},{10,... | collective-permute-start | bytes 208904 | tf_op jit(solution)/shard_map/ppermute | solution.py:73
  19.4 0.0 collective-permute-done.5.refs_1_
  19.4 2.3 %collective-permute-start.13 = (bf16[272,128]{1,0:T(8,128)(2,1)S(1)}, bf16[272,128]{1,0:T(8,128)(2,1)S(1)}, u32[]{:S(2)}, u32[]{:S(2)}) collective-permute-start(bf16[272,128]{1,0:T(8,128)(2,1)S(1)} %get-tuple-element.45), channel_id=1, source_target_pairs={{0,3},{1,2},{2,1},{3,0},{4,7},{5,6},{6,5},{7,4},{8,11},{9,10},{10,... | collective-permute-start | bytes 208904 | tf_op jit(solution)/shard_map/ppermute | solution.py:73
  21.7 0.1 collective-permute-done.6.refs_2_
  21.8 0.0 collective-permute-done.7.refs_3_
  21.8 0.0 copy-done.1
  21.8 0.6 %pack_pieces.1 = (f32[16,1024]{1,0:T(8,128)S(1)}, bf16[16,1280]{1,0:T(8,128)(2,1)S(1)}, bf16[16,1280]{1,0:T(8,128)(2,1)S(1)}, bf16[16,1280]{1,0:T(8,128)(2,1)S(1)}) custom-call(s32[8]{0:T(128)S(1)} %copy-done.1, f32[16,512]{1,0:T(8,128)S(1)} %get-tuple-element.34.refs_0_, f32[16,512]{1,0:T(8,128)S(1)} %collective-permute-done.5.refs_1_, ...), custom_call_target="tpu_custom_call" | custom-call | bytes 60000000 | tf_op jit(solution)/shard_map/pack_pieces/pallas_call | solution.py:339
  22.4 1.6 %collective-permute-start.8 = (bf16[16,1280]{1,0:T(8,128)(2,1)S(1)}, bf16[16,1280]{1,0:T(8,128)(2,1)S(1)}, u32[]{:S(2)}, u32[]{:S(2)}) collective-permute-start(bf16[16,1280]{1,0:T(8,128)(2,1)S(1)} %get-tuple-element.39), channel_id=1, source_target_pairs={{0,3},{1,2},{2,1},{3,0},{4,7},{5,6},{6,5},{7,4},{8,11},{9,10},{10,... | collective-permute-start | bytes 122888 | tf_op jit(solution)/shard_map/ppermute | solution.py:73
  23.9 0.6 %collective-permute-start.9 = (bf16[16,1280]{1,0:T(8,128)(2,1)S(1)}, bf16[16,1280]{1,0:T(8,128)(2,1)S(1)}, u32[]{:S(2)}, u32[]{:S(2)}) collective-permute-start(bf16[16,1280]{1,0:T(8,128)(2,1)S(1)} %get-tuple-element.40), channel_id=1, source_target_pairs={{0,2},{1,3},{2,0},{3,1},{4,6},{5,7},{6,4},{7,5},{8,10},{9,11},{10,... | collective-permute-start | bytes 122888 | tf_op jit(solution)/shard_map/ppermute | solution.py:73
  24.5 0.0 collective-permute-done.11.refs_1_
  24.5 1.4 %collective-permute-start.10 = (bf16[16,1280]{1,0:T(8,128)(2,1)S(1)}, bf16[16,1280]{1,0:T(8,128)(2,1)S(1)}, u32[]{:S(2)}, u32[]{:S(2)}) collective-permute-start(bf16[16,1280]{1,0:T(8,128)(2,1)S(1)} %get-tuple-element.41), channel_id=1, source_target_pairs={{0,1},{1,0},{2,3},{3,2},{4,5},{5,4},{6,7},{7,6},{8,9},{9,8},{10,11... | collective-permute-start | bytes 122888 | tf_op jit(solution)/shard_map/ppermute | solution.py:73
  25.9 0.0 collective-permute-done.12.refs_2_
  25.9 0.0 collective-permute-done.13.refs_3_
  26.0 0.3 %merge_partials.1.refs_4_ = f32[264,128]{1,0:T(8,128)S(1)} custom-call(f32[264,128]{1,0:T(8,128)S(1)} %get-tuple-element.42.refs_0_, bf16[272,128]{1,0:T(8,128)(2,1)S(1)} %collective-permute-done.11.refs_1_, bf16[272,128]{1,0:T(8,128)(2,1)S(1)} %collective-permute-done.12.refs_2_, bf16[272,128]{1,0:T(8,128)(2,1)S(1)} %collective-permute-done.13.refs_3_), custom_call_target="tpu_custom_call" | custom-call | bytes 1000 | tf_op jit(solution)/shard_map/merge_partials/pallas_call | solution.py:266
  26.3 1.0 %collective-permute-done.8.refs_1_ = bf16[16,1280]{1,0:T(8,128)(2,1)S(1)} collective-permute-done((bf16[16,1280]{1,0:T(8,128)(2,1)S(1)}, bf16[16,1280]{1,0:T(8,128)(2,1)S(1)}, u32[]{:S(2)}, u32[]{:S(2)}) %collective-permute-start.8) | collective-permute-done | bytes 40992 | tf_op jit(solution)/shard_map/ppermute | solution.py:73
  27.4 0.6 %collective-permute-done.9.refs_2_ = bf16[16,1280]{1,0:T(8,128)(2,1)S(1)} collective-permute-done((bf16[16,1280]{1,0:T(8,128)(2,1)S(1)}, bf16[16,1280]{1,0:T(8,128)(2,1)S(1)}, u32[]{:S(2)}, u32[]{:S(2)}) %collective-permute-start.9) | collective-permute-done | bytes 40992 | tf_op jit(solution)/shard_map/ppermute | solution.py:73
  27.9 0.6 %collective-permute-done.10.refs_3_ = bf16[16,1280]{1,0:T(8,128)(2,1)S(1)} collective-permute-done((bf16[16,1280]{1,0:T(8,128)(2,1)S(1)}, bf16[16,1280]{1,0:T(8,128)(2,1)S(1)}, u32[]{:S(2)}, u32[]{:S(2)}) %collective-permute-start.10) | collective-permute-done | bytes 40992 | tf_op jit(solution)/shard_map/ppermute | solution.py:73
  28.5 1.1 %finish.1 = (bf16[16,512]{1,0:T(8,128)(2,1)}, bf16[16,2048]{1,0:T(8,128)(2,1)}) custom-call(bf16[256,128]{1,0:T(8,128)(2,1)S(1)} %get-tuple-element.26.query_ref, f32[16,1024]{1,0:T(8,128)S(1)} %get-tuple-element.38.refs_0_, bf16[16,1280]{1,0:T(8,128)(2,1)S(1)} %collective-permute-done.8.refs_1_, bf16[16,1280]{1,0:T(8,128)(2,1)S(1)} %collective-permute-done.9.refs_2_, ...), custom_call_target="tpu_custom_call" | custom-call | tf_op jit(solution)/shard_map/finish/pallas_call | solution.py:437
Async XLA Ops:
  0.6 10.9 %collective-permute-start.3 = (bf16[256,2048]{1,0:T(8,128)(2,1)}, bf16[256,2048]{1,0:T(8,128)(2,1)S(1)}, u32[]{:S(2)}, u32[]{:S(2)}) collective-permute-start(bf16[256,2048]{1,0:T(8,128)(2,1)} %codes_hbm.1), channel_id=1, source_target_pairs={{0,4},{4,0},{8,12},{12,8},{16,20},{20,16},{24,28},{28,24},{1,5},{5... | collective-permute-start | bytes 3145736 | tf_op jit(solution)/shard_map/ppermute | solution.py:73
  1.1 10.8 %collective-permute-start.2 = (bf16[16,2048]{1,0:T(8,128)(2,1)}, bf16[16,2048]{1,0:T(8,128)(2,1)S(1)}, u32[]{:S(2)}, u32[]{:S(2)}) collective-permute-start(bf16[16,2048]{1,0:T(8,128)(2,1)} %bitcast.7), channel_id=1, source_target_pairs={{0,24},{4,28},{8,16},{12,20},{16,8},{20,12},{24,0},{28,4},{1,25},{... | collective-permute-start | bytes 196616 | tf_op jit(solution)/shard_map/ppermute | solution.py:73
  5.8 6.3 %collective-permute-start.1 = (bf16[16,2048]{1,0:T(8,128)(2,1)}, bf16[16,2048]{1,0:T(8,128)(2,1)S(1)}, u32[]{:S(2)}, u32[]{:S(2)}) collective-permute-start(bf16[16,2048]{1,0:T(8,128)(2,1)} %bitcast.8), channel_id=1, source_target_pairs={{0,16},{4,20},{8,24},{12,28},{16,0},{20,4},{24,8},{28,12},{1,17},{... | collective-permute-start | bytes 196616 | tf_op jit(solution)/shard_map/ppermute | solution.py:73
  5.8 6.3 %collective-permute-start = (bf16[16,2048]{1,0:T(8,128)(2,1)}, bf16[16,2048]{1,0:T(8,128)(2,1)S(1)}, u32[]{:S(2)}, u32[]{:S(2)}) collective-permute-start(bf16[16,2048]{1,0:T(8,128)(2,1)} %bitcast.9), channel_id=1, source_target_pairs={{0,8},{4,12},{8,0},{12,4},{16,24},{20,28},{24,16},{28,20},{1,9},{5... | collective-permute-start | bytes 196616 | tf_op jit(solution)/shard_map/ppermute | solution.py:73
  6.5 3.3 %collective-permute-start.4 = (bf16[256,16]{0,1:T(8,128)(2,1)}, bf16[256,16]{0,1:T(8,128)(2,1)S(1)}, u32[]{:S(2)}, u32[]{:S(2)}) collective-permute-start(bf16[256,16]{0,1:T(8,128)(2,1)} %param.11), channel_id=1, source_target_pairs={{0,4},{4,0},{8,12},{12,8},{16,20},{20,16},{24,28},{28,24},{1,5},{5... | collective-permute-start | bytes 24584 | tf_op jit(solution)/shard_map/ppermute | solution.py:73
  9.8 2.3 %copy-start = (bf16[2,8,2048]{2,1,0:T(8,128)(2,1)S(1)}, bf16[2,8,2048]{2,1,0:T(8,128)(2,1)}, u32[]{:S(2)}) copy-start(bf16[2,8,2048]{2,1,0:T(8,128)(2,1)} %param.8) | copy-start | bytes 196612
  9.8 14.7 %collective-permute-start.11 = (bf16[272,128]{1,0:T(8,128)(2,1)S(1)}, bf16[272,128]{1,0:T(8,128)(2,1)S(1)}, u32[]{:S(2)}, u32[]{:S(2)}) collective-permute-start(bf16[272,128]{1,0:T(8,128)(2,1)S(1)} %get-tuple-element.43), channel_id=1, source_target_pairs={{0,1},{1,0},{2,3},{3,2},{4,5},{5,4},{6,7},{7,6},{8,9},{9,8},{10,11... | collective-permute-start | bytes 208904 | tf_op jit(solution)/shard_map/ppermute | solution.py:73
  12.1 9.7 %copy-start.1 = (s32[8]{0:T(128)S(1)}, s32[8]{0:T(128)}, u32[]{:S(2)}) copy-start(s32[8]{0:T(128)} %owner_ref.1) | copy-start | bytes 100
  13.4 6.0 %collective-permute-start.5 = (f32[16,512]{1,0:T(8,128)S(1)}, f32[16,512]{1,0:T(8,128)S(1)}, u32[]{:S(2)}, u32[]{:S(2)}) collective-permute-start(f32[16,512]{1,0:T(8,128)S(1)} %get-tuple-element.35), channel_id=1, source_target_pairs={{0,24},{4,28},{8,16},{12,20},{16,8},{20,12},{24,0},{28,4},{1,25},{... | collective-permute-start | bytes 98312 | tf_op jit(solution)/shard_map/ppermute | solution.py:73
  17.0 4.8 %collective-permute-start.6 = (f32[16,512]{1,0:T(8,128)S(1)}, f32[16,512]{1,0:T(8,128)S(1)}, u32[]{:S(2)}, u32[]{:S(2)}) collective-permute-start(f32[16,512]{1,0:T(8,128)S(1)} %get-tuple-element.36), channel_id=1, source_target_pairs={{0,16},{4,20},{8,24},{12,28},{16,0},{20,4},{24,8},{28,12},{1,17},{... | collective-permute-start | bytes 98312 | tf_op jit(solution)/shard_map/ppermute | solution.py:73
  17.0 4.8 %collective-permute-start.7 = (f32[16,512]{1,0:T(8,128)S(1)}, f32[16,512]{1,0:T(8,128)S(1)}, u32[]{:S(2)}, u32[]{:S(2)}) collective-permute-start(f32[16,512]{1,0:T(8,128)S(1)} %get-tuple-element.37), channel_id=1, source_target_pairs={{0,8},{4,12},{8,0},{12,4},{16,24},{20,28},{24,16},{28,20},{1,9},{5... | collective-permute-start | bytes 98312 | tf_op jit(solution)/shard_map/ppermute | solution.py:73
  17.9 8.1 %collective-permute-start.12 = (bf16[272,128]{1,0:T(8,128)(2,1)S(1)}, bf16[272,128]{1,0:T(8,128)(2,1)S(1)}, u32[]{:S(2)}, u32[]{:S(2)}) collective-permute-start(bf16[272,128]{1,0:T(8,128)(2,1)S(1)} %get-tuple-element.44), channel_id=1, source_target_pairs={{0,2},{1,3},{2,0},{3,1},{4,6},{5,7},{6,4},{7,5},{8,10},{9,11},{10,... | collective-permute-start | bytes 208904 | tf_op jit(solution)/shard_map/ppermute | solution.py:73
  19.4 6.5 %collective-permute-start.13 = (bf16[272,128]{1,0:T(8,128)(2,1)S(1)}, bf16[272,128]{1,0:T(8,128)(2,1)S(1)}, u32[]{:S(2)}, u32[]{:S(2)}) collective-permute-start(bf16[272,128]{1,0:T(8,128)(2,1)S(1)} %get-tuple-element.45), channel_id=1, source_target_pairs={{0,3},{1,2},{2,1},{3,0},{4,7},{5,6},{6,5},{7,4},{8,11},{9,10},{10,... | collective-permute-start | bytes 208904 | tf_op jit(solution)/shard_map/ppermute | solution.py:73
  22.4 5.0 %collective-permute-start.8 = (bf16[16,1280]{1,0:T(8,128)(2,1)S(1)}, bf16[16,1280]{1,0:T(8,128)(2,1)S(1)}, u32[]{:S(2)}, u32[]{:S(2)}) collective-permute-start(bf16[16,1280]{1,0:T(8,128)(2,1)S(1)} %get-tuple-element.39), channel_id=1, source_target_pairs={{0,3},{1,2},{2,1},{3,0},{4,7},{5,6},{6,5},{7,4},{8,11},{9,10},{10,... | collective-permute-start | bytes 122888 | tf_op jit(solution)/shard_map/ppermute | solution.py:73
  23.9 4.0 %collective-permute-start.9 = (bf16[16,1280]{1,0:T(8,128)(2,1)S(1)}, bf16[16,1280]{1,0:T(8,128)(2,1)S(1)}, u32[]{:S(2)}, u32[]{:S(2)}) collective-permute-start(bf16[16,1280]{1,0:T(8,128)(2,1)S(1)} %get-tuple-element.40), channel_id=1, source_target_pairs={{0,2},{1,3},{2,0},{3,1},{4,6},{5,7},{6,4},{7,5},{8,10},{9,11},{10,... | collective-permute-start | bytes 122888 | tf_op jit(solution)/shard_map/ppermute | solution.py:73
  24.5 4.0 %collective-permute-start.10 = (bf16[16,1280]{1,0:T(8,128)(2,1)S(1)}, bf16[16,1280]{1,0:T(8,128)(2,1)S(1)}, u32[]{:S(2)}, u32[]{:S(2)}) collective-permute-start(bf16[16,1280]{1,0:T(8,128)(2,1)S(1)} %get-tuple-element.41), channel_id=1, source_target_pairs={{0,1},{1,0},{2,3},{3,2},{4,5},{5,4},{6,7},{7,6},{8,9},{9,8},{10,11... | collective-permute-start | bytes 122888 | tf_op jit(solution)/shard_map/ppermute | solution.py:73

commit v16 on v15

--- a/solution.py
+++ b/solution.py
@@ -16,6 +16,7 @@
 
 NEGATIVE = -1e30
 SCORE_SCALE = HD ** (-0.5)
+PART = 64
 CACHE_HINT = 120_000_000
 PROJECT_HINT = 60_000_000
 PACK_HINT = 60_000_000
@@ -111,38 +112,49 @@
     owner_hbm, lengths_hbm, scales_hbm, codes_hbm, query_hbm, cache_hbm, base_hbm,
     *refs,
 ):
-    delta_ref, base_ref, own_query_ref, parts = refs[0], refs[1], refs[2], refs[3:-7]
+    delta_ref, base_ref, own_query_ref, places_ref = refs[:4]
+    parts = refs[4:-7]
     owner_ref, lengths_ref, scales_ref, codes_ref, query_ref, cache_ref, arrived = refs[-7:]
     order = distances(len(parts))
     place = lax.axis_index("tensor")
     block = codes_ref.shape[0]
     cache_len = cache_ref.shape[0] // rows
-    owner_load = pltpu.make_async_copy(owner_hbm, owner_ref, arrived.at[0])
-    first_loads = [
-        pltpu.make_async_copy(lengths_hbm, lengths_ref, arrived.at[1]),
-        pltpu.make_async_copy(scales_hbm, scales_ref, arrived.at[2]),
-        pltpu.make_async_copy(codes_hbm, codes_ref, arrived.at[3]),
-        pltpu.make_async_copy(query_hbm, query_ref, arrived.at[4]),
-    ]
+    used = []
+
+    def load(source, target):
+        copy = pltpu.make_async_copy(source, target, arrived.at[len(used)])
+        copy.start()
+        used.append(copy)
+        return [copy]
+
+    def load_rows(source, first, target, size):
+        part = min(PART, size)
+        copies = []
+        for n in range(0, size, part):
+            start = first + n if isinstance(first, int) else pl.multiple_of(first + n, part)
+            copies += load(source.at[pl.ds(start, part)], target.at[pl.ds(n, part)])
+        return copies
+
+    def wait(copies):
+        for copy in copies:
+            copy.wait()
+
+    owner_load = load(owner_hbm, owner_ref)
+    first_loads = load(lengths_hbm, lengths_ref) + load(scales_hbm, scales_ref)
+    first_loads += load_rows(codes_hbm, 0, codes_ref, block) + load(query_hbm, query_ref)
     cache_loads = []
     for r in range(rows):
-        here = pl.ds(r * cache_len, cache_len)
-        cache_loads.append(
-            pltpu.make_async_copy(cache_hbm.at[here], cache_ref.at[here], arrived.at[5 + r])
-        )
-    for load in [owner_load] + first_loads + cache_loads:
-        load.start()
-    owner_load.wait()
+        target = cache_ref.at[pl.ds(r * cache_len, cache_len)]
+        cache_loads.append(load_rows(cache_hbm, r * cache_len, target, cache_len))
+    wait(owner_load)
     base_loads = []
     for k in range(2):
-        start = owner_ref[lax.axis_index("group") ^ k] * block
-        here = pl.ds(pl.multiple_of(start, block), block)
-        base_loads.append(
-            pltpu.make_async_copy(base_hbm.at[here], base_ref.at[k], arrived.at[5 + rows + k])
-        )
-        base_loads[k].start()
-    for load in first_loads:
-        load.wait()
+        start = pl.multiple_of(owner_ref[lax.axis_index("group") ^ k] * block, block)
+        base_loads += load_rows(base_hbm, start, base_ref.at[k], block)
+    for n in range(places_ref.shape[0]):
+        owner = owner_ref[lax.axis_index("group") ^ n]
+        places_ref[n : n + 1] = jnp.full((1, LANES), owner, jnp.int32)
+    wait(first_loads)
     dequantize(codes_ref, scales_ref, delta_ref)
 
     chunks = own // chunk
@@ -176,7 +188,7 @@
         if at < len(units):
             r, n = units[at]
             if n == 0:
-                cache_loads[r].wait()
+                wait(cache_loads[r])
             ahead.append(score(r, order[n]))
         if at == 0:
             continue
@@ -197,8 +209,7 @@
         stats[n] += [peak, total]
         if r == rows - 1:
             put_stats(parts[n], stats[n])
-    for load in base_loads:
-        load.wait()
+    wait(base_loads)
 
 
 def part_shape(height, dtype):
@@ -207,6 +218,7 @@
 
 def prepare(owner_map, lengths, scales, codes, queries, cache, base, rows, steps, own, ways):
     height = rows * own * steps
+    loads = 4 + 3 * -(-codes.shape[0] // PART) + rows * -(-cache.shape[0] // rows // PART)
     operands = [
         pltpu.with_memory_space_constraint(x, pltpu.HBM)
         for x in (owner_map, lengths, scales.T, codes, queries, cache, base)
@@ -217,11 +229,12 @@
             jax.ShapeDtypeStruct(codes.shape, jnp.bfloat16),
             jax.ShapeDtypeStruct((2,) + codes.shape, jnp.bfloat16),
             jax.ShapeDtypeStruct((height, HD), jnp.bfloat16),
+            jax.ShapeDtypeStruct((owner_map.shape[0], LANES), jnp.int32),
             part_shape(height, jnp.float32),
         ]
         + [part_shape(height, jnp.bfloat16)] * (ways - 1),
         in_specs=[HBM] * len(operands),
-        out_specs=[VMEM] * (3 + ways),
+        out_specs=[VMEM] * (4 + ways),
         scratch_shapes=[
             pltpu.SMEM(owner_map.shape, owner_map.dtype),
             pltpu.SMEM(lengths.shape, lengths.dtype),
@@ -229,13 +242,13 @@
             pltpu.VMEM(codes.shape, codes.dtype),
             pltpu.VMEM(queries.shape, queries.dtype),
             pltpu.VMEM(cache.shape, cache.dtype),
-            pltpu.SemaphoreType.DMA((7 + rows,)),
+            pltpu.SemaphoreType.DMA((loads,)),
         ],
         compiler_params=params(CACHE_KIB),
         cost_estimate=hint(CACHE_HINT),
         name="prepare",
     )(*operands)
-    return out[0], out[1], out[2], out[3:]
+    return out[0], out[1], out[2], out[3], out[4:]
 
 
 def merge_kernel(rows, span, *refs):
@@ -300,32 +313,38 @@
     )(own, mate, base, *tokens)
 
 
-def pack_kernel(pairs, ways, near, wide, owner_ref, *refs):
-    arrived, outs, ordered = refs[:pairs], refs[pairs : pairs + ways], refs[-1]
-    place = lax.axis_index("group")
+def pack_kernel(pairs, ways, near, wide, block, places_ref, *refs):
+    arrived, outs = refs[:pairs], refs[pairs:]
     to_place = lax.axis_index("tensor")
-    shards, _, block = ordered.shape
+    count = arrived[0].shape[0]
+    blocks = []
     for piece, d in zip(arrived, distances(pairs)):
         for k in range(2):
-            ordered[owner_ref[place ^ (2 * d + k)]] = piece[:, k * block : (k + 1) * block]
-    def put(out, at, values):
-        out[:, at : at + block] = values.astype(out.dtype)
+            at = 2 * d + k
+            place = jnp.broadcast_to(places_ref[at : at + 1], (count, LANES))
+            lanes = [slice(n, n + LANES) for n in range(k * block, (k + 1) * block, LANES)]
+            blocks.append((place, [piece[:, one] for one in lanes]))
+
+    def pick(which):
+        out = [jnp.zeros((count, LANES), jnp.float32)] * (block // LANES)
+        for place, values in blocks:
+            out = [jnp.where(place == which, new, old) for new, old in zip(values, out)]
+        return jnp.concatenate(out, axis=1)
 
     for out, d in zip(outs, distances(ways)):
         to = to_place ^ d
-        for n in range(near):
-            key = ordered[to * near + n]
-            put(out, n * block, key)
-            if d != 0:
-                put(out, (near + n) * block, key - key.astype(out.dtype).astype(jnp.float32))
-        start = out.shape[1] - (near + wide) * block
-        for n in range(near):
-            put(out, start + n * block, ordered[shards // 2 + to * near + n])
-        for n in range(wide):
-            put(out, start + (near + n) * block, ordered[to * wide + n])
-
-
-def pack_pieces(owner_map, arrived, block, ways, near_width, slice_width):
+        columns = []
+        keys = [pick(to * near + n) for n in range(near)]
+        columns += keys
+        if d != 0:
+            columns += [key - key.astype(out.dtype).astype(jnp.float32) for key in keys]
+        columns += [pick(pairs + to * near + n) for n in range(near)]
+        columns += [pick(to * wide + n) for n in range(wide)]
+        for n, values in enumerate(columns):
+            out[:, n * block : (n + 1) * block] = values.astype(out.dtype)
+
+
+def pack_pieces(owner_map, places, arrived, block, ways, near_width, slice_width):
     pairs = len(arrived)
     count = arrived[0].shape[0]
     shards = 2 * pairs
@@ -334,18 +353,17 @@
         piece = jax.ShapeDtypeStruct((count, 2 * near_width + slice_width), jnp.float32)
         sent = jax.ShapeDtypeStruct((count, 3 * near_width + slice_width), jnp.bfloat16)
         kernel = functools.partial(
-            pack_kernel, pairs, ways, near_width // block, slice_width // block
+            pack_kernel, pairs, ways, near_width // block, slice_width // block, block
         )
         return pl.pallas_call(
             kernel,
             out_shape=[piece] + [sent] * (ways - 1),
-            in_specs=[SMEM] + [VMEM] * pairs,
+            in_specs=[VMEM] * (1 + pairs),
             out_specs=[VMEM] * ways,
-            scratch_shapes=[pltpu.VMEM((shards, count, block), jnp.float32)],
             compiler_params=params(8192),
             cost_estimate=hint(PACK_HINT),
             name="pack_pieces",
-        )(owner_map, *arrived)
+        )(places, *arrived)
     nearest = [arrived[distances(pairs).index(d)] for d in range(pairs)]
     blocks = jnp.stack(nearest, axis=0).reshape(pairs, count, 2, block).transpose(0, 2, 1, 3)
     shard_of = jnp.zeros((shards,), jnp.int32).at[owner_map].set(
@@ -473,7 +491,7 @@
     mate_codes = swap(delta_codes, "group", 1)
     mate_scales = swap(delta_scales, "group", 1)
 
-    own_delta, base_blocks, own_query, partials = prepare(
+    own_delta, base_blocks, own_query, places, partials = prepare(
         owner_map,
         lengths,
         delta_scales,
@@ -492,7 +510,9 @@
     projected = project(own_delta, mate_delta, base_blocks, near_first(token_rows))
     arrived = exchange(near_first(projected), "group", 2)
     partials = exchange(partials, "tensor", 1)
-    pieces = pack_pieces(owner_map, arrived, owner_block, tensor_count, near_width, slice_width)
+    pieces = pack_pieces(
+        owner_map, places, arrived, owner_block, tensor_count, near_width, slice_width
+    )
     pieces = exchange(pieces, "tensor", 1)
     partial = merge(near_first(partials), rows)
     new_out, attended = finish(own_query, pieces, partial, rows, steps, heads_own, near_width)

time: 29.7 us -> 29.3 us (0.987)
  Pallas kernels: 7.05 us -> 6.72 us
    pallas_call x1, Pallas kernels: 0.58 us -> 0.11 us  [pack_pieces(): pl.pallas_call(kernel, out_shape=[piece] + [sent] * (ways - 1), in_specs=...]
  transfers between devices with their start and end apart: 14 -> 14, of which waited for: 5 -> 4; matrix products, arithmetic and copies ran while one was open for 0% -> 0% of each run, Pallas kernels for 20% -> 19%
where the time goes in v16:
time: 29.3 us; the launch traced here: 29.2 us
  starting transfers between devices  19.4 us (66%)
  Pallas kernels  6.72 us (23%)
  waiting for transfers between devices  2.38 us (8%)
  between operations  0.71 us (2%)
    ppermute x14, starting transfers between devices, swap(): return lax.ppermute(x, axis, [(k, k ^ distance) for k in range(size)])  19.4 us
    pallas_call x1, Pallas kernels, prepare(): pl.pallas_call(functools.partial(prepare_kernel, rows, steps, own, min(ow...  3.44 us
    ppermute x14, waiting for transfers between devices, swap(): return lax.ppermute(x, axis, [(k, k ^ distance) for k in range(size)])  2.38 us
    pallas_call x1, Pallas kernels, project(): pl.pallas_call(functools.partial(project_kernel, pairs), out_shape=[jax.S...  1.3 us
    pallas_call x1, Pallas kernels, finish(): pl.pallas_call(functools.partial(finish_kernel, rows, steps, own, min(own...  1.06 us
  transfers between devices with their start and end apart: 14, of which 4 were waited for; matrix products, arithmetic and copies ran while one was open for 0% of the time, Pallas kernels for 19%

profile of v16, /device:TPU:0, one launch (start us, length us, event | category | flops | bytes accessed | tf_op | source)
XLA Modules:
  0.0 29.2 jit_solution(6850643913298051929)
XLA Ops:
  0.6 0.5 %collective-permute-start.3 = (bf16[256,2048]{1,0:T(8,128)(2,1)}, bf16[256,2048]{1,0:T(8,128)(2,1)S(1)}, u32[]{:S(2)}, u32[]{:S(2)}) collective-permute-start(bf16[256,2048]{1,0:T(8,128)(2,1)} %codes_hbm.1), channel_id=1, source_target_pairs={{0,4},{4,0},{8,12},{12,8},{16,20},{20,16},{24,28},{28,24},{1,5},{5... | collective-permute-start | bytes 3145736 | tf_op jit(solution)/shard_map/ppermute | solution.py:74
  1.2 4.7 %collective-permute-start.2 = (bf16[16,2048]{1,0:T(8,128)(2,1)}, bf16[16,2048]{1,0:T(8,128)(2,1)S(1)}, u32[]{:S(2)}, u32[]{:S(2)}) collective-permute-start(bf16[16,2048]{1,0:T(8,128)(2,1)} %bitcast.7), channel_id=1, source_target_pairs={{0,24},{4,28},{8,16},{12,20},{16,8},{20,12},{24,0},{28,4},{1,25},{... | collective-permute-start | bytes 196616 | tf_op jit(solution)/shard_map/ppermute | solution.py:74
  5.8 0.0 collective-permute-start.1
  5.8 0.6 %collective-permute-start = (bf16[16,2048]{1,0:T(8,128)(2,1)}, bf16[16,2048]{1,0:T(8,128)(2,1)S(1)}, u32[]{:S(2)}, u32[]{:S(2)}) collective-permute-start(bf16[16,2048]{1,0:T(8,128)(2,1)} %bitcast.9), channel_id=1, source_target_pairs={{0,8},{4,12},{8,0},{12,4},{16,24},{20,28},{24,16},{28,20},{1,9},{5... | collective-permute-start | bytes 196616 | tf_op jit(solution)/shard_map/ppermute | solution.py:74
  6.5 0.0 collective-permute-start.4
  6.5 3.4 %prepare.1 = (bf16[256,2048]{1,0:T(8,128)(2,1)S(1)}, bf16[2,256,2048]{2,1,0:T(8,128)(2,1)S(1)}, bf16[256,128]{1,0:T(8,128)(2,1)S(1)}, s32[8,128]{1,0:T(8,128)S(1...) custom-call(s32[8]{0:T(128)} %owner_hbm.1, ...), custom_call_target="tpu_custom_call" | custom-call | bytes 120000000 | tf_op jit(solution)/shard_map/prepare/pallas_call | solution.py:226
  9.9 0.0 copy-start
  9.9 0.0 collective-permute-done.4
  9.9 1.7 %collective-permute-start.11 = (bf16[272,128]{1,0:T(8,128)(2,1)S(1)}, bf16[272,128]{1,0:T(8,128)(2,1)S(1)}, u32[]{:S(2)}, u32[]{:S(2)}) collective-permute-start(bf16[272,128]{1,0:T(8,128)(2,1)S(1)} %get-tuple-element.45), channel_id=1, source_target_pairs={{0,1},{1,0},{2,3},{3,2},{4,5},{5,4},{6,7},{7,6},{8,9},{9,8},{10,11... | collective-permute-start | bytes 208904 | tf_op jit(solution)/shard_map/ppermute | solution.py:74
  11.6 0.0 collective-permute-done.3.codes_ref
  11.6 0.5 %mate_weights.1.mate_ref = bf16[256,2048]{1,0:T(8,128)(2,1)S(1)} custom-call(bf16[256,2048]{1,0:T(8,128)(2,1)S(1)} %collective-permute-done.3.codes_ref, bf16[16,256]{1,0:T(8,128)(2,1)S(1)} %bitcast.11), custom_call_target="tpu_custom_call" | custom-call | bytes 1000 | tf_op jit(solution)/shard_map/mate_weights/pallas_call | solution.py:99
  12.1 0.0 collective-permute-done.2.refs_3_
  12.1 0.0 collective-permute-done.1.refs_2_
  12.1 0.0 collective-permute-done.refs_1_
  12.1 0.0 copy-done
  12.2 1.3 %project.1 = (f32[16,512]{1,0:T(8,128)S(1)}, f32[16,512]{1,0:T(8,128)S(1)}, f32[16,512]{1,0:T(8,128)S(1)}, f32[16,512]{1,0:T(8,128)S(1)}) custom-call(bf16[256,2048]{1,0:T(8,128)(2,1)S(1)} %get-tuple-element.29.own_ref, bf16[256,2048]{1,0:T(8,128)(2,1)S(1)} %mate_weights.1.mate_ref, bf16[2,256,2048]{2,1,0:T(8,128)(2,1)S(1)} %get-tuple-element.31.base_ref, ...), custom_call_target="tpu_custom_call" | custom-call | bytes 60000000 | tf_op jit(solution)/shard_map/project/pallas_call | solution.py:305
  13.5 3.7 %collective-permute-start.5 = (f32[16,512]{1,0:T(8,128)S(1)}, f32[16,512]{1,0:T(8,128)S(1)}, u32[]{:S(2)}, u32[]{:S(2)}) collective-permute-start(f32[16,512]{1,0:T(8,128)S(1)} %get-tuple-element.37), channel_id=1, source_target_pairs={{0,24},{4,28},{8,16},{12,20},{16,8},{20,12},{24,0},{28,4},{1,25},{... | collective-permute-start | bytes 98312 | tf_op jit(solution)/shard_map/ppermute | solution.py:74
  17.1 0.0 collective-permute-start.6
  17.1 0.8 %collective-permute-start.7 = (f32[16,512]{1,0:T(8,128)S(1)}, f32[16,512]{1,0:T(8,128)S(1)}, u32[]{:S(2)}, u32[]{:S(2)}) collective-permute-start(f32[16,512]{1,0:T(8,128)S(1)} %get-tuple-element.39), channel_id=1, source_target_pairs={{0,8},{4,12},{8,0},{12,4},{16,24},{20,28},{24,16},{28,20},{1,9},{5... | collective-permute-start | bytes 98312 | tf_op jit(solution)/shard_map/ppermute | solution.py:74
  17.9 1.5 %collective-permute-start.12 = (bf16[272,128]{1,0:T(8,128)(2,1)S(1)}, bf16[272,128]{1,0:T(8,128)(2,1)S(1)}, u32[]{:S(2)}, u32[]{:S(2)}) collective-permute-start(bf16[272,128]{1,0:T(8,128)(2,1)S(1)} %get-tuple-element.46), channel_id=1, source_target_pairs={{0,2},{1,3},{2,0},{3,1},{4,6},{5,7},{6,4},{7,5},{8,10},{9,11},{10,... | collective-permute-start | bytes 208904 | tf_op jit(solution)/shard_map/ppermute | solution.py:74
  19.4 0.0 collective-permute-done.5.refs_1_
  19.4 2.3 %collective-permute-start.13 = (bf16[272,128]{1,0:T(8,128)(2,1)S(1)}, bf16[272,128]{1,0:T(8,128)(2,1)S(1)}, u32[]{:S(2)}, u32[]{:S(2)}) collective-permute-start(bf16[272,128]{1,0:T(8,128)(2,1)S(1)} %get-tuple-element.47), channel_id=1, source_target_pairs={{0,3},{1,2},{2,1},{3,0},{4,7},{5,6},{6,5},{7,4},{8,11},{9,10},{10,... | collective-permute-start | bytes 208904 | tf_op jit(solution)/shard_map/ppermute | solution.py:74
  21.7 0.2 collective-permute-done.6.refs_2_
  21.9 0.0 collective-permute-done.7.refs_3_
  21.9 0.1 pack_pieces.1
  22.0 1.6 %collective-permute-start.8 = (bf16[16,1280]{1,0:T(8,128)(2,1)S(1)}, bf16[16,1280]{1,0:T(8,128)(2,1)S(1)}, u32[]{:S(2)}, u32[]{:S(2)}) collective-permute-start(bf16[16,1280]{1,0:T(8,128)(2,1)S(1)} %get-tuple-element.41), channel_id=1, source_target_pairs={{0,3},{1,2},{2,1},{3,0},{4,7},{5,6},{6,5},{7,4},{8,11},{9,10},{10,... | collective-permute-start | bytes 122888 | tf_op jit(solution)/shard_map/ppermute | solution.py:74
  23.6 0.5 %collective-permute-start.9 = (bf16[16,1280]{1,0:T(8,128)(2,1)S(1)}, bf16[16,1280]{1,0:T(8,128)(2,1)S(1)}, u32[]{:S(2)}, u32[]{:S(2)}) collective-permute-start(bf16[16,1280]{1,0:T(8,128)(2,1)S(1)} %get-tuple-element.42), channel_id=1, source_target_pairs={{0,2},{1,3},{2,0},{3,1},{4,6},{5,7},{6,4},{7,5},{8,10},{9,11},{10,... | collective-permute-start | bytes 122888 | tf_op jit(solution)/shard_map/ppermute | solution.py:74
  24.1 0.0 collective-permute-done.11.refs_1_
  24.1 1.5 %collective-permute-start.10 = (bf16[16,1280]{1,0:T(8,128)(2,1)S(1)}, bf16[16,1280]{1,0:T(8,128)(2,1)S(1)}, u32[]{:S(2)}, u32[]{:S(2)}) collective-permute-start(bf16[16,1280]{1,0:T(8,128)(2,1)S(1)} %get-tuple-element.43), channel_id=1, source_target_pairs={{0,1},{1,0},{2,3},{3,2},{4,5},{5,4},{6,7},{7,6},{8,9},{9,8},{10,11... | collective-permute-start | bytes 122888 | tf_op jit(solution)/shard_map/ppermute | solution.py:74
  25.6 0.0 collective-permute-done.12.refs_2_
  25.6 0.0 collective-permute-done.13.refs_3_
  25.6 0.3 %merge_partials.1.refs_4_ = f32[264,128]{1,0:T(8,128)S(1)} custom-call(f32[264,128]{1,0:T(8,128)S(1)} %get-tuple-element.44.refs_0_, bf16[272,128]{1,0:T(8,128)(2,1)S(1)} %collective-permute-done.11.refs_1_, bf16[272,128]{1,0:T(8,128)(2,1)S(1)} %collective-permute-done.12.refs_2_, bf16[272,128]{1,0:T(8,128)(2,1)S(1)} %collective-permute-done.13.refs_3_), custom_call_target="tpu_custom_call" | custom-call | bytes 1000 | tf_op jit(solution)/shard_map/merge_partials/pallas_call | solution.py:279
  26.0 1.0 %collective-permute-done.8.refs_1_ = bf16[16,1280]{1,0:T(8,128)(2,1)S(1)} collective-permute-done((bf16[16,1280]{1,0:T(8,128)(2,1)S(1)}, bf16[16,1280]{1,0:T(8,128)(2,1)S(1)}, u32[]{:S(2)}, u32[]{:S(2)}) %collective-permute-start.8) | collective-permute-done | bytes 40992 | tf_op jit(solution)/shard_map/ppermute | solution.py:74
  27.0 0.6 %collective-permute-done.9.refs_2_ = bf16[16,1280]{1,0:T(8,128)(2,1)S(1)} collective-permute-done((bf16[16,1280]{1,0:T(8,128)(2,1)S(1)}, bf16[16,1280]{1,0:T(8,128)(2,1)S(1)}, u32[]{:S(2)}, u32[]{:S(2)}) %collective-permute-start.9) | collective-permute-done | bytes 40992 | tf_op jit(solution)/shard_map/ppermute | solution.py:74
  27.6 0.5 %collective-permute-done.10.refs_3_ = bf16[16,1280]{1,0:T(8,128)(2,1)S(1)} collective-permute-done((bf16[16,1280]{1,0:T(8,128)(2,1)S(1)}, bf16[16,1280]{1,0:T(8,128)(2,1)S(1)}, u32[]{:S(2)}, u32[]{:S(2)}) %collective-permute-start.10) | collective-permute-done | bytes 40992 | tf_op jit(solution)/shard_map/ppermute | solution.py:74
  28.1 1.1 %finish.1 = (bf16[16,512]{1,0:T(8,128)(2,1)}, bf16[16,2048]{1,0:T(8,128)(2,1)}) custom-call(bf16[256,128]{1,0:T(8,128)(2,1)S(1)} %get-tuple-element.27.query_ref, f32[16,1024]{1,0:T(8,128)S(1)} %get-tuple-element.40.refs_0_, bf16[16,1280]{1,0:T(8,128)(2,1)S(1)} %collective-permute-done.8.refs_1_, bf16[16,1280]{1,0:T(8,128)(2,1)S(1)} %collective-permute-done.9.refs_2_, ...), custom_call_target="tpu_custom_call" | custom-call | tf_op jit(solution)/shard_map/finish/pallas_call | solution.py:455
Async XLA Ops:
  0.6 11.0 %collective-permute-start.3 = (bf16[256,2048]{1,0:T(8,128)(2,1)}, bf16[256,2048]{1,0:T(8,128)(2,1)S(1)}, u32[]{:S(2)}, u32[]{:S(2)}) collective-permute-start(bf16[256,2048]{1,0:T(8,128)(2,1)} %codes_hbm.1), channel_id=1, source_target_pairs={{0,4},{4,0},{8,12},{12,8},{16,20},{20,16},{24,28},{28,24},{1,5},{5... | collective-permute-start | bytes 3145736 | tf_op jit(solution)/shard_map/ppermute | solution.py:74
  1.2 11.0 %collective-permute-start.2 = (bf16[16,2048]{1,0:T(8,128)(2,1)}, bf16[16,2048]{1,0:T(8,128)(2,1)S(1)}, u32[]{:S(2)}, u32[]{:S(2)}) collective-permute-start(bf16[16,2048]{1,0:T(8,128)(2,1)} %bitcast.7), channel_id=1, source_target_pairs={{0,24},{4,28},{8,16},{12,20},{16,8},{20,12},{24,0},{28,4},{1,25},{... | collective-permute-start | bytes 196616 | tf_op jit(solution)/shard_map/ppermute | solution.py:74
  5.8 6.3 %collective-permute-start.1 = (bf16[16,2048]{1,0:T(8,128)(2,1)}, bf16[16,2048]{1,0:T(8,128)(2,1)S(1)}, u32[]{:S(2)}, u32[]{:S(2)}) collective-permute-start(bf16[16,2048]{1,0:T(8,128)(2,1)} %bitcast.8), channel_id=1, source_target_pairs={{0,16},{4,20},{8,24},{12,28},{16,0},{20,4},{24,8},{28,12},{1,17},{... | collective-permute-start | bytes 196616 | tf_op jit(solution)/shard_map/ppermute | solution.py:74
  5.8 6.3 %collective-permute-start = (bf16[16,2048]{1,0:T(8,128)(2,1)}, bf16[16,2048]{1,0:T(8,128)(2,1)S(1)}, u32[]{:S(2)}, u32[]{:S(2)}) collective-permute-start(bf16[16,2048]{1,0:T(8,128)(2,1)} %bitcast.9), channel_id=1, source_target_pairs={{0,8},{4,12},{8,0},{12,4},{16,24},{20,28},{24,16},{28,20},{1,9},{5... | collective-permute-start | bytes 196616 | tf_op jit(solution)/shard_map/ppermute | solution.py:74
  6.5 3.5 %collective-permute-start.4 = (bf16[256,16]{0,1:T(8,128)(2,1)}, bf16[256,16]{0,1:T(8,128)(2,1)S(1)}, u32[]{:S(2)}, u32[]{:S(2)}) collective-permute-start(bf16[256,16]{0,1:T(8,128)(2,1)} %param.11), channel_id=1, source_target_pairs={{0,4},{4,0},{8,12},{12,8},{16,20},{20,16},{24,28},{28,24},{1,5},{5... | collective-permute-start | bytes 24584 | tf_op jit(solution)/shard_map/ppermute | solution.py:74
  9.9 2.2 %copy-start = (bf16[2,8,2048]{2,1,0:T(8,128)(2,1)S(1)}, bf16[2,8,2048]{2,1,0:T(8,128)(2,1)}, u32[]{:S(2)}) copy-start(bf16[2,8,2048]{2,1,0:T(8,128)(2,1)} %param.8) | copy-start | bytes 196612
  9.9 14.2 %collective-permute-start.11 = (bf16[272,128]{1,0:T(8,128)(2,1)S(1)}, bf16[272,128]{1,0:T(8,128)(2,1)S(1)}, u32[]{:S(2)}, u32[]{:S(2)}) collective-permute-start(bf16[272,128]{1,0:T(8,128)(2,1)S(1)} %get-tuple-element.45), channel_id=1, source_target_pairs={{0,1},{1,0},{2,3},{3,2},{4,5},{5,4},{6,7},{7,6},{8,9},{9,8},{10,11... | collective-permute-start | bytes 208904 | tf_op jit(solution)/shard_map/ppermute | solution.py:74
  13.5 6.0 %collective-permute-start.5 = (f32[16,512]{1,0:T(8,128)S(1)}, f32[16,512]{1,0:T(8,128)S(1)}, u32[]{:S(2)}, u32[]{:S(2)}) collective-permute-start(f32[16,512]{1,0:T(8,128)S(1)} %get-tuple-element.37), channel_id=1, source_target_pairs={{0,24},{4,28},{8,16},{12,20},{16,8},{20,12},{24,0},{28,4},{1,25},{... | collective-permute-start | bytes 98312 | tf_op jit(solution)/shard_map/ppermute | solution.py:74
  17.1 4.8 %collective-permute-start.6 = (f32[16,512]{1,0:T(8,128)S(1)}, f32[16,512]{1,0:T(8,128)S(1)}, u32[]{:S(2)}, u32[]{:S(2)}) collective-permute-start(f32[16,512]{1,0:T(8,128)S(1)} %get-tuple-element.38), channel_id=1, source_target_pairs={{0,16},{4,20},{8,24},{12,28},{16,0},{20,4},{24,8},{28,12},{1,17},{... | collective-permute-start | bytes 98312 | tf_op jit(solution)/shard_map/ppermute | solution.py:74
  17.1 4.8 %collective-permute-start.7 = (f32[16,512]{1,0:T(8,128)S(1)}, f32[16,512]{1,0:T(8,128)S(1)}, u32[]{:S(2)}, u32[]{:S(2)}) collective-permute-start(f32[16,512]{1,0:T(8,128)S(1)} %get-tuple-element.39), channel_id=1, source_target_pairs={{0,8},{4,12},{8,0},{12,4},{16,24},{20,28},{24,16},{28,20},{1,9},{5... | collective-permute-start | bytes 98312 | tf_op jit(solution)/shard_map/ppermute | solution.py:74
  17.9 7.7 %collective-permute-start.12 = (bf16[272,128]{1,0:T(8,128)(2,1)S(1)}, bf16[272,128]{1,0:T(8,128)(2,1)S(1)}, u32[]{:S(2)}, u32[]{:S(2)}) collective-permute-start(bf16[272,128]{1,0:T(8,128)(2,1)S(1)} %get-tuple-element.46), channel_id=1, source_target_pairs={{0,2},{1,3},{2,0},{3,1},{4,6},{5,7},{6,4},{7,5},{8,10},{9,11},{10,... | collective-permute-start | bytes 208904 | tf_op jit(solution)/shard_map/ppermute | solution.py:74
  19.4 6.2 %collective-permute-start.13 = (bf16[272,128]{1,0:T(8,128)(2,1)S(1)}, bf16[272,128]{1,0:T(8,128)(2,1)S(1)}, u32[]{:S(2)}, u32[]{:S(2)}) collective-permute-start(bf16[272,128]{1,0:T(8,128)(2,1)S(1)} %get-tuple-element.47), channel_id=1, source_target_pairs={{0,3},{1,2},{2,1},{3,0},{4,7},{5,6},{6,5},{7,4},{8,11},{9,10},{10,... | collective-permute-start | bytes 208904 | tf_op jit(solution)/shard_map/ppermute | solution.py:74
  22.0 5.0 %collective-permute-start.8 = (bf16[16,1280]{1,0:T(8,128)(2,1)S(1)}, bf16[16,1280]{1,0:T(8,128)(2,1)S(1)}, u32[]{:S(2)}, u32[]{:S(2)}) collective-permute-start(bf16[16,1280]{1,0:T(8,128)(2,1)S(1)} %get-tuple-element.41), channel_id=1, source_target_pairs={{0,3},{1,2},{2,1},{3,0},{4,7},{5,6},{6,5},{7,4},{8,11},{9,10},{10,... | collective-permute-start | bytes 122888 | tf_op jit(solution)/shard_map/ppermute | solution.py:74
  23.6 4.0 %collective-permute-start.9 = (bf16[16,1280]{1,0:T(8,128)(2,1)S(1)}, bf16[16,1280]{1,0:T(8,128)(2,1)S(1)}, u32[]{:S(2)}, u32[]{:S(2)}) collective-permute-start(bf16[16,1280]{1,0:T(8,128)(2,1)S(1)} %get-tuple-element.42), channel_id=1, source_target_pairs={{0,2},{1,3},{2,0},{3,1},{4,6},{5,7},{6,4},{7,5},{8,10},{9,11},{10,... | collective-permute-start | bytes 122888 | tf_op jit(solution)/shard_map/ppermute | solution.py:74
  24.1 4.0 %collective-permute-start.10 = (bf16[16,1280]{1,0:T(8,128)(2,1)S(1)}, bf16[16,1280]{1,0:T(8,128)(2,1)S(1)}, u32[]{:S(2)}, u32[]{:S(2)}) collective-permute-start(bf16[16,1280]{1,0:T(8,128)(2,1)S(1)} %get-tuple-element.43), channel_id=1, source_target_pairs={{0,1},{1,0},{2,3},{3,2},{4,5},{5,4},{6,7},{7,6},{8,9},{9,8},{10,11... | collective-permute-start | bytes 122888 | tf_op jit(solution)/shard_map/ppermute | solution.py:74

commit v17 on v16

--- a/solution.py
+++ b/solution.py
@@ -21,7 +21,6 @@
 PROJECT_HINT = 60_000_000
 PACK_HINT = 60_000_000
 CACHE_KIB = 24 << 10
-WEIGHTS_KIB = 16 << 10
 PROJECT_KIB = 16 << 10
 NT = (((1,), (1,)), ((), ()))
 TN = (((0,), (0,)), ((), ()))
@@ -93,18 +92,6 @@
         lanes = slice(n * BLK, (n + 1) * BLK)
         values = codes_ref[:, lanes].astype(jnp.float32) * columns[:, n : n + 1]
         out_ref[:, lanes] = values.astype(jnp.bfloat16)
-
-
-def mate_weights(codes, scales):
-    return pl.pallas_call(
-        dequantize,
-        out_shape=jax.ShapeDtypeStruct(codes.shape, jnp.bfloat16),
-        in_specs=[VMEM, VMEM],
-        out_specs=VMEM,
-        compiler_params=params(WEIGHTS_KIB),
-        cost_estimate=hint(1000),
-        name="mate_weights",
-    )(codes, scales.T)
 
 
 def prepare_kernel(
@@ -140,12 +127,12 @@
             copy.wait()
 
     owner_load = load(owner_hbm, owner_ref)
-    first_loads = load(lengths_hbm, lengths_ref) + load(scales_hbm, scales_ref)
-    first_loads += load_rows(codes_hbm, 0, codes_ref, block) + load(query_hbm, query_ref)
+    first_loads = load(lengths_hbm, lengths_ref) + load(query_hbm, query_ref)
     cache_loads = []
     for r in range(rows):
         target = cache_ref.at[pl.ds(r * cache_len, cache_len)]
         cache_loads.append(load_rows(cache_hbm, r * cache_len, target, cache_len))
+    code_loads = load(scales_hbm, scales_ref) + load_rows(codes_hbm, 0, codes_ref, block)
     wait(owner_load)
     base_loads = []
     for k in range(2):
@@ -155,7 +142,6 @@
         owner = owner_ref[lax.axis_index("group") ^ n]
         places_ref[n : n + 1] = jnp.full((1, LANES), owner, jnp.int32)
     wait(first_loads)
-    dequantize(codes_ref, scales_ref, delta_ref)
 
     chunks = own // chunk
     height = chunk * steps
@@ -209,6 +195,8 @@
         stats[n] += [peak, total]
         if r == rows - 1:
             put_stats(parts[n], stats[n])
+    wait(code_loads)
+    dequantize(codes_ref, scales_ref, delta_ref)
     wait(base_loads)
 
 
@@ -248,7 +236,7 @@
         cost_estimate=hint(CACHE_HINT),
         name="prepare",
     )(*operands)
-    return out[0], out[1], out[2], out[3], out[4:]
+    return out[0], out[1], out[2], out[3], list(out[4:])
 
 
 def merge_kernel(rows, span, *refs):
@@ -287,30 +275,38 @@
     )(*parts)
 
 
-def project_kernel(pairs, own_ref, mate_ref, base_ref, *refs):
-    tokens, outs = refs[:pairs], refs[pairs:]
+def project_kernel(pairs, own_ref, base_ref, codes_ref, scales_ref, *refs):
+    tokens, outs, mate_ref = refs[:pairs], refs[pairs:-1], refs[-1]
     block = own_ref.shape[0]
     stacked = jnp.concatenate([ref[...] for ref in tokens], axis=0)
     count = tokens[0].shape[0]
-    for k, delta_ref in enumerate((own_ref, mate_ref)):
-        whole = (dot(base_ref[k], stacked, NT) + dot(delta_ref[...], stacked, NT)).T
+
+    def put(k, whole):
+        whole = whole.T
         for n in range(pairs):
             outs[n][:, k * block : (k + 1) * block] = whole[n * count : (n + 1) * count]
 
-
-def project(own, mate, base, tokens):
+    mine = dot(base_ref[0], stacked, NT) + dot(own_ref[...], stacked, NT)
+    other = dot(base_ref[1], stacked, NT)
+    dequantize(codes_ref, scales_ref, mate_ref)
+    put(0, mine)
+    put(1, other + dot(mate_ref[...], stacked, NT))
+
+
+def project(own, base, mate_codes, mate_scales, tokens):
     pairs = len(tokens)
     block = own.shape[0]
-    count, width = tokens[0].shape
+    count = tokens[0].shape[0]
     return pl.pallas_call(
         functools.partial(project_kernel, pairs),
         out_shape=[jax.ShapeDtypeStruct((count, 2 * block), jnp.float32)] * pairs,
-        in_specs=[VMEM] * (3 + pairs),
+        in_specs=[VMEM] * (4 + pairs),
         out_specs=[VMEM] * pairs,
+        scratch_shapes=[pltpu.VMEM(own.shape, own.dtype)],
         compiler_params=params(PROJECT_KIB),
         cost_estimate=hint(PROJECT_HINT),
         name="project",
-    )(own, mate, base, *tokens)
+    )(own, base, mate_codes, mate_scales.T, *tokens)
 
 
 def pack_kernel(pairs, ways, near, wide, block, places_ref, *refs):
@@ -504,10 +500,12 @@
         heads_own,
         tensor_count,
     )
-    mate_delta = mate_weights(mate_codes, mate_scales)
-    behind = lax.optimization_barrier((*near_first(token_rows), mate_delta, own_query))
-    token_rows, mate_delta, own_query = near_first(list(behind[:pairs])), behind[-2], behind[-1]
-    projected = project(own_delta, mate_delta, base_blocks, near_first(token_rows))
+    mate_scales, partials[-1] = lax.optimization_barrier((mate_scales, partials[-1]))
+    behind = lax.optimization_barrier((*near_first(token_rows), own_query))
+    token_rows, own_query = near_first(list(behind[:pairs])), behind[-1]
+    projected = project(
+        own_delta, base_blocks, mate_codes, mate_scales, near_first(token_rows)
+    )
     arrived = exchange(near_first(projected), "group", 2)
     partials = exchange(partials, "tensor", 1)
     pieces = pack_pieces(

time: 29.3 us -> 30 us (1.024)
  waiting for transfers between devices: 2.38 us -> 4.18 us
  starting transfers between devices: 19.4 us -> 18.5 us
    ppermute x14, waiting for transfers between devices: 2.38 us -> 4.18 us  [swap(): return lax.ppermute(x, axis, [(k, k ^ distance) for k in range(size)])]
    ppermute x14, starting transfers between devices: 19.4 us -> 18.5 us  [swap(): return lax.ppermute(x, axis, [(k, k ^ distance) for k in range(size)])]
    pallas_call x1 -> x0, Pallas kernels: 0.47 us -> none  [mate_weights(): pl.pallas_call(dequantize, out_shape=jax.ShapeDtypeStruct(codes.shape, jn...]
  transfers between devices with their start and end apart: 14 -> 14, of which waited for: 4 -> 5; matrix products, arithmetic and copies ran while one was open for 0% -> 0% of each run, Pallas kernels for 19% -> 18%
where the time goes in v17:
time: 30 us; the launch traced here: 29.9 us
  starting transfers between devices  18.5 us (62%)
  Pallas kernels  6.45 us (22%)
  waiting for transfers between devices  4.18 us (14%)
  between operations  0.68 us (2%)
    ppermute x14, starting transfers between devices, swap(): return lax.ppermute(x, axis, [(k, k ^ distance) for k in range(size)])  18.5 us
    ppermute x14, waiting for transfers between devices, swap(): return lax.ppermute(x, axis, [(k, k ^ distance) for k in range(size)])  4.18 us
    pallas_call x1, Pallas kernels, prepare(): pl.pallas_call(functools.partial(prepare_kernel, rows, steps, own, min(ow...  3.46 us
    pallas_call x1, Pallas kernels, project(): pl.pallas_call(functools.partial(project_kernel, pairs), out_shape=[jax.S...  1.48 us
    pallas_call x1, Pallas kernels, finish(): pl.pallas_call(functools.partial(finish_kernel, rows, steps, own, min(own...  1.06 us
  transfers between devices with their start and end apart: 14, of which 5 were waited for; matrix products, arithmetic and copies ran while one was open for 0% of the time, Pallas kernels for 18%

profile of v17, /device:TPU:0, one launch (start us, length us, event | category | flops | bytes accessed | tf_op | source)
XLA Modules:
  0.0 29.9 jit_solution(1697988534821693244)
XLA Ops:
  0.6 0.5 %collective-permute-start.3 = (bf16[256,2048]{1,0:T(8,128)(2,1)}, bf16[256,2048]{1,0:T(8,128)(2,1)S(1)}, u32[]{:S(2)}, u32[]{:S(2)}) collective-permute-start(bf16[256,2048]{1,0:T(8,128)(2,1)} %codes_hbm.1), channel_id=1, source_target_pairs={{0,4},{4,0},{8,12},{12,8},{16,20},{20,16},{24,28},{28,24},{1,5},{5... | collective-permute-start | bytes 3145736 | tf_op jit(solution)/shard_map/ppermute | solution.py:73
  1.2 4.7 %collective-permute-start.2 = (bf16[16,2048]{1,0:T(8,128)(2,1)}, bf16[16,2048]{1,0:T(8,128)(2,1)S(1)}, u32[]{:S(2)}, u32[]{:S(2)}) collective-permute-start(bf16[16,2048]{1,0:T(8,128)(2,1)} %bitcast.7), channel_id=1, source_target_pairs={{0,24},{4,28},{8,16},{12,20},{16,8},{20,12},{24,0},{28,4},{1,25},{... | collective-permute-start | bytes 196616 | tf_op jit(solution)/shard_map/ppermute | solution.py:73
  5.8 0.0 collective-permute-start.1
  5.8 0.7 %collective-permute-start = (bf16[16,2048]{1,0:T(8,128)(2,1)}, bf16[16,2048]{1,0:T(8,128)(2,1)S(1)}, u32[]{:S(2)}, u32[]{:S(2)}) collective-permute-start(bf16[16,2048]{1,0:T(8,128)(2,1)} %bitcast.9), channel_id=1, source_target_pairs={{0,8},{4,12},{8,0},{12,4},{16,24},{20,28},{24,16},{28,20},{1,9},{5... | collective-permute-start | bytes 196616 | tf_op jit(solution)/shard_map/ppermute | solution.py:73
  6.5 0.0 collective-permute-start.4
  6.5 0.0 copy-start
  6.5 3.5 %prepare.1 = (bf16[256,2048]{1,0:T(8,128)(2,1)S(1)}, bf16[2,256,2048]{2,1,0:T(8,128)(2,1)S(1)}, bf16[256,128]{1,0:T(8,128)(2,1)S(1)}, s32[8,128]{1,0:T(8,128)S(1...) custom-call(s32[8]{0:T(128)} %owner_hbm.1, ...), custom_call_target="tpu_custom_call" | custom-call | bytes 120000000 | tf_op jit(solution)/shard_map/prepare/pallas_call | solution.py:214
  10.0 0.0 collective-permute-done.4
  10.0 1.7 %collective-permute-start.12 = (bf16[272,128]{1,0:T(8,128)(2,1)S(1)}, bf16[272,128]{1,0:T(8,128)(2,1)S(1)}, u32[]{:S(2)}, u32[]{:S(2)}) collective-permute-start(bf16[272,128]{1,0:T(8,128)(2,1)S(1)} %get-tuple-element.48), channel_id=1, source_target_pairs={{0,2},{1,3},{2,0},{3,1},{4,6},{5,7},{6,4},{7,5},{8,10},{9,11},{10,... | collective-permute-start | bytes 208904 | tf_op jit(solution)/shard_map/ppermute | solution.py:73
  11.7 0.0 collective-permute-done.2.refs_3_
  11.7 0.4 %collective-permute-done.1.refs_2_ = bf16[16,2048]{1,0:T(8,128)(2,1)S(1)} collective-permute-done((bf16[16,2048]{1,0:T(8,128)(2,1)}, bf16[16,2048]{1,0:T(8,128)(2,1)S(1)}, u32[]{:S(2)}, u32[]{:S(2)}) %collective-permute-start.1) | collective-permute-done | bytes 65568 | tf_op jit(solution)/shard_map/ppermute | solution.py:73
  12.1 0.0 collective-permute-done.refs_1_
  12.1 0.0 collective-permute-done.3.codes_ref
  12.1 0.0 copy-done
  12.1 1.5 %project.1 = (f32[16,512]{1,0:T(8,128)S(1)}, f32[16,512]{1,0:T(8,128)S(1)}, f32[16,512]{1,0:T(8,128)S(1)}, f32[16,512]{1,0:T(8,128)S(1)}) custom-call(bf16[256,2048]{1,0:T(8,128)(2,1)S(1)} %get-tuple-element.30.own_ref, bf16[2,256,2048]{2,1,0:T(8,128)(2,1)S(1)} %get-tuple-element.31.base_ref, bf16[256,2048]{1,0:T(8,128)(2,1)S(1)} %collective-permute-done.3.codes_ref, ...), custom_call_target="tpu_custom_call" | custom-call | bytes 60000000 | tf_op jit(solution)/shard_map/project/pallas_call | solution.py:300
  13.6 3.3 %collective-permute-start.5 = (f32[16,512]{1,0:T(8,128)S(1)}, f32[16,512]{1,0:T(8,128)S(1)}, u32[]{:S(2)}, u32[]{:S(2)}) collective-permute-start(f32[16,512]{1,0:T(8,128)S(1)} %get-tuple-element.39), channel_id=1, source_target_pairs={{0,24},{4,28},{8,16},{12,20},{16,8},{20,12},{24,0},{28,4},{1,25},{... | collective-permute-start | bytes 98312 | tf_op jit(solution)/shard_map/ppermute | solution.py:73
  16.8 0.0 collective-permute-start.6
  16.8 1.2 %collective-permute-start.7 = (f32[16,512]{1,0:T(8,128)S(1)}, f32[16,512]{1,0:T(8,128)S(1)}, u32[]{:S(2)}, u32[]{:S(2)}) collective-permute-start(f32[16,512]{1,0:T(8,128)S(1)} %get-tuple-element.41), channel_id=1, source_target_pairs={{0,8},{4,12},{8,0},{12,4},{16,24},{20,28},{24,16},{28,20},{1,9},{5... | collective-permute-start | bytes 98312 | tf_op jit(solution)/shard_map/ppermute | solution.py:73
  18.0 2.4 %collective-permute-start.13 = (bf16[272,128]{1,0:T(8,128)(2,1)S(1)}, bf16[272,128]{1,0:T(8,128)(2,1)S(1)}, u32[]{:S(2)}, u32[]{:S(2)}) collective-permute-start(bf16[272,128]{1,0:T(8,128)(2,1)S(1)} %get-tuple-element.49), channel_id=1, source_target_pairs={{0,3},{1,2},{2,1},{3,0},{4,7},{5,6},{6,5},{7,4},{8,11},{9,10},{10,... | collective-permute-start | bytes 208904 | tf_op jit(solution)/shard_map/ppermute | solution.py:73
  20.5 0.0 collective-permute-done.5.refs_1_
  20.5 0.5 %collective-permute-start.11 = (bf16[272,128]{1,0:T(8,128)(2,1)S(1)}, bf16[272,128]{1,0:T(8,128)(2,1)S(1)}, u32[]{:S(2)}, u32[]{:S(2)}) collective-permute-start(bf16[272,128]{1,0:T(8,128)(2,1)S(1)} %get-tuple-element.47), channel_id=1, source_target_pairs={{0,1},{1,0},{2,3},{3,2},{4,5},{5,4},{6,7},{7,6},{8,9},{9,8},{10,11... | collective-permute-start | bytes 208904 | tf_op jit(solution)/shard_map/ppermute | solution.py:73
  21.0 0.6 %collective-permute-done.6.refs_2_ = f32[16,512]{1,0:T(8,128)S(1)} collective-permute-done((f32[16,512]{1,0:T(8,128)S(1)}, f32[16,512]{1,0:T(8,128)S(1)}, u32[]{:S(2)}, u32[]{:S(2)}) %collective-permute-start.6) | collective-permute-done | bytes 32800 | tf_op jit(solution)/shard_map/ppermute | solution.py:73
  21.7 0.0 collective-permute-done.7.refs_3_
  21.7 0.1 pack_pieces.1
  21.8 1.8 %collective-permute-start.8 = (bf16[16,1280]{1,0:T(8,128)(2,1)S(1)}, bf16[16,1280]{1,0:T(8,128)(2,1)S(1)}, u32[]{:S(2)}, u32[]{:S(2)}) collective-permute-start(bf16[16,1280]{1,0:T(8,128)(2,1)S(1)} %get-tuple-element.43), channel_id=1, source_target_pairs={{0,3},{1,2},{2,1},{3,0},{4,7},{5,6},{6,5},{7,4},{8,11},{9,10},{10,... | collective-permute-start | bytes 122888 | tf_op jit(solution)/shard_map/ppermute | solution.py:73
  23.6 1.2 %collective-permute-start.9 = (bf16[16,1280]{1,0:T(8,128)(2,1)S(1)}, bf16[16,1280]{1,0:T(8,128)(2,1)S(1)}, u32[]{:S(2)}, u32[]{:S(2)}) collective-permute-start(bf16[16,1280]{1,0:T(8,128)(2,1)S(1)} %get-tuple-element.44), channel_id=1, source_target_pairs={{0,2},{1,3},{2,0},{3,1},{4,6},{5,7},{6,4},{7,5},{8,10},{9,11},{10,... | collective-permute-start | bytes 122888 | tf_op jit(solution)/shard_map/ppermute | solution.py:73
  24.8 0.0 collective-permute-done.12.refs_2_
  24.8 0.5 %collective-permute-start.10 = (bf16[16,1280]{1,0:T(8,128)(2,1)S(1)}, bf16[16,1280]{1,0:T(8,128)(2,1)S(1)}, u32[]{:S(2)}, u32[]{:S(2)}) collective-permute-start(bf16[16,1280]{1,0:T(8,128)(2,1)S(1)} %get-tuple-element.45), channel_id=1, source_target_pairs={{0,1},{1,0},{2,3},{3,2},{4,5},{5,4},{6,7},{7,6},{8,9},{9,8},{10,11... | collective-permute-start | bytes 122888 | tf_op jit(solution)/shard_map/ppermute | solution.py:73
  25.3 0.0 collective-permute-done.13.refs_3_
  25.3 0.0 collective-permute-done.11.refs_1_
  25.3 0.3 %merge_partials.1.refs_4_ = f32[264,128]{1,0:T(8,128)S(1)} custom-call(f32[264,128]{1,0:T(8,128)S(1)} %get-tuple-element.46.refs_0_, bf16[272,128]{1,0:T(8,128)(2,1)S(1)} %collective-permute-done.11.refs_1_, bf16[272,128]{1,0:T(8,128)(2,1)S(1)} %collective-permute-done.12.refs_2_, bf16[272,128]{1,0:T(8,128)(2,1)S(1)} %collective-permute-done.13.refs_3_), custom_call_target="tpu_custom_call" | custom-call | bytes 1000 | tf_op jit(solution)/shard_map/merge_partials/pallas_call | solution.py:267
  25.7 1.2 %collective-permute-done.8.refs_1_ = bf16[16,1280]{1,0:T(8,128)(2,1)S(1)} collective-permute-done((bf16[16,1280]{1,0:T(8,128)(2,1)S(1)}, bf16[16,1280]{1,0:T(8,128)(2,1)S(1)}, u32[]{:S(2)}, u32[]{:S(2)}) %collective-permute-start.8) | collective-permute-done | bytes 40992 | tf_op jit(solution)/shard_map/ppermute | solution.py:73
  26.9 0.7 %collective-permute-done.9.refs_2_ = bf16[16,1280]{1,0:T(8,128)(2,1)S(1)} collective-permute-done((bf16[16,1280]{1,0:T(8,128)(2,1)S(1)}, bf16[16,1280]{1,0:T(8,128)(2,1)S(1)}, u32[]{:S(2)}, u32[]{:S(2)}) %collective-permute-start.9) | collective-permute-done | bytes 40992 | tf_op jit(solution)/shard_map/ppermute | solution.py:73
  27.6 1.2 %collective-permute-done.10.refs_3_ = bf16[16,1280]{1,0:T(8,128)(2,1)S(1)} collective-permute-done((bf16[16,1280]{1,0:T(8,128)(2,1)S(1)}, bf16[16,1280]{1,0:T(8,128)(2,1)S(1)}, u32[]{:S(2)}, u32[]{:S(2)}) %collective-permute-start.10) | collective-permute-done | bytes 40992 | tf_op jit(solution)/shard_map/ppermute | solution.py:73
  28.8 1.1 %finish.1 = (bf16[16,512]{1,0:T(8,128)(2,1)}, bf16[16,2048]{1,0:T(8,128)(2,1)}) custom-call(bf16[256,128]{1,0:T(8,128)(2,1)S(1)} %get-tuple-element.28.query_ref, f32[16,1024]{1,0:T(8,128)S(1)} %get-tuple-element.42.refs_0_, bf16[16,1280]{1,0:T(8,128)(2,1)S(1)} %collective-permute-done.8.refs_1_, bf16[16,1280]{1,0:T(8,128)(2,1)S(1)} %collective-permute-done.9.refs_2_, ...), custom_call_target="tpu_custom_call" | custom-call | tf_op jit(solution)/shard_map/finish/pallas_call | solution.py:451
Async XLA Ops:
  0.6 11.5 %collective-permute-start.3 = (bf16[256,2048]{1,0:T(8,128)(2,1)}, bf16[256,2048]{1,0:T(8,128)(2,1)S(1)}, u32[]{:S(2)}, u32[]{:S(2)}) collective-permute-start(bf16[256,2048]{1,0:T(8,128)(2,1)} %codes_hbm.1), channel_id=1, source_target_pairs={{0,4},{4,0},{8,12},{12,8},{16,20},{20,16},{24,28},{28,24},{1,5},{5... | collective-permute-start | bytes 3145736 | tf_op jit(solution)/shard_map/ppermute | solution.py:73
  1.2 10.5 %collective-permute-start.2 = (bf16[16,2048]{1,0:T(8,128)(2,1)}, bf16[16,2048]{1,0:T(8,128)(2,1)S(1)}, u32[]{:S(2)}, u32[]{:S(2)}) collective-permute-start(bf16[16,2048]{1,0:T(8,128)(2,1)} %bitcast.7), channel_id=1, source_target_pairs={{0,24},{4,28},{8,16},{12,20},{16,8},{20,12},{24,0},{28,4},{1,25},{... | collective-permute-start | bytes 196616 | tf_op jit(solution)/shard_map/ppermute | solution.py:73
  5.8 6.3 %collective-permute-start.1 = (bf16[16,2048]{1,0:T(8,128)(2,1)}, bf16[16,2048]{1,0:T(8,128)(2,1)S(1)}, u32[]{:S(2)}, u32[]{:S(2)}) collective-permute-start(bf16[16,2048]{1,0:T(8,128)(2,1)} %bitcast.8), channel_id=1, source_target_pairs={{0,16},{4,20},{8,24},{12,28},{16,0},{20,4},{24,8},{28,12},{1,17},{... | collective-permute-start | bytes 196616 | tf_op jit(solution)/shard_map/ppermute | solution.py:73
  5.8 6.3 %collective-permute-start = (bf16[16,2048]{1,0:T(8,128)(2,1)}, bf16[16,2048]{1,0:T(8,128)(2,1)S(1)}, u32[]{:S(2)}, u32[]{:S(2)}) collective-permute-start(bf16[16,2048]{1,0:T(8,128)(2,1)} %bitcast.9), channel_id=1, source_target_pairs={{0,8},{4,12},{8,0},{12,4},{16,24},{20,28},{24,16},{28,20},{1,9},{5... | collective-permute-start | bytes 196616 | tf_op jit(solution)/shard_map/ppermute | solution.py:73
  6.5 3.5 %collective-permute-start.4 = (bf16[256,16]{0,1:T(8,128)(2,1)}, bf16[256,16]{0,1:T(8,128)(2,1)S(1)}, u32[]{:S(2)}, u32[]{:S(2)}) collective-permute-start(bf16[256,16]{0,1:T(8,128)(2,1)} %param.11), channel_id=1, source_target_pairs={{0,4},{4,0},{8,12},{12,8},{16,20},{20,16},{24,28},{28,24},{1,5},{5... | collective-permute-start | bytes 24584 | tf_op jit(solution)/shard_map/ppermute | solution.py:73
  6.5 5.6 %copy-start = (bf16[2,8,2048]{2,1,0:T(8,128)(2,1)S(1)}, bf16[2,8,2048]{2,1,0:T(8,128)(2,1)}, u32[]{:S(2)}) copy-start(bf16[2,8,2048]{2,1,0:T(8,128)(2,1)} %param.8) | copy-start | bytes 196612
  10.0 14.8 %collective-permute-start.12 = (bf16[272,128]{1,0:T(8,128)(2,1)S(1)}, bf16[272,128]{1,0:T(8,128)(2,1)S(1)}, u32[]{:S(2)}, u32[]{:S(2)}) collective-permute-start(bf16[272,128]{1,0:T(8,128)(2,1)S(1)} %get-tuple-element.48), channel_id=1, source_target_pairs={{0,2},{1,3},{2,0},{3,1},{4,6},{5,7},{6,4},{7,5},{8,10},{9,11},{10,... | collective-permute-start | bytes 208904 | tf_op jit(solution)/shard_map/ppermute | solution.py:73
  13.6 6.9 %collective-permute-start.5 = (f32[16,512]{1,0:T(8,128)S(1)}, f32[16,512]{1,0:T(8,128)S(1)}, u32[]{:S(2)}, u32[]{:S(2)}) collective-permute-start(f32[16,512]{1,0:T(8,128)S(1)} %get-tuple-element.39), channel_id=1, source_target_pairs={{0,24},{4,28},{8,16},{12,20},{16,8},{20,12},{24,0},{28,4},{1,25},{... | collective-permute-start | bytes 98312 | tf_op jit(solution)/shard_map/ppermute | solution.py:73
  16.8 4.8 %collective-permute-start.6 = (f32[16,512]{1,0:T(8,128)S(1)}, f32[16,512]{1,0:T(8,128)S(1)}, u32[]{:S(2)}, u32[]{:S(2)}) collective-permute-start(f32[16,512]{1,0:T(8,128)S(1)} %get-tuple-element.40), channel_id=1, source_target_pairs={{0,16},{4,20},{8,24},{12,28},{16,0},{20,4},{24,8},{28,12},{1,17},{... | collective-permute-start | bytes 98312 | tf_op jit(solution)/shard_map/ppermute | solution.py:73
  16.8 4.8 %collective-permute-start.7 = (f32[16,512]{1,0:T(8,128)S(1)}, f32[16,512]{1,0:T(8,128)S(1)}, u32[]{:S(2)}, u32[]{:S(2)}) collective-permute-start(f32[16,512]{1,0:T(8,128)S(1)} %get-tuple-element.41), channel_id=1, source_target_pairs={{0,8},{4,12},{8,0},{12,4},{16,24},{20,28},{24,16},{28,20},{1,9},{5... | collective-permute-start | bytes 98312 | tf_op jit(solution)/shard_map/ppermute | solution.py:73
  18.0 7.3 %collective-permute-start.13 = (bf16[272,128]{1,0:T(8,128)(2,1)S(1)}, bf16[272,128]{1,0:T(8,128)(2,1)S(1)}, u32[]{:S(2)}, u32[]{:S(2)}) collective-permute-start(bf16[272,128]{1,0:T(8,128)(2,1)S(1)} %get-tuple-element.49), channel_id=1, source_target_pairs={{0,3},{1,2},{2,1},{3,0},{4,7},{5,6},{6,5},{7,4},{8,11},{9,10},{10,... | collective-permute-start | bytes 208904 | tf_op jit(solution)/shard_map/ppermute | solution.py:73
  20.5 4.8 %collective-permute-start.11 = (bf16[272,128]{1,0:T(8,128)(2,1)S(1)}, bf16[272,128]{1,0:T(8,128)(2,1)S(1)}, u32[]{:S(2)}, u32[]{:S(2)}) collective-permute-start(bf16[272,128]{1,0:T(8,128)(2,1)S(1)} %get-tuple-element.47), channel_id=1, source_target_pairs={{0,1},{1,0},{2,3},{3,2},{4,5},{5,4},{6,7},{7,6},{8,9},{9,8},{10,11... | collective-permute-start | bytes 208904 | tf_op jit(solution)/shard_map/ppermute | solution.py:73
  21.8 5.1 %collective-permute-start.8 = (bf16[16,1280]{1,0:T(8,128)(2,1)S(1)}, bf16[16,1280]{1,0:T(8,128)(2,1)S(1)}, u32[]{:S(2)}, u32[]{:S(2)}) collective-permute-start(bf16[16,1280]{1,0:T(8,128)(2,1)S(1)} %get-tuple-element.43), channel_id=1, source_target_pairs={{0,3},{1,2},{2,1},{3,0},{4,7},{5,6},{6,5},{7,4},{8,11},{9,10},{10,... | collective-permute-start | bytes 122888 | tf_op jit(solution)/shard_map/ppermute | solution.py:73
  23.6 4.0 %collective-permute-start.9 = (bf16[16,1280]{1,0:T(8,128)(2,1)S(1)}, bf16[16,1280]{1,0:T(8,128)(2,1)S(1)}, u32[]{:S(2)}, u32[]{:S(2)}) collective-permute-start(bf16[16,1280]{1,0:T(8,128)(2,1)S(1)} %get-tuple-element.44), channel_id=1, source_target_pairs={{0,2},{1,3},{2,0},{3,1},{4,6},{5,7},{6,4},{7,5},{8,10},{9,11},{10,... | collective-permute-start | bytes 122888 | tf_op jit(solution)/shard_map/ppermute | solution.py:73
  24.8 4.0 %collective-permute-start.10 = (bf16[16,1280]{1,0:T(8,128)(2,1)S(1)}, bf16[16,1280]{1,0:T(8,128)(2,1)S(1)}, u32[]{:S(2)}, u32[]{:S(2)}) collective-permute-start(bf16[16,1280]{1,0:T(8,128)(2,1)S(1)} %get-tuple-element.45), channel_id=1, source_target_pairs={{0,1},{1,0},{2,3},{3,2},{4,5},{5,4},{6,7},{7,6},{8,9},{9,8},{10,11... | collective-permute-start | bytes 122888 | tf_op jit(solution)/shard_map/ppermute | solution.py:73

commit v18 on v16

--- a/solution.py
+++ b/solution.py
@@ -16,7 +16,8 @@
 
 NEGATIVE = -1e30
 SCORE_SCALE = HD ** (-0.5)
-PART = 64
+PART = 256
+PREPARE_FLOPS = 1_000_000_000_000
 CACHE_HINT = 120_000_000
 PROJECT_HINT = 60_000_000
 PACK_HINT = 60_000_000
@@ -61,8 +62,8 @@
     return [(lines[2 * r], lines[2 * r + 1]) for r in range(rows)]
 
 
-def hint(size):
-    return pl.CostEstimate(flops=0, bytes_accessed=size, transcendentals=0)
+def hint(size, flops=0):
+    return pl.CostEstimate(flops=flops, bytes_accessed=size, transcendentals=0)
 
 
 def dot(left, right, dims):
@@ -245,7 +246,7 @@
             pltpu.SemaphoreType.DMA((loads,)),
         ],
         compiler_params=params(CACHE_KIB),
-        cost_estimate=hint(CACHE_HINT),
+        cost_estimate=hint(CACHE_HINT, PREPARE_FLOPS),
         name="prepare",
     )(*operands)
     return out[0], out[1], out[2], out[3], out[4:]

time: 29.3 us -> 31.8 us (1.085)
  Pallas kernels: 6.72 us -> 8.7 us
  waiting for transfers between devices: 2.38 us -> 3.32 us
  starting transfers between devices: 19.4 us -> 18.9 us
    pallas_call x1, Pallas kernels: 0.47 us -> 1.7 us  [mate_weights(): pl.pallas_call(dequantize, out_shape=jax.ShapeDtypeStruct(codes.shape, jn...]
    ppermute x14, waiting for transfers between devices: 2.38 us -> 3.32 us  [swap(): return lax.ppermute(x, axis, [(k, k ^ distance) for k in range(size)])]
    pallas_call x1, Pallas kernels: 1.3 us -> 2.2 us  [project(): pl.pallas_call(functools.partial(project_kernel, pairs), out_shape=[jax.S...]
    ppermute x14, starting transfers between devices: 19.4 us -> 18.9 us  [swap(): return lax.ppermute(x, axis, [(k, k ^ distance) for k in range(size)])]
  transfers between devices with their start and end apart: 14 -> 14, of which waited for: 4 -> 4; matrix products, arithmetic and copies ran while one was open for 0% -> 0% of each run, Pallas kernels for 19% -> 24%
where the time goes in v18:
time: 31.8 us; the launch traced here: 31.6 us
  starting transfers between devices  18.9 us (59%)
  Pallas kernels  8.7 us (27%)
  waiting for transfers between devices  3.32 us (10%)
  between operations  0.72 us (2%)
    ppermute x14, starting transfers between devices, swap(): return lax.ppermute(x, axis, [(k, k ^ distance) for k in range(size)])  18.9 us
    ppermute x14, waiting for transfers between devices, swap(): return lax.ppermute(x, axis, [(k, k ^ distance) for k in range(size)])  3.32 us
    pallas_call x1, Pallas kernels, prepare(): pl.pallas_call(functools.partial(prepare_kernel, rows, steps, own, min(ow...  3.29 us
    pallas_call x1, Pallas kernels, project(): pl.pallas_call(functools.partial(project_kernel, pairs), out_shape=[jax.S...  2.2 us
    pallas_call x1, Pallas kernels, mate_weights(): pl.pallas_call(dequantize, out_shape=jax.ShapeDtypeStruct(codes.shape, jn...  1.7 us
    pallas_call x1, Pallas kernels, finish(): pl.pallas_call(functools.partial(finish_kernel, rows, steps, own, min(own...  1.06 us
  transfers between devices with their start and end apart: 14, of which 4 were waited for; matrix products, arithmetic and copies ran while one was open for 0% of the time, Pallas kernels for 24%

profile of v18, /device:TPU:0, one launch (start us, length us, event | category | flops | bytes accessed | tf_op | source)
XLA Modules:
  0.0 31.6 jit_solution(17557642209090317816)
XLA Ops:
  0.6 5.1 %collective-permute-start.2 = (bf16[16,2048]{1,0:T(8,128)(2,1)}, bf16[16,2048]{1,0:T(8,128)(2,1)}, u32[]{:S(2)}, u32[]{:S(2)}) collective-permute-start(bf16[16,2048]{1,0:T(8,128)(2,1)} %bitcast.7), channel_id=1, source_target_pairs={{0,24},{4,28},{8,16},{12,20},{16,8},{20,12},{24,0},{28,4},{1,25},{... | collective-permute-start | bytes 196616 | tf_op jit(solution)/shard_map/ppermute | solution.py:75
  5.7 0.0 collective-permute-start.1
  5.8 0.6 %collective-permute-start = (bf16[16,2048]{1,0:T(8,128)(2,1)}, bf16[16,2048]{1,0:T(8,128)(2,1)}, u32[]{:S(2)}, u32[]{:S(2)}) collective-permute-start(bf16[16,2048]{1,0:T(8,128)(2,1)} %bitcast.9), channel_id=1, source_target_pairs={{0,8},{4,12},{8,0},{12,4},{16,24},{20,28},{24,16},{28,20},{1,9},{5... | collective-permute-start | bytes 196616 | tf_op jit(solution)/shard_map/ppermute | solution.py:75
  6.4 0.0 collective-permute-start.4
  6.4 0.5 %collective-permute-start.3 = (bf16[256,2048]{1,0:T(8,128)(2,1)}, bf16[256,2048]{1,0:T(8,128)(2,1)}, u32[]{:S(2)}, u32[]{:S(2)}) collective-permute-start(bf16[256,2048]{1,0:T(8,128)(2,1)} %codes_hbm.1), channel_id=1, source_target_pairs={{0,4},{4,0},{8,12},{12,8},{16,20},{20,16},{24,28},{28,24},{1,5},{5... | collective-permute-start | bytes 3145736 | tf_op jit(solution)/shard_map/ppermute | solution.py:75
  6.9 3.3 %prepare.1 = (bf16[256,2048]{1,0:T(8,128)(2,1)S(1)}, bf16[2,256,2048]{2,1,0:T(8,128)(2,1)S(1)}, bf16[256,128]{1,0:T(8,128)(2,1)S(1)}, s32[8,128]{1,0:T(8,128)S(1...) custom-call(s32[8]{0:T(128)} %owner_hbm.1, ...), custom_call_target="tpu_custom_call" | custom-call | flops 999999995904 | bytes 120000000 | tf_op jit(solution)/shard_map/prepare/pallas_call | solution.py:227
  10.2 0.0 copy-start
  10.2 0.0 collective-permute-done.4
  10.2 1.7 %collective-permute-start.11 = (bf16[272,128]{1,0:T(8,128)(2,1)S(1)}, bf16[272,128]{1,0:T(8,128)(2,1)S(1)}, u32[]{:S(2)}, u32[]{:S(2)}) collective-permute-start(bf16[272,128]{1,0:T(8,128)(2,1)S(1)} %get-tuple-element.45), channel_id=1, source_target_pairs={{0,1},{1,0},{2,3},{3,2},{4,5},{5,4},{6,7},{7,6},{8,9},{9,8},{10,11... | collective-permute-start | bytes 208904 | tf_op jit(solution)/shard_map/ppermute | solution.py:75
  11.9 0.0 collective-permute-done.3.codes_ref
  11.9 1.7 %mate_weights.1.mate_ref = bf16[256,2048]{1,0:T(8,128)(2,1)S(1)} custom-call(bf16[256,2048]{1,0:T(8,128)(2,1)} %collective-permute-done.3.codes_ref, bf16[16,256]{1,0:T(8,128)(2,1)} %bitcast.1.scales_ref), custom_call_target="tpu_custom_call" | custom-call | bytes 1000 | tf_op jit(solution)/shard_map/mate_weights/pallas_call | solution.py:100
  13.6 0.0 collective-permute-done.2.refs_3_
  13.6 0.0 collective-permute-done.1.refs_2_
  13.6 0.0 collective-permute-done.refs_1_
  13.7 0.0 copy-done
  13.7 2.2 %project.1 = (f32[16,512]{1,0:T(8,128)S(1)}, f32[16,512]{1,0:T(8,128)S(1)}, f32[16,512]{1,0:T(8,128)S(1)}, f32[16,512]{1,0:T(8,128)S(1)}) custom-call(bf16[256,2048]{1,0:T(8,128)(2,1)S(1)} %get-tuple-element.29.own_ref, bf16[256,2048]{1,0:T(8,128)(2,1)S(1)} %mate_weights.1.mate_ref, bf16[2,256,2048]{2,1,0:T(8,128)(2,1)S(1)} %get-tuple-element.31.base_ref, ...), custom_call_target="tpu_custom_call" | custom-call | bytes 60000000 | tf_op jit(solution)/shard_map/project/pallas_call | solution.py:306
  15.9 3.7 %collective-permute-start.5 = (f32[16,512]{1,0:T(8,128)S(1)}, f32[16,512]{1,0:T(8,128)S(1)}, u32[]{:S(2)}, u32[]{:S(2)}) collective-permute-start(f32[16,512]{1,0:T(8,128)S(1)} %get-tuple-element.37), channel_id=1, source_target_pairs={{0,24},{4,28},{8,16},{12,20},{16,8},{20,12},{24,0},{28,4},{1,25},{... | collective-permute-start | bytes 98312 | tf_op jit(solution)/shard_map/ppermute | solution.py:75
  19.5 0.0 collective-permute-start.6
  19.5 0.8 %collective-permute-start.7 = (f32[16,512]{1,0:T(8,128)S(1)}, f32[16,512]{1,0:T(8,128)S(1)}, u32[]{:S(2)}, u32[]{:S(2)}) collective-permute-start(f32[16,512]{1,0:T(8,128)S(1)} %get-tuple-element.39), channel_id=1, source_target_pairs={{0,8},{4,12},{8,0},{12,4},{16,24},{20,28},{24,16},{28,20},{1,9},{5... | collective-permute-start | bytes 98312 | tf_op jit(solution)/shard_map/ppermute | solution.py:75
  20.3 1.5 %collective-permute-start.12 = (bf16[272,128]{1,0:T(8,128)(2,1)S(1)}, bf16[272,128]{1,0:T(8,128)(2,1)S(1)}, u32[]{:S(2)}, u32[]{:S(2)}) collective-permute-start(bf16[272,128]{1,0:T(8,128)(2,1)S(1)} %get-tuple-element.46), channel_id=1, source_target_pairs={{0,2},{1,3},{2,0},{3,1},{4,6},{5,7},{6,4},{7,5},{8,10},{9,11},{10,... | collective-permute-start | bytes 208904 | tf_op jit(solution)/shard_map/ppermute | solution.py:75
  21.8 0.0 collective-permute-done.5.refs_1_
  21.8 1.4 %collective-permute-start.13 = (bf16[272,128]{1,0:T(8,128)(2,1)S(1)}, bf16[272,128]{1,0:T(8,128)(2,1)S(1)}, u32[]{:S(2)}, u32[]{:S(2)}) collective-permute-start(bf16[272,128]{1,0:T(8,128)(2,1)S(1)} %get-tuple-element.47), channel_id=1, source_target_pairs={{0,3},{1,2},{2,1},{3,0},{4,7},{5,6},{6,5},{7,4},{8,11},{9,10},{10,... | collective-permute-start | bytes 208904 | tf_op jit(solution)/shard_map/ppermute | solution.py:75
  23.2 1.1 %collective-permute-done.6.refs_2_ = f32[16,512]{1,0:T(8,128)S(1)} collective-permute-done((f32[16,512]{1,0:T(8,128)S(1)}, f32[16,512]{1,0:T(8,128)S(1)}, u32[]{:S(2)}, u32[]{:S(2)}) %collective-permute-start.6) | collective-permute-done | bytes 32800 | tf_op jit(solution)/shard_map/ppermute | solution.py:75
  24.4 0.0 collective-permute-done.7.refs_3_
  24.4 0.1 pack_pieces.1
  24.5 1.5 %collective-permute-start.8 = (bf16[16,1280]{1,0:T(8,128)(2,1)S(1)}, bf16[16,1280]{1,0:T(8,128)(2,1)S(1)}, u32[]{:S(2)}, u32[]{:S(2)}) collective-permute-start(bf16[16,1280]{1,0:T(8,128)(2,1)S(1)} %get-tuple-element.41), channel_id=1, source_target_pairs={{0,3},{1,2},{2,1},{3,0},{4,7},{5,6},{6,5},{7,4},{8,11},{9,10},{10,... | collective-permute-start | bytes 122888 | tf_op jit(solution)/shard_map/ppermute | solution.py:75
  26.0 0.5 %collective-permute-start.9 = (bf16[16,1280]{1,0:T(8,128)(2,1)S(1)}, bf16[16,1280]{1,0:T(8,128)(2,1)S(1)}, u32[]{:S(2)}, u32[]{:S(2)}) collective-permute-start(bf16[16,1280]{1,0:T(8,128)(2,1)S(1)} %get-tuple-element.42), channel_id=1, source_target_pairs={{0,2},{1,3},{2,0},{3,1},{4,6},{5,7},{6,4},{7,5},{8,10},{9,11},{10,... | collective-permute-start | bytes 122888 | tf_op jit(solution)/shard_map/ppermute | solution.py:75
  26.5 0.0 collective-permute-done.11.refs_1_
  26.5 1.5 %collective-permute-start.10 = (bf16[16,1280]{1,0:T(8,128)(2,1)S(1)}, bf16[16,1280]{1,0:T(8,128)(2,1)S(1)}, u32[]{:S(2)}, u32[]{:S(2)}) collective-permute-start(bf16[16,1280]{1,0:T(8,128)(2,1)S(1)} %get-tuple-element.43), channel_id=1, source_target_pairs={{0,1},{1,0},{2,3},{3,2},{4,5},{5,4},{6,7},{7,6},{8,9},{9,8},{10,11... | collective-permute-start | bytes 122888 | tf_op jit(solution)/shard_map/ppermute | solution.py:75
  28.0 0.0 collective-permute-done.12.refs_2_
  28.0 0.0 collective-permute-done.13.refs_3_
  28.0 0.3 %merge_partials.1.refs_4_ = f32[264,128]{1,0:T(8,128)S(1)} custom-call(f32[264,128]{1,0:T(8,128)S(1)} %get-tuple-element.44.refs_0_, bf16[272,128]{1,0:T(8,128)(2,1)S(1)} %collective-permute-done.11.refs_1_, bf16[272,128]{1,0:T(8,128)(2,1)S(1)} %collective-permute-done.12.refs_2_, bf16[272,128]{1,0:T(8,128)(2,1)S(1)} %collective-permute-done.13.refs_3_), custom_call_target="tpu_custom_call" | custom-call | bytes 1000 | tf_op jit(solution)/shard_map/merge_partials/pallas_call | solution.py:280
  28.4 1.0 %collective-permute-done.8.refs_1_ = bf16[16,1280]{1,0:T(8,128)(2,1)S(1)} collective-permute-done((bf16[16,1280]{1,0:T(8,128)(2,1)S(1)}, bf16[16,1280]{1,0:T(8,128)(2,1)S(1)}, u32[]{:S(2)}, u32[]{:S(2)}) %collective-permute-start.8) | collective-permute-done | bytes 40992 | tf_op jit(solution)/shard_map/ppermute | solution.py:75
  29.4 0.6 %collective-permute-done.9.refs_2_ = bf16[16,1280]{1,0:T(8,128)(2,1)S(1)} collective-permute-done((bf16[16,1280]{1,0:T(8,128)(2,1)S(1)}, bf16[16,1280]{1,0:T(8,128)(2,1)S(1)}, u32[]{:S(2)}, u32[]{:S(2)}) %collective-permute-start.9) | collective-permute-done | bytes 40992 | tf_op jit(solution)/shard_map/ppermute | solution.py:75
  30.0 0.5 %collective-permute-done.10.refs_3_ = bf16[16,1280]{1,0:T(8,128)(2,1)S(1)} collective-permute-done((bf16[16,1280]{1,0:T(8,128)(2,1)S(1)}, bf16[16,1280]{1,0:T(8,128)(2,1)S(1)}, u32[]{:S(2)}, u32[]{:S(2)}) %collective-permute-start.10) | collective-permute-done | bytes 40992 | tf_op jit(solution)/shard_map/ppermute | solution.py:75
  30.5 1.1 %finish.1 = (bf16[16,512]{1,0:T(8,128)(2,1)}, bf16[16,2048]{1,0:T(8,128)(2,1)}) custom-call(bf16[256,128]{1,0:T(8,128)(2,1)S(1)} %get-tuple-element.27.query_ref, f32[16,1024]{1,0:T(8,128)S(1)} %get-tuple-element.40.refs_0_, bf16[16,1280]{1,0:T(8,128)(2,1)S(1)} %collective-permute-done.8.refs_1_, bf16[16,1280]{1,0:T(8,128)(2,1)S(1)} %collective-permute-done.9.refs_2_, ...), custom_call_target="tpu_custom_call" | custom-call | tf_op jit(solution)/shard_map/finish/pallas_call | solution.py:456
Async XLA Ops:
  0.6 13.0 %collective-permute-start.2 = (bf16[16,2048]{1,0:T(8,128)(2,1)}, bf16[16,2048]{1,0:T(8,128)(2,1)}, u32[]{:S(2)}, u32[]{:S(2)}) collective-permute-start(bf16[16,2048]{1,0:T(8,128)(2,1)} %bitcast.7), channel_id=1, source_target_pairs={{0,24},{4,28},{8,16},{12,20},{16,8},{20,12},{24,0},{28,4},{1,25},{... | collective-permute-start | bytes 196616 | tf_op jit(solution)/shard_map/ppermute | solution.py:75
  5.7 7.9 %collective-permute-start.1 = (bf16[16,2048]{1,0:T(8,128)(2,1)}, bf16[16,2048]{1,0:T(8,128)(2,1)}, u32[]{:S(2)}, u32[]{:S(2)}) collective-permute-start(bf16[16,2048]{1,0:T(8,128)(2,1)} %bitcast.8), channel_id=1, source_target_pairs={{0,16},{4,20},{8,24},{12,28},{16,0},{20,4},{24,8},{28,12},{1,17},{... | collective-permute-start | bytes 196616 | tf_op jit(solution)/shard_map/ppermute | solution.py:75
  5.8 7.9 %collective-permute-start = (bf16[16,2048]{1,0:T(8,128)(2,1)}, bf16[16,2048]{1,0:T(8,128)(2,1)}, u32[]{:S(2)}, u32[]{:S(2)}) collective-permute-start(bf16[16,2048]{1,0:T(8,128)(2,1)} %bitcast.9), channel_id=1, source_target_pairs={{0,8},{4,12},{8,0},{12,4},{16,24},{20,28},{24,16},{28,20},{1,9},{5... | collective-permute-start | bytes 196616 | tf_op jit(solution)/shard_map/ppermute | solution.py:75
  6.4 3.8 %collective-permute-start.4 = (bf16[256,16]{0,1:T(8,128)(2,1)}, bf16[256,16]{0,1:T(8,128)(2,1)}, u32[]{:S(2)}, u32[]{:S(2)}) collective-permute-start(bf16[256,16]{0,1:T(8,128)(2,1)} %param.11), channel_id=1, source_target_pairs={{0,4},{4,0},{8,12},{12,8},{16,20},{20,16},{24,28},{28,24},{1,5},{5... | collective-permute-start | bytes 24584 | tf_op jit(solution)/shard_map/ppermute | solution.py:75
  6.4 5.5 %collective-permute-start.3 = (bf16[256,2048]{1,0:T(8,128)(2,1)}, bf16[256,2048]{1,0:T(8,128)(2,1)}, u32[]{:S(2)}, u32[]{:S(2)}) collective-permute-start(bf16[256,2048]{1,0:T(8,128)(2,1)} %codes_hbm.1), channel_id=1, source_target_pairs={{0,4},{4,0},{8,12},{12,8},{16,20},{20,16},{24,28},{28,24},{1,5},{5... | collective-permute-start | bytes 3145736 | tf_op jit(solution)/shard_map/ppermute | solution.py:75
  10.2 3.5 %copy-start = (bf16[2,8,2048]{2,1,0:T(8,128)(2,1)S(1)}, bf16[2,8,2048]{2,1,0:T(8,128)(2,1)}, u32[]{:S(2)}) copy-start(bf16[2,8,2048]{2,1,0:T(8,128)(2,1)} %param.8) | copy-start | bytes 196612
  10.2 16.3 %collective-permute-start.11 = (bf16[272,128]{1,0:T(8,128)(2,1)S(1)}, bf16[272,128]{1,0:T(8,128)(2,1)S(1)}, u32[]{:S(2)}, u32[]{:S(2)}) collective-permute-start(bf16[272,128]{1,0:T(8,128)(2,1)S(1)} %get-tuple-element.45), channel_id=1, source_target_pairs={{0,1},{1,0},{2,3},{3,2},{4,5},{5,4},{6,7},{7,6},{8,9},{9,8},{10,11... | collective-permute-start | bytes 208904 | tf_op jit(solution)/shard_map/ppermute | solution.py:75
  15.9 6.0 %collective-permute-start.5 = (f32[16,512]{1,0:T(8,128)S(1)}, f32[16,512]{1,0:T(8,128)S(1)}, u32[]{:S(2)}, u32[]{:S(2)}) collective-permute-start(f32[16,512]{1,0:T(8,128)S(1)} %get-tuple-element.37), channel_id=1, source_target_pairs={{0,24},{4,28},{8,16},{12,20},{16,8},{20,12},{24,0},{28,4},{1,25},{... | collective-permute-start | bytes 98312 | tf_op jit(solution)/shard_map/ppermute | solution.py:75
  19.5 4.8 %collective-permute-start.6 = (f32[16,512]{1,0:T(8,128)S(1)}, f32[16,512]{1,0:T(8,128)S(1)}, u32[]{:S(2)}, u32[]{:S(2)}) collective-permute-start(f32[16,512]{1,0:T(8,128)S(1)} %get-tuple-element.38), channel_id=1, source_target_pairs={{0,16},{4,20},{8,24},{12,28},{16,0},{20,4},{24,8},{28,12},{1,17},{... | collective-permute-start | bytes 98312 | tf_op jit(solution)/shard_map/ppermute | solution.py:75
  19.5 4.8 %collective-permute-start.7 = (f32[16,512]{1,0:T(8,128)S(1)}, f32[16,512]{1,0:T(8,128)S(1)}, u32[]{:S(2)}, u32[]{:S(2)}) collective-permute-start(f32[16,512]{1,0:T(8,128)S(1)} %get-tuple-element.39), channel_id=1, source_target_pairs={{0,8},{4,12},{8,0},{12,4},{16,24},{20,28},{24,16},{28,20},{1,9},{5... | collective-permute-start | bytes 98312 | tf_op jit(solution)/shard_map/ppermute | solution.py:75
  20.3 7.7 %collective-permute-start.12 = (bf16[272,128]{1,0:T(8,128)(2,1)S(1)}, bf16[272,128]{1,0:T(8,128)(2,1)S(1)}, u32[]{:S(2)}, u32[]{:S(2)}) collective-permute-start(bf16[272,128]{1,0:T(8,128)(2,1)S(1)} %get-tuple-element.46), channel_id=1, source_target_pairs={{0,2},{1,3},{2,0},{3,1},{4,6},{5,7},{6,4},{7,5},{8,10},{9,11},{10,... | collective-permute-start | bytes 208904 | tf_op jit(solution)/shard_map/ppermute | solution.py:75
  21.8 6.2 %collective-permute-start.13 = (bf16[272,128]{1,0:T(8,128)(2,1)S(1)}, bf16[272,128]{1,0:T(8,128)(2,1)S(1)}, u32[]{:S(2)}, u32[]{:S(2)}) collective-permute-start(bf16[272,128]{1,0:T(8,128)(2,1)S(1)} %get-tuple-element.47), channel_id=1, source_target_pairs={{0,3},{1,2},{2,1},{3,0},{4,7},{5,6},{6,5},{7,4},{8,11},{9,10},{10,... | collective-permute-start | bytes 208904 | tf_op jit(solution)/shard_map/ppermute | solution.py:75
  24.5 5.0 %collective-permute-start.8 = (bf16[16,1280]{1,0:T(8,128)(2,1)S(1)}, bf16[16,1280]{1,0:T(8,128)(2,1)S(1)}, u32[]{:S(2)}, u32[]{:S(2)}) collective-permute-start(bf16[16,1280]{1,0:T(8,128)(2,1)S(1)} %get-tuple-element.41), channel_id=1, source_target_pairs={{0,3},{1,2},{2,1},{3,0},{4,7},{5,6},{6,5},{7,4},{8,11},{9,10},{10,... | collective-permute-start | bytes 122888 | tf_op jit(solution)/shard_map/ppermute | solution.py:75
  26.0 4.0 %collective-permute-start.9 = (bf16[16,1280]{1,0:T(8,128)(2,1)S(1)}, bf16[16,1280]{1,0:T(8,128)(2,1)S(1)}, u32[]{:S(2)}, u32[]{:S(2)}) collective-permute-start(bf16[16,1280]{1,0:T(8,128)(2,1)S(1)} %get-tuple-element.42), channel_id=1, source_target_pairs={{0,2},{1,3},{2,0},{3,1},{4,6},{5,7},{6,4},{7,5},{8,10},{9,11},{10,... | collective-permute-start | bytes 122888 | tf_op jit(solution)/shard_map/ppermute | solution.py:75
  26.5 4.0 %collective-permute-start.10 = (bf16[16,1280]{1,0:T(8,128)(2,1)S(1)}, bf16[16,1280]{1,0:T(8,128)(2,1)S(1)}, u32[]{:S(2)}, u32[]{:S(2)}) collective-permute-start(bf16[16,1280]{1,0:T(8,128)(2,1)S(1)} %get-tuple-element.43), channel_id=1, source_target_pairs={{0,1},{1,0},{2,3},{3,2},{4,5},{5,4},{6,7},{7,6},{8,9},{9,8},{10,11... | collective-permute-start | bytes 122888 | tf_op jit(solution)/shard_map/ppermute | solution.py:75

commit v19 on v18

--- a/solution.py
+++ b/solution.py
@@ -17,7 +17,7 @@
 NEGATIVE = -1e30
 SCORE_SCALE = HD ** (-0.5)
 PART = 256
-PREPARE_FLOPS = 1_000_000_000_000
+PREPARE_FLOPS = 15_000_000_000
 CACHE_HINT = 120_000_000
 PROJECT_HINT = 60_000_000
 PACK_HINT = 60_000_000

time: 31.8 us -> 29.6 us (0.931)
  Pallas kernels: 8.7 us -> 6.57 us
    pallas_call x1, Pallas kernels: 1.7 us -> 0.47 us  [mate_weights(): pl.pallas_call(dequantize, out_shape=jax.ShapeDtypeStruct(codes.shape, jn...]
    pallas_call x1, Pallas kernels: 2.2 us -> 1.3 us  [project(): pl.pallas_call(functools.partial(project_kernel, pairs), out_shape=[jax.S...]
  transfers between devices with their start and end apart: 14 -> 14, of which waited for: 4 -> 4; matrix products, arithmetic and copies ran while one was open for 0% -> 0% of each run, Pallas kernels for 24% -> 19%
where the time goes in v19:
time: 29.6 us; the launch traced here: 29.5 us
  starting transfers between devices  18.9 us (64%)
  Pallas kernels  6.57 us (22%)
  waiting for transfers between devices  3.3 us (11%)
  between operations  0.71 us (2%)
    ppermute x14, starting transfers between devices, swap(): return lax.ppermute(x, axis, [(k, k ^ distance) for k in range(size)])  18.9 us
    ppermute x14, waiting for transfers between devices, swap(): return lax.ppermute(x, axis, [(k, k ^ distance) for k in range(size)])  3.3 us
    pallas_call x1, Pallas kernels, prepare(): pl.pallas_call(functools.partial(prepare_kernel, rows, steps, own, min(ow...  3.29 us
    pallas_call x1, Pallas kernels, project(): pl.pallas_call(functools.partial(project_kernel, pairs), out_shape=[jax.S...  1.3 us
    pallas_call x1, Pallas kernels, finish(): pl.pallas_call(functools.partial(finish_kernel, rows, steps, own, min(own...  1.06 us
  transfers between devices with their start and end apart: 14, of which 4 were waited for; matrix products, arithmetic and copies ran while one was open for 0% of the time, Pallas kernels for 19%

profile of v19, /device:TPU:0, one launch (start us, length us, event | category | flops | bytes accessed | tf_op | source)
XLA Modules:
  0.0 29.5 jit_solution(2283772122776887239)
XLA Ops:
  0.6 5.1 %collective-permute-start.2 = (bf16[16,2048]{1,0:T(8,128)(2,1)}, bf16[16,2048]{1,0:T(8,128)(2,1)S(1)}, u32[]{:S(2)}, u32[]{:S(2)}) collective-permute-start(bf16[16,2048]{1,0:T(8,128)(2,1)} %bitcast.7), channel_id=1, source_target_pairs={{0,24},{4,28},{8,16},{12,20},{16,8},{20,12},{24,0},{28,4},{1,25},{... | collective-permute-start | bytes 196616 | tf_op jit(solution)/shard_map/ppermute | solution.py:75
  5.7 0.0 collective-permute-start.1
  5.8 0.6 %collective-permute-start = (bf16[16,2048]{1,0:T(8,128)(2,1)}, bf16[16,2048]{1,0:T(8,128)(2,1)S(1)}, u32[]{:S(2)}, u32[]{:S(2)}) collective-permute-start(bf16[16,2048]{1,0:T(8,128)(2,1)} %bitcast.9), channel_id=1, source_target_pairs={{0,8},{4,12},{8,0},{12,4},{16,24},{20,28},{24,16},{28,20},{1,9},{5... | collective-permute-start | bytes 196616 | tf_op jit(solution)/shard_map/ppermute | solution.py:75
  6.4 0.0 collective-permute-start.4
  6.4 0.5 %collective-permute-start.3 = (bf16[256,2048]{1,0:T(8,128)(2,1)}, bf16[256,2048]{1,0:T(8,128)(2,1)S(1)}, u32[]{:S(2)}, u32[]{:S(2)}) collective-permute-start(bf16[256,2048]{1,0:T(8,128)(2,1)} %codes_hbm.1), channel_id=1, source_target_pairs={{0,4},{4,0},{8,12},{12,8},{16,20},{20,16},{24,28},{28,24},{1,5},{5... | collective-permute-start | bytes 3145736 | tf_op jit(solution)/shard_map/ppermute | solution.py:75
  6.9 3.3 %prepare.1 = (bf16[256,2048]{1,0:T(8,128)(2,1)S(1)}, bf16[2,256,2048]{2,1,0:T(8,128)(2,1)S(1)}, bf16[256,128]{1,0:T(8,128)(2,1)S(1)}, s32[8,128]{1,0:T(8,128)S(1...) custom-call(s32[8]{0:T(128)} %owner_hbm.1, ...), custom_call_target="tpu_custom_call" | custom-call | flops 15000000512 | bytes 120000000 | tf_op jit(solution)/shard_map/prepare/pallas_call | solution.py:227
  10.2 0.0 copy-start
  10.2 0.0 collective-permute-done.4
  10.2 1.7 %collective-permute-start.11 = (bf16[272,128]{1,0:T(8,128)(2,1)S(1)}, bf16[272,128]{1,0:T(8,128)(2,1)S(1)}, u32[]{:S(2)}, u32[]{:S(2)}) collective-permute-start(bf16[272,128]{1,0:T(8,128)(2,1)S(1)} %get-tuple-element.45), channel_id=1, source_target_pairs={{0,1},{1,0},{2,3},{3,2},{4,5},{5,4},{6,7},{7,6},{8,9},{9,8},{10,11... | collective-permute-start | bytes 208904 | tf_op jit(solution)/shard_map/ppermute | solution.py:75
  11.9 0.0 collective-permute-done.3.codes_ref
  11.9 0.5 %mate_weights.1.mate_ref = bf16[256,2048]{1,0:T(8,128)(2,1)S(1)} custom-call(bf16[256,2048]{1,0:T(8,128)(2,1)S(1)} %collective-permute-done.3.codes_ref, bf16[16,256]{1,0:T(8,128)(2,1)S(1)} %bitcast.11), custom_call_target="tpu_custom_call" | custom-call | bytes 1000 | tf_op jit(solution)/shard_map/mate_weights/pallas_call | solution.py:100
  12.4 0.0 collective-permute-done.2.refs_3_
  12.4 0.0 collective-permute-done.1.refs_2_
  12.4 0.0 collective-permute-done.refs_1_
  12.4 0.0 copy-done
  12.4 1.3 %project.1 = (f32[16,512]{1,0:T(8,128)S(1)}, f32[16,512]{1,0:T(8,128)S(1)}, f32[16,512]{1,0:T(8,128)S(1)}, f32[16,512]{1,0:T(8,128)S(1)}) custom-call(bf16[256,2048]{1,0:T(8,128)(2,1)S(1)} %get-tuple-element.29.own_ref, bf16[256,2048]{1,0:T(8,128)(2,1)S(1)} %mate_weights.1.mate_ref, bf16[2,256,2048]{2,1,0:T(8,128)(2,1)S(1)} %get-tuple-element.31.base_ref, ...), custom_call_target="tpu_custom_call" | custom-call | bytes 60000000 | tf_op jit(solution)/shard_map/project/pallas_call | solution.py:306
  13.7 3.7 %collective-permute-start.5 = (f32[16,512]{1,0:T(8,128)S(1)}, f32[16,512]{1,0:T(8,128)S(1)}, u32[]{:S(2)}, u32[]{:S(2)}) collective-permute-start(f32[16,512]{1,0:T(8,128)S(1)} %get-tuple-element.37), channel_id=1, source_target_pairs={{0,24},{4,28},{8,16},{12,20},{16,8},{20,12},{24,0},{28,4},{1,25},{... | collective-permute-start | bytes 98312 | tf_op jit(solution)/shard_map/ppermute | solution.py:75
  17.4 0.0 collective-permute-start.6
  17.4 0.8 %collective-permute-start.7 = (f32[16,512]{1,0:T(8,128)S(1)}, f32[16,512]{1,0:T(8,128)S(1)}, u32[]{:S(2)}, u32[]{:S(2)}) collective-permute-start(f32[16,512]{1,0:T(8,128)S(1)} %get-tuple-element.39), channel_id=1, source_target_pairs={{0,8},{4,12},{8,0},{12,4},{16,24},{20,28},{24,16},{28,20},{1,9},{5... | collective-permute-start | bytes 98312 | tf_op jit(solution)/shard_map/ppermute | solution.py:75
  18.2 1.5 %collective-permute-start.12 = (bf16[272,128]{1,0:T(8,128)(2,1)S(1)}, bf16[272,128]{1,0:T(8,128)(2,1)S(1)}, u32[]{:S(2)}, u32[]{:S(2)}) collective-permute-start(bf16[272,128]{1,0:T(8,128)(2,1)S(1)} %get-tuple-element.46), channel_id=1, source_target_pairs={{0,2},{1,3},{2,0},{3,1},{4,6},{5,7},{6,4},{7,5},{8,10},{9,11},{10,... | collective-permute-start | bytes 208904 | tf_op jit(solution)/shard_map/ppermute | solution.py:75
  19.7 0.0 collective-permute-done.5.refs_1_
  19.7 1.4 %collective-permute-start.13 = (bf16[272,128]{1,0:T(8,128)(2,1)S(1)}, bf16[272,128]{1,0:T(8,128)(2,1)S(1)}, u32[]{:S(2)}, u32[]{:S(2)}) collective-permute-start(bf16[272,128]{1,0:T(8,128)(2,1)S(1)} %get-tuple-element.47), channel_id=1, source_target_pairs={{0,3},{1,2},{2,1},{3,0},{4,7},{5,6},{6,5},{7,4},{8,11},{9,10},{10,... | collective-permute-start | bytes 208904 | tf_op jit(solution)/shard_map/ppermute | solution.py:75
  21.1 1.1 %collective-permute-done.6.refs_2_ = f32[16,512]{1,0:T(8,128)S(1)} collective-permute-done((f32[16,512]{1,0:T(8,128)S(1)}, f32[16,512]{1,0:T(8,128)S(1)}, u32[]{:S(2)}, u32[]{:S(2)}) %collective-permute-start.6) | collective-permute-done | bytes 32800 | tf_op jit(solution)/shard_map/ppermute | solution.py:75
  22.2 0.0 collective-permute-done.7.refs_3_
  22.2 0.1 pack_pieces.1
  22.3 1.6 %collective-permute-start.8 = (bf16[16,1280]{1,0:T(8,128)(2,1)S(1)}, bf16[16,1280]{1,0:T(8,128)(2,1)S(1)}, u32[]{:S(2)}, u32[]{:S(2)}) collective-permute-start(bf16[16,1280]{1,0:T(8,128)(2,1)S(1)} %get-tuple-element.41), channel_id=1, source_target_pairs={{0,3},{1,2},{2,1},{3,0},{4,7},{5,6},{6,5},{7,4},{8,11},{9,10},{10,... | collective-permute-start | bytes 122888 | tf_op jit(solution)/shard_map/ppermute | solution.py:75
  23.9 0.5 %collective-permute-start.9 = (bf16[16,1280]{1,0:T(8,128)(2,1)S(1)}, bf16[16,1280]{1,0:T(8,128)(2,1)S(1)}, u32[]{:S(2)}, u32[]{:S(2)}) collective-permute-start(bf16[16,1280]{1,0:T(8,128)(2,1)S(1)} %get-tuple-element.42), channel_id=1, source_target_pairs={{0,2},{1,3},{2,0},{3,1},{4,6},{5,7},{6,4},{7,5},{8,10},{9,11},{10,... | collective-permute-start | bytes 122888 | tf_op jit(solution)/shard_map/ppermute | solution.py:75
  24.4 0.0 collective-permute-done.11.refs_1_
  24.4 1.5 %collective-permute-start.10 = (bf16[16,1280]{1,0:T(8,128)(2,1)S(1)}, bf16[16,1280]{1,0:T(8,128)(2,1)S(1)}, u32[]{:S(2)}, u32[]{:S(2)}) collective-permute-start(bf16[16,1280]{1,0:T(8,128)(2,1)S(1)} %get-tuple-element.43), channel_id=1, source_target_pairs={{0,1},{1,0},{2,3},{3,2},{4,5},{5,4},{6,7},{7,6},{8,9},{9,8},{10,11... | collective-permute-start | bytes 122888 | tf_op jit(solution)/shard_map/ppermute | solution.py:75
  25.9 0.0 collective-permute-done.12.refs_2_
  25.9 0.0 collective-permute-done.13.refs_3_
  25.9 0.3 %merge_partials.1.refs_4_ = f32[264,128]{1,0:T(8,128)S(1)} custom-call(f32[264,128]{1,0:T(8,128)S(1)} %get-tuple-element.44.refs_0_, bf16[272,128]{1,0:T(8,128)(2,1)S(1)} %collective-permute-done.11.refs_1_, bf16[272,128]{1,0:T(8,128)(2,1)S(1)} %collective-permute-done.12.refs_2_, bf16[272,128]{1,0:T(8,128)(2,1)S(1)} %collective-permute-done.13.refs_3_), custom_call_target="tpu_custom_call" | custom-call | bytes 1000 | tf_op jit(solution)/shard_map/merge_partials/pallas_call | solution.py:280
  26.2 1.0 %collective-permute-done.8.refs_1_ = bf16[16,1280]{1,0:T(8,128)(2,1)S(1)} collective-permute-done((bf16[16,1280]{1,0:T(8,128)(2,1)S(1)}, bf16[16,1280]{1,0:T(8,128)(2,1)S(1)}, u32[]{:S(2)}, u32[]{:S(2)}) %collective-permute-start.8) | collective-permute-done | bytes 40992 | tf_op jit(solution)/shard_map/ppermute | solution.py:75
  27.3 0.6 %collective-permute-done.9.refs_2_ = bf16[16,1280]{1,0:T(8,128)(2,1)S(1)} collective-permute-done((bf16[16,1280]{1,0:T(8,128)(2,1)S(1)}, bf16[16,1280]{1,0:T(8,128)(2,1)S(1)}, u32[]{:S(2)}, u32[]{:S(2)}) %collective-permute-start.9) | collective-permute-done | bytes 40992 | tf_op jit(solution)/shard_map/ppermute | solution.py:75
  27.9 0.5 %collective-permute-done.10.refs_3_ = bf16[16,1280]{1,0:T(8,128)(2,1)S(1)} collective-permute-done((bf16[16,1280]{1,0:T(8,128)(2,1)S(1)}, bf16[16,1280]{1,0:T(8,128)(2,1)S(1)}, u32[]{:S(2)}, u32[]{:S(2)}) %collective-permute-start.10) | collective-permute-done | bytes 40992 | tf_op jit(solution)/shard_map/ppermute | solution.py:75
  28.4 1.1 %finish.1 = (bf16[16,512]{1,0:T(8,128)(2,1)}, bf16[16,2048]{1,0:T(8,128)(2,1)}) custom-call(bf16[256,128]{1,0:T(8,128)(2,1)S(1)} %get-tuple-element.27.query_ref, f32[16,1024]{1,0:T(8,128)S(1)} %get-tuple-element.40.refs_0_, bf16[16,1280]{1,0:T(8,128)(2,1)S(1)} %collective-permute-done.8.refs_1_, bf16[16,1280]{1,0:T(8,128)(2,1)S(1)} %collective-permute-done.9.refs_2_, ...), custom_call_target="tpu_custom_call" | custom-call | tf_op jit(solution)/shard_map/finish/pallas_call | solution.py:456
Async XLA Ops:
  0.6 11.8 %collective-permute-start.2 = (bf16[16,2048]{1,0:T(8,128)(2,1)}, bf16[16,2048]{1,0:T(8,128)(2,1)S(1)}, u32[]{:S(2)}, u32[]{:S(2)}) collective-permute-start(bf16[16,2048]{1,0:T(8,128)(2,1)} %bitcast.7), channel_id=1, source_target_pairs={{0,24},{4,28},{8,16},{12,20},{16,8},{20,12},{24,0},{28,4},{1,25},{... | collective-permute-start | bytes 196616 | tf_op jit(solution)/shard_map/ppermute | solution.py:75
  5.7 6.7 %collective-permute-start.1 = (bf16[16,2048]{1,0:T(8,128)(2,1)}, bf16[16,2048]{1,0:T(8,128)(2,1)S(1)}, u32[]{:S(2)}, u32[]{:S(2)}) collective-permute-start(bf16[16,2048]{1,0:T(8,128)(2,1)} %bitcast.8), channel_id=1, source_target_pairs={{0,16},{4,20},{8,24},{12,28},{16,0},{20,4},{24,8},{28,12},{1,17},{... | collective-permute-start | bytes 196616 | tf_op jit(solution)/shard_map/ppermute | solution.py:75
  5.8 6.7 %collective-permute-start = (bf16[16,2048]{1,0:T(8,128)(2,1)}, bf16[16,2048]{1,0:T(8,128)(2,1)S(1)}, u32[]{:S(2)}, u32[]{:S(2)}) collective-permute-start(bf16[16,2048]{1,0:T(8,128)(2,1)} %bitcast.9), channel_id=1, source_target_pairs={{0,8},{4,12},{8,0},{12,4},{16,24},{20,28},{24,16},{28,20},{1,9},{5... | collective-permute-start | bytes 196616 | tf_op jit(solution)/shard_map/ppermute | solution.py:75
  6.4 3.8 %collective-permute-start.4 = (bf16[256,16]{0,1:T(8,128)(2,1)}, bf16[256,16]{0,1:T(8,128)(2,1)S(1)}, u32[]{:S(2)}, u32[]{:S(2)}) collective-permute-start(bf16[256,16]{0,1:T(8,128)(2,1)} %param.11), channel_id=1, source_target_pairs={{0,4},{4,0},{8,12},{12,8},{16,20},{20,16},{24,28},{28,24},{1,5},{5... | collective-permute-start | bytes 24584 | tf_op jit(solution)/shard_map/ppermute | solution.py:75
  6.4 5.5 %collective-permute-start.3 = (bf16[256,2048]{1,0:T(8,128)(2,1)}, bf16[256,2048]{1,0:T(8,128)(2,1)S(1)}, u32[]{:S(2)}, u32[]{:S(2)}) collective-permute-start(bf16[256,2048]{1,0:T(8,128)(2,1)} %codes_hbm.1), channel_id=1, source_target_pairs={{0,4},{4,0},{8,12},{12,8},{16,20},{20,16},{24,28},{28,24},{1,5},{5... | collective-permute-start | bytes 3145736 | tf_op jit(solution)/shard_map/ppermute | solution.py:75
  10.2 2.2 %copy-start = (bf16[2,8,2048]{2,1,0:T(8,128)(2,1)S(1)}, bf16[2,8,2048]{2,1,0:T(8,128)(2,1)}, u32[]{:S(2)}) copy-start(bf16[2,8,2048]{2,1,0:T(8,128)(2,1)} %param.8) | copy-start | bytes 196612
  10.2 14.2 %collective-permute-start.11 = (bf16[272,128]{1,0:T(8,128)(2,1)S(1)}, bf16[272,128]{1,0:T(8,128)(2,1)S(1)}, u32[]{:S(2)}, u32[]{:S(2)}) collective-permute-start(bf16[272,128]{1,0:T(8,128)(2,1)S(1)} %get-tuple-element.45), channel_id=1, source_target_pairs={{0,1},{1,0},{2,3},{3,2},{4,5},{5,4},{6,7},{7,6},{8,9},{9,8},{10,11... | collective-permute-start | bytes 208904 | tf_op jit(solution)/shard_map/ppermute | solution.py:75
  13.7 6.0 %collective-permute-start.5 = (f32[16,512]{1,0:T(8,128)S(1)}, f32[16,512]{1,0:T(8,128)S(1)}, u32[]{:S(2)}, u32[]{:S(2)}) collective-permute-start(f32[16,512]{1,0:T(8,128)S(1)} %get-tuple-element.37), channel_id=1, source_target_pairs={{0,24},{4,28},{8,16},{12,20},{16,8},{20,12},{24,0},{28,4},{1,25},{... | collective-permute-start | bytes 98312 | tf_op jit(solution)/shard_map/ppermute | solution.py:75
  17.4 4.8 %collective-permute-start.6 = (f32[16,512]{1,0:T(8,128)S(1)}, f32[16,512]{1,0:T(8,128)S(1)}, u32[]{:S(2)}, u32[]{:S(2)}) collective-permute-start(f32[16,512]{1,0:T(8,128)S(1)} %get-tuple-element.38), channel_id=1, source_target_pairs={{0,16},{4,20},{8,24},{12,28},{16,0},{20,4},{24,8},{28,12},{1,17},{... | collective-permute-start | bytes 98312 | tf_op jit(solution)/shard_map/ppermute | solution.py:75
  17.4 4.8 %collective-permute-start.7 = (f32[16,512]{1,0:T(8,128)S(1)}, f32[16,512]{1,0:T(8,128)S(1)}, u32[]{:S(2)}, u32[]{:S(2)}) collective-permute-start(f32[16,512]{1,0:T(8,128)S(1)} %get-tuple-element.39), channel_id=1, source_target_pairs={{0,8},{4,12},{8,0},{12,4},{16,24},{20,28},{24,16},{28,20},{1,9},{5... | collective-permute-start | bytes 98312 | tf_op jit(solution)/shard_map/ppermute | solution.py:75
  18.2 7.7 %collective-permute-start.12 = (bf16[272,128]{1,0:T(8,128)(2,1)S(1)}, bf16[272,128]{1,0:T(8,128)(2,1)S(1)}, u32[]{:S(2)}, u32[]{:S(2)}) collective-permute-start(bf16[272,128]{1,0:T(8,128)(2,1)S(1)} %get-tuple-element.46), channel_id=1, source_target_pairs={{0,2},{1,3},{2,0},{3,1},{4,6},{5,7},{6,4},{7,5},{8,10},{9,11},{10,... | collective-permute-start | bytes 208904 | tf_op jit(solution)/shard_map/ppermute | solution.py:75
  19.7 6.2 %collective-permute-start.13 = (bf16[272,128]{1,0:T(8,128)(2,1)S(1)}, bf16[272,128]{1,0:T(8,128)(2,1)S(1)}, u32[]{:S(2)}, u32[]{:S(2)}) collective-permute-start(bf16[272,128]{1,0:T(8,128)(2,1)S(1)} %get-tuple-element.47), channel_id=1, source_target_pairs={{0,3},{1,2},{2,1},{3,0},{4,7},{5,6},{6,5},{7,4},{8,11},{9,10},{10,... | collective-permute-start | bytes 208904 | tf_op jit(solution)/shard_map/ppermute | solution.py:75
  22.3 5.0 %collective-permute-start.8 = (bf16[16,1280]{1,0:T(8,128)(2,1)S(1)}, bf16[16,1280]{1,0:T(8,128)(2,1)S(1)}, u32[]{:S(2)}, u32[]{:S(2)}) collective-permute-start(bf16[16,1280]{1,0:T(8,128)(2,1)S(1)} %get-tuple-element.41), channel_id=1, source_target_pairs={{0,3},{1,2},{2,1},{3,0},{4,7},{5,6},{6,5},{7,4},{8,11},{9,10},{10,... | collective-permute-start | bytes 122888 | tf_op jit(solution)/shard_map/ppermute | solution.py:75
  23.9 4.0 %collective-permute-start.9 = (bf16[16,1280]{1,0:T(8,128)(2,1)S(1)}, bf16[16,1280]{1,0:T(8,128)(2,1)S(1)}, u32[]{:S(2)}, u32[]{:S(2)}) collective-permute-start(bf16[16,1280]{1,0:T(8,128)(2,1)S(1)} %get-tuple-element.42), channel_id=1, source_target_pairs={{0,2},{1,3},{2,0},{3,1},{4,6},{5,7},{6,4},{7,5},{8,10},{9,11},{10,... | collective-permute-start | bytes 122888 | tf_op jit(solution)/shard_map/ppermute | solution.py:75
  24.4 4.0 %collective-permute-start.10 = (bf16[16,1280]{1,0:T(8,128)(2,1)S(1)}, bf16[16,1280]{1,0:T(8,128)(2,1)S(1)}, u32[]{:S(2)}, u32[]{:S(2)}) collective-permute-start(bf16[16,1280]{1,0:T(8,128)(2,1)S(1)} %get-tuple-element.43), channel_id=1, source_target_pairs={{0,1},{1,0},{2,3},{3,2},{4,5},{5,4},{6,7},{7,6},{8,9},{9,8},{10,11... | collective-permute-start | bytes 122888 | tf_op jit(solution)/shard_map/ppermute | solution.py:75

commit v20 on v17

--- a/solution.py
+++ b/solution.py
@@ -16,7 +16,8 @@
 
 NEGATIVE = -1e30
 SCORE_SCALE = HD ** (-0.5)
-PART = 64
+PART = 256
+PREPARE_FLOPS = 15_000_000_000
 CACHE_HINT = 120_000_000
 PROJECT_HINT = 60_000_000
 PACK_HINT = 60_000_000
@@ -60,8 +61,8 @@
     return [(lines[2 * r], lines[2 * r + 1]) for r in range(rows)]
 
 
-def hint(size):
-    return pl.CostEstimate(flops=0, bytes_accessed=size, transcendentals=0)
+def hint(size, flops=0):
+    return pl.CostEstimate(flops=flops, bytes_accessed=size, transcendentals=0)
 
 
 def dot(left, right, dims):
@@ -127,12 +128,12 @@
             copy.wait()
 
     owner_load = load(owner_hbm, owner_ref)
-    first_loads = load(lengths_hbm, lengths_ref) + load(query_hbm, query_ref)
+    first_loads = load(lengths_hbm, lengths_ref) + load(scales_hbm, scales_ref)
+    first_loads += load_rows(codes_hbm, 0, codes_ref, block) + load(query_hbm, query_ref)
     cache_loads = []
     for r in range(rows):
         target = cache_ref.at[pl.ds(r * cache_len, cache_len)]
         cache_loads.append(load_rows(cache_hbm, r * cache_len, target, cache_len))
-    code_loads = load(scales_hbm, scales_ref) + load_rows(codes_hbm, 0, codes_ref, block)
     wait(owner_load)
     base_loads = []
     for k in range(2):
@@ -142,6 +143,7 @@
         owner = owner_ref[lax.axis_index("group") ^ n]
         places_ref[n : n + 1] = jnp.full((1, LANES), owner, jnp.int32)
     wait(first_loads)
+    dequantize(codes_ref, scales_ref, delta_ref)
 
     chunks = own // chunk
     height = chunk * steps
@@ -195,8 +197,6 @@
         stats[n] += [peak, total]
         if r == rows - 1:
             put_stats(parts[n], stats[n])
-    wait(code_loads)
-    dequantize(codes_ref, scales_ref, delta_ref)
     wait(base_loads)
 
 
@@ -233,7 +233,7 @@
             pltpu.SemaphoreType.DMA((loads,)),
         ],
         compiler_params=params(CACHE_KIB),
-        cost_estimate=hint(CACHE_HINT),
+        cost_estimate=hint(CACHE_HINT, PREPARE_FLOPS),
         name="prepare",
     )(*operands)
     return out[0], out[1], out[2], out[3], list(out[4:])

time: 30 us -> 30.3 us (1.010)
  starting transfers between devices: 18.5 us -> 18.9 us
    ppermute x14, starting transfers between devices: 18.5 us -> 18.9 us  [swap(): return lax.ppermute(x, axis, [(k, k ^ distance) for k in range(size)])]
  transfers between devices with their start and end apart: 14 -> 14, of which waited for: 5 -> 4; matrix products, arithmetic and copies ran while one was open for 0% -> 0% of each run, Pallas kernels for 18% -> 17%
where the time goes in v20:
time: 30.3 us; the launch traced here: 30.1 us
  starting transfers between devices  18.9 us (62%)
  Pallas kernels  6.31 us (21%)
  waiting for transfers between devices  4.27 us (14%)
  between operations  0.69 us (2%)
    ppermute x14, starting transfers between devices, swap(): return lax.ppermute(x, axis, [(k, k ^ distance) for k in range(size)])  18.9 us
    ppermute x14, waiting for transfers between devices, swap(): return lax.ppermute(x, axis, [(k, k ^ distance) for k in range(size)])  4.27 us
    pallas_call x1, Pallas kernels, prepare(): pl.pallas_call(functools.partial(prepare_kernel, rows, steps, own, min(ow...  3.32 us
    pallas_call x1, Pallas kernels, project(): pl.pallas_call(functools.partial(project_kernel, pairs), out_shape=[jax.S...  1.48 us
    pallas_call x1, Pallas kernels, finish(): pl.pallas_call(functools.partial(finish_kernel, rows, steps, own, min(own...  1.06 us
  transfers between devices with their start and end apart: 14, of which 4 were waited for; matrix products, arithmetic and copies ran while one was open for 0% of the time, Pallas kernels for 17%

profile of v20, /device:TPU:0, one launch (start us, length us, event | category | flops | bytes accessed | tf_op | source)
XLA Modules:
  0.0 30.1 jit_solution(16119849331100807409)
XLA Ops:
  0.6 5.1 %collective-permute-start.2 = (bf16[16,2048]{1,0:T(8,128)(2,1)}, bf16[16,2048]{1,0:T(8,128)(2,1)S(1)}, u32[]{:S(2)}, u32[]{:S(2)}) collective-permute-start(bf16[16,2048]{1,0:T(8,128)(2,1)} %bitcast.7), channel_id=1, source_target_pairs={{0,24},{4,28},{8,16},{12,20},{16,8},{20,12},{24,0},{28,4},{1,25},{... | collective-permute-start | bytes 196616 | tf_op jit(solution)/shard_map/ppermute | solution.py:74
  5.7 0.0 collective-permute-start.1
  5.8 0.6 %collective-permute-start = (bf16[16,2048]{1,0:T(8,128)(2,1)}, bf16[16,2048]{1,0:T(8,128)(2,1)S(1)}, u32[]{:S(2)}, u32[]{:S(2)}) collective-permute-start(bf16[16,2048]{1,0:T(8,128)(2,1)} %bitcast.9), channel_id=1, source_target_pairs={{0,8},{4,12},{8,0},{12,4},{16,24},{20,28},{24,16},{28,20},{1,9},{5... | collective-permute-start | bytes 196616 | tf_op jit(solution)/shard_map/ppermute | solution.py:74
  6.4 0.0 collective-permute-start.4
  6.4 0.5 %collective-permute-start.3 = (bf16[256,2048]{1,0:T(8,128)(2,1)}, bf16[256,2048]{1,0:T(8,128)(2,1)S(1)}, u32[]{:S(2)}, u32[]{:S(2)}) collective-permute-start(bf16[256,2048]{1,0:T(8,128)(2,1)} %codes_hbm.1), channel_id=1, source_target_pairs={{0,4},{4,0},{8,12},{12,8},{16,20},{20,16},{24,28},{28,24},{1,5},{5... | collective-permute-start | bytes 3145736 | tf_op jit(solution)/shard_map/ppermute | solution.py:74
  6.9 0.0 copy-start
  6.9 3.3 %prepare.1 = (bf16[256,2048]{1,0:T(8,128)(2,1)S(1)}, bf16[2,256,2048]{2,1,0:T(8,128)(2,1)S(1)}, bf16[256,128]{1,0:T(8,128)(2,1)S(1)}, s32[8,128]{1,0:T(8,128)S(1...) custom-call(s32[8]{0:T(128)} %owner_hbm.1, ...), custom_call_target="tpu_custom_call" | custom-call | flops 15000000512 | bytes 120000000 | tf_op jit(solution)/shard_map/prepare/pallas_call | solution.py:214
  10.2 0.0 collective-permute-done.4
  10.2 1.7 %collective-permute-start.12 = (bf16[272,128]{1,0:T(8,128)(2,1)S(1)}, bf16[272,128]{1,0:T(8,128)(2,1)S(1)}, u32[]{:S(2)}, u32[]{:S(2)}) collective-permute-start(bf16[272,128]{1,0:T(8,128)(2,1)S(1)} %get-tuple-element.48), channel_id=1, source_target_pairs={{0,2},{1,3},{2,0},{3,1},{4,6},{5,7},{6,4},{7,5},{8,10},{9,11},{10,... | collective-permute-start | bytes 208904 | tf_op jit(solution)/shard_map/ppermute | solution.py:74
  12.0 0.0 collective-permute-done.2.refs_3_
  12.0 0.0 collective-permute-done.1.refs_2_
  12.0 0.0 collective-permute-done.refs_1_
  12.0 0.0 collective-permute-done.3.codes_ref
  12.0 0.0 copy-done
  12.0 1.5 %project.1 = (f32[16,512]{1,0:T(8,128)S(1)}, f32[16,512]{1,0:T(8,128)S(1)}, f32[16,512]{1,0:T(8,128)S(1)}, f32[16,512]{1,0:T(8,128)S(1)}) custom-call(bf16[256,2048]{1,0:T(8,128)(2,1)S(1)} %get-tuple-element.30.own_ref, bf16[2,256,2048]{2,1,0:T(8,128)(2,1)S(1)} %get-tuple-element.31.base_ref, bf16[256,2048]{1,0:T(8,128)(2,1)S(1)} %collective-permute-done.3.codes_ref, ...), custom_call_target="tpu_custom_call" | custom-call | bytes 60000000 | tf_op jit(solution)/shard_map/project/pallas_call | solution.py:300
  13.5 3.7 %collective-permute-start.5 = (f32[16,512]{1,0:T(8,128)S(1)}, f32[16,512]{1,0:T(8,128)S(1)}, u32[]{:S(2)}, u32[]{:S(2)}) collective-permute-start(f32[16,512]{1,0:T(8,128)S(1)} %get-tuple-element.39), channel_id=1, source_target_pairs={{0,24},{4,28},{8,16},{12,20},{16,8},{20,12},{24,0},{28,4},{1,25},{... | collective-permute-start | bytes 98312 | tf_op jit(solution)/shard_map/ppermute | solution.py:74
  17.1 0.0 collective-permute-start.6
  17.1 0.8 %collective-permute-start.7 = (f32[16,512]{1,0:T(8,128)S(1)}, f32[16,512]{1,0:T(8,128)S(1)}, u32[]{:S(2)}, u32[]{:S(2)}) collective-permute-start(f32[16,512]{1,0:T(8,128)S(1)} %get-tuple-element.41), channel_id=1, source_target_pairs={{0,8},{4,12},{8,0},{12,4},{16,24},{20,28},{24,16},{28,20},{1,9},{5... | collective-permute-start | bytes 98312 | tf_op jit(solution)/shard_map/ppermute | solution.py:74
  17.9 2.0 %collective-permute-start.13 = (bf16[272,128]{1,0:T(8,128)(2,1)S(1)}, bf16[272,128]{1,0:T(8,128)(2,1)S(1)}, u32[]{:S(2)}, u32[]{:S(2)}) collective-permute-start(bf16[272,128]{1,0:T(8,128)(2,1)S(1)} %get-tuple-element.49), channel_id=1, source_target_pairs={{0,3},{1,2},{2,1},{3,0},{4,7},{5,6},{6,5},{7,4},{8,11},{9,10},{10,... | collective-permute-start | bytes 208904 | tf_op jit(solution)/shard_map/ppermute | solution.py:74
  19.9 0.0 collective-permute-done.5.refs_1_
  19.9 0.9 %collective-permute-start.11 = (bf16[272,128]{1,0:T(8,128)(2,1)S(1)}, bf16[272,128]{1,0:T(8,128)(2,1)S(1)}, u32[]{:S(2)}, u32[]{:S(2)}) collective-permute-start(bf16[272,128]{1,0:T(8,128)(2,1)S(1)} %get-tuple-element.47), channel_id=1, source_target_pairs={{0,1},{1,0},{2,3},{3,2},{4,5},{5,4},{6,7},{7,6},{8,9},{9,8},{10,11... | collective-permute-start | bytes 208904 | tf_op jit(solution)/shard_map/ppermute | solution.py:74
  20.8 1.1 %collective-permute-done.6.refs_2_ = f32[16,512]{1,0:T(8,128)S(1)} collective-permute-done((f32[16,512]{1,0:T(8,128)S(1)}, f32[16,512]{1,0:T(8,128)S(1)}, u32[]{:S(2)}, u32[]{:S(2)}) %collective-permute-start.6) | collective-permute-done | bytes 32800 | tf_op jit(solution)/shard_map/ppermute | solution.py:74
  22.0 0.0 collective-permute-done.7.refs_3_
  22.0 0.1 pack_pieces.1
  22.1 1.5 %collective-permute-start.8 = (bf16[16,1280]{1,0:T(8,128)(2,1)S(1)}, bf16[16,1280]{1,0:T(8,128)(2,1)S(1)}, u32[]{:S(2)}, u32[]{:S(2)}) collective-permute-start(bf16[16,1280]{1,0:T(8,128)(2,1)S(1)} %get-tuple-element.43), channel_id=1, source_target_pairs={{0,3},{1,2},{2,1},{3,0},{4,7},{5,6},{6,5},{7,4},{8,11},{9,10},{10,... | collective-permute-start | bytes 122888 | tf_op jit(solution)/shard_map/ppermute | solution.py:74
  23.6 1.5 %collective-permute-start.9 = (bf16[16,1280]{1,0:T(8,128)(2,1)S(1)}, bf16[16,1280]{1,0:T(8,128)(2,1)S(1)}, u32[]{:S(2)}, u32[]{:S(2)}) collective-permute-start(bf16[16,1280]{1,0:T(8,128)(2,1)S(1)} %get-tuple-element.44), channel_id=1, source_target_pairs={{0,2},{1,3},{2,0},{3,1},{4,6},{5,7},{6,4},{7,5},{8,10},{9,11},{10,... | collective-permute-start | bytes 122888 | tf_op jit(solution)/shard_map/ppermute | solution.py:74
  25.1 0.0 collective-permute-done.12.refs_2_
  25.1 0.5 %collective-permute-start.10 = (bf16[16,1280]{1,0:T(8,128)(2,1)S(1)}, bf16[16,1280]{1,0:T(8,128)(2,1)S(1)}, u32[]{:S(2)}, u32[]{:S(2)}) collective-permute-start(bf16[16,1280]{1,0:T(8,128)(2,1)S(1)} %get-tuple-element.45), channel_id=1, source_target_pairs={{0,1},{1,0},{2,3},{3,2},{4,5},{5,4},{6,7},{7,6},{8,9},{9,8},{10,11... | collective-permute-start | bytes 122888 | tf_op jit(solution)/shard_map/ppermute | solution.py:74
  25.6 0.0 collective-permute-done.13.refs_3_
  25.6 0.0 collective-permute-done.11.refs_1_
  25.6 0.3 %merge_partials.1.refs_4_ = f32[264,128]{1,0:T(8,128)S(1)} custom-call(f32[264,128]{1,0:T(8,128)S(1)} %get-tuple-element.46.refs_0_, bf16[272,128]{1,0:T(8,128)(2,1)S(1)} %collective-permute-done.11.refs_1_, bf16[272,128]{1,0:T(8,128)(2,1)S(1)} %collective-permute-done.12.refs_2_, bf16[272,128]{1,0:T(8,128)(2,1)S(1)} %collective-permute-done.13.refs_3_), custom_call_target="tpu_custom_call" | custom-call | bytes 1000 | tf_op jit(solution)/shard_map/merge_partials/pallas_call | solution.py:267
  26.0 1.0 %collective-permute-done.8.refs_1_ = bf16[16,1280]{1,0:T(8,128)(2,1)S(1)} collective-permute-done((bf16[16,1280]{1,0:T(8,128)(2,1)S(1)}, bf16[16,1280]{1,0:T(8,128)(2,1)S(1)}, u32[]{:S(2)}, u32[]{:S(2)}) %collective-permute-start.8) | collective-permute-done | bytes 40992 | tf_op jit(solution)/shard_map/ppermute | solution.py:74
  27.0 0.5 %collective-permute-done.9.refs_2_ = bf16[16,1280]{1,0:T(8,128)(2,1)S(1)} collective-permute-done((bf16[16,1280]{1,0:T(8,128)(2,1)S(1)}, bf16[16,1280]{1,0:T(8,128)(2,1)S(1)}, u32[]{:S(2)}, u32[]{:S(2)}) %collective-permute-start.9) | collective-permute-done | bytes 40992 | tf_op jit(solution)/shard_map/ppermute | solution.py:74
  27.6 1.5 %collective-permute-done.10.refs_3_ = bf16[16,1280]{1,0:T(8,128)(2,1)S(1)} collective-permute-done((bf16[16,1280]{1,0:T(8,128)(2,1)S(1)}, bf16[16,1280]{1,0:T(8,128)(2,1)S(1)}, u32[]{:S(2)}, u32[]{:S(2)}) %collective-permute-start.10) | collective-permute-done | bytes 40992 | tf_op jit(solution)/shard_map/ppermute | solution.py:74
  29.1 1.1 %finish.1 = (bf16[16,512]{1,0:T(8,128)(2,1)}, bf16[16,2048]{1,0:T(8,128)(2,1)}) custom-call(bf16[256,128]{1,0:T(8,128)(2,1)S(1)} %get-tuple-element.28.query_ref, f32[16,1024]{1,0:T(8,128)S(1)} %get-tuple-element.42.refs_0_, bf16[16,1280]{1,0:T(8,128)(2,1)S(1)} %collective-permute-done.8.refs_1_, bf16[16,1280]{1,0:T(8,128)(2,1)S(1)} %collective-permute-done.9.refs_2_, ...), custom_call_target="tpu_custom_call" | custom-call | tf_op jit(solution)/shard_map/finish/pallas_call | solution.py:451
Async XLA Ops:
  0.6 11.3 %collective-permute-start.2 = (bf16[16,2048]{1,0:T(8,128)(2,1)}, bf16[16,2048]{1,0:T(8,128)(2,1)S(1)}, u32[]{:S(2)}, u32[]{:S(2)}) collective-permute-start(bf16[16,2048]{1,0:T(8,128)(2,1)} %bitcast.7), channel_id=1, source_target_pairs={{0,24},{4,28},{8,16},{12,20},{16,8},{20,12},{24,0},{28,4},{1,25},{... | collective-permute-start | bytes 196616 | tf_op jit(solution)/shard_map/ppermute | solution.py:74
  5.7 6.2 %collective-permute-start.1 = (bf16[16,2048]{1,0:T(8,128)(2,1)}, bf16[16,2048]{1,0:T(8,128)(2,1)S(1)}, u32[]{:S(2)}, u32[]{:S(2)}) collective-permute-start(bf16[16,2048]{1,0:T(8,128)(2,1)} %bitcast.8), channel_id=1, source_target_pairs={{0,16},{4,20},{8,24},{12,28},{16,0},{20,4},{24,8},{28,12},{1,17},{... | collective-permute-start | bytes 196616 | tf_op jit(solution)/shard_map/ppermute | solution.py:74
  5.8 6.2 %collective-permute-start = (bf16[16,2048]{1,0:T(8,128)(2,1)}, bf16[16,2048]{1,0:T(8,128)(2,1)S(1)}, u32[]{:S(2)}, u32[]{:S(2)}) collective-permute-start(bf16[16,2048]{1,0:T(8,128)(2,1)} %bitcast.9), channel_id=1, source_target_pairs={{0,8},{4,12},{8,0},{12,4},{16,24},{20,28},{24,16},{28,20},{1,9},{5... | collective-permute-start | bytes 196616 | tf_op jit(solution)/shard_map/ppermute | solution.py:74
  6.4 3.8 %collective-permute-start.4 = (bf16[256,16]{0,1:T(8,128)(2,1)}, bf16[256,16]{0,1:T(8,128)(2,1)S(1)}, u32[]{:S(2)}, u32[]{:S(2)}) collective-permute-start(bf16[256,16]{0,1:T(8,128)(2,1)} %param.11), channel_id=1, source_target_pairs={{0,4},{4,0},{8,12},{12,8},{16,20},{20,16},{24,28},{28,24},{1,5},{5... | collective-permute-start | bytes 24584 | tf_op jit(solution)/shard_map/ppermute | solution.py:74
  6.4 5.6 %collective-permute-start.3 = (bf16[256,2048]{1,0:T(8,128)(2,1)}, bf16[256,2048]{1,0:T(8,128)(2,1)S(1)}, u32[]{:S(2)}, u32[]{:S(2)}) collective-permute-start(bf16[256,2048]{1,0:T(8,128)(2,1)} %codes_hbm.1), channel_id=1, source_target_pairs={{0,4},{4,0},{8,12},{12,8},{16,20},{20,16},{24,28},{28,24},{1,5},{5... | collective-permute-start | bytes 3145736 | tf_op jit(solution)/shard_map/ppermute | solution.py:74
  6.9 5.1 %copy-start = (bf16[2,8,2048]{2,1,0:T(8,128)(2,1)S(1)}, bf16[2,8,2048]{2,1,0:T(8,128)(2,1)}, u32[]{:S(2)}) copy-start(bf16[2,8,2048]{2,1,0:T(8,128)(2,1)} %param.8) | copy-start | bytes 196612
  10.2 14.8 %collective-permute-start.12 = (bf16[272,128]{1,0:T(8,128)(2,1)S(1)}, bf16[272,128]{1,0:T(8,128)(2,1)S(1)}, u32[]{:S(2)}, u32[]{:S(2)}) collective-permute-start(bf16[272,128]{1,0:T(8,128)(2,1)S(1)} %get-tuple-element.48), channel_id=1, source_target_pairs={{0,2},{1,3},{2,0},{3,1},{4,6},{5,7},{6,4},{7,5},{8,10},{9,11},{10,... | collective-permute-start | bytes 208904 | tf_op jit(solution)/shard_map/ppermute | solution.py:74
  13.5 6.5 %collective-permute-start.5 = (f32[16,512]{1,0:T(8,128)S(1)}, f32[16,512]{1,0:T(8,128)S(1)}, u32[]{:S(2)}, u32[]{:S(2)}) collective-permute-start(f32[16,512]{1,0:T(8,128)S(1)} %get-tuple-element.39), channel_id=1, source_target_pairs={{0,24},{4,28},{8,16},{12,20},{16,8},{20,12},{24,0},{28,4},{1,25},{... | collective-permute-start | bytes 98312 | tf_op jit(solution)/shard_map/ppermute | solution.py:74
  17.1 4.8 %collective-permute-start.6 = (f32[16,512]{1,0:T(8,128)S(1)}, f32[16,512]{1,0:T(8,128)S(1)}, u32[]{:S(2)}, u32[]{:S(2)}) collective-permute-start(f32[16,512]{1,0:T(8,128)S(1)} %get-tuple-element.40), channel_id=1, source_target_pairs={{0,16},{4,20},{8,24},{12,28},{16,0},{20,4},{24,8},{28,12},{1,17},{... | collective-permute-start | bytes 98312 | tf_op jit(solution)/shard_map/ppermute | solution.py:74
  17.1 4.8 %collective-permute-start.7 = (f32[16,512]{1,0:T(8,128)S(1)}, f32[16,512]{1,0:T(8,128)S(1)}, u32[]{:S(2)}, u32[]{:S(2)}) collective-permute-start(f32[16,512]{1,0:T(8,128)S(1)} %get-tuple-element.41), channel_id=1, source_target_pairs={{0,8},{4,12},{8,0},{12,4},{16,24},{20,28},{24,16},{28,20},{1,9},{5... | collective-permute-start | bytes 98312 | tf_op jit(solution)/shard_map/ppermute | solution.py:74
  17.9 7.7 %collective-permute-start.13 = (bf16[272,128]{1,0:T(8,128)(2,1)S(1)}, bf16[272,128]{1,0:T(8,128)(2,1)S(1)}, u32[]{:S(2)}, u32[]{:S(2)}) collective-permute-start(bf16[272,128]{1,0:T(8,128)(2,1)S(1)} %get-tuple-element.49), channel_id=1, source_target_pairs={{0,3},{1,2},{2,1},{3,0},{4,7},{5,6},{6,5},{7,4},{8,11},{9,10},{10,... | collective-permute-start | bytes 208904 | tf_op jit(solution)/shard_map/ppermute | solution.py:74
  19.9 5.7 %collective-permute-start.11 = (bf16[272,128]{1,0:T(8,128)(2,1)S(1)}, bf16[272,128]{1,0:T(8,128)(2,1)S(1)}, u32[]{:S(2)}, u32[]{:S(2)}) collective-permute-start(bf16[272,128]{1,0:T(8,128)(2,1)S(1)} %get-tuple-element.47), channel_id=1, source_target_pairs={{0,1},{1,0},{2,3},{3,2},{4,5},{5,4},{6,7},{7,6},{8,9},{9,8},{10,11... | collective-permute-start | bytes 208904 | tf_op jit(solution)/shard_map/ppermute | solution.py:74
  22.1 5.0 %collective-permute-start.8 = (bf16[16,1280]{1,0:T(8,128)(2,1)S(1)}, bf16[16,1280]{1,0:T(8,128)(2,1)S(1)}, u32[]{:S(2)}, u32[]{:S(2)}) collective-permute-start(bf16[16,1280]{1,0:T(8,128)(2,1)S(1)} %get-tuple-element.43), channel_id=1, source_target_pairs={{0,3},{1,2},{2,1},{3,0},{4,7},{5,6},{6,5},{7,4},{8,11},{9,10},{10,... | collective-permute-start | bytes 122888 | tf_op jit(solution)/shard_map/ppermute | solution.py:74
  23.6 4.0 %collective-permute-start.9 = (bf16[16,1280]{1,0:T(8,128)(2,1)S(1)}, bf16[16,1280]{1,0:T(8,128)(2,1)S(1)}, u32[]{:S(2)}, u32[]{:S(2)}) collective-permute-start(bf16[16,1280]{1,0:T(8,128)(2,1)S(1)} %get-tuple-element.44), channel_id=1, source_target_pairs={{0,2},{1,3},{2,0},{3,1},{4,6},{5,7},{6,4},{7,5},{8,10},{9,11},{10,... | collective-permute-start | bytes 122888 | tf_op jit(solution)/shard_map/ppermute | solution.py:74
  25.1 4.0 %collective-permute-start.10 = (bf16[16,1280]{1,0:T(8,128)(2,1)S(1)}, bf16[16,1280]{1,0:T(8,128)(2,1)S(1)}, u32[]{:S(2)}, u32[]{:S(2)}) collective-permute-start(bf16[16,1280]{1,0:T(8,128)(2,1)S(1)} %get-tuple-element.45), channel_id=1, source_target_pairs={{0,1},{1,0},{2,3},{3,2},{4,5},{5,4},{6,7},{7,6},{8,9},{9,8},{10,11... | collective-permute-start | bytes 122888 | tf_op jit(solution)/shard_map/ppermute | solution.py:74

commit v21 on v20

--- a/solution.py
+++ b/solution.py
@@ -500,7 +500,8 @@
         heads_own,
         tensor_count,
     )
-    mate_scales, partials[-1] = lax.optimization_barrier((mate_scales, partials[-1]))
+    mate_scales, sent = lax.optimization_barrier((mate_scales, partials[1:]))
+    partials = partials[:1] + list(sent)
     behind = lax.optimization_barrier((*near_first(token_rows), own_query))
     token_rows, own_query = near_first(list(behind[:pairs])), behind[-1]
     projected = project(

time: 30.3 us -> 29.3 us (0.967)
  waiting for transfers between devices: 4.27 us -> 2.75 us
  starting transfers between devices: 18.9 us -> 19.4 us
    ppermute x14, waiting for transfers between devices: 4.27 us -> 2.75 us  [swap(): return lax.ppermute(x, axis, [(k, k ^ distance) for k in range(size)])]
    ppermute x14, starting transfers between devices: 18.9 us -> 19.4 us  [swap(): return lax.ppermute(x, axis, [(k, k ^ distance) for k in range(size)])]
  transfers between devices with their start and end apart: 14 -> 14, of which waited for: 4 -> 4; matrix products, arithmetic and copies ran while one was open for 0% -> 0% of each run, Pallas kernels for 17% -> 18%
where the time goes in v21:
time: 29.3 us; the launch traced here: 29.2 us
  starting transfers between devices  19.4 us (66%)
  Pallas kernels  6.31 us (22%)
  waiting for transfers between devices  2.75 us (9%)
  between operations  0.69 us (2%)
    ppermute x14, starting transfers between devices, swap(): return lax.ppermute(x, axis, [(k, k ^ distance) for k in range(size)])  19.4 us
    pallas_call x1, Pallas kernels, prepare(): pl.pallas_call(functools.partial(prepare_kernel, rows, steps, own, min(ow...  3.32 us
    ppermute x14, waiting for transfers between devices, swap(): return lax.ppermute(x, axis, [(k, k ^ distance) for k in range(size)])  2.75 us
    pallas_call x1, Pallas kernels, project(): pl.pallas_call(functools.partial(project_kernel, pairs), out_shape=[jax.S...  1.48 us
    pallas_call x1, Pallas kernels, finish(): pl.pallas_call(functools.partial(finish_kernel, rows, steps, own, min(own...  1.06 us
  transfers between devices with their start and end apart: 14, of which 4 were waited for; matrix products, arithmetic and copies ran while one was open for 0% of the time, Pallas kernels for 18%

profile of v21, /device:TPU:0, one launch (start us, length us, event | category | flops | bytes accessed | tf_op | source)
XLA Modules:
  0.0 29.2 jit_solution(4814528306111171841)
XLA Ops:
  0.6 5.1 %collective-permute-start.2 = (bf16[16,2048]{1,0:T(8,128)(2,1)}, bf16[16,2048]{1,0:T(8,128)(2,1)S(1)}, u32[]{:S(2)}, u32[]{:S(2)}) collective-permute-start(bf16[16,2048]{1,0:T(8,128)(2,1)} %bitcast.7), channel_id=1, source_target_pairs={{0,24},{4,28},{8,16},{12,20},{16,8},{20,12},{24,0},{28,4},{1,25},{... | collective-permute-start | bytes 196616 | tf_op jit(solution)/shard_map/ppermute | solution.py:74
  5.7 0.0 collective-permute-start.1
  5.8 0.6 %collective-permute-start = (bf16[16,2048]{1,0:T(8,128)(2,1)}, bf16[16,2048]{1,0:T(8,128)(2,1)S(1)}, u32[]{:S(2)}, u32[]{:S(2)}) collective-permute-start(bf16[16,2048]{1,0:T(8,128)(2,1)} %bitcast.9), channel_id=1, source_target_pairs={{0,8},{4,12},{8,0},{12,4},{16,24},{20,28},{24,16},{28,20},{1,9},{5... | collective-permute-start | bytes 196616 | tf_op jit(solution)/shard_map/ppermute | solution.py:74
  6.4 0.0 collective-permute-start.4
  6.4 0.5 %collective-permute-start.3 = (bf16[256,2048]{1,0:T(8,128)(2,1)}, bf16[256,2048]{1,0:T(8,128)(2,1)S(1)}, u32[]{:S(2)}, u32[]{:S(2)}) collective-permute-start(bf16[256,2048]{1,0:T(8,128)(2,1)} %codes_hbm.1), channel_id=1, source_target_pairs={{0,4},{4,0},{8,12},{12,8},{16,20},{20,16},{24,28},{28,24},{1,5},{5... | collective-permute-start | bytes 3145736 | tf_op jit(solution)/shard_map/ppermute | solution.py:74
  6.9 0.0 copy-start
  6.9 3.3 %prepare.1 = (bf16[256,2048]{1,0:T(8,128)(2,1)S(1)}, bf16[2,256,2048]{2,1,0:T(8,128)(2,1)S(1)}, bf16[256,128]{1,0:T(8,128)(2,1)S(1)}, s32[8,128]{1,0:T(8,128)S(1...) custom-call(s32[8]{0:T(128)} %owner_hbm.1, ...), custom_call_target="tpu_custom_call" | custom-call | flops 15000000512 | bytes 120000000 | tf_op jit(solution)/shard_map/prepare/pallas_call | solution.py:214
  10.2 0.0 collective-permute-done.4
  10.2 1.7 %collective-permute-start.11 = (bf16[272,128]{1,0:T(8,128)(2,1)S(1)}, bf16[272,128]{1,0:T(8,128)(2,1)S(1)}, u32[]{:S(2)}, u32[]{:S(2)}) collective-permute-start(bf16[272,128]{1,0:T(8,128)(2,1)S(1)} %get-tuple-element.51), channel_id=1, source_target_pairs={{0,1},{1,0},{2,3},{3,2},{4,5},{5,4},{6,7},{7,6},{8,9},{9,8},{10,11... | collective-permute-start | bytes 208904 | tf_op jit(solution)/shard_map/ppermute | solution.py:74
  11.9 0.0 collective-permute-done.2.refs_3_
  11.9 0.0 collective-permute-done.1.refs_2_
  11.9 0.0 collective-permute-done.refs_1_
  12.0 0.0 collective-permute-done.3.codes_ref
  12.0 0.0 copy-done
  12.0 1.5 %project.1 = (f32[16,512]{1,0:T(8,128)S(1)}, f32[16,512]{1,0:T(8,128)S(1)}, f32[16,512]{1,0:T(8,128)S(1)}, f32[16,512]{1,0:T(8,128)S(1)}) custom-call(bf16[256,2048]{1,0:T(8,128)(2,1)S(1)} %get-tuple-element.32.own_ref, bf16[2,256,2048]{2,1,0:T(8,128)(2,1)S(1)} %get-tuple-element.33.base_ref, bf16[256,2048]{1,0:T(8,128)(2,1)S(1)} %collective-permute-done.3.codes_ref, ...), custom_call_target="tpu_custom_call" | custom-call | bytes 60000000 | tf_op jit(solution)/shard_map/project/pallas_call | solution.py:300
  13.4 3.7 %collective-permute-start.5 = (f32[16,512]{1,0:T(8,128)S(1)}, f32[16,512]{1,0:T(8,128)S(1)}, u32[]{:S(2)}, u32[]{:S(2)}) collective-permute-start(f32[16,512]{1,0:T(8,128)S(1)} %get-tuple-element.43), channel_id=1, source_target_pairs={{0,24},{4,28},{8,16},{12,20},{16,8},{20,12},{24,0},{28,4},{1,25},{... | collective-permute-start | bytes 98312 | tf_op jit(solution)/shard_map/ppermute | solution.py:74
  17.1 0.0 collective-permute-start.6
  17.1 0.8 %collective-permute-start.7 = (f32[16,512]{1,0:T(8,128)S(1)}, f32[16,512]{1,0:T(8,128)S(1)}, u32[]{:S(2)}, u32[]{:S(2)}) collective-permute-start(f32[16,512]{1,0:T(8,128)S(1)} %get-tuple-element.45), channel_id=1, source_target_pairs={{0,8},{4,12},{8,0},{12,4},{16,24},{20,28},{24,16},{28,20},{1,9},{5... | collective-permute-start | bytes 98312 | tf_op jit(solution)/shard_map/ppermute | solution.py:74
  17.9 1.5 %collective-permute-start.12 = (bf16[272,128]{1,0:T(8,128)(2,1)S(1)}, bf16[272,128]{1,0:T(8,128)(2,1)S(1)}, u32[]{:S(2)}, u32[]{:S(2)}) collective-permute-start(bf16[272,128]{1,0:T(8,128)(2,1)S(1)} %get-tuple-element.52), channel_id=1, source_target_pairs={{0,2},{1,3},{2,0},{3,1},{4,6},{5,7},{6,4},{7,5},{8,10},{9,11},{10,... | collective-permute-start | bytes 208904 | tf_op jit(solution)/shard_map/ppermute | solution.py:74
  19.4 0.0 collective-permute-done.5.refs_1_
  19.4 1.9 %collective-permute-start.13 = (bf16[272,128]{1,0:T(8,128)(2,1)S(1)}, bf16[272,128]{1,0:T(8,128)(2,1)S(1)}, u32[]{:S(2)}, u32[]{:S(2)}) collective-permute-start(bf16[272,128]{1,0:T(8,128)(2,1)S(1)} %get-tuple-element.53), channel_id=1, source_target_pairs={{0,3},{1,2},{2,1},{3,0},{4,7},{5,6},{6,5},{7,4},{8,11},{9,10},{10,... | collective-permute-start | bytes 208904 | tf_op jit(solution)/shard_map/ppermute | solution.py:74
  21.3 0.6 %collective-permute-done.6.refs_2_ = f32[16,512]{1,0:T(8,128)S(1)} collective-permute-done((f32[16,512]{1,0:T(8,128)S(1)}, f32[16,512]{1,0:T(8,128)S(1)}, u32[]{:S(2)}, u32[]{:S(2)}) %collective-permute-start.6) | collective-permute-done | bytes 32800 | tf_op jit(solution)/shard_map/ppermute | solution.py:74
  21.9 0.0 collective-permute-done.7.refs_3_
  21.9 0.1 pack_pieces.1
  22.0 1.6 %collective-permute-start.8 = (bf16[16,1280]{1,0:T(8,128)(2,1)S(1)}, bf16[16,1280]{1,0:T(8,128)(2,1)S(1)}, u32[]{:S(2)}, u32[]{:S(2)}) collective-permute-start(bf16[16,1280]{1,0:T(8,128)(2,1)S(1)} %get-tuple-element.47), channel_id=1, source_target_pairs={{0,3},{1,2},{2,1},{3,0},{4,7},{5,6},{6,5},{7,4},{8,11},{9,10},{10,... | collective-permute-start | bytes 122888 | tf_op jit(solution)/shard_map/ppermute | solution.py:74
  23.6 0.5 %collective-permute-start.9 = (bf16[16,1280]{1,0:T(8,128)(2,1)S(1)}, bf16[16,1280]{1,0:T(8,128)(2,1)S(1)}, u32[]{:S(2)}, u32[]{:S(2)}) collective-permute-start(bf16[16,1280]{1,0:T(8,128)(2,1)S(1)} %get-tuple-element.48), channel_id=1, source_target_pairs={{0,2},{1,3},{2,0},{3,1},{4,6},{5,7},{6,4},{7,5},{8,10},{9,11},{10,... | collective-permute-start | bytes 122888 | tf_op jit(solution)/shard_map/ppermute | solution.py:74
  24.1 0.0 collective-permute-done.11.refs_1_
  24.1 1.5 %collective-permute-start.10 = (bf16[16,1280]{1,0:T(8,128)(2,1)S(1)}, bf16[16,1280]{1,0:T(8,128)(2,1)S(1)}, u32[]{:S(2)}, u32[]{:S(2)}) collective-permute-start(bf16[16,1280]{1,0:T(8,128)(2,1)S(1)} %get-tuple-element.49), channel_id=1, source_target_pairs={{0,1},{1,0},{2,3},{3,2},{4,5},{5,4},{6,7},{7,6},{8,9},{9,8},{10,11... | collective-permute-start | bytes 122888 | tf_op jit(solution)/shard_map/ppermute | solution.py:74
  25.6 0.0 collective-permute-done.12.refs_2_
  25.6 0.0 collective-permute-done.13.refs_3_
  25.6 0.3 %merge_partials.1.refs_4_ = f32[264,128]{1,0:T(8,128)S(1)} custom-call(f32[264,128]{1,0:T(8,128)S(1)} %get-tuple-element.50.refs_0_, bf16[272,128]{1,0:T(8,128)(2,1)S(1)} %collective-permute-done.11.refs_1_, bf16[272,128]{1,0:T(8,128)(2,1)S(1)} %collective-permute-done.12.refs_2_, bf16[272,128]{1,0:T(8,128)(2,1)S(1)} %collective-permute-done.13.refs_3_), custom_call_target="tpu_custom_call" | custom-call | bytes 1000 | tf_op jit(solution)/shard_map/merge_partials/pallas_call | solution.py:267
  26.0 1.0 %collective-permute-done.8.refs_1_ = bf16[16,1280]{1,0:T(8,128)(2,1)S(1)} collective-permute-done((bf16[16,1280]{1,0:T(8,128)(2,1)S(1)}, bf16[16,1280]{1,0:T(8,128)(2,1)S(1)}, u32[]{:S(2)}, u32[]{:S(2)}) %collective-permute-start.8) | collective-permute-done | bytes 40992 | tf_op jit(solution)/shard_map/ppermute | solution.py:74
  27.0 0.6 %collective-permute-done.9.refs_2_ = bf16[16,1280]{1,0:T(8,128)(2,1)S(1)} collective-permute-done((bf16[16,1280]{1,0:T(8,128)(2,1)S(1)}, bf16[16,1280]{1,0:T(8,128)(2,1)S(1)}, u32[]{:S(2)}, u32[]{:S(2)}) %collective-permute-start.9) | collective-permute-done | bytes 40992 | tf_op jit(solution)/shard_map/ppermute | solution.py:74
  27.6 0.5 %collective-permute-done.10.refs_3_ = bf16[16,1280]{1,0:T(8,128)(2,1)S(1)} collective-permute-done((bf16[16,1280]{1,0:T(8,128)(2,1)S(1)}, bf16[16,1280]{1,0:T(8,128)(2,1)S(1)}, u32[]{:S(2)}, u32[]{:S(2)}) %collective-permute-start.10) | collective-permute-done | bytes 40992 | tf_op jit(solution)/shard_map/ppermute | solution.py:74
  28.1 1.1 %finish.1 = (bf16[16,512]{1,0:T(8,128)(2,1)}, bf16[16,2048]{1,0:T(8,128)(2,1)}) custom-call(bf16[256,128]{1,0:T(8,128)(2,1)S(1)} %get-tuple-element.30.query_ref, f32[16,1024]{1,0:T(8,128)S(1)} %get-tuple-element.46.refs_0_, bf16[16,1280]{1,0:T(8,128)(2,1)S(1)} %collective-permute-done.8.refs_1_, bf16[16,1280]{1,0:T(8,128)(2,1)S(1)} %collective-permute-done.9.refs_2_, ...), custom_call_target="tpu_custom_call" | custom-call | tf_op jit(solution)/shard_map/finish/pallas_call | solution.py:451
Async XLA Ops:
  0.6 11.3 %collective-permute-start.2 = (bf16[16,2048]{1,0:T(8,128)(2,1)}, bf16[16,2048]{1,0:T(8,128)(2,1)S(1)}, u32[]{:S(2)}, u32[]{:S(2)}) collective-permute-start(bf16[16,2048]{1,0:T(8,128)(2,1)} %bitcast.7), channel_id=1, source_target_pairs={{0,24},{4,28},{8,16},{12,20},{16,8},{20,12},{24,0},{28,4},{1,25},{... | collective-permute-start | bytes 196616 | tf_op jit(solution)/shard_map/ppermute | solution.py:74
  5.7 6.2 %collective-permute-start.1 = (bf16[16,2048]{1,0:T(8,128)(2,1)}, bf16[16,2048]{1,0:T(8,128)(2,1)S(1)}, u32[]{:S(2)}, u32[]{:S(2)}) collective-permute-start(bf16[16,2048]{1,0:T(8,128)(2,1)} %bitcast.8), channel_id=1, source_target_pairs={{0,16},{4,20},{8,24},{12,28},{16,0},{20,4},{24,8},{28,12},{1,17},{... | collective-permute-start | bytes 196616 | tf_op jit(solution)/shard_map/ppermute | solution.py:74
  5.8 6.2 %collective-permute-start = (bf16[16,2048]{1,0:T(8,128)(2,1)}, bf16[16,2048]{1,0:T(8,128)(2,1)S(1)}, u32[]{:S(2)}, u32[]{:S(2)}) collective-permute-start(bf16[16,2048]{1,0:T(8,128)(2,1)} %bitcast.9), channel_id=1, source_target_pairs={{0,8},{4,12},{8,0},{12,4},{16,24},{20,28},{24,16},{28,20},{1,9},{5... | collective-permute-start | bytes 196616 | tf_op jit(solution)/shard_map/ppermute | solution.py:74
  6.4 3.8 %collective-permute-start.4 = (bf16[256,16]{0,1:T(8,128)(2,1)}, bf16[256,16]{0,1:T(8,128)(2,1)S(1)}, u32[]{:S(2)}, u32[]{:S(2)}) collective-permute-start(bf16[256,16]{0,1:T(8,128)(2,1)} %param.11), channel_id=1, source_target_pairs={{0,4},{4,0},{8,12},{12,8},{16,20},{20,16},{24,28},{28,24},{1,5},{5... | collective-permute-start | bytes 24584 | tf_op jit(solution)/shard_map/ppermute | solution.py:74
  6.4 5.6 %collective-permute-start.3 = (bf16[256,2048]{1,0:T(8,128)(2,1)}, bf16[256,2048]{1,0:T(8,128)(2,1)S(1)}, u32[]{:S(2)}, u32[]{:S(2)}) collective-permute-start(bf16[256,2048]{1,0:T(8,128)(2,1)} %codes_hbm.1), channel_id=1, source_target_pairs={{0,4},{4,0},{8,12},{12,8},{16,20},{20,16},{24,28},{28,24},{1,5},{5... | collective-permute-start | bytes 3145736 | tf_op jit(solution)/shard_map/ppermute | solution.py:74
  6.9 5.1 %copy-start = (bf16[2,8,2048]{2,1,0:T(8,128)(2,1)S(1)}, bf16[2,8,2048]{2,1,0:T(8,128)(2,1)}, u32[]{:S(2)}) copy-start(bf16[2,8,2048]{2,1,0:T(8,128)(2,1)} %param.8) | copy-start | bytes 196612
  10.2 13.9 %collective-permute-start.11 = (bf16[272,128]{1,0:T(8,128)(2,1)S(1)}, bf16[272,128]{1,0:T(8,128)(2,1)S(1)}, u32[]{:S(2)}, u32[]{:S(2)}) collective-permute-start(bf16[272,128]{1,0:T(8,128)(2,1)S(1)} %get-tuple-element.51), channel_id=1, source_target_pairs={{0,1},{1,0},{2,3},{3,2},{4,5},{5,4},{6,7},{7,6},{8,9},{9,8},{10,11... | collective-permute-start | bytes 208904 | tf_op jit(solution)/shard_map/ppermute | solution.py:74
  13.4 6.0 %collective-permute-start.5 = (f32[16,512]{1,0:T(8,128)S(1)}, f32[16,512]{1,0:T(8,128)S(1)}, u32[]{:S(2)}, u32[]{:S(2)}) collective-permute-start(f32[16,512]{1,0:T(8,128)S(1)} %get-tuple-element.43), channel_id=1, source_target_pairs={{0,24},{4,28},{8,16},{12,20},{16,8},{20,12},{24,0},{28,4},{1,25},{... | collective-permute-start | bytes 98312 | tf_op jit(solution)/shard_map/ppermute | solution.py:74
  17.1 4.8 %collective-permute-start.6 = (f32[16,512]{1,0:T(8,128)S(1)}, f32[16,512]{1,0:T(8,128)S(1)}, u32[]{:S(2)}, u32[]{:S(2)}) collective-permute-start(f32[16,512]{1,0:T(8,128)S(1)} %get-tuple-element.44), channel_id=1, source_target_pairs={{0,16},{4,20},{8,24},{12,28},{16,0},{20,4},{24,8},{28,12},{1,17},{... | collective-permute-start | bytes 98312 | tf_op jit(solution)/shard_map/ppermute | solution.py:74
  17.1 4.8 %collective-permute-start.7 = (f32[16,512]{1,0:T(8,128)S(1)}, f32[16,512]{1,0:T(8,128)S(1)}, u32[]{:S(2)}, u32[]{:S(2)}) collective-permute-start(f32[16,512]{1,0:T(8,128)S(1)} %get-tuple-element.45), channel_id=1, source_target_pairs={{0,8},{4,12},{8,0},{12,4},{16,24},{20,28},{24,16},{28,20},{1,9},{5... | collective-permute-start | bytes 98312 | tf_op jit(solution)/shard_map/ppermute | solution.py:74
  17.9 7.7 %collective-permute-start.12 = (bf16[272,128]{1,0:T(8,128)(2,1)S(1)}, bf16[272,128]{1,0:T(8,128)(2,1)S(1)}, u32[]{:S(2)}, u32[]{:S(2)}) collective-permute-start(bf16[272,128]{1,0:T(8,128)(2,1)S(1)} %get-tuple-element.52), channel_id=1, source_target_pairs={{0,2},{1,3},{2,0},{3,1},{4,6},{5,7},{6,4},{7,5},{8,10},{9,11},{10,... | collective-permute-start | bytes 208904 | tf_op jit(solution)/shard_map/ppermute | solution.py:74
  19.4 6.2 %collective-permute-start.13 = (bf16[272,128]{1,0:T(8,128)(2,1)S(1)}, bf16[272,128]{1,0:T(8,128)(2,1)S(1)}, u32[]{:S(2)}, u32[]{:S(2)}) collective-permute-start(bf16[272,128]{1,0:T(8,128)(2,1)S(1)} %get-tuple-element.53), channel_id=1, source_target_pairs={{0,3},{1,2},{2,1},{3,0},{4,7},{5,6},{6,5},{7,4},{8,11},{9,10},{10,... | collective-permute-start | bytes 208904 | tf_op jit(solution)/shard_map/ppermute | solution.py:74
  22.0 5.0 %collective-permute-start.8 = (bf16[16,1280]{1,0:T(8,128)(2,1)S(1)}, bf16[16,1280]{1,0:T(8,128)(2,1)S(1)}, u32[]{:S(2)}, u32[]{:S(2)}) collective-permute-start(bf16[16,1280]{1,0:T(8,128)(2,1)S(1)} %get-tuple-element.47), channel_id=1, source_target_pairs={{0,3},{1,2},{2,1},{3,0},{4,7},{5,6},{6,5},{7,4},{8,11},{9,10},{10,... | collective-permute-start | bytes 122888 | tf_op jit(solution)/shard_map/ppermute | solution.py:74
  23.6 4.0 %collective-permute-start.9 = (bf16[16,1280]{1,0:T(8,128)(2,1)S(1)}, bf16[16,1280]{1,0:T(8,128)(2,1)S(1)}, u32[]{:S(2)}, u32[]{:S(2)}) collective-permute-start(bf16[16,1280]{1,0:T(8,128)(2,1)S(1)} %get-tuple-element.48), channel_id=1, source_target_pairs={{0,2},{1,3},{2,0},{3,1},{4,6},{5,7},{6,4},{7,5},{8,10},{9,11},{10,... | collective-permute-start | bytes 122888 | tf_op jit(solution)/shard_map/ppermute | solution.py:74
  24.1 4.0 %collective-permute-start.10 = (bf16[16,1280]{1,0:T(8,128)(2,1)S(1)}, bf16[16,1280]{1,0:T(8,128)(2,1)S(1)}, u32[]{:S(2)}, u32[]{:S(2)}) collective-permute-start(bf16[16,1280]{1,0:T(8,128)(2,1)S(1)} %get-tuple-element.49), channel_id=1, source_target_pairs={{0,1},{1,0},{2,3},{3,2},{4,5},{5,4},{6,7},{7,6},{8,9},{9,8},{10,11... | collective-permute-start | bytes 122888 | tf_op jit(solution)/shard_map/ppermute | solution.py:74

commit v22 on v16

--- a/solution.py
+++ b/solution.py
@@ -16,7 +16,7 @@
 
 NEGATIVE = -1e30
 SCORE_SCALE = HD ** (-0.5)
-PART = 64
+PART = 256
 CACHE_HINT = 120_000_000
 PROJECT_HINT = 60_000_000
 PACK_HINT = 60_000_000

time: 29.3 us -> 29.3 us (level)
  transfers between devices with their start and end apart: 14 -> 14, of which waited for: 4 -> 5; matrix products, arithmetic and copies ran while one was open for 0% -> 0% of each run, Pallas kernels for 19% -> 19%
where the time goes in v22:
time: 29.3 us; the launch traced here: 29.1 us
  starting transfers between devices  19.4 us (66%)
  Pallas kernels  6.56 us (22%)
  waiting for transfers between devices  2.49 us (8%)
  between operations  0.69 us (2%)
    ppermute x14, starting transfers between devices, swap(): return lax.ppermute(x, axis, [(k, k ^ distance) for k in range(size)])  19.4 us
    pallas_call x1, Pallas kernels, prepare(): pl.pallas_call(functools.partial(prepare_kernel, rows, steps, own, min(ow...  3.29 us
    ppermute x14, waiting for transfers between devices, swap(): return lax.ppermute(x, axis, [(k, k ^ distance) for k in range(size)])  2.49 us
    pallas_call x1, Pallas kernels, project(): pl.pallas_call(functools.partial(project_kernel, pairs), out_shape=[jax.S...  1.29 us
    pallas_call x1, Pallas kernels, finish(): pl.pallas_call(functools.partial(finish_kernel, rows, steps, own, min(own...  1.06 us
  transfers between devices with their start and end apart: 14, of which 5 were waited for; matrix products, arithmetic and copies ran while one was open for 0% of the time, Pallas kernels for 19%

profile of v22, /device:TPU:0, one launch (start us, length us, event | category | flops | bytes accessed | tf_op | source)
XLA Modules:
  0.0 29.1 jit_solution(3323615241709226608)
XLA Ops:
  0.6 0.5 %collective-permute-start.3 = (bf16[256,2048]{1,0:T(8,128)(2,1)}, bf16[256,2048]{1,0:T(8,128)(2,1)S(1)}, u32[]{:S(2)}, u32[]{:S(2)}) collective-permute-start(bf16[256,2048]{1,0:T(8,128)(2,1)} %codes_hbm.1), channel_id=1, source_target_pairs={{0,4},{4,0},{8,12},{12,8},{16,20},{20,16},{24,28},{28,24},{1,5},{5... | collective-permute-start | bytes 3145736 | tf_op jit(solution)/shard_map/ppermute | solution.py:74
  1.2 4.7 %collective-permute-start.2 = (bf16[16,2048]{1,0:T(8,128)(2,1)}, bf16[16,2048]{1,0:T(8,128)(2,1)S(1)}, u32[]{:S(2)}, u32[]{:S(2)}) collective-permute-start(bf16[16,2048]{1,0:T(8,128)(2,1)} %bitcast.7), channel_id=1, source_target_pairs={{0,24},{4,28},{8,16},{12,20},{16,8},{20,12},{24,0},{28,4},{1,25},{... | collective-permute-start | bytes 196616 | tf_op jit(solution)/shard_map/ppermute | solution.py:74
  5.8 0.0 collective-permute-start.1
  5.8 0.6 %collective-permute-start = (bf16[16,2048]{1,0:T(8,128)(2,1)}, bf16[16,2048]{1,0:T(8,128)(2,1)S(1)}, u32[]{:S(2)}, u32[]{:S(2)}) collective-permute-start(bf16[16,2048]{1,0:T(8,128)(2,1)} %bitcast.9), channel_id=1, source_target_pairs={{0,8},{4,12},{8,0},{12,4},{16,24},{20,28},{24,16},{28,20},{1,9},{5... | collective-permute-start | bytes 196616 | tf_op jit(solution)/shard_map/ppermute | solution.py:74
  6.5 0.0 collective-permute-start.4
  6.5 3.3 %prepare.1 = (bf16[256,2048]{1,0:T(8,128)(2,1)S(1)}, bf16[2,256,2048]{2,1,0:T(8,128)(2,1)S(1)}, bf16[256,128]{1,0:T(8,128)(2,1)S(1)}, s32[8,128]{1,0:T(8,128)S(1...) custom-call(s32[8]{0:T(128)} %owner_hbm.1, ...), custom_call_target="tpu_custom_call" | custom-call | bytes 120000000 | tf_op jit(solution)/shard_map/prepare/pallas_call | solution.py:226
  9.8 0.0 copy-start
  9.8 0.0 collective-permute-done.4
  9.8 1.7 %collective-permute-start.11 = (bf16[272,128]{1,0:T(8,128)(2,1)S(1)}, bf16[272,128]{1,0:T(8,128)(2,1)S(1)}, u32[]{:S(2)}, u32[]{:S(2)}) collective-permute-start(bf16[272,128]{1,0:T(8,128)(2,1)S(1)} %get-tuple-element.45), channel_id=1, source_target_pairs={{0,1},{1,0},{2,3},{3,2},{4,5},{5,4},{6,7},{7,6},{8,9},{9,8},{10,11... | collective-permute-start | bytes 208904 | tf_op jit(solution)/shard_map/ppermute | solution.py:74
  11.5 0.0 collective-permute-done.3.codes_ref
  11.5 0.5 %mate_weights.1.mate_ref = bf16[256,2048]{1,0:T(8,128)(2,1)S(1)} custom-call(bf16[256,2048]{1,0:T(8,128)(2,1)S(1)} %collective-permute-done.3.codes_ref, bf16[16,256]{1,0:T(8,128)(2,1)S(1)} %bitcast.11), custom_call_target="tpu_custom_call" | custom-call | bytes 1000 | tf_op jit(solution)/shard_map/mate_weights/pallas_call | solution.py:99
  12.0 0.0 collective-permute-done.2.refs_3_
  12.0 0.1 collective-permute-done.1.refs_2_
  12.1 0.0 collective-permute-done.refs_1_
  12.1 0.0 copy-done
  12.1 1.3 %project.1 = (f32[16,512]{1,0:T(8,128)S(1)}, f32[16,512]{1,0:T(8,128)S(1)}, f32[16,512]{1,0:T(8,128)S(1)}, f32[16,512]{1,0:T(8,128)S(1)}) custom-call(bf16[256,2048]{1,0:T(8,128)(2,1)S(1)} %get-tuple-element.29.own_ref, bf16[256,2048]{1,0:T(8,128)(2,1)S(1)} %mate_weights.1.mate_ref, bf16[2,256,2048]{2,1,0:T(8,128)(2,1)S(1)} %get-tuple-element.31.base_ref, ...), custom_call_target="tpu_custom_call" | custom-call | bytes 60000000 | tf_op jit(solution)/shard_map/project/pallas_call | solution.py:305
  13.4 3.6 %collective-permute-start.5 = (f32[16,512]{1,0:T(8,128)S(1)}, f32[16,512]{1,0:T(8,128)S(1)}, u32[]{:S(2)}, u32[]{:S(2)}) collective-permute-start(f32[16,512]{1,0:T(8,128)S(1)} %get-tuple-element.37), channel_id=1, source_target_pairs={{0,24},{4,28},{8,16},{12,20},{16,8},{20,12},{24,0},{28,4},{1,25},{... | collective-permute-start | bytes 98312 | tf_op jit(solution)/shard_map/ppermute | solution.py:74
  17.0 0.0 collective-permute-start.6
  17.0 0.9 %collective-permute-start.7 = (f32[16,512]{1,0:T(8,128)S(1)}, f32[16,512]{1,0:T(8,128)S(1)}, u32[]{:S(2)}, u32[]{:S(2)}) collective-permute-start(f32[16,512]{1,0:T(8,128)S(1)} %get-tuple-element.39), channel_id=1, source_target_pairs={{0,8},{4,12},{8,0},{12,4},{16,24},{20,28},{24,16},{28,20},{1,9},{5... | collective-permute-start | bytes 98312 | tf_op jit(solution)/shard_map/ppermute | solution.py:74
  17.9 1.5 %collective-permute-start.12 = (bf16[272,128]{1,0:T(8,128)(2,1)S(1)}, bf16[272,128]{1,0:T(8,128)(2,1)S(1)}, u32[]{:S(2)}, u32[]{:S(2)}) collective-permute-start(bf16[272,128]{1,0:T(8,128)(2,1)S(1)} %get-tuple-element.46), channel_id=1, source_target_pairs={{0,2},{1,3},{2,0},{3,1},{4,6},{5,7},{6,4},{7,5},{8,10},{9,11},{10,... | collective-permute-start | bytes 208904 | tf_op jit(solution)/shard_map/ppermute | solution.py:74
  19.4 0.0 collective-permute-done.5.refs_1_
  19.4 2.3 %collective-permute-start.13 = (bf16[272,128]{1,0:T(8,128)(2,1)S(1)}, bf16[272,128]{1,0:T(8,128)(2,1)S(1)}, u32[]{:S(2)}, u32[]{:S(2)}) collective-permute-start(bf16[272,128]{1,0:T(8,128)(2,1)S(1)} %get-tuple-element.47), channel_id=1, source_target_pairs={{0,3},{1,2},{2,1},{3,0},{4,7},{5,6},{6,5},{7,4},{8,11},{9,10},{10,... | collective-permute-start | bytes 208904 | tf_op jit(solution)/shard_map/ppermute | solution.py:74
  21.7 0.1 collective-permute-done.6.refs_2_
  21.8 0.0 collective-permute-done.7.refs_3_
  21.8 0.1 pack_pieces.1
  21.9 1.6 %collective-permute-start.8 = (bf16[16,1280]{1,0:T(8,128)(2,1)S(1)}, bf16[16,1280]{1,0:T(8,128)(2,1)S(1)}, u32[]{:S(2)}, u32[]{:S(2)}) collective-permute-start(bf16[16,1280]{1,0:T(8,128)(2,1)S(1)} %get-tuple-element.41), channel_id=1, source_target_pairs={{0,3},{1,2},{2,1},{3,0},{4,7},{5,6},{6,5},{7,4},{8,11},{9,10},{10,... | collective-permute-start | bytes 122888 | tf_op jit(solution)/shard_map/ppermute | solution.py:74
  23.5 0.6 %collective-permute-start.9 = (bf16[16,1280]{1,0:T(8,128)(2,1)S(1)}, bf16[16,1280]{1,0:T(8,128)(2,1)S(1)}, u32[]{:S(2)}, u32[]{:S(2)}) collective-permute-start(bf16[16,1280]{1,0:T(8,128)(2,1)S(1)} %get-tuple-element.42), channel_id=1, source_target_pairs={{0,2},{1,3},{2,0},{3,1},{4,6},{5,7},{6,4},{7,5},{8,10},{9,11},{10,... | collective-permute-start | bytes 122888 | tf_op jit(solution)/shard_map/ppermute | solution.py:74
  24.0 0.0 collective-permute-done.11.refs_1_
  24.0 1.4 %collective-permute-start.10 = (bf16[16,1280]{1,0:T(8,128)(2,1)S(1)}, bf16[16,1280]{1,0:T(8,128)(2,1)S(1)}, u32[]{:S(2)}, u32[]{:S(2)}) collective-permute-start(bf16[16,1280]{1,0:T(8,128)(2,1)S(1)} %get-tuple-element.43), channel_id=1, source_target_pairs={{0,1},{1,0},{2,3},{3,2},{4,5},{5,4},{6,7},{7,6},{8,9},{9,8},{10,11... | collective-permute-start | bytes 122888 | tf_op jit(solution)/shard_map/ppermute | solution.py:74
  25.5 0.0 collective-permute-done.12.refs_2_
  25.5 0.0 collective-permute-done.13.refs_3_
  25.5 0.3 %merge_partials.1.refs_4_ = f32[264,128]{1,0:T(8,128)S(1)} custom-call(f32[264,128]{1,0:T(8,128)S(1)} %get-tuple-element.44.refs_0_, bf16[272,128]{1,0:T(8,128)(2,1)S(1)} %collective-permute-done.11.refs_1_, bf16[272,128]{1,0:T(8,128)(2,1)S(1)} %collective-permute-done.12.refs_2_, bf16[272,128]{1,0:T(8,128)(2,1)S(1)} %collective-permute-done.13.refs_3_), custom_call_target="tpu_custom_call" | custom-call | bytes 1000 | tf_op jit(solution)/shard_map/merge_partials/pallas_call | solution.py:279
  25.8 1.0 %collective-permute-done.8.refs_1_ = bf16[16,1280]{1,0:T(8,128)(2,1)S(1)} collective-permute-done((bf16[16,1280]{1,0:T(8,128)(2,1)S(1)}, bf16[16,1280]{1,0:T(8,128)(2,1)S(1)}, u32[]{:S(2)}, u32[]{:S(2)}) %collective-permute-start.8) | collective-permute-done | bytes 40992 | tf_op jit(solution)/shard_map/ppermute | solution.py:74
  26.9 0.6 %collective-permute-done.9.refs_2_ = bf16[16,1280]{1,0:T(8,128)(2,1)S(1)} collective-permute-done((bf16[16,1280]{1,0:T(8,128)(2,1)S(1)}, bf16[16,1280]{1,0:T(8,128)(2,1)S(1)}, u32[]{:S(2)}, u32[]{:S(2)}) %collective-permute-start.9) | collective-permute-done | bytes 40992 | tf_op jit(solution)/shard_map/ppermute | solution.py:74
  27.5 0.6 %collective-permute-done.10.refs_3_ = bf16[16,1280]{1,0:T(8,128)(2,1)S(1)} collective-permute-done((bf16[16,1280]{1,0:T(8,128)(2,1)S(1)}, bf16[16,1280]{1,0:T(8,128)(2,1)S(1)}, u32[]{:S(2)}, u32[]{:S(2)}) %collective-permute-start.10) | collective-permute-done | bytes 40992 | tf_op jit(solution)/shard_map/ppermute | solution.py:74
  28.0 1.1 %finish.1 = (bf16[16,512]{1,0:T(8,128)(2,1)}, bf16[16,2048]{1,0:T(8,128)(2,1)}) custom-call(bf16[256,128]{1,0:T(8,128)(2,1)S(1)} %get-tuple-element.27.query_ref, f32[16,1024]{1,0:T(8,128)S(1)} %get-tuple-element.40.refs_0_, bf16[16,1280]{1,0:T(8,128)(2,1)S(1)} %collective-permute-done.8.refs_1_, bf16[16,1280]{1,0:T(8,128)(2,1)S(1)} %collective-permute-done.9.refs_2_, ...), custom_call_target="tpu_custom_call" | custom-call | tf_op jit(solution)/shard_map/finish/pallas_call | solution.py:455
Async XLA Ops:
  0.6 10.9 %collective-permute-start.3 = (bf16[256,2048]{1,0:T(8,128)(2,1)}, bf16[256,2048]{1,0:T(8,128)(2,1)S(1)}, u32[]{:S(2)}, u32[]{:S(2)}) collective-permute-start(bf16[256,2048]{1,0:T(8,128)(2,1)} %codes_hbm.1), channel_id=1, source_target_pairs={{0,4},{4,0},{8,12},{12,8},{16,20},{20,16},{24,28},{28,24},{1,5},{5... | collective-permute-start | bytes 3145736 | tf_op jit(solution)/shard_map/ppermute | solution.py:74
  1.2 10.8 %collective-permute-start.2 = (bf16[16,2048]{1,0:T(8,128)(2,1)}, bf16[16,2048]{1,0:T(8,128)(2,1)S(1)}, u32[]{:S(2)}, u32[]{:S(2)}) collective-permute-start(bf16[16,2048]{1,0:T(8,128)(2,1)} %bitcast.7), channel_id=1, source_target_pairs={{0,24},{4,28},{8,16},{12,20},{16,8},{20,12},{24,0},{28,4},{1,25},{... | collective-permute-start | bytes 196616 | tf_op jit(solution)/shard_map/ppermute | solution.py:74
  5.8 6.3 %collective-permute-start.1 = (bf16[16,2048]{1,0:T(8,128)(2,1)}, bf16[16,2048]{1,0:T(8,128)(2,1)S(1)}, u32[]{:S(2)}, u32[]{:S(2)}) collective-permute-start(bf16[16,2048]{1,0:T(8,128)(2,1)} %bitcast.8), channel_id=1, source_target_pairs={{0,16},{4,20},{8,24},{12,28},{16,0},{20,4},{24,8},{28,12},{1,17},{... | collective-permute-start | bytes 196616 | tf_op jit(solution)/shard_map/ppermute | solution.py:74
  5.8 6.3 %collective-permute-start = (bf16[16,2048]{1,0:T(8,128)(2,1)}, bf16[16,2048]{1,0:T(8,128)(2,1)S(1)}, u32[]{:S(2)}, u32[]{:S(2)}) collective-permute-start(bf16[16,2048]{1,0:T(8,128)(2,1)} %bitcast.9), channel_id=1, source_target_pairs={{0,8},{4,12},{8,0},{12,4},{16,24},{20,28},{24,16},{28,20},{1,9},{5... | collective-permute-start | bytes 196616 | tf_op jit(solution)/shard_map/ppermute | solution.py:74
  6.5 3.3 %collective-permute-start.4 = (bf16[256,16]{0,1:T(8,128)(2,1)}, bf16[256,16]{0,1:T(8,128)(2,1)S(1)}, u32[]{:S(2)}, u32[]{:S(2)}) collective-permute-start(bf16[256,16]{0,1:T(8,128)(2,1)} %param.11), channel_id=1, source_target_pairs={{0,4},{4,0},{8,12},{12,8},{16,20},{20,16},{24,28},{28,24},{1,5},{5... | collective-permute-start | bytes 24584 | tf_op jit(solution)/shard_map/ppermute | solution.py:74
  9.8 2.3 %copy-start = (bf16[2,8,2048]{2,1,0:T(8,128)(2,1)S(1)}, bf16[2,8,2048]{2,1,0:T(8,128)(2,1)}, u32[]{:S(2)}) copy-start(bf16[2,8,2048]{2,1,0:T(8,128)(2,1)} %param.8) | copy-start | bytes 196612
  9.8 14.2 %collective-permute-start.11 = (bf16[272,128]{1,0:T(8,128)(2,1)S(1)}, bf16[272,128]{1,0:T(8,128)(2,1)S(1)}, u32[]{:S(2)}, u32[]{:S(2)}) collective-permute-start(bf16[272,128]{1,0:T(8,128)(2,1)S(1)} %get-tuple-element.45), channel_id=1, source_target_pairs={{0,1},{1,0},{2,3},{3,2},{4,5},{5,4},{6,7},{7,6},{8,9},{9,8},{10,11... | collective-permute-start | bytes 208904 | tf_op jit(solution)/shard_map/ppermute | solution.py:74
  13.4 6.0 %collective-permute-start.5 = (f32[16,512]{1,0:T(8,128)S(1)}, f32[16,512]{1,0:T(8,128)S(1)}, u32[]{:S(2)}, u32[]{:S(2)}) collective-permute-start(f32[16,512]{1,0:T(8,128)S(1)} %get-tuple-element.37), channel_id=1, source_target_pairs={{0,24},{4,28},{8,16},{12,20},{16,8},{20,12},{24,0},{28,4},{1,25},{... | collective-permute-start | bytes 98312 | tf_op jit(solution)/shard_map/ppermute | solution.py:74
  17.0 4.8 %collective-permute-start.6 = (f32[16,512]{1,0:T(8,128)S(1)}, f32[16,512]{1,0:T(8,128)S(1)}, u32[]{:S(2)}, u32[]{:S(2)}) collective-permute-start(f32[16,512]{1,0:T(8,128)S(1)} %get-tuple-element.38), channel_id=1, source_target_pairs={{0,16},{4,20},{8,24},{12,28},{16,0},{20,4},{24,8},{28,12},{1,17},{... | collective-permute-start | bytes 98312 | tf_op jit(solution)/shard_map/ppermute | solution.py:74
  17.0 4.8 %collective-permute-start.7 = (f32[16,512]{1,0:T(8,128)S(1)}, f32[16,512]{1,0:T(8,128)S(1)}, u32[]{:S(2)}, u32[]{:S(2)}) collective-permute-start(f32[16,512]{1,0:T(8,128)S(1)} %get-tuple-element.39), channel_id=1, source_target_pairs={{0,8},{4,12},{8,0},{12,4},{16,24},{20,28},{24,16},{28,20},{1,9},{5... | collective-permute-start | bytes 98312 | tf_op jit(solution)/shard_map/ppermute | solution.py:74
  17.9 7.6 %collective-permute-start.12 = (bf16[272,128]{1,0:T(8,128)(2,1)S(1)}, bf16[272,128]{1,0:T(8,128)(2,1)S(1)}, u32[]{:S(2)}, u32[]{:S(2)}) collective-permute-start(bf16[272,128]{1,0:T(8,128)(2,1)S(1)} %get-tuple-element.46), channel_id=1, source_target_pairs={{0,2},{1,3},{2,0},{3,1},{4,6},{5,7},{6,4},{7,5},{8,10},{9,11},{10,... | collective-permute-start | bytes 208904 | tf_op jit(solution)/shard_map/ppermute | solution.py:74
  19.4 6.1 %collective-permute-start.13 = (bf16[272,128]{1,0:T(8,128)(2,1)S(1)}, bf16[272,128]{1,0:T(8,128)(2,1)S(1)}, u32[]{:S(2)}, u32[]{:S(2)}) collective-permute-start(bf16[272,128]{1,0:T(8,128)(2,1)S(1)} %get-tuple-element.47), channel_id=1, source_target_pairs={{0,3},{1,2},{2,1},{3,0},{4,7},{5,6},{6,5},{7,4},{8,11},{9,10},{10,... | collective-permute-start | bytes 208904 | tf_op jit(solution)/shard_map/ppermute | solution.py:74
  21.9 5.0 %collective-permute-start.8 = (bf16[16,1280]{1,0:T(8,128)(2,1)S(1)}, bf16[16,1280]{1,0:T(8,128)(2,1)S(1)}, u32[]{:S(2)}, u32[]{:S(2)}) collective-permute-start(bf16[16,1280]{1,0:T(8,128)(2,1)S(1)} %get-tuple-element.41), channel_id=1, source_target_pairs={{0,3},{1,2},{2,1},{3,0},{4,7},{5,6},{6,5},{7,4},{8,11},{9,10},{10,... | collective-permute-start | bytes 122888 | tf_op jit(solution)/shard_map/ppermute | solution.py:74
  23.5 4.0 %collective-permute-start.9 = (bf16[16,1280]{1,0:T(8,128)(2,1)S(1)}, bf16[16,1280]{1,0:T(8,128)(2,1)S(1)}, u32[]{:S(2)}, u32[]{:S(2)}) collective-permute-start(bf16[16,1280]{1,0:T(8,128)(2,1)S(1)} %get-tuple-element.42), channel_id=1, source_target_pairs={{0,2},{1,3},{2,0},{3,1},{4,6},{5,7},{6,4},{7,5},{8,10},{9,11},{10,... | collective-permute-start | bytes 122888 | tf_op jit(solution)/shard_map/ppermute | solution.py:74
  24.0 4.0 %collective-permute-start.10 = (bf16[16,1280]{1,0:T(8,128)(2,1)S(1)}, bf16[16,1280]{1,0:T(8,128)(2,1)S(1)}, u32[]{:S(2)}, u32[]{:S(2)}) collective-permute-start(bf16[16,1280]{1,0:T(8,128)(2,1)S(1)} %get-tuple-element.43), channel_id=1, source_target_pairs={{0,1},{1,0},{2,3},{3,2},{4,5},{5,4},{6,7},{7,6},{8,9},{9,8},{10,11... | collective-permute-start | bytes 122888 | tf_op jit(solution)/shard_map/ppermute | solution.py:74

commit v23 on v20

--- a/solution.py
+++ b/solution.py
@@ -500,7 +500,7 @@
         heads_own,
         tensor_count,
     )
-    mate_scales, partials[-1] = lax.optimization_barrier((mate_scales, partials[-1]))
+    mate_scales, partials[2] = lax.optimization_barrier((mate_scales, partials[2]))
     behind = lax.optimization_barrier((*near_first(token_rows), own_query))
     token_rows, own_query = near_first(list(behind[:pairs])), behind[-1]
     projected = project(

time: 30.3 us -> 29.3 us (0.967)
  waiting for transfers between devices: 4.27 us -> 3.28 us
    ppermute x14, waiting for transfers between devices: 4.27 us -> 3.28 us  [swap(): return lax.ppermute(x, axis, [(k, k ^ distance) for k in range(size)])]
  transfers between devices with their start and end apart: 14 -> 14, of which waited for: 4 -> 4; matrix products, arithmetic and copies ran while one was open for 0% -> 0% of each run, Pallas kernels for 17% -> 18%
where the time goes in v23:
time: 29.3 us; the launch traced here: 29.2 us
  starting transfers between devices  18.9 us (65%)
  Pallas kernels  6.31 us (22%)
  waiting for transfers between devices  3.28 us (11%)
  between operations  0.69 us (2%)
    ppermute x14, starting transfers between devices, swap(): return lax.ppermute(x, axis, [(k, k ^ distance) for k in range(size)])  18.9 us
    pallas_call x1, Pallas kernels, prepare(): pl.pallas_call(functools.partial(prepare_kernel, rows, steps, own, min(ow...  3.32 us
    ppermute x14, waiting for transfers between devices, swap(): return lax.ppermute(x, axis, [(k, k ^ distance) for k in range(size)])  3.28 us
    pallas_call x1, Pallas kernels, project(): pl.pallas_call(functools.partial(project_kernel, pairs), out_shape=[jax.S...  1.48 us
    pallas_call x1, Pallas kernels, finish(): pl.pallas_call(functools.partial(finish_kernel, rows, steps, own, min(own...  1.06 us
  transfers between devices with their start and end apart: 14, of which 4 were waited for; matrix products, arithmetic and copies ran while one was open for 0% of the time, Pallas kernels for 18%

profile of v23, /device:TPU:0, one launch (start us, length us, event | category | flops | bytes accessed | tf_op | source)
XLA Modules:
  0.0 29.2 jit_solution(17728066759121535250)
XLA Ops:
  0.6 5.1 %collective-permute-start.2 = (bf16[16,2048]{1,0:T(8,128)(2,1)}, bf16[16,2048]{1,0:T(8,128)(2,1)S(1)}, u32[]{:S(2)}, u32[]{:S(2)}) collective-permute-start(bf16[16,2048]{1,0:T(8,128)(2,1)} %bitcast.7), channel_id=1, source_target_pairs={{0,24},{4,28},{8,16},{12,20},{16,8},{20,12},{24,0},{28,4},{1,25},{... | collective-permute-start | bytes 196616 | tf_op jit(solution)/shard_map/ppermute | solution.py:74
  5.7 0.0 collective-permute-start.1
  5.8 0.6 %collective-permute-start = (bf16[16,2048]{1,0:T(8,128)(2,1)}, bf16[16,2048]{1,0:T(8,128)(2,1)S(1)}, u32[]{:S(2)}, u32[]{:S(2)}) collective-permute-start(bf16[16,2048]{1,0:T(8,128)(2,1)} %bitcast.9), channel_id=1, source_target_pairs={{0,8},{4,12},{8,0},{12,4},{16,24},{20,28},{24,16},{28,20},{1,9},{5... | collective-permute-start | bytes 196616 | tf_op jit(solution)/shard_map/ppermute | solution.py:74
  6.4 0.0 collective-permute-start.4
  6.4 0.5 %collective-permute-start.3 = (bf16[256,2048]{1,0:T(8,128)(2,1)}, bf16[256,2048]{1,0:T(8,128)(2,1)S(1)}, u32[]{:S(2)}, u32[]{:S(2)}) collective-permute-start(bf16[256,2048]{1,0:T(8,128)(2,1)} %codes_hbm.1), channel_id=1, source_target_pairs={{0,4},{4,0},{8,12},{12,8},{16,20},{20,16},{24,28},{28,24},{1,5},{5... | collective-permute-start | bytes 3145736 | tf_op jit(solution)/shard_map/ppermute | solution.py:74
  6.9 0.0 copy-start
  6.9 3.3 %prepare.1 = (bf16[256,2048]{1,0:T(8,128)(2,1)S(1)}, bf16[2,256,2048]{2,1,0:T(8,128)(2,1)S(1)}, bf16[256,128]{1,0:T(8,128)(2,1)S(1)}, s32[8,128]{1,0:T(8,128)S(1...) custom-call(s32[8]{0:T(128)} %owner_hbm.1, ...), custom_call_target="tpu_custom_call" | custom-call | flops 15000000512 | bytes 120000000 | tf_op jit(solution)/shard_map/prepare/pallas_call | solution.py:214
  10.2 0.0 collective-permute-done.4
  10.2 1.7 %collective-permute-start.11 = (bf16[272,128]{1,0:T(8,128)(2,1)S(1)}, bf16[272,128]{1,0:T(8,128)(2,1)S(1)}, u32[]{:S(2)}, u32[]{:S(2)}) collective-permute-start(bf16[272,128]{1,0:T(8,128)(2,1)S(1)} %get-tuple-element.47), channel_id=1, source_target_pairs={{0,1},{1,0},{2,3},{3,2},{4,5},{5,4},{6,7},{7,6},{8,9},{9,8},{10,11... | collective-permute-start | bytes 208904 | tf_op jit(solution)/shard_map/ppermute | solution.py:74
  11.9 0.0 collective-permute-done.2.refs_3_
  11.9 0.0 collective-permute-done.1.refs_2_
  11.9 0.0 collective-permute-done.refs_1_
  12.0 0.0 collective-permute-done.3.codes_ref
  12.0 0.0 copy-done
  12.0 1.5 %project.1 = (f32[16,512]{1,0:T(8,128)S(1)}, f32[16,512]{1,0:T(8,128)S(1)}, f32[16,512]{1,0:T(8,128)S(1)}, f32[16,512]{1,0:T(8,128)S(1)}) custom-call(bf16[256,2048]{1,0:T(8,128)(2,1)S(1)} %get-tuple-element.30.own_ref, bf16[2,256,2048]{2,1,0:T(8,128)(2,1)S(1)} %get-tuple-element.31.base_ref, bf16[256,2048]{1,0:T(8,128)(2,1)S(1)} %collective-permute-done.3.codes_ref, ...), custom_call_target="tpu_custom_call" | custom-call | bytes 60000000 | tf_op jit(solution)/shard_map/project/pallas_call | solution.py:300
  13.4 3.7 %collective-permute-start.5 = (f32[16,512]{1,0:T(8,128)S(1)}, f32[16,512]{1,0:T(8,128)S(1)}, u32[]{:S(2)}, u32[]{:S(2)}) collective-permute-start(f32[16,512]{1,0:T(8,128)S(1)} %get-tuple-element.39), channel_id=1, source_target_pairs={{0,24},{4,28},{8,16},{12,20},{16,8},{20,12},{24,0},{28,4},{1,25},{... | collective-permute-start | bytes 98312 | tf_op jit(solution)/shard_map/ppermute | solution.py:74
  17.1 0.0 collective-permute-start.6
  17.1 0.8 %collective-permute-start.7 = (f32[16,512]{1,0:T(8,128)S(1)}, f32[16,512]{1,0:T(8,128)S(1)}, u32[]{:S(2)}, u32[]{:S(2)}) collective-permute-start(f32[16,512]{1,0:T(8,128)S(1)} %get-tuple-element.41), channel_id=1, source_target_pairs={{0,8},{4,12},{8,0},{12,4},{16,24},{20,28},{24,16},{28,20},{1,9},{5... | collective-permute-start | bytes 98312 | tf_op jit(solution)/shard_map/ppermute | solution.py:74
  17.9 2.0 %collective-permute-start.13 = (bf16[272,128]{1,0:T(8,128)(2,1)S(1)}, bf16[272,128]{1,0:T(8,128)(2,1)S(1)}, u32[]{:S(2)}, u32[]{:S(2)}) collective-permute-start(bf16[272,128]{1,0:T(8,128)(2,1)S(1)} %get-tuple-element.49), channel_id=1, source_target_pairs={{0,3},{1,2},{2,1},{3,0},{4,7},{5,6},{6,5},{7,4},{8,11},{9,10},{10,... | collective-permute-start | bytes 208904 | tf_op jit(solution)/shard_map/ppermute | solution.py:74
  19.9 0.0 collective-permute-done.5.refs_1_
  19.9 0.9 %collective-permute-start.12 = (bf16[272,128]{1,0:T(8,128)(2,1)S(1)}, bf16[272,128]{1,0:T(8,128)(2,1)S(1)}, u32[]{:S(2)}, u32[]{:S(2)}) collective-permute-start(bf16[272,128]{1,0:T(8,128)(2,1)S(1)} %get-tuple-element.48), channel_id=1, source_target_pairs={{0,2},{1,3},{2,0},{3,1},{4,6},{5,7},{6,4},{7,5},{8,10},{9,11},{10,... | collective-permute-start | bytes 208904 | tf_op jit(solution)/shard_map/ppermute | solution.py:74
  20.8 1.1 %collective-permute-done.6.refs_2_ = f32[16,512]{1,0:T(8,128)S(1)} collective-permute-done((f32[16,512]{1,0:T(8,128)S(1)}, f32[16,512]{1,0:T(8,128)S(1)}, u32[]{:S(2)}, u32[]{:S(2)}) %collective-permute-start.6) | collective-permute-done | bytes 32800 | tf_op jit(solution)/shard_map/ppermute | solution.py:74
  21.9 0.0 collective-permute-done.7.refs_3_
  21.9 0.1 pack_pieces.1
  22.0 1.6 %collective-permute-start.8 = (bf16[16,1280]{1,0:T(8,128)(2,1)S(1)}, bf16[16,1280]{1,0:T(8,128)(2,1)S(1)}, u32[]{:S(2)}, u32[]{:S(2)}) collective-permute-start(bf16[16,1280]{1,0:T(8,128)(2,1)S(1)} %get-tuple-element.43), channel_id=1, source_target_pairs={{0,3},{1,2},{2,1},{3,0},{4,7},{5,6},{6,5},{7,4},{8,11},{9,10},{10,... | collective-permute-start | bytes 122888 | tf_op jit(solution)/shard_map/ppermute | solution.py:74
  23.6 0.5 %collective-permute-start.9 = (bf16[16,1280]{1,0:T(8,128)(2,1)S(1)}, bf16[16,1280]{1,0:T(8,128)(2,1)S(1)}, u32[]{:S(2)}, u32[]{:S(2)}) collective-permute-start(bf16[16,1280]{1,0:T(8,128)(2,1)S(1)} %get-tuple-element.44), channel_id=1, source_target_pairs={{0,2},{1,3},{2,0},{3,1},{4,6},{5,7},{6,4},{7,5},{8,10},{9,11},{10,... | collective-permute-start | bytes 122888 | tf_op jit(solution)/shard_map/ppermute | solution.py:74
  24.1 0.0 collective-permute-done.11.refs_1_
  24.1 1.5 %collective-permute-start.10 = (bf16[16,1280]{1,0:T(8,128)(2,1)S(1)}, bf16[16,1280]{1,0:T(8,128)(2,1)S(1)}, u32[]{:S(2)}, u32[]{:S(2)}) collective-permute-start(bf16[16,1280]{1,0:T(8,128)(2,1)S(1)} %get-tuple-element.45), channel_id=1, source_target_pairs={{0,1},{1,0},{2,3},{3,2},{4,5},{5,4},{6,7},{7,6},{8,9},{9,8},{10,11... | collective-permute-start | bytes 122888 | tf_op jit(solution)/shard_map/ppermute | solution.py:74
  25.6 0.0 collective-permute-done.13.refs_3_
  25.6 0.0 collective-permute-done.12.refs_2_
  25.6 0.3 %merge_partials.1.refs_4_ = f32[264,128]{1,0:T(8,128)S(1)} custom-call(f32[264,128]{1,0:T(8,128)S(1)} %get-tuple-element.46.refs_0_, bf16[272,128]{1,0:T(8,128)(2,1)S(1)} %collective-permute-done.11.refs_1_, bf16[272,128]{1,0:T(8,128)(2,1)S(1)} %collective-permute-done.12.refs_2_, bf16[272,128]{1,0:T(8,128)(2,1)S(1)} %collective-permute-done.13.refs_3_), custom_call_target="tpu_custom_call" | custom-call | bytes 1000 | tf_op jit(solution)/shard_map/merge_partials/pallas_call | solution.py:267
  26.0 1.0 %collective-permute-done.8.refs_1_ = bf16[16,1280]{1,0:T(8,128)(2,1)S(1)} collective-permute-done((bf16[16,1280]{1,0:T(8,128)(2,1)S(1)}, bf16[16,1280]{1,0:T(8,128)(2,1)S(1)}, u32[]{:S(2)}, u32[]{:S(2)}) %collective-permute-start.8) | collective-permute-done | bytes 40992 | tf_op jit(solution)/shard_map/ppermute | solution.py:74
  27.0 0.6 %collective-permute-done.9.refs_2_ = bf16[16,1280]{1,0:T(8,128)(2,1)S(1)} collective-permute-done((bf16[16,1280]{1,0:T(8,128)(2,1)S(1)}, bf16[16,1280]{1,0:T(8,128)(2,1)S(1)}, u32[]{:S(2)}, u32[]{:S(2)}) %collective-permute-start.9) | collective-permute-done | bytes 40992 | tf_op jit(solution)/shard_map/ppermute | solution.py:74
  27.6 0.5 %collective-permute-done.10.refs_3_ = bf16[16,1280]{1,0:T(8,128)(2,1)S(1)} collective-permute-done((bf16[16,1280]{1,0:T(8,128)(2,1)S(1)}, bf16[16,1280]{1,0:T(8,128)(2,1)S(1)}, u32[]{:S(2)}, u32[]{:S(2)}) %collective-permute-start.10) | collective-permute-done | bytes 40992 | tf_op jit(solution)/shard_map/ppermute | solution.py:74
  28.1 1.1 %finish.1 = (bf16[16,512]{1,0:T(8,128)(2,1)}, bf16[16,2048]{1,0:T(8,128)(2,1)}) custom-call(bf16[256,128]{1,0:T(8,128)(2,1)S(1)} %get-tuple-element.28.query_ref, f32[16,1024]{1,0:T(8,128)S(1)} %get-tuple-element.42.refs_0_, bf16[16,1280]{1,0:T(8,128)(2,1)S(1)} %collective-permute-done.8.refs_1_, bf16[16,1280]{1,0:T(8,128)(2,1)S(1)} %collective-permute-done.9.refs_2_, ...), custom_call_target="tpu_custom_call" | custom-call | tf_op jit(solution)/shard_map/finish/pallas_call | solution.py:451
Async XLA Ops:
  0.6 11.3 %collective-permute-start.2 = (bf16[16,2048]{1,0:T(8,128)(2,1)}, bf16[16,2048]{1,0:T(8,128)(2,1)S(1)}, u32[]{:S(2)}, u32[]{:S(2)}) collective-permute-start(bf16[16,2048]{1,0:T(8,128)(2,1)} %bitcast.7), channel_id=1, source_target_pairs={{0,24},{4,28},{8,16},{12,20},{16,8},{20,12},{24,0},{28,4},{1,25},{... | collective-permute-start | bytes 196616 | tf_op jit(solution)/shard_map/ppermute | solution.py:74
  5.7 6.2 %collective-permute-start.1 = (bf16[16,2048]{1,0:T(8,128)(2,1)}, bf16[16,2048]{1,0:T(8,128)(2,1)S(1)}, u32[]{:S(2)}, u32[]{:S(2)}) collective-permute-start(bf16[16,2048]{1,0:T(8,128)(2,1)} %bitcast.8), channel_id=1, source_target_pairs={{0,16},{4,20},{8,24},{12,28},{16,0},{20,4},{24,8},{28,12},{1,17},{... | collective-permute-start | bytes 196616 | tf_op jit(solution)/shard_map/ppermute | solution.py:74
  5.8 6.2 %collective-permute-start = (bf16[16,2048]{1,0:T(8,128)(2,1)}, bf16[16,2048]{1,0:T(8,128)(2,1)S(1)}, u32[]{:S(2)}, u32[]{:S(2)}) collective-permute-start(bf16[16,2048]{1,0:T(8,128)(2,1)} %bitcast.9), channel_id=1, source_target_pairs={{0,8},{4,12},{8,0},{12,4},{16,24},{20,28},{24,16},{28,20},{1,9},{5... | collective-permute-start | bytes 196616 | tf_op jit(solution)/shard_map/ppermute | solution.py:74
  6.4 3.8 %collective-permute-start.4 = (bf16[256,16]{0,1:T(8,128)(2,1)}, bf16[256,16]{0,1:T(8,128)(2,1)S(1)}, u32[]{:S(2)}, u32[]{:S(2)}) collective-permute-start(bf16[256,16]{0,1:T(8,128)(2,1)} %param.11), channel_id=1, source_target_pairs={{0,4},{4,0},{8,12},{12,8},{16,20},{20,16},{24,28},{28,24},{1,5},{5... | collective-permute-start | bytes 24584 | tf_op jit(solution)/shard_map/ppermute | solution.py:74
  6.4 5.6 %collective-permute-start.3 = (bf16[256,2048]{1,0:T(8,128)(2,1)}, bf16[256,2048]{1,0:T(8,128)(2,1)S(1)}, u32[]{:S(2)}, u32[]{:S(2)}) collective-permute-start(bf16[256,2048]{1,0:T(8,128)(2,1)} %codes_hbm.1), channel_id=1, source_target_pairs={{0,4},{4,0},{8,12},{12,8},{16,20},{20,16},{24,28},{28,24},{1,5},{5... | collective-permute-start | bytes 3145736 | tf_op jit(solution)/shard_map/ppermute | solution.py:74
  6.9 5.1 %copy-start = (bf16[2,8,2048]{2,1,0:T(8,128)(2,1)S(1)}, bf16[2,8,2048]{2,1,0:T(8,128)(2,1)}, u32[]{:S(2)}) copy-start(bf16[2,8,2048]{2,1,0:T(8,128)(2,1)} %param.8) | copy-start | bytes 196612
  10.2 13.9 %collective-permute-start.11 = (bf16[272,128]{1,0:T(8,128)(2,1)S(1)}, bf16[272,128]{1,0:T(8,128)(2,1)S(1)}, u32[]{:S(2)}, u32[]{:S(2)}) collective-permute-start(bf16[272,128]{1,0:T(8,128)(2,1)S(1)} %get-tuple-element.47), channel_id=1, source_target_pairs={{0,1},{1,0},{2,3},{3,2},{4,5},{5,4},{6,7},{7,6},{8,9},{9,8},{10,11... | collective-permute-start | bytes 208904 | tf_op jit(solution)/shard_map/ppermute | solution.py:74
  13.4 6.5 %collective-permute-start.5 = (f32[16,512]{1,0:T(8,128)S(1)}, f32[16,512]{1,0:T(8,128)S(1)}, u32[]{:S(2)}, u32[]{:S(2)}) collective-permute-start(f32[16,512]{1,0:T(8,128)S(1)} %get-tuple-element.39), channel_id=1, source_target_pairs={{0,24},{4,28},{8,16},{12,20},{16,8},{20,12},{24,0},{28,4},{1,25},{... | collective-permute-start | bytes 98312 | tf_op jit(solution)/shard_map/ppermute | solution.py:74
  17.1 4.8 %collective-permute-start.6 = (f32[16,512]{1,0:T(8,128)S(1)}, f32[16,512]{1,0:T(8,128)S(1)}, u32[]{:S(2)}, u32[]{:S(2)}) collective-permute-start(f32[16,512]{1,0:T(8,128)S(1)} %get-tuple-element.40), channel_id=1, source_target_pairs={{0,16},{4,20},{8,24},{12,28},{16,0},{20,4},{24,8},{28,12},{1,17},{... | collective-permute-start | bytes 98312 | tf_op jit(solution)/shard_map/ppermute | solution.py:74
  17.1 4.8 %collective-permute-start.7 = (f32[16,512]{1,0:T(8,128)S(1)}, f32[16,512]{1,0:T(8,128)S(1)}, u32[]{:S(2)}, u32[]{:S(2)}) collective-permute-start(f32[16,512]{1,0:T(8,128)S(1)} %get-tuple-element.41), channel_id=1, source_target_pairs={{0,8},{4,12},{8,0},{12,4},{16,24},{20,28},{24,16},{28,20},{1,9},{5... | collective-permute-start | bytes 98312 | tf_op jit(solution)/shard_map/ppermute | solution.py:74
  17.9 7.7 %collective-permute-start.13 = (bf16[272,128]{1,0:T(8,128)(2,1)S(1)}, bf16[272,128]{1,0:T(8,128)(2,1)S(1)}, u32[]{:S(2)}, u32[]{:S(2)}) collective-permute-start(bf16[272,128]{1,0:T(8,128)(2,1)S(1)} %get-tuple-element.49), channel_id=1, source_target_pairs={{0,3},{1,2},{2,1},{3,0},{4,7},{5,6},{6,5},{7,4},{8,11},{9,10},{10,... | collective-permute-start | bytes 208904 | tf_op jit(solution)/shard_map/ppermute | solution.py:74
  19.9 5.7 %collective-permute-start.12 = (bf16[272,128]{1,0:T(8,128)(2,1)S(1)}, bf16[272,128]{1,0:T(8,128)(2,1)S(1)}, u32[]{:S(2)}, u32[]{:S(2)}) collective-permute-start(bf16[272,128]{1,0:T(8,128)(2,1)S(1)} %get-tuple-element.48), channel_id=1, source_target_pairs={{0,2},{1,3},{2,0},{3,1},{4,6},{5,7},{6,4},{7,5},{8,10},{9,11},{10,... | collective-permute-start | bytes 208904 | tf_op jit(solution)/shard_map/ppermute | solution.py:74
  22.0 5.0 %collective-permute-start.8 = (bf16[16,1280]{1,0:T(8,128)(2,1)S(1)}, bf16[16,1280]{1,0:T(8,128)(2,1)S(1)}, u32[]{:S(2)}, u32[]{:S(2)}) collective-permute-start(bf16[16,1280]{1,0:T(8,128)(2,1)S(1)} %get-tuple-element.43), channel_id=1, source_target_pairs={{0,3},{1,2},{2,1},{3,0},{4,7},{5,6},{6,5},{7,4},{8,11},{9,10},{10,... | collective-permute-start | bytes 122888 | tf_op jit(solution)/shard_map/ppermute | solution.py:74
  23.6 4.0 %collective-permute-start.9 = (bf16[16,1280]{1,0:T(8,128)(2,1)S(1)}, bf16[16,1280]{1,0:T(8,128)(2,1)S(1)}, u32[]{:S(2)}, u32[]{:S(2)}) collective-permute-start(bf16[16,1280]{1,0:T(8,128)(2,1)S(1)} %get-tuple-element.44), channel_id=1, source_target_pairs={{0,2},{1,3},{2,0},{3,1},{4,6},{5,7},{6,4},{7,5},{8,10},{9,11},{10,... | collective-permute-start | bytes 122888 | tf_op jit(solution)/shard_map/ppermute | solution.py:74
  24.1 4.0 %collective-permute-start.10 = (bf16[16,1280]{1,0:T(8,128)(2,1)S(1)}, bf16[16,1280]{1,0:T(8,128)(2,1)S(1)}, u32[]{:S(2)}, u32[]{:S(2)}) collective-permute-start(bf16[16,1280]{1,0:T(8,128)(2,1)S(1)} %get-tuple-element.45), channel_id=1, source_target_pairs={{0,1},{1,0},{2,3},{3,2},{4,5},{5,4},{6,7},{7,6},{8,9},{9,8},{10,11... | collective-permute-start | bytes 122888 | tf_op jit(solution)/shard_map/ppermute | solution.py:74
